TPU v7x, 32 devices: a whole 2x2x4 slice. The times are simulated.
32 devices in a mesh: frame: 8 (over z, core), row: 4 (over y, x).
Axes of the slice: x: 2, y: 2, z: 4, core: 2. Of those that a mesh axis runs over, the one named last changes fastest.
Arguments:
- tokens: bfloat16 [16, 8, 16, 16, 1024], P('frame', None, 'row'), may hold values from -6 to 6
- cotangent: bfloat16 [16, 8, 16, 16, 1024], P('frame', None, 'row'), may hold values from -6 to 6
- noise_levels: int32 [16, 8], P('frame'), may hold values from 0 to 1023
- frame_times: int32 [16, 8], P('frame'), may hold values from 0 to 23, as said below
- step_count: int32 [1], replicated, may hold values from 1 to 20
- qkv_master: float32 [1024, 3072], P(None, ('frame', 'row')), may hold values from -0.25 to 0.25
- qkv_momentum: float32 [1024, 3072], P(None, ('frame', 'row')), may hold values from -0.0012207031 to 0.0012207031
- out_master: float32 [1024, 1024], P(('frame', 'row')), may hold values from -1.25 to 1.25
- out_momentum: float32 [1024, 1024], P(('frame', 'row')), may hold values from -0.0012207031 to 0.0012207031
- up_master: float32 [1024, 4096], P(None, ('frame', 'row')), may hold values from -0.253125 to 0.253125
- up_momentum: float32 [1024, 4096], P(None, ('frame', 'row')), may hold values from -0.0012207031 to 0.0012207031
- down_master: float32 [4096, 1024], P(('frame', 'row')), may hold values from -0.09375 to 0.09375
- down_momentum: float32 [4096, 1024], P(('frame', 'row')), may hold values from -0.0012207031 to 0.0012207031
- ada_master: float32 [1024, 6144], P(None, ('frame', 'row')), may hold values from -0.1875 to 0.1875
- ada_first: float32 [1024, 6144], P(None, ('frame', 'row')), may hold values from -0.00015258789 to 0.00015258789
- ada_second: float32 [1024, 6144], P(None, ('frame', 'row')), may hold values from 1.5053373e-09 to 2.0071164e-08
- table_master: float32 [1024, 1024], P(('frame', 'row')), may hold values from -5 to 5
- table_first: float32 [1024, 1024], P(('frame', 'row')), may hold values from -0.00015258789 to 0.00015258789
- table_second: float32 [1024, 1024], P(('frame', 'row')), may hold values from 1.5053373e-09 to 2.0071164e-08
- bias_master: float32 [6144], P(('frame', 'row')), may hold values from -3 to 3
- bias_first: float32 [6144], P(('frame', 'row')), may hold values from -0.00015258789 to 0.00015258789
- bias_second: float32 [6144], P(('frame', 'row')), may hold values from 1.5053373e-09 to 2.0071164e-08
Outputs:
- block_out: bfloat16 [16, 8, 16, 16, 1024], P('frame', None, 'row')
- input_grad: float32 [16, 8, 16, 16, 1024], P('frame', None, 'row')
- grad_norm: float32 [1], replicated
- qkv_momentum_new: float32 [1024, 3072], P(None, ('frame', 'row'))
- qkv_master_new: float32 [1024, 3072], P(None, ('frame', 'row'))
- out_momentum_new: float32 [1024, 1024], P(('frame', 'row'))
- out_master_new: float32 [1024, 1024], P(('frame', 'row'))
- up_momentum_new: float32 [1024, 4096], P(None, ('frame', 'row'))
- up_master_new: float32 [1024, 4096], P(None, ('frame', 'row'))
- down_momentum_new: float32 [4096, 1024], P(('frame', 'row'))
- down_master_new: float32 [4096, 1024], P(('frame', 'row'))
- ada_first_new: float32 [1024, 6144], P(None, ('frame', 'row'))
- ada_second_new: float32 [1024, 6144], P(None, ('frame', 'row'))
- ada_master_new: float32 [1024, 6144], P(None, ('frame', 'row'))
- table_first_new: float32 [1024, 1024], P(('frame', 'row'))
- table_clipped: float32 [1024, 1024], P(('frame', 'row'))
- table_master_new: float32 [1024, 1024], P(('frame', 'row'))
- bias_first_new: float32 [6144], P(('frame', 'row'))
- bias_second_new: float32 [6144], P(('frame', 'row'))
- bias_master_new: float32 [6144], P(('frame', 'row'))
Inputs may be any that keep to these rules, and one draw needn't show every extreme that they name: `frame_times`: within each clip the times rise strictly; the first frame has time 0 and the last 23.
All inputs are finite; a program needn't handle non-finite values.
Results may differ from a plain program's by a relative error of at most 0.02.
The roundings to bfloat16 on the way count: a program that leaves them out, or rounds other values in their place, can miss the bound.
Values may be sent and summed in bfloat16 or wider, within the bound.
A program may use at most 384 MiB of HBM per device.

v0:
```python
import math

import jax
import jax.numpy as jnp
from jax import lax
from jax.sharding import PartitionSpec as P

D = 1024
HEADS = 16
HD = 64
FF = 4096


highest = lax.Precision.HIGHEST
newton_one = 3.4445
newton_two = -4.775
newton_three = 2.0315
momentum_decay = 0.95
muon_rate = 1.5
weight_decay = 0.01
beta_first = 0.9
beta_second = 0.95
adam_floor = 1e-08
norm_floor = 1e-06
clip_limit = 1.0
rotary_base = 10000.0
group_heads = 4


def layer_norm(values):
    centered = values - jnp.mean(values, axis=-1, keepdims=True)
    return centered * lax.rsqrt(jnp.mean(centered * centered, axis=-1, keepdims=True) + norm_floor)


def modulate(values, shift_part, scaling):
    return layer_norm(values) * (1.0 + scaling) + shift_part


def gelu_tanh(values):
    return jax.nn.gelu(values, approximate=True)


def rounded(values):
    return lax.optimization_barrier(values.astype(jnp.bfloat16)).astype(jnp.float32)


def rotary_angles(time_grid, row_grid, column_grid):
    quarter_pairs = HD // 4
    eighth_pairs = HD // 8
    time_rates = rotary_base ** (-jnp.arange(quarter_pairs, dtype=jnp.float32) / quarter_pairs)
    space_rates = rotary_base ** (-jnp.arange(eighth_pairs, dtype=jnp.float32) / eighth_pairs)
    return jnp.concatenate(
        [
            time_grid[..., None] * time_rates,
            row_grid[..., None] * space_rates,
            column_grid[..., None] * space_rates,
        ],
        axis=-1,
    )


def rotate(values, angles):
    paired = values.reshape(values.shape[:-1] + (values.shape[-1] // 2, 2))
    cosine = jnp.cos(angles)[..., None, :]
    sine = jnp.sin(angles)[..., None, :]
    first_part = paired[..., 0] * cosine - paired[..., 1] * sine
    second_part = paired[..., 0] * sine + paired[..., 1] * cosine
    return jnp.stack([first_part, second_part], axis=-1).reshape(values.shape)


def adam_update(grad_item, first, second, master, rate, clip_factor, step_value):
    clipped = clip_factor * grad_item
    first_new = beta_first * first + (1.0 - beta_first) * clipped
    second_new = beta_second * second + (1.0 - beta_second) * clipped * clipped
    first_fix = 1.0 - beta_first**step_value
    second_fix = 1.0 - beta_second**step_value
    master_new = master * (1.0 - rate * weight_decay) - rate * (first_new / first_fix) / (
        jnp.sqrt(second_new / second_fix) + adam_floor
    )
    return (first_new, second_new, master_new)


def per_device(
    tokens,
    cotangent,
    noise_levels,
    frame_times,
    step_count,
    qkv_master,
    qkv_momentum,
    out_master,
    out_momentum,
    up_master,
    up_momentum,
    down_master,
    down_momentum,
    ada_master,
    ada_first,
    ada_second,
    table_master,
    table_first,
    table_second,
    bias_master,
    bias_first,
    bias_second,
):
    low_type = jnp.bfloat16
    full_type = jnp.float32
    clip_count, frames, rows_dev, columns, model_width = tokens.shape
    seq_local = frames * rows_dev * columns
    row_devices = lax.axis_size("row")
    seq_full = seq_local * row_devices
    token_total = clip_count * seq_local
    frame_total = clip_count * frames
    attn_scale = 1.0 / math.sqrt(HD)
    shape_five = (clip_count, frames, rows_dev, columns, model_width)
    w_qkv, w_out, w_up, w_down, w_ada, w_table, w_bias = (
        lax.all_gather(qkv_master.astype(low_type), ("frame", "row"), axis=1, tiled=True),
        lax.all_gather(out_master.astype(low_type), ("frame", "row"), axis=0, tiled=True),
        lax.all_gather(up_master.astype(low_type), ("frame", "row"), axis=1, tiled=True),
        lax.all_gather(down_master.astype(low_type), ("frame", "row"), axis=0, tiled=True),
        lax.all_gather(ada_master.astype(low_type), ("frame", "row"), axis=1, tiled=True),
        lax.all_gather(table_master.astype(low_type), ("frame", "row"), axis=0, tiled=True),
        lax.all_gather(bias_master.astype(low_type), ("frame", "row"), axis=0, tiled=True),
    )
    level_flat = noise_levels.reshape(frame_total)
    level_hot = (
        level_flat[:, None] == jnp.arange(w_table.shape[0], dtype=jnp.int32)[None, :]
    ).astype(low_type)
    embedded = jnp.dot(level_hot, w_table, preferred_element_type=full_type)
    cond_low = jax.nn.silu(embedded).astype(low_type)
    modulation = jnp.dot(cond_low, w_ada, preferred_element_type=full_type) + w_bias.astype(
        full_type
    )
    mod_five = modulation.reshape(clip_count, frames, 1, 1, 6 * model_width)
    pieces = [
        mod_five[..., piece_index * model_width : (piece_index + 1) * model_width]
        for piece_index in range(6)
    ]
    shift_one, scale_one, gate_one, shift_two, scale_two, gate_two = pieces
    grid_shape = (clip_count, frames, rows_dev, columns)
    row_first = lax.axis_index("row") * rows_dev
    time_grid = jnp.broadcast_to(frame_times.astype(full_type)[:, :, None, None], grid_shape)
    row_grid = jnp.broadcast_to(
        (row_first + jnp.arange(rows_dev, dtype=jnp.int32)).astype(full_type)[None, None, :, None],
        grid_shape,
    )
    column_grid = jnp.broadcast_to(
        jnp.arange(columns, dtype=jnp.int32).astype(full_type)[None, None, None, :], grid_shape
    )
    angles = rotary_angles(time_grid, row_grid, column_grid).reshape(clip_count, seq_local, HD // 2)
    inputs_full = tokens.astype(full_type)
    hidden_one = (
        modulate(inputs_full, shift_one, scale_one)
        .astype(low_type)
        .reshape(token_total, model_width)
    )
    projected = jnp.dot(hidden_one, w_qkv, preferred_element_type=full_type).reshape(
        clip_count, seq_local, 3, HEADS, HD
    )
    queries = rotate(projected[:, :, 0], angles).astype(low_type)
    keys_rot = rotate(projected[:, :, 1], angles).astype(low_type)
    values_low = projected[:, :, 2].astype(low_type)
    keys_whole, values_whole = (
        lax.all_gather(keys_rot.reshape(shape_five), "row", axis=2, tiled=True),
        lax.all_gather(values_low.reshape(shape_five), "row", axis=2, tiled=True),
    )
    keys_seq = keys_whole.reshape(clip_count, seq_full, HEADS, HD)
    values_seq = values_whole.reshape(clip_count, seq_full, HEADS, HD)

    def attend_clip(operands):
        query_block, key_block, value_block = operands
        outputs = []
        log_totals = []
        for group_index in range(HEADS // group_heads):
            head_first = group_index * group_heads
            head_last = head_first + group_heads
            scores = (
                jnp.einsum(
                    "qhd,khd->hqk",
                    query_block[:, head_first:head_last],
                    key_block[:, head_first:head_last],
                    preferred_element_type=full_type,
                )
                * attn_scale
            )
            top_score = jnp.max(scores, axis=-1, keepdims=True)
            raised = jnp.exp(scores - top_score)
            total_weight = jnp.sum(raised, axis=-1, keepdims=True)
            prob_low = (raised / total_weight).astype(low_type)
            outputs.append(
                jnp.einsum(
                    "hqk,khd->qhd",
                    prob_low,
                    value_block[:, head_first:head_last],
                    preferred_element_type=full_type,
                )
            )
            log_totals.append((top_score + jnp.log(total_weight))[..., 0])
        return (jnp.concatenate(outputs, axis=1), jnp.concatenate(log_totals, axis=0))

    attended_full, log_total = lax.map(attend_clip, (queries, keys_seq, values_seq))
    attended = attended_full.astype(low_type).reshape(token_total, model_width)
    branch_one = jnp.dot(attended, w_out, preferred_element_type=full_type).reshape(shape_five)
    middle = inputs_full + gate_one * branch_one
    hidden_two = (
        modulate(middle, shift_two, scale_two).astype(low_type).reshape(token_total, model_width)
    )
    up_value = jnp.dot(hidden_two, w_up, preferred_element_type=full_type)
    activated = gelu_tanh(up_value).astype(low_type)
    branch_two = jnp.dot(activated, w_down, preferred_element_type=full_type).reshape(shape_five)
    block_out = (middle + gate_two * branch_two).astype(low_type)
    w_qkv, w_out, w_up, w_down, w_ada = (
        lax.all_gather(qkv_master.astype(low_type), ("frame", "row"), axis=1, tiled=True),
        lax.all_gather(out_master.astype(low_type), ("frame", "row"), axis=0, tiled=True),
        lax.all_gather(up_master.astype(low_type), ("frame", "row"), axis=1, tiled=True),
        lax.all_gather(down_master.astype(low_type), ("frame", "row"), axis=0, tiled=True),
        lax.all_gather(ada_master.astype(low_type), ("frame", "row"), axis=1, tiled=True),
    )
    upstream = cotangent.astype(full_type)
    d_branch_two = (upstream * gate_two).astype(low_type).reshape(token_total, model_width)
    d_gate_two = jnp.sum(upstream * branch_two, axis=(2, 3))
    grad_down = jnp.einsum("tf,td->fd", activated, d_branch_two, preferred_element_type=full_type)
    d_activated = jnp.einsum("td,fd->tf", d_branch_two, w_down, preferred_element_type=full_type)
    d_up = jax.vjp(gelu_tanh, up_value)[1](d_activated)[0].astype(low_type)
    grad_up = jnp.einsum("td,tf->df", hidden_two, d_up, preferred_element_type=full_type)
    d_hidden_two = jnp.einsum("tf,df->td", d_up, w_up, preferred_element_type=full_type).reshape(
        shape_five
    )
    d_middle_part, d_shift_two, d_scale_two = jax.vjp(modulate, middle, shift_two, scale_two)[1](
        d_hidden_two
    )
    d_middle = upstream + d_middle_part
    d_gate_one = jnp.sum(d_middle * branch_one, axis=(2, 3))
    d_branch_one = (d_middle * gate_one).astype(low_type).reshape(token_total, model_width)
    grad_out = jnp.einsum("td,te->de", attended, d_branch_one, preferred_element_type=full_type)
    d_attended = (
        jnp.einsum("te,de->td", d_branch_one, w_out, preferred_element_type=full_type)
        .astype(low_type)
        .reshape(clip_count, seq_local, HEADS, HD)
    )

    def attend_back(operands):
        query_block, key_block, value_block, log_block, grad_block = operands
        query_parts = []
        key_parts = []
        value_parts = []
        for group_index in range(HEADS // group_heads):
            head_first = group_index * group_heads
            head_last = head_first + group_heads
            query_group = query_block[:, head_first:head_last]
            key_group = key_block[:, head_first:head_last]
            value_group = value_block[:, head_first:head_last]
            grad_group = grad_block[:, head_first:head_last]
            scores = (
                jnp.einsum("qhd,khd->hqk", query_group, key_group, preferred_element_type=full_type)
                * attn_scale
            )
            prob_full = jnp.exp(scores - log_block[head_first:head_last][..., None])
            grad_prob = jnp.einsum(
                "qhd,khd->hqk", grad_group, value_group, preferred_element_type=full_type
            )
            inner_sum = jnp.sum(prob_full * grad_prob, axis=-1, keepdims=True)
            grad_scores = (prob_full * (grad_prob - inner_sum)).astype(low_type)
            query_parts.append(
                jnp.einsum("hqk,khd->qhd", grad_scores, key_group, preferred_element_type=full_type)
                * attn_scale
            )
            key_parts.append(
                jnp.einsum(
                    "hqk,qhd->khd", grad_scores, query_group, preferred_element_type=full_type
                )
                * attn_scale
            )
            value_parts.append(
                jnp.einsum(
                    "hqk,qhd->khd",
                    prob_full.astype(low_type),
                    grad_group,
                    preferred_element_type=full_type,
                )
            )
        return (
            jnp.concatenate(query_parts, axis=1),
            jnp.concatenate(key_parts, axis=1),
            jnp.concatenate(value_parts, axis=1),
        )

    grad_query, grad_key, grad_value = lax.map(
        attend_back, (queries, keys_seq, values_seq, log_total, d_attended)
    )
    gathered_shape = (clip_count, frames, rows_dev * row_devices, columns, model_width)
    key_sums, value_sums = (
        lax.psum_scatter(
            grad_key.reshape(gathered_shape).astype(jnp.bfloat16),
            "row",
            scatter_dimension=2,
            tiled=True,
        ).astype(jnp.float32),
        lax.psum_scatter(
            grad_value.reshape(gathered_shape).astype(jnp.bfloat16),
            "row",
            scatter_dimension=2,
            tiled=True,
        ).astype(jnp.float32),
    )
    d_queries = rounded(grad_query)
    d_keys = rounded(key_sums).reshape(clip_count, seq_local, HEADS, HD)
    d_values = rounded(value_sums).reshape(clip_count, seq_local, HEADS, HD)
    d_projected = (
        jnp.stack([rotate(d_queries, -angles), rotate(d_keys, -angles), d_values], axis=2)
        .astype(low_type)
        .reshape(token_total, 3 * model_width)
    )
    grad_qkv = jnp.einsum("td,te->de", hidden_one, d_projected, preferred_element_type=full_type)
    d_hidden_one = jnp.einsum(
        "te,de->td", d_projected, w_qkv, preferred_element_type=full_type
    ).reshape(shape_five)
    d_input_part, d_shift_one, d_scale_one = jax.vjp(modulate, inputs_full, shift_one, scale_one)[
        1
    ](d_hidden_one)
    input_grad = d_middle + d_input_part
    frame_shape = (frame_total, model_width)
    d_modulation = jnp.concatenate(
        [
            d_shift_one.reshape(frame_shape),
            d_scale_one.reshape(frame_shape),
            d_gate_one.reshape(frame_shape),
            d_shift_two.reshape(frame_shape),
            d_scale_two.reshape(frame_shape),
            d_gate_two.reshape(frame_shape),
        ],
        axis=1,
    )
    mod_mine = (
        lax.psum_scatter(d_modulation.astype(jnp.bfloat16), "row", scatter_dimension=0, tiled=True)
        .astype(jnp.float32)
        .astype(low_type)
    )
    frames_mine = frame_total // row_devices
    first_frame = lax.axis_index("row") * frames_mine
    cond_mine = lax.dynamic_slice_in_dim(cond_low, first_frame, frames_mine, 0)
    embedded_mine = lax.dynamic_slice_in_dim(embedded, first_frame, frames_mine, 0)
    hot_mine = lax.dynamic_slice_in_dim(level_hot, first_frame, frames_mine, 0)
    grad_ada = jnp.einsum("fd,fe->de", cond_mine, mod_mine, preferred_element_type=full_type)
    grad_bias = jnp.sum(mod_mine.astype(full_type), axis=0)
    d_cond = jnp.einsum("fe,de->fd", mod_mine, w_ada, preferred_element_type=full_type)
    d_embedded = jax.vjp(jax.nn.silu, embedded_mine)[1](d_cond)[0]
    grad_table = jnp.einsum("fl,fd->ld", hot_mine.astype(full_type), d_embedded, precision=highest)
    g_qkv, g_out, g_up, g_down, g_ada, g_table, g_bias = (
        lax.psum_scatter(grad_qkv, ("frame", "row"), scatter_dimension=1, tiled=True),
        lax.psum_scatter(grad_out, ("frame", "row"), scatter_dimension=0, tiled=True),
        lax.psum_scatter(grad_up, ("frame", "row"), scatter_dimension=1, tiled=True),
        lax.psum_scatter(grad_down, ("frame", "row"), scatter_dimension=0, tiled=True),
        lax.psum_scatter(grad_ada, ("frame", "row"), scatter_dimension=1, tiled=True),
        lax.psum_scatter(grad_table, ("frame", "row"), scatter_dimension=0, tiled=True),
        lax.psum_scatter(grad_bias, ("frame", "row"), scatter_dimension=0, tiled=True),
    )
    muon_grads = (g_qkv, g_out, g_up, g_down)
    muon_moments = (qkv_momentum, out_momentum, up_momentum, down_momentum)
    muon_masters = (qkv_master, out_master, up_master, down_master)
    flipped = (True, False, True, False)
    factors = (math.sqrt(3.0), 1.0, math.sqrt(FF / D), math.sqrt(FF / D))
    adam_local = jnp.sum(g_ada * g_ada) + jnp.sum(g_table * g_table) + jnp.sum(g_bias * g_bias)
    local_total = adam_local + sum((jnp.sum(item * item) for item in muon_grads))
    norm_value = jnp.sqrt(lax.psum(local_total, ("frame", "row")))
    clip_factor = jnp.minimum(1.0, clip_limit / (norm_value + 1e-06))
    clipped_all = [clip_factor * item for item in muon_grads]
    moments_new = [
        momentum_decay * moment + clipped for moment, clipped in zip(muon_moments, clipped_all)
    ]
    updates = [
        clipped + momentum_decay * moment for clipped, moment in zip(clipped_all, moments_new)
    ]
    frob_parts = lax.psum(
        (
            jnp.sum(updates[0] * updates[0]),
            jnp.sum(updates[1] * updates[1]),
            jnp.sum(updates[2] * updates[2]),
            jnp.sum(updates[3] * updates[3]),
        ),
        ("frame", "row"),
    )
    frob_squares = jnp.stack(frob_parts)
    blocks = []
    for member in range(4):
        scaled = updates[member] / (jnp.sqrt(frob_squares[member]) + 1e-07)
        blocks.append(scaled.T if flipped[member] else scaled)
    for newton_step in range(5):
        gram_terms = [jnp.dot(block.T, block, precision=highest) for block in blocks]
        gram_shares = (
            lax.psum_scatter(gram_terms[0], ("frame", "row"), scatter_dimension=0, tiled=True),
            lax.psum_scatter(gram_terms[1], ("frame", "row"), scatter_dimension=0, tiled=True),
            lax.psum_scatter(gram_terms[2], ("frame", "row"), scatter_dimension=0, tiled=True),
            lax.psum_scatter(gram_terms[3], ("frame", "row"), scatter_dimension=0, tiled=True),
        )
        grams = (
            lax.all_gather(
                gram_shares[0].astype(jnp.bfloat16), ("frame", "row"), axis=0, tiled=True
            ).astype(jnp.float32),
            lax.all_gather(
                gram_shares[1].astype(jnp.bfloat16), ("frame", "row"), axis=0, tiled=True
            ).astype(jnp.float32),
            lax.all_gather(
                gram_shares[2].astype(jnp.bfloat16), ("frame", "row"), axis=0, tiled=True
            ).astype(jnp.float32),
            lax.all_gather(
                gram_shares[3].astype(jnp.bfloat16), ("frame", "row"), axis=0, tiled=True
            ).astype(jnp.float32),
        )
        next_blocks = []
        for member in range(4):
            product = jnp.dot(blocks[member], grams[member], precision=highest)
            next_blocks.append(
                newton_one * blocks[member]
                + newton_two * product
                + newton_three * jnp.dot(product, grams[member], precision=highest)
            )
        blocks = next_blocks
    masters_new = []
    for member in range(4):
        ortho = blocks[member].T if flipped[member] else blocks[member]
        masters_new.append(
            muon_masters[member] * (1.0 - muon_rate * weight_decay)
            - muon_rate * factors[member] * ortho
        )
    step_value = step_count.astype(full_type)[0]
    ada_first_new, ada_second_new, ada_master_new = adam_update(
        g_ada, ada_first, ada_second, ada_master, 0.03, clip_factor, step_value
    )
    table_clipped = clip_factor * g_table
    table_first_new, table_second_new, table_master_new = adam_update(
        g_table, table_first, table_second, table_master, 0.5, clip_factor, step_value
    )
    bias_first_new, bias_second_new, bias_master_new = adam_update(
        g_bias, bias_first, bias_second, bias_master, 0.5, clip_factor, step_value
    )
    return (
        block_out,
        input_grad,
        norm_value.reshape(1),
        moments_new[0],
        masters_new[0],
        moments_new[1],
        masters_new[1],
        moments_new[2],
        masters_new[2],
        moments_new[3],
        masters_new[3],
        ada_first_new,
        ada_second_new,
        ada_master_new,
        table_first_new,
        table_clipped,
        table_master_new,
        bias_first_new,
        bias_second_new,
        bias_master_new,
    )


def solution(mesh):
    return jax.shard_map(
        per_device,
        mesh=mesh,
        in_specs=(
            P("frame", None, "row", None, None),
            P("frame", None, "row", None, None),
            P("frame", None),
            P("frame", None),
            P(),
            P(None, ("frame", "row")),
            P(None, ("frame", "row")),
            P(("frame", "row"), None),
            P(("frame", "row"), None),
            P(None, ("frame", "row")),
            P(None, ("frame", "row")),
            P(("frame", "row"), None),
            P(("frame", "row"), None),
            P(None, ("frame", "row")),
            P(None, ("frame", "row")),
            P(None, ("frame", "row")),
            P(("frame", "row"), None),
            P(("frame", "row"), None),
            P(("frame", "row"), None),
            P(("frame", "row")),
            P(("frame", "row")),
            P(("frame", "row")),
        ),
        out_specs=(
            P("frame", None, "row", None, None),
            P("frame", None, "row", None, None),
            P(),
            P(None, ("frame", "row")),
            P(None, ("frame", "row")),
            P(("frame", "row"), None),
            P(("frame", "row"), None),
            P(None, ("frame", "row")),
            P(None, ("frame", "row")),
            P(("frame", "row"), None),
            P(("frame", "row"), None),
            P(None, ("frame", "row")),
            P(None, ("frame", "row")),
            P(None, ("frame", "row")),
            P(("frame", "row"), None),
            P(("frame", "row"), None),
            P(("frame", "row"), None),
            P(("frame", "row")),
            P(("frame", "row")),
            P(("frame", "row")),
        ),
        check_vma=False,
    )
```

profile of v0, /device:TPU:8, one launch (start us, length us, event | category | flops | bytes accessed | tf_op | source)
XLA Modules:
  0.0 7277.5 jit_solution(16568473029458819093)
XLA Ops:
  70.9 96.0 %all-gather.31.cloned.1.call-done = bf16[1024,6144]{0,1:T(8,128)(2,1)} async-done(((bf16[1024,192]{0,1:T(8,128)(2,1)}), bf16[1024,6144]{0,1:T(8,128)(2,1)}) %all-gather.31.cloned.1.call-update) | async-done | bytes 12582928 | tf_op jit(solution)/shard_map/all_gather | solution.py:122
  500.3 96.6 %while.26 = (s32[]{:T(128)}, bf16[2,512,16,64]{1,3,2,0:T(8,128)(2,1)S(1)}, f32[2,16,512]{2,1,0:T(8,128)}, bf16[2,2048,16,64]{1,3,2,0:T(8,128)(2,1)}, bf16[2,512,...) while((s32[]{:T(128)}, bf16[2,512,16,64]{1,3,2,0:T(8,128)(2,1)S(1)}, ...), condition=%wide.region_11.12_spmd, body=%wide.region_2.11_spmd.sunk | while | flops 4450172928 | bytes 246743184 | solution.py:202
  765.4 390.2 %while.27 = (s32[]{:T(128)}, bf16[2,512,16,64]{1,3,2,0:T(8,128)(2,1)}, bf16[2,2048,16,64]{1,3,2,0:T(8,128)(2,1)}, bf16[2,2048,16,64]{1,3,2,0:T(8,128)(2,1)}, bf1...) while((s32[]{:T(128)}, ...), condition=%wide.region_21.22_spmd, body=%wide.region_16.21_spmd.sunk | while | flops 10981728256 | bytes 674464128 | solution.py:289
  1250.5 299.3 %all-reduce.12.cloned.1.call-done = (bf16[2,8,16,16,1024]{4,3,2,1,0:T(8,128)(2,1)}, bf16[2,8,16,16,1024]{4,3,2,1,0:T(8,128)(2,1)}) async-done(((bf16[2,8,16,16,1024]{4,3,2,1,0:T(8,128)(2,1)}, bf16[2,8,16,16,1024]{4,3,2,1,0:T(8,128)(2,1)}), (bf16[2,8,16,16,1024]{4,3,2,1,0:T(8,128)(2,1)}, bf16[2,8,16,16,1024]{4,3,2,1,0:T(8,128)(2,1)})) %all-reduce.12.cloned.1.call-update) | async-done | bytes 16777232
  1920.9 89.3 %reduce-scatter.35.cloned.1.call-done = f32[32,1024]{1,0:T(8,128)} async-done(((f32[1024,1024]{1,0:T(8,128)}), f32[32,1024]{1,0:T(8,128)}) %reduce-scatter.35.cloned.1.call-update) | async-done | bytes 131088 | tf_op jit(solution)/shard_map/reduce_scatter | solution.py:356
  2011.8 168.7 %reduce-scatter.37.cloned.1.call-done = f32[1024,96]{0,1:T(8,128)} async-done(((f32[1024,3072]{0,1:T(8,128)}), f32[1024,96]{0,1:T(8,128)}) %reduce-scatter.37.cloned.1.call-update) | async-done | bytes 393232 | tf_op jit(solution)/shard_map/reduce_scatter | solution.py:351
  2183.6 356.5 %reduce-scatter.41.cloned.1.call-done = f32[1024,128]{1,0:T(8,128)} async-done(((f32[1024,4096]{1,0:T(8,128)}), f32[1024,128]{1,0:T(8,128)}) %reduce-scatter.41.cloned.1.call-update) | async-done | bytes 524304 | tf_op jit(solution)/shard_map/reduce_scatter | solution.py:353
  2542.5 358.8 %reduce-scatter.43.cloned.1.call-done = f32[128,1024]{0,1:T(8,128)} async-done(((f32[4096,1024]{0,1:T(8,128)}), f32[128,1024]{0,1:T(8,128)}) %reduce-scatter.43.cloned.1.call-update) | async-done | bytes 524304 | tf_op jit(solution)/shard_map/reduce_scatter | solution.py:354
  2903.9 251.6 %reduce-scatter.33.cloned.1.call-done = f32[1024,192]{0,1:T(8,128)} async-done(((f32[1024,6144]{0,1:T(8,128)}), f32[1024,192]{0,1:T(8,128)}) %reduce-scatter.33.cloned.1.call-update) | async-done | bytes 786448 | tf_op jit(solution)/shard_map/reduce_scatter | solution.py:355
  3270.1 113.7 %reduce-scatter.75.cloned.1.call-done = f32[32,1024]{1,0:T(8,128)} async-done(((f32[1024,1024]{1,0:T(8,128)}), f32[32,1024]{1,0:T(8,128)}) %reduce-scatter.75.cloned.1.call-update) | async-done | bytes 131088 | tf_op jit(solution)/shard_map/reduce_scatter | solution.py:395
  3385.5 139.4 %reduce-scatter.65.cloned.1.call-done = f32[32,1024]{1,0:T(8,128)} async-done(((f32[1024,1024]{1,0:T(8,128)}), f32[32,1024]{1,0:T(8,128)}) %reduce-scatter.65.cloned.1.call-update) | async-done | bytes 131088 | tf_op jit(solution)/shard_map/reduce_scatter | solution.py:394
  3526.5 140.1 %reduce-scatter.55.cloned.1.call-done = f32[32,1024]{1,0:T(8,128)} async-done(((f32[1024,1024]{1,0:T(8,128)}), f32[32,1024]{1,0:T(8,128)}) %reduce-scatter.55.cloned.1.call-update) | async-done | bytes 131088 | tf_op jit(solution)/shard_map/reduce_scatter | solution.py:393
  3668.2 140.5 %reduce-scatter.45.cloned.1.call-done = f32[32,1024]{1,0:T(8,128)} async-done(((f32[1024,1024]{1,0:T(8,128)}), f32[32,1024]{1,0:T(8,128)}) %reduce-scatter.45.cloned.1.call-update) | async-done | bytes 131088 | tf_op jit(solution)/shard_map/reduce_scatter | solution.py:392
  3810.7 65.6 all-gather.75.cloned.1.call-done
  4062.3 122.8 %reduce-scatter.77.cloned.1.call-done = f32[32,1024]{1,0:T(8,128)} async-done(((f32[1024,1024]{1,0:T(8,128)}), f32[32,1024]{1,0:T(8,128)}) %reduce-scatter.77.cloned.1.call-update) | async-done | bytes 131088 | tf_op jit(solution)/shard_map/reduce_scatter | solution.py:395
  4186.7 140.3 %reduce-scatter.67.cloned.1.call-done = f32[32,1024]{1,0:T(8,128)} async-done(((f32[1024,1024]{1,0:T(8,128)}), f32[32,1024]{1,0:T(8,128)}) %reduce-scatter.67.cloned.1.call-update) | async-done | bytes 131088 | tf_op jit(solution)/shard_map/reduce_scatter | solution.py:394
  4328.7 140.4 %reduce-scatter.57.cloned.1.call-done = f32[32,1024]{1,0:T(8,128)} async-done(((f32[1024,1024]{1,0:T(8,128)}), f32[32,1024]{1,0:T(8,128)}) %reduce-scatter.57.cloned.1.call-update) | async-done | bytes 131088 | tf_op jit(solution)/shard_map/reduce_scatter | solution.py:393
  4470.7 140.1 %reduce-scatter.47.cloned.1.call-done = f32[32,1024]{1,0:T(8,128)} async-done(((f32[1024,1024]{1,0:T(8,128)}), f32[32,1024]{1,0:T(8,128)}) %reduce-scatter.47.cloned.1.call-update) | async-done | bytes 131088 | tf_op jit(solution)/shard_map/reduce_scatter | solution.py:392
  4612.6 66.1 all-gather.77.cloned.1.call-done
  4864.7 122.9 %reduce-scatter.79.cloned.1.call-done = f32[32,1024]{1,0:T(8,128)} async-done(((f32[1024,1024]{1,0:T(8,128)}), f32[32,1024]{1,0:T(8,128)}) %reduce-scatter.79.cloned.1.call-update) | async-done | bytes 131088 | tf_op jit(solution)/shard_map/reduce_scatter | solution.py:395
  4989.2 140.2 %reduce-scatter.69.cloned.1.call-done = f32[32,1024]{1,0:T(8,128)} async-done(((f32[1024,1024]{1,0:T(8,128)}), f32[32,1024]{1,0:T(8,128)}) %reduce-scatter.69.cloned.1.call-update) | async-done | bytes 131088 | tf_op jit(solution)/shard_map/reduce_scatter | solution.py:394
  5131.0 140.1 %reduce-scatter.59.cloned.1.call-done = f32[32,1024]{1,0:T(8,128)} async-done(((f32[1024,1024]{1,0:T(8,128)}), f32[32,1024]{1,0:T(8,128)}) %reduce-scatter.59.cloned.1.call-update) | async-done | bytes 131088 | tf_op jit(solution)/shard_map/reduce_scatter | solution.py:393
  5272.7 141.0 %reduce-scatter.49.cloned.1.call-done = f32[32,1024]{1,0:T(8,128)} async-done(((f32[1024,1024]{1,0:T(8,128)}), f32[32,1024]{1,0:T(8,128)}) %reduce-scatter.49.cloned.1.call-update) | async-done | bytes 131088 | tf_op jit(solution)/shard_map/reduce_scatter | solution.py:392
  5668.1 121.2 %reduce-scatter.81.cloned.1.call-done = f32[32,1024]{1,0:T(8,128)} async-done(((f32[1024,1024]{1,0:T(8,128)}), f32[32,1024]{1,0:T(8,128)}) %reduce-scatter.81.cloned.1.call-update) | async-done | bytes 131088 | tf_op jit(solution)/shard_map/reduce_scatter | solution.py:395
  5790.9 140.5 %reduce-scatter.71.cloned.1.call-done = f32[32,1024]{1,0:T(8,128)} async-done(((f32[1024,1024]{1,0:T(8,128)}), f32[32,1024]{1,0:T(8,128)}) %reduce-scatter.71.cloned.1.call-update) | async-done | bytes 131088 | tf_op jit(solution)/shard_map/reduce_scatter | solution.py:394
  5933.0 139.4 %reduce-scatter.61.cloned.1.call-done = f32[32,1024]{1,0:T(8,128)} async-done(((f32[1024,1024]{1,0:T(8,128)}), f32[32,1024]{1,0:T(8,128)}) %reduce-scatter.61.cloned.1.call-update) | async-done | bytes 131088 | tf_op jit(solution)/shard_map/reduce_scatter | solution.py:393
  6074.1 140.1 %reduce-scatter.51.cloned.1.call-done = f32[32,1024]{1,0:T(8,128)} async-done(((f32[1024,1024]{1,0:T(8,128)}), f32[32,1024]{1,0:T(8,128)}) %reduce-scatter.51.cloned.1.call-update) | async-done | bytes 131088 | tf_op jit(solution)/shard_map/reduce_scatter | solution.py:392
  6216.0 66.1 all-gather.81.cloned.1.call-done
  6469.2 120.8 %reduce-scatter.83.cloned.1.call-done = f32[32,1024]{1,0:T(8,128)} async-done(((f32[1024,1024]{1,0:T(8,128)}), f32[32,1024]{1,0:T(8,128)}) %reduce-scatter.83.cloned.1.call-update) | async-done | bytes 131088 | tf_op jit(solution)/shard_map/reduce_scatter | solution.py:395
  6591.7 140.2 %reduce-scatter.73.cloned.1.call-done = f32[32,1024]{1,0:T(8,128)} async-done(((f32[1024,1024]{1,0:T(8,128)}), f32[32,1024]{1,0:T(8,128)}) %reduce-scatter.73.cloned.1.call-update) | async-done | bytes 131088 | tf_op jit(solution)/shard_map/reduce_scatter | solution.py:394
  6733.5 140.3 %reduce-scatter.63.cloned.1.call-done = f32[32,1024]{1,0:T(8,128)} async-done(((f32[1024,1024]{1,0:T(8,128)}), f32[32,1024]{1,0:T(8,128)}) %reduce-scatter.63.cloned.1.call-update) | async-done | bytes 131088 | tf_op jit(solution)/shard_map/reduce_scatter | solution.py:393
  6875.6 140.0 %reduce-scatter.53.cloned.1.call-done = f32[32,1024]{1,0:T(8,128)} async-done(((f32[1024,1024]{1,0:T(8,128)}), f32[32,1024]{1,0:T(8,128)}) %reduce-scatter.53.cloned.1.call-update) | async-done | bytes 131088 | tf_op jit(solution)/shard_map/reduce_scatter | solution.py:392
  (691 shorter events, 2720.5 us)
Async XLA Ops:
  356.7 1193.2 %all-reduce.12.cloned.1.call-start = ((), (), s32[]{:S(2)}) async-start(), calls=%async_computation.81 | async-start | bytes 33554432
  1241.4 494.2 %all-reduce.10.cloned.1.call-start = ((), (), s32[]{:S(2)}) async-start(), calls=%async_computation.80 | async-start | bytes 393216
  1769.9 770.1 %reduce-scatter.41.cloned.1.call-start = ((), (), s32[]{:S(2)}) async-start(), calls=%async_computation.38 | async-start | bytes 17301504 | tf_op jit(solution)/shard_map/reduce_scatter | solution.py:353
  1786.1 1115.2 %reduce-scatter.43.cloned.1.call-start = ((), (), s32[]{:S(2)}) async-start(), calls=%async_computation.39 | async-start | bytes 17301504 | tf_op jit(solution)/shard_map/reduce_scatter | solution.py:354
  1803.8 1351.6 %reduce-scatter.33.cloned.1.call-start = ((), (), s32[]{:S(2)}) async-start(), calls=%async_computation.34 | async-start | bytes 25952256 | tf_op jit(solution)/shard_map/reduce_scatter | solution.py:355
  1815.7 1568.2 %reduce-scatter.75.cloned.1.call-start = ((), (), s32[]{:S(2)}) async-start(), calls=%async_computation.70 | async-start | bytes 4325376 | tf_op jit(solution)/shard_map/reduce_scatter | solution.py:395
  3264.1 544.6 %reduce-scatter.45.cloned.1.call-start = ((), (), s32[]{:S(2)}) async-start(), calls=%async_computation.40 | async-start | bytes 4325376 | tf_op jit(solution)/shard_map/reduce_scatter | solution.py:392
  3270.1 606.2 %all-gather.75.cloned.1.call-start = ((), (), s32[]{:S(2)}) async-start(), calls=%async_computation.71 | async-start | bytes 2162688 | tf_op jit(solution)/shard_map/all_gather | solution.py:407
  3385.4 549.6 %all-gather.65.cloned.1.call-start = ((), (), s32[]{:S(2)}) async-start(), calls=%async_computation.61 | async-start | bytes 2162688 | tf_op jit(solution)/shard_map/all_gather | solution.py:404
  3526.5 467.2 %all-gather.55.cloned.1.call-start = ((), (), s32[]{:S(2)}) async-start(), calls=%async_computation.51 | async-start | bytes 2162688 | tf_op jit(solution)/shard_map/all_gather | solution.py:401
  3888.1 438.9 %reduce-scatter.67.cloned.1.call-start = ((), (), s32[]{:S(2)}) async-start(), calls=%async_computation.62 | async-start | bytes 4325376 | tf_op jit(solution)/shard_map/reduce_scatter | solution.py:394
  3947.8 521.3 %reduce-scatter.57.cloned.1.call-start = ((), (), s32[]{:S(2)}) async-start(), calls=%async_computation.52 | async-start | bytes 4325376 | tf_op jit(solution)/shard_map/reduce_scatter | solution.py:393
  4004.3 606.5 %reduce-scatter.47.cloned.1.call-start = ((), (), s32[]{:S(2)}) async-start(), calls=%async_computation.42 | async-start | bytes 4325376 | tf_op jit(solution)/shard_map/reduce_scatter | solution.py:392
  4062.2 616.5 %all-gather.77.cloned.1.call-start = ((), (), s32[]{:S(2)}) async-start(), calls=%async_computation.73 | async-start | bytes 2162688 | tf_op jit(solution)/shard_map/all_gather | solution.py:407
  4186.7 550.6 %all-gather.67.cloned.1.call-start = ((), (), s32[]{:S(2)}) async-start(), calls=%async_computation.63 | async-start | bytes 2162688 | tf_op jit(solution)/shard_map/all_gather | solution.py:404
  4328.6 467.3 %all-gather.57.cloned.1.call-start = ((), (), s32[]{:S(2)}) async-start(), calls=%async_computation.53 | async-start | bytes 2162688 | tf_op jit(solution)/shard_map/all_gather | solution.py:401
  4751.7 519.5 %reduce-scatter.59.cloned.1.call-start = ((), (), s32[]{:S(2)}) async-start(), calls=%async_computation.54 | async-start | bytes 4325376 | tf_op jit(solution)/shard_map/reduce_scatter | solution.py:393
  4806.5 607.2 %reduce-scatter.49.cloned.1.call-start = ((), (), s32[]{:S(2)}) async-start(), calls=%async_computation.44 | async-start | bytes 4325376 | tf_op jit(solution)/shard_map/reduce_scatter | solution.py:392
  4864.6 616.3 %all-gather.79.cloned.1.call-start = ((), (), s32[]{:S(2)}) async-start(), calls=%async_computation.75 | async-start | bytes 2162688 | tf_op jit(solution)/shard_map/all_gather | solution.py:407
  4989.1 550.5 %all-gather.69.cloned.1.call-start = ((), (), s32[]{:S(2)}) async-start(), calls=%async_computation.65 | async-start | bytes 2162688 | tf_op jit(solution)/shard_map/all_gather | solution.py:404
  5130.9 467.3 %all-gather.59.cloned.1.call-start = ((), (), s32[]{:S(2)}) async-start(), calls=%async_computation.55 | async-start | bytes 2162688 | tf_op jit(solution)/shard_map/all_gather | solution.py:401
  5493.7 437.7 %reduce-scatter.71.cloned.1.call-start = ((), (), s32[]{:S(2)}) async-start(), calls=%async_computation.66 | async-start | bytes 4325376 | tf_op jit(solution)/shard_map/reduce_scatter | solution.py:394
  5553.4 519.0 %reduce-scatter.61.cloned.1.call-start = ((), (), s32[]{:S(2)}) async-start(), calls=%async_computation.56 | async-start | bytes 4325376 | tf_op jit(solution)/shard_map/reduce_scatter | solution.py:393
  5608.9 605.3 %reduce-scatter.51.cloned.1.call-start = ((), (), s32[]{:S(2)}) async-start(), calls=%async_computation.46 | async-start | bytes 4325376 | tf_op jit(solution)/shard_map/reduce_scatter | solution.py:392
  5668.1 614.1 %all-gather.81.cloned.1.call-start = ((), (), s32[]{:S(2)}) async-start(), calls=%async_computation.77 | async-start | bytes 2162688 | tf_op jit(solution)/shard_map/all_gather | solution.py:407
  5790.9 549.8 %all-gather.71.cloned.1.call-start = ((), (), s32[]{:S(2)}) async-start(), calls=%async_computation.67 | async-start | bytes 2162688 | tf_op jit(solution)/shard_map/all_gather | solution.py:404
  5933.0 466.3 %all-gather.61.cloned.1.call-start = ((), (), s32[]{:S(2)}) async-start(), calls=%async_computation.57 | async-start | bytes 2162688 | tf_op jit(solution)/shard_map/all_gather | solution.py:401
  6355.4 518.4 %reduce-scatter.63.cloned.1.call-start = ((), (), s32[]{:S(2)}) async-start(), calls=%async_computation.58 | async-start | bytes 4325376 | tf_op jit(solution)/shard_map/reduce_scatter | solution.py:393
  6409.9 605.8 %reduce-scatter.53.cloned.1.call-start = ((), (), s32[]{:S(2)}) async-start(), calls=%async_computation.48 | async-start | bytes 4325376 | tf_op jit(solution)/shard_map/reduce_scatter | solution.py:392
  6469.2 614.1 %all-gather.83.cloned.1.call-start = ((), (), s32[]{:S(2)}) async-start(), calls=%async_computation.79 | async-start | bytes 2162688 | tf_op jit(solution)/shard_map/all_gather | solution.py:407
  6591.6 549.8 %all-gather.73.cloned.1.call-start = ((), (), s32[]{:S(2)}) async-start(), calls=%async_computation.69 | async-start | bytes 2162688 | tf_op jit(solution)/shard_map/all_gather | solution.py:404
  6733.5 466.7 %all-gather.63.cloned.1.call-start = ((), (), s32[]{:S(2)}) async-start(), calls=%async_computation.59 | async-start | bytes 2162688 | tf_op jit(solution)/shard_map/all_gather | solution.py:401
  (137 other events, 21056.1 us)
Sparse Core Ops, SparseCore 0:
  71.7 95.1 all-gather.30
  275.1 86.0 all-gather.34
  363.4 87.5 all-gather.36
  513.4 77.1 all-gather.42
  594.0 88.9 all-gather.40
  1241.5 308.2 all-reduce.11
  1737.9 130.3 reduce-scatter.38
  1870.4 139.7 reduce-scatter.34
  2016.2 164.1 reduce-scatter.36
  2182.7 357.2 reduce-scatter.40
  2542.3 359.0 reduce-scatter.42
  2908.8 246.6 reduce-scatter.32
  3252.5 131.3 reduce-scatter.74
  3386.0 138.8 reduce-scatter.64
  3527.2 139.3 reduce-scatter.54
  3668.7 139.8 reduce-scatter.44
  4054.6 130.4 reduce-scatter.76
  4187.2 139.7 reduce-scatter.66
  4329.2 139.8 reduce-scatter.56
  4471.3 139.3 reduce-scatter.46
  4856.8 130.7 reduce-scatter.78
  4989.9 139.4 reduce-scatter.68
  5131.7 139.4 reduce-scatter.58
  5273.2 140.4 reduce-scatter.48
  5659.3 129.9 reduce-scatter.80
  5791.6 139.7 reduce-scatter.70
  5933.5 138.8 reduce-scatter.60
  6074.7 139.3 reduce-scatter.50
  6460.0 130.0 reduce-scatter.82
  6592.4 139.5 reduce-scatter.72
  6734.0 139.7 reduce-scatter.62
  6876.1 139.4 reduce-scatter.52
  (24 shorter events, 1372.8 us)
where the time goes:
time: 7300 us; the launch traced here: 7280 us
  waiting for transfers between devices  5600 us (77%)
  matrix products  738 us (10%)
  local copies, waits for them, and re-layouts  477 us (7%)
  other arithmetic  257 us (4%)
  blocking collectives  171 us (2%)
    reduce_scatter x5, waiting for transfers between devices, per_device(): lax.psum_scatter(gram_terms[0], ('frame', 'row'), scatter_dimension=0, ti...  702 us
    reduce_scatter x5, waiting for transfers between devices, per_device(): lax.psum_scatter(gram_terms[2], ('frame', 'row'), scatter_dimension=0, ti...  701 us
    reduce_scatter x5, waiting for transfers between devices, per_device(): lax.psum_scatter(gram_terms[1], ('frame', 'row'), scatter_dimension=0, ti...  700 us
    reduce_scatter x5, waiting for transfers between devices, per_device(): lax.psum_scatter(gram_terms[3], ('frame', 'row'), scatter_dimension=0, ti...  602 us
    reduce_scatter x1, waiting for transfers between devices, per_device(): lax.psum_scatter(grad_down, ('frame', 'row'), scatter_dimension=0, tiled=...  359 us
    reduce_scatter x1, waiting for transfers between devices, per_device(): lax.psum_scatter(grad_up, ('frame', 'row'), scatter_dimension=1, tiled=True)  356 us
    unnamed x58, waiting for transfers between devices  337 us
    all_gather x5, waiting for transfers between devices, per_device(): lax.all_gather(gram_shares[3].astype(jnp.bfloat16), ('frame', 'row'), axi...  317 us
  transfers between devices with their start and end apart: 56, of which 53 were waited for; matrix products, arithmetic and copies ran while one was open for 10% of the time, Pallas kernels for 0%

commit v1 on v0

--- a/solution.py
+++ b/solution.py
@@ -3,6 +3,8 @@
 import jax
 import jax.numpy as jnp
 from jax import lax
+from jax.experimental import pallas as pl
+from jax.experimental.pallas import tpu as pltpu
 from jax.sharding import PartitionSpec as P
 
 D = 1024
@@ -78,6 +80,184 @@
         jnp.sqrt(second_new / second_fix) + adam_floor
     )
     return (first_new, second_new, master_new)
+
+
+def halve(value, dim, axis, bit):
+    mine = (lax.axis_index(axis) >> bit) & 1
+    keep = lax.dynamic_index_in_dim(value, mine, dim, keepdims=False)
+    send = lax.dynamic_index_in_dim(value, 1 - mine, dim, keepdims=False)
+    size = lax.axis_size(axis)
+    pairs = [(index, index ^ (1 << bit)) for index in range(size)]
+    came = lax.ppermute(send.astype(jnp.bfloat16), axis, pairs)
+    return keep.astype(jnp.float32) + came.astype(jnp.float32)
+
+
+def halve_all(value, names, order):
+    names = list(names)
+    for name in order:
+        dim = names.index(name)
+        value = halve(value, dim, name[0], name[1])
+        names.pop(dim)
+    return value
+
+
+def scatter_sum(value):
+    frame_bits = lax.axis_size("frame").bit_length() - 1
+    row_bits = lax.axis_size("row").bit_length() - 1
+    names = [("frame", bit) for bit in reversed(range(frame_bits))]
+    names += [("row", bit) for bit in reversed(range(row_bits))]
+    value = value.reshape((2,) * (frame_bits + row_bits) + value.shape[1:])
+    value = halve_all(value, names, [("frame", 0)])
+    names.remove(("frame", 0))
+    upward = [("row", bit) for bit in range(row_bits)]
+    width = value.shape[-1] // 2
+    left = halve_all(value[..., :width], names, upward)
+    right = halve_all(value[..., width:], names, upward[::-1])
+    names = names[: frame_bits - 1]
+    value = jnp.concatenate([left, right], axis=-1)
+    return halve_all(value, names, [("frame", bit) for bit in range(1, frame_bits)])
+
+
+def split_two(value):
+    high = value.astype(jnp.bfloat16)
+    return high, (value - high.astype(jnp.float32)).astype(jnp.bfloat16)
+
+
+def dot_low(left, right):
+    return lax.dot_general(left, right, (((1,), (0,)), ((), ())), preferred_element_type=jnp.float32)
+
+
+def newton_kernel(all_ref, mine_ref, out_ref, a_ref, q_ref, t_ref, ah, al, nh, nl, th, tl, qh, ql):
+    width = a_ref.shape[0]
+    rows = 256
+    steps = width // rows
+    depth = all_ref.shape[0]
+
+    def block(index):
+        return pl.ds(pl.multiple_of(index * rows, rows), rows)
+
+    def gram(index, total):
+        columns = block(index)
+
+        def part(k, value):
+            deep = pl.ds(pl.multiple_of(k * 1024, 1024), 1024)
+            return value + lax.dot_general(
+                all_ref[deep, columns],
+                all_ref[deep, :],
+                (((0,), (0,)), ((), ())),
+                preferred_element_type=jnp.float32,
+            )
+
+        value = lax.fori_loop(0, depth // 1024, part, jnp.zeros((rows, width), jnp.float32))
+        a_ref[columns, :] = value
+        row_at = lax.broadcasted_iota(jnp.int32, (rows, width), 0) + index * rows
+        column_at = lax.broadcasted_iota(jnp.int32, (rows, width), 1)
+        return total + jnp.sum(jnp.where(row_at == column_at, value, 0.0))
+
+    squares = 0.0
+    for index in range(steps):
+        squares = gram(index, squares)
+    squares = jnp.full((1, 1), squares, jnp.float32)
+    inverse = 1.0 / (jnp.sqrt(squares) + 1e-07)
+
+    def first_split(index, carry):
+        at = block(index)
+        value = a_ref[at, :] * inverse * inverse
+        a_ref[at, :] = value
+        high, rest = split_two(value)
+        ah[at, :] = high
+        al[at, :] = rest
+        return carry
+
+    lax.fori_loop(0, steps, first_split, 0)
+
+    def three(lh, ll, rh, rl):
+        return dot_low(lh, rh) + dot_low(lh, rl) + dot_low(ll, rh)
+
+    def one_step(number, exact, last):
+        def make_n(index, carry):
+            at = block(index)
+            if exact:
+                square = three(ah[at, :], al[at, :], ah[...], al[...])
+            else:
+                square = dot_low(ah[at, :], ah[...])
+            value = newton_two * a_ref[at, :] + newton_three * square
+            high, rest = split_two(value)
+            nh[at, :] = high
+            if exact:
+                nl[at, :] = rest
+            return carry
+
+        lax.fori_loop(0, steps, make_n, 0)
+
+        def make_q(index, carry):
+            at = block(index)
+            if number == 0:
+                row_at = lax.broadcasted_iota(jnp.int32, (rows, width), 0) + index * rows
+                column_at = lax.broadcasted_iota(jnp.int32, (rows, width), 1)
+                value = nh[at, :].astype(jnp.float32) + jnp.where(row_at == column_at, newton_one, 0.0)
+            elif exact:
+                value = newton_one * q_ref[at, :] + three(qh[at, :], ql[at, :], nh[...], nl[...])
+            else:
+                value = newton_one * q_ref[at, :] + dot_low(qh[at, :], nh[...]) + dot_low(ql[at, :], nh[...])
+            q_ref[at, :] = value
+            high, rest = split_two(value)
+            qh[at, :] = high
+            ql[at, :] = rest
+            return carry
+
+        lax.fori_loop(0, steps, make_q, 0)
+        if last:
+            return
+
+        def make_t(index, carry):
+            at = block(index)
+            if exact:
+                value = newton_one * a_ref[at, :] + three(ah[at, :], al[at, :], nh[...], nl[...])
+            else:
+                value = newton_one * a_ref[at, :] + dot_low(ah[at, :], nh[...]) + dot_low(al[at, :], nh[...])
+            t_ref[at, :] = value
+            high, rest = split_two(value)
+            th[at, :] = high
+            tl[at, :] = rest
+            return carry
+
+        lax.fori_loop(0, steps, make_t, 0)
+
+        def make_a(index, carry):
+            at = block(index)
+            if exact:
+                value = newton_one * t_ref[at, :] + three(nh[at, :], nl[at, :], th[...], tl[...])
+            else:
+                value = newton_one * t_ref[at, :] + dot_low(nh[at, :], th[...]) + dot_low(nh[at, :], tl[...])
+            a_ref[at, :] = value
+            high, rest = split_two(value)
+            ah[at, :] = high
+            al[at, :] = rest
+            return carry
+
+        lax.fori_loop(0, steps, make_a, 0)
+
+    for number in range(5):
+        one_step(number, number >= 2, number == 4)
+
+    mine = mine_ref[...]
+    out_ref[...] = ((dot_low(mine, qh[...]) + dot_low(mine, ql[...])) * inverse).astype(out_ref.dtype)
+
+
+def newton(everything, mine):
+    width = everything.shape[1]
+    full = pltpu.VMEM((width, width), jnp.float32)
+    low = pltpu.VMEM((width, width), jnp.bfloat16)
+    return pl.pallas_call(
+        newton_kernel,
+        out_shape=jax.ShapeDtypeStruct(mine.shape, jnp.bfloat16),
+        in_specs=[pl.BlockSpec(memory_space=pltpu.VMEM)] * 2,
+        out_specs=pl.BlockSpec(memory_space=pltpu.VMEM),
+        scratch_shapes=[full] * 3 + [low] * 8,
+        compiler_params=pltpu.CompilerParams(vmem_limit_bytes=52 * 1024 * 1024),
+        cost_estimate=pl.CostEstimate(flops=110 * 10**9, bytes_accessed=12 * 10**6, transcendentals=0),
+    )(everything, mine)
 
 
 def per_device(
@@ -210,20 +390,13 @@
     activated = gelu_tanh(up_value).astype(low_type)
     branch_two = jnp.dot(activated, w_down, preferred_element_type=full_type).reshape(shape_five)
     block_out = (middle + gate_two * branch_two).astype(low_type)
-    w_qkv, w_out, w_up, w_down, w_ada = (
-        lax.all_gather(qkv_master.astype(low_type), ("frame", "row"), axis=1, tiled=True),
-        lax.all_gather(out_master.astype(low_type), ("frame", "row"), axis=0, tiled=True),
-        lax.all_gather(up_master.astype(low_type), ("frame", "row"), axis=1, tiled=True),
-        lax.all_gather(down_master.astype(low_type), ("frame", "row"), axis=0, tiled=True),
-        lax.all_gather(ada_master.astype(low_type), ("frame", "row"), axis=1, tiled=True),
-    )
     upstream = cotangent.astype(full_type)
     d_branch_two = (upstream * gate_two).astype(low_type).reshape(token_total, model_width)
     d_gate_two = jnp.sum(upstream * branch_two, axis=(2, 3))
     grad_down = jnp.einsum("tf,td->fd", activated, d_branch_two, preferred_element_type=full_type)
     d_activated = jnp.einsum("td,fd->tf", d_branch_two, w_down, preferred_element_type=full_type)
     d_up = jax.vjp(gelu_tanh, up_value)[1](d_activated)[0].astype(low_type)
-    grad_up = jnp.einsum("td,tf->df", hidden_two, d_up, preferred_element_type=full_type)
+    grad_up = jnp.einsum("tf,td->fd", d_up, hidden_two, preferred_element_type=full_type)
     d_hidden_two = jnp.einsum("tf,df->td", d_up, w_up, preferred_element_type=full_type).reshape(
         shape_five
     )
@@ -312,7 +485,7 @@
         .astype(low_type)
         .reshape(token_total, 3 * model_width)
     )
-    grad_qkv = jnp.einsum("td,te->de", hidden_one, d_projected, preferred_element_type=full_type)
+    grad_qkv = jnp.einsum("te,td->ed", d_projected, hidden_one, preferred_element_type=full_type)
     d_hidden_one = jnp.einsum(
         "te,de->td", d_projected, w_qkv, preferred_element_type=full_type
     ).reshape(shape_five)
@@ -332,94 +505,89 @@
         ],
         axis=1,
     )
+    frame_devices = lax.axis_size("frame")
+    device_total = frame_devices * row_devices
+    both = ("frame", "row")
+    levels_all = lax.all_gather(level_flat, "frame", axis=0, tiled=True)
+    embedded_all = lax.all_gather(embedded.astype(low_type), "frame", axis=0, tiled=True).astype(
+        full_type
+    )
+    cond_all = jax.nn.silu(embedded_all).astype(low_type)
+    ada_width = ada_master.shape[1]
+    mod_parts = lax.all_to_all(
+        jnp.moveaxis(d_modulation.reshape(frame_total, device_total, ada_width), 1, 0),
+        both,
+        split_axis=0,
+        concat_axis=0,
+        tiled=True,
+    )
     mod_mine = (
-        lax.psum_scatter(d_modulation.astype(jnp.bfloat16), "row", scatter_dimension=0, tiled=True)
-        .astype(jnp.float32)
+        jnp.sum(mod_parts.reshape(frame_devices, row_devices, frame_total, ada_width), axis=1)
+        .reshape(frame_devices * frame_total, ada_width)
         .astype(low_type)
     )
-    frames_mine = frame_total // row_devices
-    first_frame = lax.axis_index("row") * frames_mine
-    cond_mine = lax.dynamic_slice_in_dim(cond_low, first_frame, frames_mine, 0)
-    embedded_mine = lax.dynamic_slice_in_dim(embedded, first_frame, frames_mine, 0)
-    hot_mine = lax.dynamic_slice_in_dim(level_hot, first_frame, frames_mine, 0)
-    grad_ada = jnp.einsum("fd,fe->de", cond_mine, mod_mine, preferred_element_type=full_type)
-    grad_bias = jnp.sum(mod_mine.astype(full_type), axis=0)
-    d_cond = jnp.einsum("fe,de->fd", mod_mine, w_ada, preferred_element_type=full_type)
-    d_embedded = jax.vjp(jax.nn.silu, embedded_mine)[1](d_cond)[0]
-    grad_table = jnp.einsum("fl,fd->ld", hot_mine.astype(full_type), d_embedded, precision=highest)
-    g_qkv, g_out, g_up, g_down, g_ada, g_table, g_bias = (
-        lax.psum_scatter(grad_qkv, ("frame", "row"), scatter_dimension=1, tiled=True),
-        lax.psum_scatter(grad_out, ("frame", "row"), scatter_dimension=0, tiled=True),
-        lax.psum_scatter(grad_up, ("frame", "row"), scatter_dimension=1, tiled=True),
-        lax.psum_scatter(grad_down, ("frame", "row"), scatter_dimension=0, tiled=True),
-        lax.psum_scatter(grad_ada, ("frame", "row"), scatter_dimension=1, tiled=True),
-        lax.psum_scatter(grad_table, ("frame", "row"), scatter_dimension=0, tiled=True),
-        lax.psum_scatter(grad_bias, ("frame", "row"), scatter_dimension=0, tiled=True),
-    )
+    g_ada = jnp.einsum("fd,fe->de", cond_all, mod_mine, preferred_element_type=full_type)
+    g_bias = jnp.sum(mod_mine.astype(full_type), axis=0)
+    d_cond = lax.psum(
+        jnp.einsum("fe,de->fd", mod_mine, ada_master.astype(low_type), preferred_element_type=full_type),
+        both,
+    )
+    d_embedded = jax.vjp(jax.nn.silu, embedded_all)[1](d_cond)[0]
+    device_index = lax.axis_index("frame") * row_devices + lax.axis_index("row")
+    level_rows = table_master.shape[0]
+    hot_mine = (
+        levels_all[None, :]
+        == (device_index * level_rows + jnp.arange(level_rows, dtype=jnp.int32))[:, None]
+    ).astype(full_type)
+    g_table = jnp.dot(hot_mine, d_embedded, precision=highest)
+    heights = (qkv_master.shape[1], out_master.shape[0], up_master.shape[1], down_master.shape[0])
+    early = scatter_sum(
+        jnp.concatenate(
+            [
+                grad_down.reshape(device_total, heights[3], model_width),
+                grad_up.reshape(device_total, heights[2], model_width),
+                grad_out.reshape(device_total, heights[1], model_width),
+            ],
+            axis=1,
+        )
+    )
+    g_down = early[: heights[3]]
+    g_up = early[heights[3] : heights[3] + heights[2]]
+    g_out = early[heights[3] + heights[2] :]
+    g_qkv = scatter_sum(grad_qkv.reshape(device_total, heights[0], model_width))
     muon_grads = (g_qkv, g_out, g_up, g_down)
+    flipped = (True, False, True, False)
+
+    def tall(value, member):
+        return value.T if flipped[member] else value
+
     muon_moments = (qkv_momentum, out_momentum, up_momentum, down_momentum)
     muon_masters = (qkv_master, out_master, up_master, down_master)
-    flipped = (True, False, True, False)
     factors = (math.sqrt(3.0), 1.0, math.sqrt(FF / D), math.sqrt(FF / D))
     adam_local = jnp.sum(g_ada * g_ada) + jnp.sum(g_table * g_table) + jnp.sum(g_bias * g_bias)
     local_total = adam_local + sum((jnp.sum(item * item) for item in muon_grads))
-    norm_value = jnp.sqrt(lax.psum(local_total, ("frame", "row")))
+    norm_value = jnp.sqrt(lax.psum(local_total, both))
     clip_factor = jnp.minimum(1.0, clip_limit / (norm_value + 1e-06))
-    clipped_all = [clip_factor * item for item in muon_grads]
-    moments_new = [
-        momentum_decay * moment + clipped for moment, clipped in zip(muon_moments, clipped_all)
-    ]
-    updates = [
-        clipped + momentum_decay * moment for clipped, moment in zip(clipped_all, moments_new)
-    ]
-    frob_parts = lax.psum(
-        (
-            jnp.sum(updates[0] * updates[0]),
-            jnp.sum(updates[1] * updates[1]),
-            jnp.sum(updates[2] * updates[2]),
-            jnp.sum(updates[3] * updates[3]),
-        ),
-        ("frame", "row"),
-    )
-    frob_squares = jnp.stack(frob_parts)
-    blocks = []
+    moments_new = []
+    pieces = []
+    slot = max(heights)
     for member in range(4):
-        scaled = updates[member] / (jnp.sqrt(frob_squares[member]) + 1e-07)
-        blocks.append(scaled.T if flipped[member] else scaled)
-    for newton_step in range(5):
-        gram_terms = [jnp.dot(block.T, block, precision=highest) for block in blocks]
-        gram_shares = (
-            lax.psum_scatter(gram_terms[0], ("frame", "row"), scatter_dimension=0, tiled=True),
-            lax.psum_scatter(gram_terms[1], ("frame", "row"), scatter_dimension=0, tiled=True),
-            lax.psum_scatter(gram_terms[2], ("frame", "row"), scatter_dimension=0, tiled=True),
-            lax.psum_scatter(gram_terms[3], ("frame", "row"), scatter_dimension=0, tiled=True),
-        )
-        grams = (
-            lax.all_gather(
-                gram_shares[0].astype(jnp.bfloat16), ("frame", "row"), axis=0, tiled=True
-            ).astype(jnp.float32),
-            lax.all_gather(
-                gram_shares[1].astype(jnp.bfloat16), ("frame", "row"), axis=0, tiled=True
-            ).astype(jnp.float32),
-            lax.all_gather(
-                gram_shares[2].astype(jnp.bfloat16), ("frame", "row"), axis=0, tiled=True
-            ).astype(jnp.float32),
-            lax.all_gather(
-                gram_shares[3].astype(jnp.bfloat16), ("frame", "row"), axis=0, tiled=True
-            ).astype(jnp.float32),
-        )
-        next_blocks = []
-        for member in range(4):
-            product = jnp.dot(blocks[member], grams[member], precision=highest)
-            next_blocks.append(
-                newton_one * blocks[member]
-                + newton_two * product
-                + newton_three * jnp.dot(product, grams[member], precision=highest)
-            )
-        blocks = next_blocks
+        clipped = clip_factor * muon_grads[member]
+        moment = momentum_decay * tall(muon_moments[member], member) + clipped
+        update = (clipped + momentum_decay * moment).astype(low_type)
+        moments_new.append(tall(moment, member))
+        pieces.append(jnp.pad(update, ((0, slot - heights[member]), (0, 0))))
+    slab = jnp.stack(pieces * (row_devices // 4))
+    updates = lax.all_to_all(slab, "row", split_axis=0, concat_axis=0, tiled=True).reshape(
+        row_devices * slot, model_width
+    )
+    everything = lax.all_gather(updates, "frame", axis=0, tiled=True)
+    ortho_rows = newton(everything, updates).reshape(row_devices, slot, model_width)
+    ortho_mine = lax.all_to_all(ortho_rows, "row", split_axis=0, concat_axis=0, tiled=True)
+    blocks = [tall(ortho_mine[member, : heights[member]].astype(full_type), member) for member in range(4)]
     masters_new = []
     for member in range(4):
-        ortho = blocks[member].T if flipped[member] else blocks[member]
+        ortho = blocks[member]
         masters_new.append(
             muon_masters[member] * (1.0 - muon_rate * weight_decay)
             - muon_rate * factors[member] * ortho

time: 7300 us -> 2530 us (0.35)
  waiting for transfers between devices: 5600 us -> 748 us
  matrix products: 738 us -> 582 us
  Pallas kernels: 0 us -> 129 us
    reduce_scatter x26 -> x0, waiting for transfers between devices: 3980 us -> none  [the longest x5 702 us: per_device(): lax.psum_scatter(gram_terms[0], ('frame', 'row'), scatter_dimension=0, ti...]
    all_gather x20 -> x1, waiting for transfers between devices: 1020 us -> 77 us  [per_device(): everything = lax.all_gather(updates, 'frame', axis=0, tiled=True)]
    dot_general x65 -> x5, matrix products: 276 us -> 28.3 us  [the longest x1 14.9 us: per_device(): jnp.einsum('tf,td->fd', d_up, hidden_two, preferred_element_type=full_type)]
    unnamed x58 -> x12, waiting for transfers between devices: 337 us -> 139 us
    ppermute x0 -> x14, waiting for transfers between devices: none -> 159 us  [halve(): came = lax.ppermute(send.astype(jnp.bfloat16), axis, pairs)]
    pallas_call x0 -> x1, Pallas kernels: none -> 129 us  [newton(): pl.pallas_call(newton_kernel, out_shape=jax.ShapeDtypeStruct(mine.shape,...]
    psum x0 -> x1, waiting for transfers between devices: none -> 118 us  [per_device(): lax.psum(jnp.einsum('fe,de->fd', mod_mine, ada_master.astype(low_type), p...]
  transfers between devices with their start and end apart: 56 -> 27, of which waited for: 53 -> 16; matrix products, arithmetic and copies ran while one was open for 10% -> 48% of each run, Pallas kernels for 0% -> 0%
where the time goes in v1:
time: 2530 us; the launch traced here: 2510 us
  waiting for transfers between devices  748 us (30%)
  matrix products  582 us (23%)
  local copies, waits for them, and re-layouts  544 us (22%)
  other arithmetic  308 us (12%)
  blocking collectives  140 us (6%)
  Pallas kernels  129 us (5%)
  starting transfers between devices  26.5 us (1%)
    ppermute x14, waiting for transfers between devices, halve(): came = lax.ppermute(send.astype(jnp.bfloat16), axis, pairs)  159 us
    unnamed x12, waiting for transfers between devices  139 us
    pallas_call x1, Pallas kernels, newton(): pl.pallas_call(newton_kernel, out_shape=jax.ShapeDtypeStruct(mine.shape,...  129 us
    psum x1, waiting for transfers between devices, per_device(): lax.psum(jnp.einsum('fe,de->fd', mod_mine, ada_master.astype(low_type), p...  118 us
    dot_general x8, matrix products, attend_back(): jnp.einsum('qhd,khd->hqk', grad_group, value_group, preferred_element_typ...  101 us
    all_gather x1, waiting for transfers between devices, per_device(): lax.all_gather(ada_master.astype(low_type), ('frame', 'row'), axis=1, til...  96 us
    convert_element_type x8, other arithmetic, attend_back(): grad_scores = (prob_full * (grad_prob - inner_sum)).astype(low_type)  87.7 us
    all_gather x1, waiting for transfers between devices, per_device(): everything = lax.all_gather(updates, 'frame', axis=0, tiled=True)  77 us
  transfers between devices with their start and end apart: 27, of which 16 were waited for; matrix products, arithmetic and copies ran while one was open for 48% of the time, Pallas kernels for 0%

profile of v1, /device:TPU:8, one launch (start us, length us, event | category | flops | bytes accessed | tf_op | source)
XLA Modules:
  0.0 2510.1 jit_solution(14297517068474236213)
XLA Ops:
  15.5 40.7 %all-reduce.2 = bf16[6144]{0:T(1024)(128)(2,1)S(1)} all-reduce(bf16[6144]{0:T(1024)(128)(2,1)S(1)} %dynamic-update-slice), channel_id=1, replica_groups=mesh['frame'=8,'row'=4] {'frame','row'}, use_global_device_ids=true, to_apply=%add.2 | all-reduce | flops 6144 | bytes 24576
  70.8 96.0 %all-gather.12.cloned.1.call-done = bf16[1024,6144]{0,1:T(8,128)(2,1)} async-done(((bf16[1024,192]{0,1:T(8,128)(2,1)}), bf16[1024,6144]{0,1:T(8,128)(2,1)}) %all-gather.12.cloned.1.call-update) | async-done | bytes 12582928 | tf_op jit(solution)/shard_map/all_gather | solution.py:302
  178.8 60.0 %all-gather.14.cloned.1.call-done = bf16[1024,3072]{0,1:T(8,128)(2,1)} async-done(((bf16[1024,96]{0,1:T(8,128)(2,1)}), bf16[1024,3072]{0,1:T(8,128)(2,1)}) %all-gather.14.cloned.1.call-update) | async-done | bytes 6291472 | tf_op jit(solution)/shard_map/all_gather | solution.py:298
  301.7 23.0 copy.147
  370.3 40.6 %all-gather.18.cloned.1.call-done = bf16[2,8,16,16,1024]{4,3,1,0,2:T(8,128)(2,1)} async-done(((bf16[2,8,4,16,1024]{4,3,1,0,2:T(8,128)(2,1)}), bf16[2,8,16,16,1024]{4,3,1,0,2:T(8,128)(2,1)}) %all-gather.18.cloned.1.call-update) | async-done | bytes 8388624 | tf_op jit(solution)/shard_map/all_gather | solution.py:345
  419.5 22.3 reshape.364
  441.8 18.8 copy.150
  460.6 40.2 %all-gather.16.cloned.1.call-done = bf16[2,8,16,16,1024]{4,3,2,1,0:T(8,128)(2,1)} async-done(((bf16[2,8,4,16,1024]{4,3,2,1,0:T(8,128)(2,1)}), bf16[2,8,16,16,1024]{4,3,2,1,0:T(8,128)(2,1)}) %all-gather.16.cloned.1.call-update) | async-done | bytes 8388624 | tf_op jit(solution)/shard_map/all_gather | solution.py:346
  500.8 22.1 reshape.363
  522.9 18.4 copy.149
  541.5 178.7 %while.26 = (s32[]{:T(128)}, bf16[2,512,16,64]{1,3,2,0:T(8,128)(2,1)S(1)}, f32[2,16,512]{2,1,0:T(8,128)}, bf16[2,2048,16,64]{1,3,2,0:T(8,128)(2,1)}, bf16[2,512,...) while((s32[]{:T(128)}, bf16[2,512,16,64]{1,3,2,0:T(8,128)(2,1)S(1)}, ...), condition=%wide.region_11.12_spmd, body=%wide.region_2.11_spmd.sunk | while | flops 4450172928 | bytes 316477280 | solution.py:382
  745.0 28.9 %fusion.186 = (bf16[4096,1024]{0,1:T(8,128)(2,1)}, bf16[4096,1024]{0,1:T(8,128)(2,1)}, f32[1024,4096]{1,0:T(8,128)}) fusion(f32[1024,4096]{1,0:T(8,128)} %fusion.294, bf16[1024,1024]{1,0:T(8,128)(2,1)S(1)} %bitcast.604, bf16[1024,4096]{1,0:T(8,128)(2,1)} %all-gather.22.cloned.1.call-done), kind=kOutput, calls=%fused_computation.224 | convolution fusion | flops 8682209280 | bytes 60817408 | tf_op jit(solution)/shard_map/dot_general | solution.py:389
  785.9 24.7 fusion.189
  889.1 23.7 pad_maximum_fusion
  937.4 440.2 %while.27 = (s32[]{:T(128)}, bf16[2,512,16,64]{1,3,2,0:T(8,128)(2,1)}, bf16[2,2048,16,64]{1,3,2,0:T(8,128)(2,1)}, bf16[2,2048,16,64]{1,3,2,0:T(8,128)(2,1)}, bf1...) while((s32[]{:T(128)}, ...), condition=%wide.region_21.22_spmd, body=%wide.region_16.21_spmd.sunk | while | flops 10981728256 | bytes 926291584 | solution.py:462
  1377.6 20.3 copy.157
  1397.9 22.6 convert_element_type.370
  1420.5 20.3 copy.161
  1440.8 22.6 convert_element_type.372
  1491.7 97.8 %collective-permute-done.10 = bf16[2,2,2,288,512]{4,3,0,1,2:T(8,128)(2,1)} collective-permute-done((bf16[2,2,2,288,512]{4,3,0,1,2:T(8,128)(2,1)S(1)}, bf16[2,2,2,288,512]{4,3,0,1,2:T(8,128)(2,1)}, u32[]{:S(2)}, u32[]{:S(2)}) %collective-permute-start.10) | collective-permute-done | bytes 2359328 | tf_op jit(solution)/shard_map/ppermute | solution.py:91
  1602.1 35.9 %collective-permute-done.11 = bf16[2,2,288,512]{3,2,0,1:T(8,128)(2,1)} collective-permute-done((bf16[2,2,288,512]{3,2,0,1:T(8,128)(2,1)S(1)}, bf16[2,2,288,512]{3,2,0,1:T(8,128)(2,1)}, u32[]{:S(2)}, u32[]{:S(2)}) %collective-permute-start.11) | collective-permute-done | bytes 1179680 | tf_op jit(solution)/shard_map/ppermute | solution.py:91
  1648.1 28.6 %all-reduce.3 = s32[128]{0:T(128)S(1)} all-reduce(s32[128]{0:T(128)S(1)} %dynamic-update-slice.1), channel_id=1, replica_groups=mesh['frame'=8,'row'=4] {'frame'}, use_global_device_ids=true, to_apply=%add.3 | all-reduce | flops 128 | bytes 1024
  1700.1 138.6 %all-reduce.12.cloned.1.call-done = (bf16[2,8,16,16,1024]{4,3,2,1,0:T(8,128)(2,1)}, bf16[2,8,16,16,1024]{4,3,2,1,0:T(8,128)(2,1)}) async-done(((bf16[2,8,16,16,1024]{4,3,2,1,0:T(8,128)(2,1)}, bf16[2,8,16,16,1024]{4,3,2,1,0:T(8,128)(2,1)}), (bf16[2,8,16,16,1024]{4,3,2,1,0:T(8,128)(2,1)}, bf16[2,8,16,16,1024]{4,3,2,1,0:T(8,128)(2,1)})) %all-reduce.12.cloned.1.call-update) | async-done | bytes 16777232
  1842.9 25.6 %copy.158 = f32[2,8,4,16,1024]{3,2,1,4,0:T(4,128)} copy(bf16[2,8,4,16,1024]{4,3,2,1,0:T(8,128)(2,1)} %get-tuple-element.413) | data formatting | bytes 6291456 | tf_op jit(solution)/shard_map/reshape;reshape | solution.py:65
  1868.6 29.0 %reshape.389 = f32[2,512,16,32,2]{1,4,3,2,0:T(2,128)} reshape(f32[2,8,4,16,1024]{3,2,1,4,0:T(4,128)} %copy.158) | data formatting | bytes 8388608 | tf_op jit(solution)/shard_map/reshape;reshape | solution.py:65
  1941.3 20.7 copy.163
  1980.4 16.6 convert_element_type.374
  2081.8 118.4 %all-reduce.10.cloned.1.call-done = f32[128,1024]{1,0:T(8,128)} async-done(((f32[128,1024]{1,0:T(8,128)}), f32[128,1024]{1,0:T(8,128)}) %all-reduce.10.cloned.1.call-update) | async-done | bytes 524304 | tf_op jit(solution)/shard_map/psum | solution.py:531
  2210.4 39.1 %psum.15 = f32[]{:T(128)} all-reduce(f32[]{:T(128)S(6)} %add.422), channel_id=1, replica_groups=mesh['frame'=8,'row'=4] {'frame','row'}, use_global_device_ids=true, to_apply=%region_42.43 | all-reduce | flops 1 | bytes 8 | tf_op jit(solution)/shard_map/psum | solution.py:569
  2256.1 17.2 all_to_all.15
  2274.4 77.0 %all-gather.26.cloned.1.call-done.all_ref = bf16[4096,1024]{1,0:T(8,128)(2,1)} async-done(((bf16[512,1024]{1,0:T(8,128)(2,1)}), bf16[4096,1024]{1,0:T(8,128)(2,1)}) %all-gather.26.cloned.1.call-update) | async-done | bytes 8388624 | tf_op jit(solution)/shard_map/all_gather | solution.py:584
  2351.4 129.3 %shard_map.365 = bf16[512,1024]{1,0:T(8,128)(2,1)} custom-call(bf16[4096,1024]{1,0:T(8,128)(2,1)} %all-gather.26.cloned.1.call-done.all_ref, bf16[512,1024]{1,0:T(8,128)(2,1)} %bitcast.603), custom_call_target="tpu_custom_call" | custom-call | flops 109999996928 | bytes 12000000 | tf_op jit(solution)/shard_map/pallas_call | solution.py:252
  (621 shorter events, 1157.9 us)
Async XLA Ops:
  7.2 61.0 %all-gather.10.cloned.1.call-start = ((), (), s32[]{:S(2)}) async-start(), calls=%async_computation.3 | async-start | bytes 2162688 | tf_op jit(solution)/shard_map/all_gather | solution.py:303
  9.0 157.9 %all-gather.12.cloned.1.call-start = ((), (), s32[]{:S(2)}) async-start(), calls=%async_computation.4 | async-start | bytes 12976128 | tf_op jit(solution)/shard_map/all_gather | solution.py:302
  11.0 227.8 %all-gather.14.cloned.1.call-start = ((), (), s32[]{:S(2)}) async-start(), calls=%async_computation.5 | async-start | bytes 6488064 | tf_op jit(solution)/shard_map/all_gather | solution.py:298
  12.7 341.5 %all-gather.24.cloned.1.call-start = ((), (), s32[]{:S(2)}) async-start(), calls=%async_computation.10 | async-start | bytes 8650752 | tf_op jit(solution)/shard_map/all_gather | solution.py:301
  14.6 396.3 %all-gather.18.cloned.1.call-start = ((), (), s32[]{:S(2)}) async-start(), calls=%async_computation.7 | async-start | bytes 10485760 | tf_op jit(solution)/shard_map/all_gather | solution.py:345
  324.7 176.1 %all-gather.16.cloned.1.call-start = ((), (), s32[]{:S(2)}) async-start(), calls=%async_computation.6 | async-start | bytes 10485760 | tf_op jit(solution)/shard_map/all_gather | solution.py:346
  338.9 396.2 %all-gather.20.cloned.1.call-start = ((), (), s32[]{:S(2)}) async-start(), calls=%async_computation.8 | async-start | bytes 2162688 | tf_op jit(solution)/shard_map/all_gather | solution.py:299
  339.6 405.4 %all-gather.22.cloned.1.call-start = ((), (), s32[]{:S(2)}) async-start(), calls=%async_computation.9 | async-start | bytes 8650752 | tf_op jit(solution)/shard_map/all_gather | solution.py:300
  340.4 1498.3 %all-reduce.12.cloned.1.call-start = ((), (), s32[]{:S(2)}) async-start(), calls=%async_computation.13 | async-start | bytes 33554432
  924.0 539.4 %collective-permute-start.7 = (bf16[2,2,2,2,288,1024]{5,4,0,1,3,2:T(8,128)(2,1)}, bf16[2,2,2,2,288,1024]{5,4,0,1,3,2:T(8,128)(2,1)}, u32[]{:S(2)}, u32[]{:S(2)}) collective-permute-start(bf16[2,2,2,2,288,1024]{5,4,0,1,3,2:T(8,128)(2,1)} %fusion.187), channel_id=1, source_target_pairs={{0,4},{4,0},{8,12},{12,8},{16,20},{20,16},{24,28},{28,24},{1,5},{5... | collective-permute-start | bytes 28311560 | tf_op jit(solution)/shard_map/ppermute | solution.py:91
  1484.9 104.6 %collective-permute-start.10 = (bf16[2,2,2,288,512]{4,3,0,1,2:T(8,128)(2,1)S(1)}, bf16[2,2,2,288,512]{4,3,0,1,2:T(8,128)(2,1)}, u32[]{:S(2)}, u32[]{:S(2)}) collective-permute-start(bf16[2,2,2,288,512]{4,3,0,1,2:T(8,128)(2,1)S(1)} %fusion.210), channel_id=1, source_target_pairs={{0,2},{1,3},{2,0},{3,1},{4,6},{5,7},{6,4},{7,5},{8,10},{9,11},{10,... | collective-permute-start | bytes 7077896 | tf_op jit(solution)/shard_map/ppermute | solution.py:91
  1490.7 104.8 %collective-permute-start.8 = (bf16[2,2,2,288,512]{4,3,0,1,2:T(8,128)(2,1)}, bf16[2,2,2,288,512]{4,3,0,1,2:T(8,128)(2,1)}, u32[]{:S(2)}, u32[]{:S(2)}) collective-permute-start(bf16[2,2,2,288,512]{4,3,0,1,2:T(8,128)(2,1)} %fusion.209), channel_id=1, source_target_pairs={{0,1},{1,0},{2,3},{3,2},{4,5},{5,4},{6,7},{7,6},{8,9},{9,8},{10,11... | collective-permute-start | bytes 7077896 | tf_op jit(solution)/shard_map/ppermute | solution.py:91
  1594.0 44.0 %collective-permute-start.11 = (bf16[2,2,288,512]{3,2,0,1:T(8,128)(2,1)S(1)}, bf16[2,2,288,512]{3,2,0,1:T(8,128)(2,1)}, u32[]{:S(2)}, u32[]{:S(2)}) collective-permute-start(bf16[2,2,288,512]{3,2,0,1:T(8,128)(2,1)S(1)} %fusion.220), channel_id=1, source_target_pairs={{0,1},{1,0},{2,3},{3,2},{4,5},{5,4},{6,7},{7,6},{8,9},{9,8},{10,11... | collective-permute-start | bytes 3538952 | tf_op jit(solution)/shard_map/ppermute | solution.py:91
  1600.7 39.8 %collective-permute-start.9 = (bf16[2,2,288,512]{3,2,0,1:T(8,128)(2,1)S(1)}, bf16[2,2,288,512]{3,2,0,1:T(8,128)(2,1)}, u32[]{:S(2)}, u32[]{:S(2)}) collective-permute-start(bf16[2,2,288,512]{3,2,0,1:T(8,128)(2,1)S(1)} %fusion.219), channel_id=1, source_target_pairs={{0,2},{1,3},{2,0},{3,1},{4,6},{5,7},{6,4},{7,5},{8,10},{9,11},{10,... | collective-permute-start | bytes 3538952 | tf_op jit(solution)/shard_map/ppermute | solution.py:91
  1644.8 50.9 %collective-permute-start.12 = (bf16[2,288,1024]{2,1,0:T(8,128)(2,1)}, bf16[2,288,1024]{2,1,0:T(8,128)(2,1)S(1)}, u32[]{:S(2)}, u32[]{:S(2)}) collective-permute-start(bf16[2,288,1024]{2,1,0:T(8,128)(2,1)} %fusion.221), channel_id=1, source_target_pairs={{0,8},{4,12},{8,0},{12,4},{16,24},{20,28},{24,16},{28,20},{1,9},{5... | collective-permute-start | bytes 3538952 | tf_op jit(solution)/shard_map/ppermute | solution.py:91
  1697.7 332.2 %collective-permute-start.13 = (bf16[288,1024]{1,0:T(8,128)(2,1)S(1)}, bf16[288,1024]{1,0:T(8,128)(2,1)}, u32[]{:S(2)}, u32[]{:S(2)}) collective-permute-start(bf16[288,1024]{1,0:T(8,128)(2,1)S(1)} %fusion.230), channel_id=1, source_target_pairs={{0,16},{4,20},{8,24},{12,28},{16,0},{20,4},{24,8},{28,12},{1,17},{... | collective-permute-start | bytes 1769480 | tf_op jit(solution)/shard_map/ppermute | solution.py:91
  1980.4 42.3 %collective-permute-start = (bf16[2,2,2,2,96,1024]{5,4,0,1,3,2:T(8,128)(2,1)}, bf16[2,2,2,2,96,1024]{5,4,0,1,3,2:T(8,128)(2,1)}, u32[]{:S(2)}, u32[]{:S(2)}) collective-permute-start(bf16[2,2,2,2,96,1024]{5,4,0,1,3,2:T(8,128)(2,1)} %fusion.208), channel_id=1, source_target_pairs={{0,4},{4,0},{8,12},{12,8},{16,20},{20,16},{24,28},{28,24},{1,5},{5... | collective-permute-start | bytes 9437192 | tf_op jit(solution)/shard_map/ppermute | solution.py:91
  2016.7 21.5 all-to-all-start
  2022.6 177.6 %all-reduce.10.cloned.1.call-start = ((), (), s32[]{:S(2)}) async-start(), calls=%async_computation.11 | async-start | bytes 1048576 | tf_op jit(solution)/shard_map/psum | solution.py:531
  2028.3 22.1 collective-permute-start.3
  2032.6 20.7 collective-permute-start.1
  2052.4 11.1 collective-permute-start.4
  2056.7 10.7 collective-permute-start.2
  2068.8 9.9 collective-permute-start.5
  2069.6 281.8 %all-gather.26.cloned.1.call-start = ((), (), s32[]{:S(2)}) async-start(), calls=%async_computation.12 | async-start | bytes 9437184 | tf_op jit(solution)/shard_map/all_gather | solution.py:584
  2079.9 125.1 %collective-permute-start.6 = (bf16[96,1024]{1,0:T(8,128)(2,1)S(1)}, bf16[96,1024]{1,0:T(8,128)(2,1)S(1)}, u32[]{:S(2)}, u32[]{:S(2)}) collective-permute-start(bf16[96,1024]{1,0:T(8,128)(2,1)S(1)} %fusion.251), channel_id=1, source_target_pairs={{0,16},{4,20},{8,24},{12,28},{16,0},{20,4},{24,8},{28,12},{1,17},{... | collective-permute-start | bytes 589832 | tf_op jit(solution)/shard_map/ppermute | solution.py:91
  2274.3 210.4 %copy-start.90 = (f32[192]{0:T(256)S(1)}, f32[192]{0:T(256)}, u32[]{:S(2)}) copy-start(f32[192]{0:T(256)} %param.45) | copy-start | bytes 2308
  2274.3 212.0 %copy-start.76 = (f32[32,1024]{1,0:T(8,128)S(1)}, f32[32,1024]{1,0:T(8,128)}, u32[]{:S(2)}) copy-start(f32[32,1024]{1,0:T(8,128)} %param.42) | copy-start | bytes 393220
  2274.3 212.0 %copy-start.87 = (f32[32,1024]{1,0:T(8,128)S(1)}, f32[32,1024]{1,0:T(8,128)}, u32[]{:S(2)}) copy-start(f32[32,1024]{1,0:T(8,128)} %param.44) | copy-start | bytes 393220
  2274.4 211.9 %copy-start.88 = (f32[32,1024]{1,0:T(8,128)S(1)}, f32[32,1024]{1,0:T(8,128)}, u32[]{:S(2)}) copy-start(f32[32,1024]{1,0:T(8,128)} %param.43) | copy-start | bytes 393220
  2274.4 211.9 %copy-start.89 = (f32[32,1024]{1,0:T(8,128)S(1)}, f32[32,1024]{1,0:T(8,128)}, u32[]{:S(2)}) copy-start(f32[32,1024]{1,0:T(8,128)} %get-tuple-element.410) | copy-start | bytes 393220
  2480.7 18.0 all-to-all-start.2
  (144 other events, 2625.1 us)
Sparse Core Ops, SparseCore 0:
  11.5 56.6 all-gather.9
  71.6 95.1 all-gather.11
  170.3 68.4 all-gather.13
  242.1 76.0 all-gather.23
  324.8 86.0 all-gather.17
  413.2 87.6 all-gather.15
  504.2 55.5 all-gather.19
  563.2 90.1 all-gather.21
  1463.5 375.2 all-reduce.11
  2069.7 130.4 all-reduce.9
  2273.5 77.8 all-gather.25

commit v2 on v1

--- a/solution.py
+++ b/solution.py
@@ -1,3 +1,4 @@
+import functools
 import math
 
 import jax
@@ -26,24 +27,6 @@
 norm_floor = 1e-06
 clip_limit = 1.0
 rotary_base = 10000.0
-group_heads = 4
-
-
-def layer_norm(values):
-    centered = values - jnp.mean(values, axis=-1, keepdims=True)
-    return centered * lax.rsqrt(jnp.mean(centered * centered, axis=-1, keepdims=True) + norm_floor)
-
-
-def modulate(values, shift_part, scaling):
-    return layer_norm(values) * (1.0 + scaling) + shift_part
-
-
-def gelu_tanh(values):
-    return jax.nn.gelu(values, approximate=True)
-
-
-def rounded(values):
-    return lax.optimization_barrier(values.astype(jnp.bfloat16)).astype(jnp.float32)
 
 
 def rotary_angles(time_grid, row_grid, column_grid):
@@ -61,15 +44,6 @@
     )
 
 
-def rotate(values, angles):
-    paired = values.reshape(values.shape[:-1] + (values.shape[-1] // 2, 2))
-    cosine = jnp.cos(angles)[..., None, :]
-    sine = jnp.sin(angles)[..., None, :]
-    first_part = paired[..., 0] * cosine - paired[..., 1] * sine
-    second_part = paired[..., 0] * sine + paired[..., 1] * cosine
-    return jnp.stack([first_part, second_part], axis=-1).reshape(values.shape)
-
-
 def adam_update(grad_item, first, second, master, rate, clip_factor, step_value):
     clipped = clip_factor * grad_item
     first_new = beta_first * first + (1.0 - beta_first) * clipped
@@ -101,14 +75,18 @@
     return value
 
 
-def scatter_sum(value):
+def scatter_sum(pairs, name):
     frame_bits = lax.axis_size("frame").bit_length() - 1
     row_bits = lax.axis_size("row").bit_length() - 1
-    names = [("frame", bit) for bit in reversed(range(frame_bits))]
+    parity = (lax.axis_index("frame") & 1).astype(jnp.int32).reshape(1)
+    send = weight_sums(1 - parity, pairs, jnp.bfloat16, name + "_send")
+    size = lax.axis_size("frame")
+    came = lax.ppermute(send, "frame", [(index, index ^ 1) for index in range(size)])
+    keep = weight_sums(parity, pairs, jnp.float32, name + "_keep")
+    value = keep + came.astype(jnp.float32)
+    names = [("frame", bit) for bit in reversed(range(1, frame_bits))]
     names += [("row", bit) for bit in reversed(range(row_bits))]
-    value = value.reshape((2,) * (frame_bits + row_bits) + value.shape[1:])
-    value = halve_all(value, names, [("frame", 0)])
-    names.remove(("frame", 0))
+    value = value.reshape((2,) * len(names) + value.shape[2:])
     upward = [("row", bit) for bit in range(row_bits)]
     width = value.shape[-1] // 2
     left = halve_all(value[..., :width], names, upward)
@@ -258,6 +236,508 @@
         compiler_params=pltpu.CompilerParams(vmem_limit_bytes=52 * 1024 * 1024),
         cost_estimate=pl.CostEstimate(flops=110 * 10**9, bytes_accessed=12 * 10**6, transcendentals=0),
     )(everything, mine)
+
+
+def dot_nt(left, right):
+    return lax.dot_general(left, right, (((1,), (1,)), ((), ())), preferred_element_type=jnp.float32)
+
+
+def dot_tn(left, right):
+    return lax.dot_general(left, right, (((0,), (0,)), ((), ())), preferred_element_type=jnp.float32)
+
+
+MIB = 1024 * 1024
+
+
+def vmem_params(mib, semantics=None):
+    return pltpu.CompilerParams(vmem_limit_bytes=mib * MIB, dimension_semantics=semantics)
+
+
+def whole_spec(array):
+    zeros = (0,) * array.ndim
+    return pl.BlockSpec(array.shape, lambda *_: zeros, pipeline_mode=pl.Buffered(1))
+
+
+def turned(value, cosine, sine):
+    even = lax.broadcasted_iota(jnp.int32, value.shape, 1) % 2 == 0
+    width = value.shape[1]
+    swapped = jnp.where(even, pltpu.roll(value, width - 1, 1), pltpu.roll(value, 1, 1))
+    return value * cosine + swapped * sine
+
+
+def framed(value, frames):
+    rows, width = value.shape
+    return value.reshape(frames, rows // frames, width)
+
+
+def norm_parts(value):
+    mean = jnp.mean(value, axis=-1, keepdims=True)
+    centered = value - mean
+    root = lax.rsqrt(jnp.mean(centered * centered, axis=-1, keepdims=True) + norm_floor)
+    return centered * root, root
+
+
+def project_kernel(slots, me_ref, x_ref, mod_ref, cos_ref, sin_ref, w_ref, hid_ref, *out_refs):
+    frames = mod_ref.shape[1]
+    group = D // slots
+    normed, _ = norm_parts(x_ref[0].astype(jnp.float32))
+    normed = framed(normed, frames)
+    shift = mod_ref[0, :, 0:D][:, None, :]
+    scaling = mod_ref[0, :, D : 2 * D][:, None, :]
+    hidden = (normed * (1.0 + scaling) + shift).reshape(x_ref.shape[1], D).astype(jnp.bfloat16)
+    hid_ref[0] = hidden
+    cosine = cos_ref[...]
+    sine = sin_ref[...]
+    me = me_ref[0]
+    for slot in range(slots):
+        peer = me ^ slot
+        for part in range(3):
+            rows = pl.ds(pl.multiple_of(part * D + peer * group, group), group)
+            value = dot_nt(hidden, w_ref[rows, :])
+            if part == 2:
+                out_refs[slot][part] = value.astype(jnp.bfloat16)
+                continue
+            for first in range(0, group, 128):
+                piece = turned(value[:, first : first + 128], cosine, sine)
+                if part == 0:
+                    piece = piece * (1.0 / math.sqrt(HD))
+                out_refs[slot][part, :, first : first + 128] = piece.astype(jnp.bfloat16)
+
+
+def project(me, clip, tokens, mod, cosine, sine, w_qkv, slots):
+    count, tall_rows, _ = tokens.shape
+    tile = 256
+    steps = tall_rows // tile
+    group = D // slots
+    out_shape = [jax.ShapeDtypeStruct((1, tall_rows, D), jnp.bfloat16)]
+    out_shape += [jax.ShapeDtypeStruct((3, tall_rows, group), jnp.bfloat16)] * slots
+    return pl.pallas_call(
+        functools.partial(project_kernel, slots),
+        grid=(steps,),
+        in_specs=[
+            pl.BlockSpec(memory_space=pltpu.SMEM),
+            pl.BlockSpec((1, tile, D), lambda i: (clip, i, 0)),
+            pl.BlockSpec((1, mod.shape[1], 6 * D), lambda i: (clip * steps + i, 0, 0)),
+            pl.BlockSpec((tile, 128), lambda i: (clip * steps + i, 0)),
+            pl.BlockSpec((tile, 128), lambda i: (clip * steps + i, 0)),
+            whole_spec(w_qkv),
+        ],
+        out_specs=[pl.BlockSpec((1, tile, D), lambda i: (0, i, 0))]
+        + [pl.BlockSpec((3, tile, group), lambda i: (0, i, 0))] * slots,
+        out_shape=out_shape,
+        compiler_params=vmem_params(48),
+        cost_estimate=pl.CostEstimate(
+            flops=6 * tall_rows * D * D, bytes_accessed=10 * MIB, transcendentals=0
+        ),
+        name="project",
+    )(me, tokens, mod, cosine, sine, w_qkv)
+
+
+def head_mask(shape, head, axis):
+    return lax.broadcasted_iota(jnp.int32, shape, axis) // HD == head
+
+
+def attend_kernel(slots, tile, *refs):
+    ins, outs = refs[:slots], refs[slots : 2 * slots]
+    full_ref, log_ref, qs, ks, vs = refs[2 * slots :]
+    length = ins[0].shape[1]
+    for slot in range(slots):
+        rows = slice(slot * length, (slot + 1) * length)
+        qs[rows, :] = ins[slot][0]
+        ks[rows, :] = ins[slot][1]
+        vs[rows, :] = ins[slot][2]
+
+    def one(index, carry):
+        rows = pl.ds(pl.multiple_of(index * tile, tile), tile)
+        query = qs[rows, :]
+        first = head_mask((tile, 128), 0, 1)
+        parts = []
+        logs = []
+        for head in range(2):
+            masked = jnp.where(first if head == 0 else ~first, query, jnp.zeros_like(query))
+            scores = dot_nt(masked, ks[...])
+            top = jnp.max(scores, axis=-1, keepdims=True)
+            raised = jnp.exp(scores - top)
+            total = jnp.sum(raised, axis=-1, keepdims=True)
+            parts.append(dot_low(raised.astype(jnp.bfloat16), vs[...]) * (1.0 / total))
+            logs.append(top + jnp.log(total))
+        full_ref[rows, :] = jnp.where(first, parts[0], parts[1])
+        log_ref[rows, :] = jnp.where(first, logs[0], logs[1])
+        return carry
+
+    lax.fori_loop(0, slots * length // tile, one, 0)
+    for slot in range(slots):
+        rows = slice(slot * length, (slot + 1) * length)
+        outs[slot][...] = full_ref[rows, :].astype(jnp.bfloat16)
+
+
+def attend(pieces):
+    slots = len(pieces)
+    _, length, group = pieces[0].shape
+    total = slots * length
+    scratch = pltpu.VMEM((total, 128), jnp.bfloat16)
+    outs = pl.pallas_call(
+        functools.partial(attend_kernel, slots, 256),
+        grid=(group // 128,),
+        in_specs=[pl.BlockSpec((3, length, 128), lambda i: (0, 0, i))] * slots,
+        out_specs=[pl.BlockSpec((length, 128), lambda i: (0, i))] * slots
+        + [pl.BlockSpec((total, 128), lambda i: (0, i))] * 2,
+        out_shape=[jax.ShapeDtypeStruct((length, group), jnp.bfloat16)] * slots
+        + [jax.ShapeDtypeStruct((total, group), jnp.float32)] * 2,
+        scratch_shapes=[scratch] * 3,
+        compiler_params=vmem_params(48),
+        cost_estimate=pl.CostEstimate(
+            flops=16 * total * total * group, bytes_accessed=8 * MIB, transcendentals=total * total * 4
+        ),
+        name="attend",
+    )(*pieces)
+    return outs[:slots], outs[slots], outs[slots + 1]
+
+
+def attend_back_kernel(slots, tile, *refs):
+    ins, grads = refs[:slots], refs[slots : 2 * slots]
+    full_ref, log_ref = refs[2 * slots : 2 * slots + 2]
+    outs = refs[2 * slots + 2 : 3 * slots + 2]
+    qs, ks, vs, gs, q_turned, g_turned, dq, dk, dv = refs[3 * slots + 2 :]
+    length = ins[0].shape[1]
+    total = slots * length
+    for slot in range(slots):
+        rows = slice(slot * length, (slot + 1) * length)
+        qs[rows, :] = ins[slot][0]
+        ks[rows, :] = ins[slot][1]
+        vs[rows, :] = ins[slot][2]
+        gs[rows, :] = grads[slot][...]
+        q_turned[:, rows] = ins[slot][0].T
+        g_turned[:, rows] = grads[slot][...].T
+    dk[...] = jnp.zeros_like(dk)
+    dv[...] = jnp.zeros_like(dv)
+
+    def one(index, carry):
+        rows = pl.ds(pl.multiple_of(index * tile, tile), tile)
+        first = head_mask((tile, 128), 0, 1)
+        upper = head_mask((128, tile), 0, 0)
+        query, grad = qs[rows, :], gs[rows, :]
+        query_t, grad_t = q_turned[:, rows], g_turned[:, rows]
+        product = grad.astype(jnp.float32) * full_ref[rows, :]
+        masks = (first, ~first)
+        masks_t = (upper, ~upper)
+        zero = jnp.zeros_like(query)
+        zero_t = jnp.zeros_like(query_t)
+        q_low = [jnp.where(mask, query, zero) for mask in masks]
+        g_low = [jnp.where(mask, grad, zero) for mask in masks]
+        qt_low = [jnp.where(mask, query_t, zero_t) for mask in masks_t]
+        gt_low = [jnp.where(mask, grad_t, zero_t) for mask in masks_t]
+        inner = [jnp.sum(jnp.where(mask, product, 0.0), axis=-1, keepdims=True) for mask in masks]
+        logs = [log_ref[rows, 0:1], log_ref[rows, HD : HD + 1]]
+
+        def inside(k_index, sums):
+            at = pl.ds(pl.multiple_of(k_index * tile, tile), tile)
+            key, value = ks[at, :], vs[at, :]
+            out = []
+            for head in range(2):
+                probs = jnp.exp(dot_nt(q_low[head], key) - logs[head])
+                d_probs = dot_nt(g_low[head], value)
+                d_scores = (probs * (d_probs - inner[head])).astype(jnp.bfloat16)
+                dv[:, at] += dot_low(gt_low[head], probs.astype(jnp.bfloat16))
+                dk[:, at] += dot_low(qt_low[head], d_scores)
+                out.append(sums[head] + dot_low(d_scores, key))
+            return tuple(out)
+
+        start = jnp.zeros((tile, 128), jnp.float32)
+        sums = lax.fori_loop(0, total // tile, inside, (start, start))
+        dq[rows, :] = (jnp.where(first, sums[0], sums[1]) * (1.0 / math.sqrt(HD))).astype(jnp.bfloat16)
+        return carry
+
+    lax.fori_loop(0, total // tile, one, 0)
+    for slot in range(slots):
+        rows = slice(slot * length, (slot + 1) * length)
+        outs[slot][0] = dq[rows, :]
+        outs[slot][1] = dk[:, rows].T.astype(jnp.bfloat16)
+        outs[slot][2] = dv[:, rows].T.astype(jnp.bfloat16)
+
+
+def attend_back(pieces, grads, full, logs):
+    slots = len(pieces)
+    _, length, group = pieces[0].shape
+    total = slots * length
+    low = pltpu.VMEM((total, 128), jnp.bfloat16)
+    low_t = pltpu.VMEM((128, total), jnp.bfloat16)
+    full_t = pltpu.VMEM((128, total), jnp.float32)
+    return pl.pallas_call(
+        functools.partial(attend_back_kernel, slots, 512),
+        grid=(group // 128,),
+        in_specs=[pl.BlockSpec((3, length, 128), lambda i: (0, 0, i))] * slots
+        + [pl.BlockSpec((length, 128), lambda i: (0, i))] * slots
+        + [pl.BlockSpec((total, 128), lambda i: (0, i))] * 2,
+        out_specs=[pl.BlockSpec((3, length, 128), lambda i: (0, 0, i))] * slots,
+        out_shape=[jax.ShapeDtypeStruct((3, length, group), jnp.bfloat16)] * slots,
+        scratch_shapes=[low] * 4 + [low_t] * 2 + [low] + [full_t] * 2,
+        compiler_params=vmem_params(48),
+        cost_estimate=pl.CostEstimate(
+            flops=40 * total * total * group, bytes_accessed=12 * MIB, transcendentals=total * total * 4
+        ),
+        name="attend_back",
+    )(*pieces, *grads, full, logs)
+
+
+def middle_kernel(slots, me_ref, x_ref, cot_ref, mod_ref, wo_ref, wu_ref, wd_ref, *refs):
+    att_refs = refs[:slots]
+    datt_refs = refs[slots : 2 * slots]
+    (
+        out_ref,
+        att_ref,
+        h2_ref,
+        act_ref,
+        db2_ref,
+        dup_ref,
+        db1_ref,
+        dmid_ref,
+        sums_ref,
+        slope,
+    ) = refs[2 * slots :]
+    frames = mod_ref.shape[1]
+    rows = x_ref.shape[1]
+    group = D // slots
+    me = me_ref[0]
+
+    def mod(index):
+        return mod_ref[0, :, index * D : (index + 1) * D][:, None, :]
+
+    def spread(value, index, plus=0.0):
+        return (framed(value, frames) * (mod(index) + plus)).reshape(rows, D)
+
+    def frame_sum(value):
+        return jnp.sum(framed(value, frames), axis=1)
+
+    branch = jnp.zeros((rows, D), jnp.float32)
+    for slot in range(slots):
+        at = pl.ds(pl.multiple_of((me ^ slot) * group, group), group)
+        piece = att_refs[slot][...]
+        att_ref[:, at] = piece
+        branch += dot_low(piece, wo_ref[at, :])
+    middle = x_ref[0].astype(jnp.float32) + spread(branch, 2)
+    normed, root = norm_parts(middle)
+    hidden = (framed(spread(normed, 4, 1.0), frames) + mod(3)).reshape(rows, D).astype(jnp.bfloat16)
+    h2_ref[...] = hidden
+    wide = 1024
+    curve = math.sqrt(2.0 / math.pi)
+    branch_two = jnp.zeros((rows, D), jnp.float32)
+    for first in range(0, FF, wide):
+        cut = slice(first, first + wide)
+        up = dot_nt(hidden, wu_ref[cut, :])
+        square = up * up
+        bent = jnp.tanh(curve * up * (1.0 + 0.044715 * square))
+        half = 0.5 * (1.0 + bent)
+        active = (up * half).astype(jnp.bfloat16)
+        slope[:, cut] = half + 0.5 * up * (1.0 - bent * bent) * (curve * (1.0 + 3 * 0.044715 * square))
+        act_ref[:, cut] = active
+        branch_two += dot_low(active, wd_ref[cut, :])
+    cot = cot_ref[0].astype(jnp.float32)
+    out_ref[0] = (middle + spread(branch_two, 5)).astype(jnp.bfloat16)
+    sums_ref[0, 3] = frame_sum(cot * branch_two)
+    d_branch_two = spread(cot, 5).astype(jnp.bfloat16)
+    db2_ref[...] = d_branch_two
+    d_hidden = jnp.zeros((rows, D), jnp.float32)
+    for first in range(0, FF, wide):
+        cut = slice(first, first + wide)
+        d_up = (dot_nt(d_branch_two, wd_ref[cut, :]) * slope[:, cut]).astype(jnp.bfloat16)
+        dup_ref[:, cut] = d_up
+        d_hidden += dot_low(d_up, wu_ref[cut, :])
+    sums_ref[0, 1] = frame_sum(d_hidden)
+    sums_ref[0, 2] = frame_sum(d_hidden * normed)
+    inner = spread(d_hidden, 4, 1.0)
+    d_middle = cot + root * (
+        inner
+        - jnp.mean(inner, axis=-1, keepdims=True)
+        - normed * jnp.mean(inner * normed, axis=-1, keepdims=True)
+    )
+    dmid_ref[...] = d_middle
+    sums_ref[0, 0] = frame_sum(d_middle * branch)
+    d_branch = spread(d_middle, 2).astype(jnp.bfloat16)
+    db1_ref[...] = d_branch
+    for slot in range(slots):
+        at = pl.ds(pl.multiple_of((me ^ slot) * group, group), group)
+        datt_refs[slot][...] = dot_nt(d_branch, wo_ref[at, :]).astype(jnp.bfloat16)
+
+
+def middle(me, clip, tokens, cotangent, mod, w_out, w_up, w_down, attended):
+    slots = len(attended)
+    count, length, _ = tokens.shape
+    tile = 256
+    steps = length // tile
+    group = D // slots
+    frames = mod.shape[1]
+    low = jnp.bfloat16
+
+    def flat(width, kind=low):
+        return jax.ShapeDtypeStruct((length, width), kind)
+
+    def flat_spec(width):
+        return pl.BlockSpec((tile, width), lambda i: (i, 0))
+
+    outs = pl.pallas_call(
+        functools.partial(middle_kernel, slots),
+        grid=(steps,),
+        in_specs=[
+            pl.BlockSpec(memory_space=pltpu.SMEM),
+            pl.BlockSpec((1, tile, D), lambda i: (clip, i, 0)),
+            pl.BlockSpec((1, tile, D), lambda i: (clip, i, 0)),
+            pl.BlockSpec((1, frames, 6 * D), lambda i: (clip * steps + i, 0, 0)),
+            whole_spec(w_out),
+            whole_spec(w_up),
+            whole_spec(w_down),
+        ]
+        + [flat_spec(group)] * slots,
+        out_specs=[flat_spec(group)] * slots
+        + [pl.BlockSpec((1, tile, D), lambda i: (0, i, 0))]
+        + [flat_spec(width) for width in (D, D, FF, D, FF, D, D)]
+        + [pl.BlockSpec((1, 4, frames, D), lambda i: (i, 0, 0, 0))],
+        out_shape=[flat(group)] * slots
+        + [jax.ShapeDtypeStruct((1, length, D), low)]
+        + [flat(D), flat(D), flat(FF), flat(D), flat(FF), flat(D), flat(D, jnp.float32)]
+        + [jax.ShapeDtypeStruct((steps, 4, frames, D), jnp.float32)],
+        scratch_shapes=[pltpu.VMEM((tile, FF), jnp.float32)],
+        compiler_params=vmem_params(58),
+        cost_estimate=pl.CostEstimate(
+            flops=2 * length * D * (2 * D + 4 * FF), bytes_accessed=40 * MIB, transcendentals=length * FF
+        ),
+        name="middle",
+    )(me, tokens, cotangent, mod, w_out, w_up, w_down, *attended)
+    return outs[:slots], outs[slots:]
+
+
+def last_kernel(slots, me_ref, x_ref, mod_ref, cos_ref, sin_ref, w_ref, dmid_ref, *refs):
+    pieces = refs[:slots]
+    dproj_ref, grad_ref, sums_ref = refs[slots:]
+    frames = mod_ref.shape[1]
+    rows = x_ref.shape[1]
+    group = D // slots
+    me = me_ref[0]
+    cosine = cos_ref[...]
+    sine = -sin_ref[...]
+    d_hidden = jnp.zeros((rows, D), jnp.float32)
+    for slot in range(slots):
+        peer = me ^ slot
+        for part in range(3):
+            base = pl.multiple_of(part * D + peer * group, group)
+            if part == 2:
+                value = pieces[slot][part]
+            else:
+                value = jnp.concatenate(
+                    [
+                        turned(pieces[slot][part, :, at : at + 128].astype(jnp.float32), cosine, sine)
+                        for at in range(0, group, 128)
+                    ],
+                    axis=1,
+                ).astype(jnp.bfloat16)
+            dproj_ref[:, pl.ds(base, group)] = value
+            d_hidden += dot_low(value, w_ref[pl.ds(base, group), :])
+    normed, root = norm_parts(x_ref[0].astype(jnp.float32))
+    scaling = mod_ref[0, :, D : 2 * D][:, None, :]
+    sums_ref[0, 0] = jnp.sum(framed(d_hidden, frames), axis=1)
+    sums_ref[0, 1] = jnp.sum(framed(d_hidden * normed, frames), axis=1)
+    inner = (framed(d_hidden, frames) * (1.0 + scaling)).reshape(rows, D)
+    grad_ref[0] = dmid_ref[...] + root * (
+        inner
+        - jnp.mean(inner, axis=-1, keepdims=True)
+        - normed * jnp.mean(inner * normed, axis=-1, keepdims=True)
+    )
+
+
+def last(me, clip, tokens, mod, cosine, sine, w_qkv, d_middle, pieces):
+    slots = len(pieces)
+    count, length, _ = tokens.shape
+    tile = 256
+    steps = length // tile
+    group = D // slots
+    frames = mod.shape[1]
+    return pl.pallas_call(
+        functools.partial(last_kernel, slots),
+        grid=(steps,),
+        in_specs=[
+            pl.BlockSpec(memory_space=pltpu.SMEM),
+            pl.BlockSpec((1, tile, D), lambda i: (clip, i, 0)),
+            pl.BlockSpec((1, frames, 6 * D), lambda i: (clip * steps + i, 0, 0)),
+            pl.BlockSpec((tile, 128), lambda i: (clip * steps + i, 0)),
+            pl.BlockSpec((tile, 128), lambda i: (clip * steps + i, 0)),
+            whole_spec(w_qkv),
+            pl.BlockSpec((tile, D), lambda i: (i, 0)),
+        ]
+        + [pl.BlockSpec((3, tile, group), lambda i: (0, i, 0))] * slots,
+        out_specs=[
+            pl.BlockSpec((tile, 3 * D), lambda i: (i, 0)),
+            pl.BlockSpec((1, tile, D), lambda i: (0, i, 0)),
+            pl.BlockSpec((1, 2, frames, D), lambda i: (i, 0, 0, 0)),
+        ],
+        out_shape=[
+            jax.ShapeDtypeStruct((length, 3 * D), jnp.bfloat16),
+            jax.ShapeDtypeStruct((1, length, D), jnp.float32),
+            jax.ShapeDtypeStruct((steps, 2, frames, D), jnp.float32),
+        ],
+        compiler_params=vmem_params(48),
+        cost_estimate=pl.CostEstimate(
+            flops=6 * length * D * D, bytes_accessed=20 * MIB, transcendentals=0
+        ),
+        name="last",
+    )(me, tokens, mod, cosine, sine, w_qkv, d_middle, *pieces)
+
+
+def weight_kernel(doubled, split_ref, *refs):
+    members = len(doubled)
+    out_ref = refs[-1]
+    first = 0
+    for member in range(members):
+        left = refs[4 * member : 4 * member + 2]
+        right = refs[4 * member + 2 : 4 * member + 4]
+        value = dot_tn(left[0][...], right[0][...]) + dot_tn(left[1][...], right[1][...])
+        if doubled[member]:
+            half = value.shape[0] // 2
+            value = jnp.where(split_ref[0] == 0, value[:half], value[half:])
+        height = value.shape[0] // out_ref.shape[1]
+        out_ref[0, :, first : first + height, :] = value.reshape(
+            out_ref.shape[1], height, value.shape[1]
+        ).astype(out_ref.dtype)
+        first += height
+
+
+def weight_sums(keep, pairs, kind, name):
+    frame_devices = lax.axis_size("frame")
+    row_devices = lax.axis_size("row")
+    specs, operands, doubled = [], [], []
+    height = 0
+    for left, right in pairs:
+        width = left[0].shape[1] // frame_devices
+        height += width // row_devices
+        doubled.append(width % 128 != 0)
+        if doubled[-1]:
+            spec = pl.BlockSpec((left[0].shape[0], 2 * width), lambda i, s: (0, i))
+        else:
+            spec = pl.BlockSpec((left[0].shape[0], width), lambda i, s: (0, 2 * i + s[0]))
+        specs += [spec] * 2
+        specs += [pl.BlockSpec(right[0].shape, lambda i, s: (0, 0))] * 2
+        operands += [*left, *right]
+    flops = sum(4 * left[0].shape[0] * left[0].shape[1] * D // 2 for left, _ in pairs)
+    return pl.pallas_call(
+        functools.partial(weight_kernel, tuple(doubled)),
+        grid_spec=pltpu.PrefetchScalarGridSpec(
+            num_scalar_prefetch=1,
+            grid=(frame_devices // 2,),
+            in_specs=specs,
+            out_specs=pl.BlockSpec((1, row_devices, height, D), lambda i, s: (i, 0, 0, 0)),
+        ),
+        out_shape=jax.ShapeDtypeStruct((frame_devices // 2, row_devices, height, D), kind),
+        compiler_params=vmem_params(48),
+        cost_estimate=pl.CostEstimate(flops=flops, bytes_accessed=30 * MIB, transcendentals=0),
+        name=name,
+    )(keep, *operands)
+
+
+def swap(slots):
+    size = lax.axis_size("row")
+    out = [slots[0]]
+    for slot in range(1, size):
+        out.append(lax.ppermute(slots[slot], "row", [(index, index ^ slot) for index in range(size)]))
+    return out
 
 
 def per_device(
@@ -289,19 +769,17 @@
     clip_count, frames, rows_dev, columns, model_width = tokens.shape
     seq_local = frames * rows_dev * columns
     row_devices = lax.axis_size("row")
-    seq_full = seq_local * row_devices
     token_total = clip_count * seq_local
     frame_total = clip_count * frames
-    attn_scale = 1.0 / math.sqrt(HD)
     shape_five = (clip_count, frames, rows_dev, columns, model_width)
-    w_qkv, w_out, w_up, w_down, w_ada, w_table, w_bias = (
-        lax.all_gather(qkv_master.astype(low_type), ("frame", "row"), axis=1, tiled=True),
-        lax.all_gather(out_master.astype(low_type), ("frame", "row"), axis=0, tiled=True),
-        lax.all_gather(up_master.astype(low_type), ("frame", "row"), axis=1, tiled=True),
-        lax.all_gather(down_master.astype(low_type), ("frame", "row"), axis=0, tiled=True),
+    w_table, w_ada, w_bias = (
+        lax.all_gather(table_master.astype(low_type), ("frame", "row"), axis=0, tiled=True),
         lax.all_gather(ada_master.astype(low_type), ("frame", "row"), axis=1, tiled=True),
-        lax.all_gather(table_master.astype(low_type), ("frame", "row"), axis=0, tiled=True),
         lax.all_gather(bias_master.astype(low_type), ("frame", "row"), axis=0, tiled=True),
+    )
+    w_qkv, w_out, w_up, w_down = (
+        lax.all_gather(item.astype(low_type), ("frame", "row"), axis=0, tiled=True)
+        for item in (qkv_master.T, out_master, up_master.T, down_master)
     )
     level_flat = noise_levels.reshape(frame_total)
     level_hot = (
@@ -312,12 +790,6 @@
     modulation = jnp.dot(cond_low, w_ada, preferred_element_type=full_type) + w_bias.astype(
         full_type
     )
-    mod_five = modulation.reshape(clip_count, frames, 1, 1, 6 * model_width)
-    pieces = [
-        mod_five[..., piece_index * model_width : (piece_index + 1) * model_width]
-        for piece_index in range(6)
-    ]
-    shift_one, scale_one, gate_one, shift_two, scale_two, gate_two = pieces
     grid_shape = (clip_count, frames, rows_dev, columns)
     row_first = lax.axis_index("row") * rows_dev
     time_grid = jnp.broadcast_to(frame_times.astype(full_type)[:, :, None, None], grid_shape)
@@ -329,180 +801,57 @@
         jnp.arange(columns, dtype=jnp.int32).astype(full_type)[None, None, None, :], grid_shape
     )
     angles = rotary_angles(time_grid, row_grid, column_grid).reshape(clip_count, seq_local, HD // 2)
-    inputs_full = tokens.astype(full_type)
-    hidden_one = (
-        modulate(inputs_full, shift_one, scale_one)
-        .astype(low_type)
-        .reshape(token_total, model_width)
-    )
-    projected = jnp.dot(hidden_one, w_qkv, preferred_element_type=full_type).reshape(
-        clip_count, seq_local, 3, HEADS, HD
-    )
-    queries = rotate(projected[:, :, 0], angles).astype(low_type)
-    keys_rot = rotate(projected[:, :, 1], angles).astype(low_type)
-    values_low = projected[:, :, 2].astype(low_type)
-    keys_whole, values_whole = (
-        lax.all_gather(keys_rot.reshape(shape_five), "row", axis=2, tiled=True),
-        lax.all_gather(values_low.reshape(shape_five), "row", axis=2, tiled=True),
-    )
-    keys_seq = keys_whole.reshape(clip_count, seq_full, HEADS, HD)
-    values_seq = values_whole.reshape(clip_count, seq_full, HEADS, HD)
-
-    def attend_clip(operands):
-        query_block, key_block, value_block = operands
-        outputs = []
-        log_totals = []
-        for group_index in range(HEADS // group_heads):
-            head_first = group_index * group_heads
-            head_last = head_first + group_heads
-            scores = (
-                jnp.einsum(
-                    "qhd,khd->hqk",
-                    query_block[:, head_first:head_last],
-                    key_block[:, head_first:head_last],
-                    preferred_element_type=full_type,
-                )
-                * attn_scale
-            )
-            top_score = jnp.max(scores, axis=-1, keepdims=True)
-            raised = jnp.exp(scores - top_score)
-            total_weight = jnp.sum(raised, axis=-1, keepdims=True)
-            prob_low = (raised / total_weight).astype(low_type)
-            outputs.append(
-                jnp.einsum(
-                    "hqk,khd->qhd",
-                    prob_low,
-                    value_block[:, head_first:head_last],
-                    preferred_element_type=full_type,
-                )
-            )
-            log_totals.append((top_score + jnp.log(total_weight))[..., 0])
-        return (jnp.concatenate(outputs, axis=1), jnp.concatenate(log_totals, axis=0))
-
-    attended_full, log_total = lax.map(attend_clip, (queries, keys_seq, values_seq))
-    attended = attended_full.astype(low_type).reshape(token_total, model_width)
-    branch_one = jnp.dot(attended, w_out, preferred_element_type=full_type).reshape(shape_five)
-    middle = inputs_full + gate_one * branch_one
-    hidden_two = (
-        modulate(middle, shift_two, scale_two).astype(low_type).reshape(token_total, model_width)
-    )
-    up_value = jnp.dot(hidden_two, w_up, preferred_element_type=full_type)
-    activated = gelu_tanh(up_value).astype(low_type)
-    branch_two = jnp.dot(activated, w_down, preferred_element_type=full_type).reshape(shape_five)
-    block_out = (middle + gate_two * branch_two).astype(low_type)
-    upstream = cotangent.astype(full_type)
-    d_branch_two = (upstream * gate_two).astype(low_type).reshape(token_total, model_width)
-    d_gate_two = jnp.sum(upstream * branch_two, axis=(2, 3))
-    grad_down = jnp.einsum("tf,td->fd", activated, d_branch_two, preferred_element_type=full_type)
-    d_activated = jnp.einsum("td,fd->tf", d_branch_two, w_down, preferred_element_type=full_type)
-    d_up = jax.vjp(gelu_tanh, up_value)[1](d_activated)[0].astype(low_type)
-    grad_up = jnp.einsum("tf,td->fd", d_up, hidden_two, preferred_element_type=full_type)
-    d_hidden_two = jnp.einsum("tf,df->td", d_up, w_up, preferred_element_type=full_type).reshape(
-        shape_five
-    )
-    d_middle_part, d_shift_two, d_scale_two = jax.vjp(modulate, middle, shift_two, scale_two)[1](
-        d_hidden_two
-    )
-    d_middle = upstream + d_middle_part
-    d_gate_one = jnp.sum(d_middle * branch_one, axis=(2, 3))
-    d_branch_one = (d_middle * gate_one).astype(low_type).reshape(token_total, model_width)
-    grad_out = jnp.einsum("td,te->de", attended, d_branch_one, preferred_element_type=full_type)
-    d_attended = (
-        jnp.einsum("te,de->td", d_branch_one, w_out, preferred_element_type=full_type)
-        .astype(low_type)
-        .reshape(clip_count, seq_local, HEADS, HD)
-    )
-
-    def attend_back(operands):
-        query_block, key_block, value_block, log_block, grad_block = operands
-        query_parts = []
-        key_parts = []
-        value_parts = []
-        for group_index in range(HEADS // group_heads):
-            head_first = group_index * group_heads
-            head_last = head_first + group_heads
-            query_group = query_block[:, head_first:head_last]
-            key_group = key_block[:, head_first:head_last]
-            value_group = value_block[:, head_first:head_last]
-            grad_group = grad_block[:, head_first:head_last]
-            scores = (
-                jnp.einsum("qhd,khd->hqk", query_group, key_group, preferred_element_type=full_type)
-                * attn_scale
-            )
-            prob_full = jnp.exp(scores - log_block[head_first:head_last][..., None])
-            grad_prob = jnp.einsum(
-                "qhd,khd->hqk", grad_group, value_group, preferred_element_type=full_type
-            )
-            inner_sum = jnp.sum(prob_full * grad_prob, axis=-1, keepdims=True)
-            grad_scores = (prob_full * (grad_prob - inner_sum)).astype(low_type)
-            query_parts.append(
-                jnp.einsum("hqk,khd->qhd", grad_scores, key_group, preferred_element_type=full_type)
-                * attn_scale
-            )
-            key_parts.append(
-                jnp.einsum(
-                    "hqk,qhd->khd", grad_scores, query_group, preferred_element_type=full_type
-                )
-                * attn_scale
-            )
-            value_parts.append(
-                jnp.einsum(
-                    "hqk,qhd->khd",
-                    prob_full.astype(low_type),
-                    grad_group,
-                    preferred_element_type=full_type,
-                )
-            )
-        return (
-            jnp.concatenate(query_parts, axis=1),
-            jnp.concatenate(key_parts, axis=1),
-            jnp.concatenate(value_parts, axis=1),
+    flat_angles = angles.reshape(token_total, HD // 2)
+    pair_sign = jnp.tile(jnp.array([-1.0, 1.0], full_type), HD)
+    cosine = jnp.tile(jnp.repeat(jnp.cos(flat_angles), 2, axis=1), (1, 2))
+    sine = jnp.tile(jnp.repeat(jnp.sin(flat_angles), 2, axis=1), (1, 2)) * pair_sign
+    tile_count = token_total // 256
+    mod = modulation.reshape(tile_count, frame_total // tile_count, 6 * model_width)
+    me = lax.axis_index("row").astype(jnp.int32).reshape(1)
+    tokens_flat = tokens.reshape(clip_count, seq_local, model_width)
+    cotangent_flat = cotangent.reshape(clip_count, seq_local, model_width)
+    clips = range(clip_count)
+    hidden_one, pieces = [], []
+    for clip in clips:
+        hidden, *slots = project(me, clip, tokens_flat, mod, cosine, sine, w_qkv, row_devices)
+        hidden_one.append(hidden[0])
+        pieces.append(swap(slots))
+    attended, full, logs = [], [], []
+    for clip in clips:
+        slots, full_clip, log_clip = attend(pieces[clip])
+        attended.append(swap(slots))
+        full.append(full_clip)
+        logs.append(log_clip)
+    d_attended, middles = [], []
+    for clip in clips:
+        slots, others = middle(
+            me, clip, tokens_flat, cotangent_flat, mod, w_out, w_up, w_down, attended[clip]
         )
-
-    grad_query, grad_key, grad_value = lax.map(
-        attend_back, (queries, keys_seq, values_seq, log_total, d_attended)
-    )
-    gathered_shape = (clip_count, frames, rows_dev * row_devices, columns, model_width)
-    key_sums, value_sums = (
-        lax.psum_scatter(
-            grad_key.reshape(gathered_shape).astype(jnp.bfloat16),
-            "row",
-            scatter_dimension=2,
-            tiled=True,
-        ).astype(jnp.float32),
-        lax.psum_scatter(
-            grad_value.reshape(gathered_shape).astype(jnp.bfloat16),
-            "row",
-            scatter_dimension=2,
-            tiled=True,
-        ).astype(jnp.float32),
-    )
-    d_queries = rounded(grad_query)
-    d_keys = rounded(key_sums).reshape(clip_count, seq_local, HEADS, HD)
-    d_values = rounded(value_sums).reshape(clip_count, seq_local, HEADS, HD)
-    d_projected = (
-        jnp.stack([rotate(d_queries, -angles), rotate(d_keys, -angles), d_values], axis=2)
-        .astype(low_type)
-        .reshape(token_total, 3 * model_width)
-    )
-    grad_qkv = jnp.einsum("te,td->ed", d_projected, hidden_one, preferred_element_type=full_type)
-    d_hidden_one = jnp.einsum(
-        "te,de->td", d_projected, w_qkv, preferred_element_type=full_type
-    ).reshape(shape_five)
-    d_input_part, d_shift_one, d_scale_one = jax.vjp(modulate, inputs_full, shift_one, scale_one)[
-        1
-    ](d_hidden_one)
-    input_grad = d_middle + d_input_part
-    frame_shape = (frame_total, model_width)
+        d_attended.append(swap(slots))
+        middles.append(others)
+    block_out = jnp.concatenate([item[0] for item in middles], axis=0).reshape(shape_five)
+    att_low, hidden_two, activated, d_branch_two, d_up, d_branch_one, d_middle, two_sums = (
+        [item[index] for item in middles] for index in range(1, 9)
+    )
+    early = scatter_sum(
+        [(activated, d_branch_two), (d_up, hidden_two), (att_low, d_branch_one)], "early"
+    )
+    d_pieces = [
+        swap(attend_back(pieces[clip], d_attended[clip], full[clip], logs[clip])) for clip in clips
+    ]
+    lasts = [
+        last(me, clip, tokens_flat, mod, cosine, sine, w_qkv, d_middle[clip], d_pieces[clip])
+        for clip in clips
+    ]
+    input_grad = jnp.concatenate([item[1] for item in lasts], axis=0).reshape(shape_five)
+    g_qkv = scatter_sum([([item[0] for item in lasts], hidden_one)], "late")
+
+    def frames_of(sums, index):
+        return jnp.concatenate([item[:, index].reshape(frames, model_width) for item in sums], axis=0)
+
+    one_sums = [item[2] for item in lasts]
     d_modulation = jnp.concatenate(
-        [
-            d_shift_one.reshape(frame_shape),
-            d_scale_one.reshape(frame_shape),
-            d_gate_one.reshape(frame_shape),
-            d_shift_two.reshape(frame_shape),
-            d_scale_two.reshape(frame_shape),
-            d_gate_two.reshape(frame_shape),
-        ],
+        [frames_of(one_sums, 0), frames_of(one_sums, 1)] + [frames_of(two_sums, index) for index in range(4)],
         axis=1,
     )
     frame_devices = lax.axis_size("frame")
@@ -541,20 +890,9 @@
     ).astype(full_type)
     g_table = jnp.dot(hot_mine, d_embedded, precision=highest)
     heights = (qkv_master.shape[1], out_master.shape[0], up_master.shape[1], down_master.shape[0])
-    early = scatter_sum(
-        jnp.concatenate(
-            [
-                grad_down.reshape(device_total, heights[3], model_width),
-                grad_up.reshape(device_total, heights[2], model_width),
-                grad_out.reshape(device_total, heights[1], model_width),
-            ],
-            axis=1,
-        )
-    )
     g_down = early[: heights[3]]
     g_up = early[heights[3] : heights[3] + heights[2]]
     g_out = early[heights[3] + heights[2] :]
-    g_qkv = scatter_sum(grad_qkv.reshape(device_total, heights[0], model_width))
     muon_grads = (g_qkv, g_out, g_up, g_down)
     flipped = (True, False, True, False)
 

time: 2530 us -> 1360 us (0.54)
  matrix products: 582 us -> 16.3 us
  local copies, waits for them, and re-layouts: 544 us -> 64.5 us
  Pallas kernels: 129 us -> 443 us
  other arithmetic: 308 us -> 57.8 us
  waiting for transfers between devices: 748 us -> 574 us
    dot_general x68 -> x0, matrix products: 564 us -> none  [the longest x8 101 us: attend_back(): jnp.einsum('qhd,khd->hqk', grad_group, value_group, preferred_element_typ...]
    pallas_call x0 -> x14, Pallas kernels: none -> 314 us  [the longest x2 103 us: attend_back(): pl.pallas_call(functools.partial(attend_back_kernel, slots, 512), grid=(g...]
    convert_element_type x13 -> x1, local copies, waits for them, and re-layouts: 193 us -> 0.01 us  [per_device(): mod_mine = jnp.sum(mod_parts.reshape(frame_devices, row_devices, frame_to...]
    unnamed x12 -> x8, waiting for transfers between devices: 139 us -> 0.13 us
    ppermute x14 -> x12, waiting for transfers between devices: 159 us -> 57.4 us  [halve(): came = lax.ppermute(send.astype(jnp.bfloat16), axis, pairs)]
    convert_element_type x17 -> x4, other arithmetic: 104 us -> 3.86 us  [per_device(): item.astype(low_type)]
    reduce_sum x15 -> x0, other arithmetic: 70.2 us -> none  [the longest x8 52.6 us: attend_clip(): total_weight = jnp.sum(raised, axis=-1, keepdims=True)]
    while x143 -> x0, local copies, waits for them, and re-layouts: 64.7 us -> none  [the longest x2 37.2 us: per_device(): lax.map(attend_clip, (queries, keys_seq, values_seq))]
  transfers between devices with their start and end apart: 27 -> 48, of which waited for: 16 -> 22; matrix products, arithmetic and copies ran while one was open for 48% -> 8% of each run, Pallas kernels for 0% -> 23%
where the time goes in v2:
time: 1360 us; the launch traced here: 1350 us
  waiting for transfers between devices  574 us (42%)
  Pallas kernels  443 us (33%)
  blocking collectives  118 us (9%)
  local copies, waits for them, and re-layouts  64.5 us (5%)
  other arithmetic  57.8 us (4%)
  starting transfers between devices  50.6 us (4%)
  between operations  23.6 us (2%)
  matrix products  16.3 us (1%)
    all_gather x4, waiting for transfers between devices, per_device(): lax.all_gather(item.astype(low_type), ('frame', 'row'), axis=0, tiled=True)  180 us
    pallas_call x1, Pallas kernels, newton(): pl.pallas_call(newton_kernel, out_shape=jax.ShapeDtypeStruct(mine.shape,...  129 us
    pallas_call x2, Pallas kernels, attend_back(): pl.pallas_call(functools.partial(attend_back_kernel, slots, 512), grid=(g...  103 us
    psum x1, waiting for transfers between devices, per_device(): lax.psum(jnp.einsum('fe,de->fd', mod_mine, ada_master.astype(low_type), p...  102 us
    all_gather x1, waiting for transfers between devices, per_device(): lax.all_gather(ada_master.astype(low_type), ('frame', 'row'), axis=1, til...  96 us
    all_gather x1, waiting for transfers between devices, per_device(): everything = lax.all_gather(updates, 'frame', axis=0, tiled=True)  73.1 us
    pallas_call x2, Pallas kernels, middle(): pl.pallas_call(functools.partial(middle_kernel, slots), grid=(steps,), in...  66.5 us
    pallas_call x2, Pallas kernels, attend(): pl.pallas_call(functools.partial(attend_kernel, slots, 256), grid=(group...  64 us
  transfers between devices with their start and end apart: 48, of which 22 were waited for; matrix products, arithmetic and copies ran while one was open for 8% of the time, Pallas kernels for 23%

profile of v2, /device:TPU:8, one launch (start us, length us, event | category | flops | bytes accessed | tf_op | source)
XLA Modules:
  0.0 1348.0 jit_solution(7884903666983896739)
XLA Ops:
  15.7 40.7 %all-reduce.2 = bf16[6144]{0:T(1024)(128)(2,1)S(1)} all-reduce(bf16[6144]{0:T(1024)(128)(2,1)S(1)} %dynamic-update-slice), channel_id=1, replica_groups=mesh['frame'=8,'row'=4] {'frame','row'}, use_global_device_ids=true, to_apply=%add.2 | all-reduce | flops 6144 | bytes 24576
  58.9 9.4 all-gather.8.cloned.1.call-done
  70.9 96.0 %all-gather.10.cloned.1.call-done = bf16[1024,6144]{0,1:T(8,128)(2,1)} async-done(((bf16[1024,192]{0,1:T(8,128)(2,1)}), bf16[1024,6144]{0,1:T(8,128)(2,1)}) %all-gather.10.cloned.1.call-update) | async-done | bytes 12582928 | tf_op jit(solution)/shard_map/all_gather | solution.py:777
  175.0 63.9 %all-gather.18.cloned.1.call-done.w_ref = bf16[3072,1024]{1,0:T(8,128)(2,1)} async-done(((bf16[96,1024]{1,0:T(8,128)(2,1)}), bf16[3072,1024]{1,0:T(8,128)(2,1)}) %all-gather.18.cloned.1.call-update) | async-done | bytes 6291472 | tf_op jit(solution)/shard_map/all_gather | solution.py:781
  238.9 8.5 project.3
  261.5 9.1 collective-permute-done.6.refs_1_
  272.3 16.6 %collective-permute-done.8.refs_3_ = bf16[3,512,256]{2,1,0:T(8,128)(2,1)} collective-permute-done((bf16[3,512,256]{2,1,0:T(8,128)(2,1)}, bf16[3,512,256]{2,1,0:T(8,128)(2,1)}, u32[]{:S(2)}, u32[]{:S(2)}) %collective-permute-start.8) | collective-permute-done | bytes 786464 | tf_op jit(solution)/shard_map/ppermute | solution.py:739
  289.0 32.5 %attend.3 = (bf16[512,256]{1,0:T(8,128)(2,1)S(1)}, bf16[512,256]{1,0:T(8,128)(2,1)S(1)}, bf16[512,256]{1,0:T(8,128)(2,1)}, bf16[512,256]{1,0:T(8,128)(2,1)S(1)},...) custom-call(bf16[3,512,256]{2,1,0:T(8,128)(2,1)S(1)} %copy-done.27, bf16[3,512,256]{2,1,0:T(8,128)(2,1)} %collective-permute-done.6.refs_1_, ...), custom_call_target="tpu_custom_call" | custom-call | flops 17179869184 | bytes 8388608 | tf_op jit(solution)/shard_map/attend/pallas_call | solution.py:379
  326.2 31.5 %attend.2 = (bf16[512,256]{1,0:T(8,128)(2,1)S(1)}, bf16[512,256]{1,0:T(8,128)(2,1)}, bf16[512,256]{1,0:T(8,128)(2,1)}, bf16[512,256]{1,0:T(8,128)(2,1)}, f32[2048,256]{1,0:T(8,128)}, /*index=5*/f32[2048,256]{1,0:T(8,128)}) custom-call(bf16[3,512,256]{2,1,0:T(8,128)(2,1)S(1)} %get-tuple-element.82.refs_0_, ...), custom_call_target="tpu_custom_call" | custom-call | flops 17179869184 | bytes 8388608 | tf_op jit(solution)/shard_map/attend/pallas_call | solution.py:379
  362.6 35.5 %all-gather.14.cloned.1.call-done.wu_ref = bf16[4096,1024]{1,0:T(8,128)(2,1)} async-done(((bf16[128,1024]{1,0:T(8,128)(2,1)}), bf16[4096,1024]{1,0:T(8,128)(2,1)}) %all-gather.14.cloned.1.call-update) | async-done | bytes 8388624 | tf_op jit(solution)/shard_map/all_gather | solution.py:781
  398.2 80.9 %all-gather.16.cloned.1.call-done.wd_ref = bf16[4096,1024]{1,0:T(8,128)(2,1)} async-done(((bf16[128,1024]{1,0:T(8,128)(2,1)}), bf16[4096,1024]{1,0:T(8,128)(2,1)}) %all-gather.16.cloned.1.call-update) | async-done | bytes 8388624 | tf_op jit(solution)/shard_map/all_gather | solution.py:781
  479.0 33.1 %middle.3 = (bf16[512,256]{1,0:T(8,128)(2,1)}, bf16[512,256]{1,0:T(8,128)(2,1)}, bf16[512,256]{1,0:T(8,128)(2,1)}, bf16[512,256]{1,0:T(8,128)(2,1)}, bf16[1,512,...) custom-call(s32[1]{0:T(128)} %bitcast.me_ref, ...), custom_call_target="tpu_custom_call" | custom-call | flops 19327352832 | bytes 41943040 | tf_op jit(solution)/shard_map/middle/pallas_call | solution.py:578
  515.7 33.4 %middle.2 = (bf16[512,256]{1,0:T(8,128)(2,1)}, bf16[512,256]{1,0:T(8,128)(2,1)}, bf16[512,256]{1,0:T(8,128)(2,1)}, bf16[512,256]{1,0:T(8,128)(2,1)}, bf16[1,512,...) custom-call(s32[1]{0:T(128)} %bitcast.me_ref, ...), custom_call_target="tpu_custom_call" | custom-call | flops 19327352832 | bytes 41943040 | tf_op jit(solution)/shard_map/middle/pallas_call | solution.py:578
  554.9 16.0 %early_keep.1 = f32[4,4,288,1024]{3,2,1,0:T(8,128)} custom-call(s32[1]{0:T(128)} %bitcast.13.split_ref, bf16[512,4096]{1,0:T(8,128)(2,1)} %get-tuple-element.132.refs_0_, bf16[512,4096]{1,0:T(8,128)(2,1)} %get-tuple-element.133.refs_1_, bf16[512,1024]{1,0:T(8,128)(2,1)S(1)} %copy-done.11, bf16[512,1024]{1,0:T(8,128)(2,1)S(1)} %copy-done.8, ...), custom_call_target="tpu_custom_call" | custom-call | flops 9663676416 | bytes 31457280 | tf_op jit(solution)/shard_map/early_keep/pallas_call | solution.py:720
  570.9 14.8 %early_send.1 = bf16[4,4,288,1024]{3,2,1,0:T(8,128)(2,1)} custom-call(s32[1]{0:T(128)S(6)} %sub.66.split_ref, bf16[512,4096]{1,0:T(8,128)(2,1)} %get-tuple-element.132.refs_0_, bf16[512,4096]{1,0:T(8,128)(2,1)} %get-tuple-element.133.refs_1_, bf16[512,1024]{1,0:T(8,128)(2,1)S(1)} %copy-done.11, bf16[512,1024]{1,0:T(8,128)(2,1)S(1)} %copy-done.8, ...), custom_call_target="tpu_custom_call" | custom-call | flops 9663676416 | bytes 31457280 | tf_op jit(solution)/shard_map/early_send/pallas_call | solution.py:720
  587.3 51.7 %attend_back.3 = (bf16[3,512,256]{2,1,0:T(8,128)(2,1)S(1)}, bf16[3,512,256]{2,1,0:T(8,128)(2,1)S(1)}, bf16[3,512,256]{2,1,0:T(8,128)(2,1)S(1)}, bf16[3,512,256]{2,1,0:T(8,128)(2,1)}) custom-call(bf16[3,512,256]{2,1,0:T(8,128)(2,1)S(1)} %copy-done.28, bf16[3,512,256]{2,1,0:T(8,128)(2,1)} %collective-permute-done.6.refs_1_, ...), custom_call_target="tpu_custom_call" | custom-call | flops 42949672960 | bytes 12582912 | tf_op jit(solution)/shard_map/attend_back/pallas_call | solution.py:466
  643.4 51.6 %attend_back.2 = (bf16[3,512,256]{2,1,0:T(8,128)(2,1)S(1)}, bf16[3,512,256]{2,1,0:T(8,128)(2,1)}, bf16[3,512,256]{2,1,0:T(8,128)(2,1)}, bf16[3,512,256]{2,1,0:T(8,128)(2,1)}) custom-call(bf16[3,512,256]{2,1,0:T(8,128)(2,1)S(1)} %copy-done.25, bf16[3,512,256]{2,1,0:T(8,128)(2,1)S(1)} %copy-done.21, bf16[3,512,256]{2,1,0:T(8,128)(2,1)} %copy-done.22, ...), custom_call_target="tpu_custom_call" | custom-call | flops 42949672960 | bytes 12582912 | tf_op jit(solution)/shard_map/attend_back/pallas_call | solution.py:466
  717.7 9.7 last.3
  735.4 9.5 last.2
  752.5 10.2 convert_add_fusion
  787.1 8.4 all-reduce.3
  795.5 12.4 all_gather.37
  817.3 16.4 %all-to-all-done = f32[32,16,192]{2,1,0:T(8,128)} async-done(((f32[32,16,192]{2,1,0:T(8,128)}), f32[32,16,192]{2,1,0:T(8,128)}, u32[]{:S(2)}, u32[]{:S(2)}) %all-to-all-start) | async-done | bytes 393248 | tf_op jit(solution)/shard_map/all_to_all | solution.py:866
  863.7 12.5 collective-permute-done.33
  876.5 9.6 collective-permute-done.35
  907.1 12.2 collective-permute-done.36
  933.6 102.2 %all-reduce.6.cloned.1.call-done = f32[128,1024]{1,0:T(8,128)} async-done(((f32[128,1024]{1,0:T(8,128)}), f32[128,1024]{1,0:T(8,128)}) %all-reduce.6.cloned.1.call-update) | async-done | bytes 524304 | tf_op jit(solution)/shard_map/psum | solution.py:880
  1048.0 39.2 %psum.15 = f32[]{:T(128)} all-reduce(f32[]{:T(128)S(6)} %add.258), channel_id=1, replica_groups=mesh['frame'=8,'row'=4] {'frame','row'}, use_global_device_ids=true, to_apply=%region_10.11 | all-reduce | flops 1 | bytes 8 | tf_op jit(solution)/shard_map/psum | solution.py:907
  1093.7 17.3 %all_to_all.15 = bf16[4,128,1024]{2,1,0:T(8,128)(2,1)} all-to-all(bf16[4,128,1024]{2,1,0:T(8,128)(2,1)S(1)} %pad_maximum_fusion.2), channel_id=1, replica_groups=mesh['frame'=8,'row'=4] {'row'}, dimensions={0} | all-to-all | bytes 2097152 | tf_op jit(solution)/shard_map/all_to_all | solution.py:919
  1115.9 73.1 %all-gather.20.cloned.1.call-done.all_ref = bf16[4096,1024]{1,0:T(8,128)(2,1)} async-done(((bf16[512,1024]{1,0:T(8,128)(2,1)}), bf16[4096,1024]{1,0:T(8,128)(2,1)}) %all-gather.20.cloned.1.call-update) | async-done | bytes 8388624 | tf_op jit(solution)/shard_map/all_gather | solution.py:922
  1189.1 129.3 %shard_map.374 = bf16[512,1024]{1,0:T(8,128)(2,1)} custom-call(bf16[4096,1024]{1,0:T(8,128)(2,1)} %all-gather.20.cloned.1.call-done.all_ref, bf16[512,1024]{1,0:T(8,128)(2,1)} %bitcast.155), custom_call_target="tpu_custom_call" | custom-call | flops 109999996928 | bytes 12000000 | tf_op jit(solution)/shard_map/pallas_call | solution.py:230
  1328.3 8.1 all-to-all-done.2
  (408 shorter events, 229.0 us)
Async XLA Ops:
  7.2 61.1 %all-gather.8.cloned.1.call-start = ((), (), s32[]{:S(2)}) async-start(), calls=%async_computation.3 | async-start | bytes 2162688 | tf_op jit(solution)/shard_map/all_gather | solution.py:776
  8.9 158.0 %all-gather.10.cloned.1.call-start = ((), (), s32[]{:S(2)}) async-start(), calls=%async_computation.4 | async-start | bytes 12976128 | tf_op jit(solution)/shard_map/all_gather | solution.py:777
  11.0 227.9 %all-gather.18.cloned.1.call-start = ((), (), s32[]{:S(2)}) async-start(), calls=%async_computation.8 | async-start | bytes 6488064 | tf_op jit(solution)/shard_map/all_gather | solution.py:781
  12.7 349.9 %all-gather.12.cloned.1.call-start = ((), (), s32[]{:S(2)}) async-start(), calls=%async_computation.5 | async-start | bytes 2162688 | tf_op jit(solution)/shard_map/all_gather | solution.py:781
  13.5 384.7 %all-gather.14.cloned.1.call-start = ((), (), s32[]{:S(2)}) async-start(), calls=%async_computation.6 | async-start | bytes 8650752 | tf_op jit(solution)/shard_map/all_gather | solution.py:781
  14.5 464.5 %all-gather.16.cloned.1.call-start = ((), (), s32[]{:S(2)}) async-start(), calls=%async_computation.7 | async-start | bytes 8650752 | tf_op jit(solution)/shard_map/all_gather | solution.py:781
  259.5 64.3 %collective-permute-start = (bf16[3,512,256]{2,1,0:T(8,128)(2,1)S(1)}, bf16[3,512,256]{2,1,0:T(8,128)(2,1)S(1)}, u32[]{:S(2)}, u32[]{:S(2)}) collective-permute-start(bf16[3,512,256]{2,1,0:T(8,128)(2,1)S(1)} %get-tuple-element.83), channel_id=1, source_target_pairs={{0,1},{1,0},{2,3},{3,2},{4,5},{5,4},{6,7},{7,6},{8,9},{9,8},{10,11... | collective-permute-start | bytes 2359304 | tf_op jit(solution)/shard_map/ppermute | solution.py:739
  260.9 64.7 %collective-permute-start.1 = (bf16[3,512,256]{2,1,0:T(8,128)(2,1)S(1)}, bf16[3,512,256]{2,1,0:T(8,128)(2,1)S(1)}, u32[]{:S(2)}, u32[]{:S(2)}) collective-permute-start(bf16[3,512,256]{2,1,0:T(8,128)(2,1)S(1)} %get-tuple-element.84), channel_id=1, source_target_pairs={{0,2},{1,3},{2,0},{3,1},{4,6},{5,7},{6,4},{7,5},{8,10},{9,11},{10,... | collective-permute-start | bytes 2359304 | tf_op jit(solution)/shard_map/ppermute | solution.py:739
  270.7 55.6 %collective-permute-start.2 = (bf16[3,512,256]{2,1,0:T(8,128)(2,1)S(1)}, bf16[3,512,256]{2,1,0:T(8,128)(2,1)S(1)}, u32[]{:S(2)}, u32[]{:S(2)}) collective-permute-start(bf16[3,512,256]{2,1,0:T(8,128)(2,1)S(1)} %get-tuple-element.85), channel_id=1, source_target_pairs={{0,3},{1,2},{2,1},{3,0},{4,7},{5,6},{6,5},{7,4},{8,11},{9,10},{10,... | collective-permute-start | bytes 2359304 | tf_op jit(solution)/shard_map/ppermute | solution.py:739
  322.7 156.3 %collective-permute-start.10 = (bf16[512,256]{1,0:T(8,128)(2,1)}, bf16[512,256]{1,0:T(8,128)(2,1)}, u32[]{:S(2)}, u32[]{:S(2)}) collective-permute-start(bf16[512,256]{1,0:T(8,128)(2,1)} %get-tuple-element.97), channel_id=1, source_target_pairs={{0,2},{1,3},{2,0},{3,1},{4,6},{5,7},{6,4},{7,5},{8,10},{9,11},{10,... | collective-permute-start | bytes 786440 | tf_op jit(solution)/shard_map/ppermute | solution.py:739
  323.8 155.3 %collective-permute-start.11 = (bf16[512,256]{1,0:T(8,128)(2,1)S(1)}, bf16[512,256]{1,0:T(8,128)(2,1)}, u32[]{:S(2)}, u32[]{:S(2)}) collective-permute-start(bf16[512,256]{1,0:T(8,128)(2,1)S(1)} %get-tuple-element.98), channel_id=1, source_target_pairs={{0,3},{1,2},{2,1},{3,0},{4,7},{5,6},{6,5},{7,4},{8,11},{9,10},{10,... | collective-permute-start | bytes 786440 | tf_op jit(solution)/shard_map/ppermute | solution.py:739
  358.4 155.8 %collective-permute-start.3 = (bf16[512,256]{1,0:T(8,128)(2,1)}, bf16[512,256]{1,0:T(8,128)(2,1)}, u32[]{:S(2)}, u32[]{:S(2)}) collective-permute-start(bf16[512,256]{1,0:T(8,128)(2,1)} %get-tuple-element.87), channel_id=1, source_target_pairs={{0,1},{1,0},{2,3},{3,2},{4,5},{5,4},{6,7},{7,6},{8,9},{9,8},{10,11... | collective-permute-start | bytes 786440 | tf_op jit(solution)/shard_map/ppermute | solution.py:739
  359.0 156.7 %collective-permute-start.4 = (bf16[512,256]{1,0:T(8,128)(2,1)}, bf16[512,256]{1,0:T(8,128)(2,1)}, u32[]{:S(2)}, u32[]{:S(2)}) collective-permute-start(bf16[512,256]{1,0:T(8,128)(2,1)} %get-tuple-element.88), channel_id=1, source_target_pairs={{0,2},{1,3},{2,0},{3,1},{4,6},{5,7},{6,4},{7,5},{8,10},{9,11},{10,... | collective-permute-start | bytes 786440 | tf_op jit(solution)/shard_map/ppermute | solution.py:739
  360.7 155.0 %collective-permute-start.5 = (bf16[512,256]{1,0:T(8,128)(2,1)}, bf16[512,256]{1,0:T(8,128)(2,1)}, u32[]{:S(2)}, u32[]{:S(2)}) collective-permute-start(bf16[512,256]{1,0:T(8,128)(2,1)} %get-tuple-element.89), channel_id=1, source_target_pairs={{0,3},{1,2},{2,1},{3,0},{4,7},{5,6},{6,5},{7,4},{8,11},{9,10},{10,... | collective-permute-start | bytes 786440 | tf_op jit(solution)/shard_map/ppermute | solution.py:739
  512.1 73.6 %collective-permute-start.18 = (bf16[512,256]{1,0:T(8,128)(2,1)}, bf16[512,256]{1,0:T(8,128)(2,1)S(1)}, u32[]{:S(2)}, u32[]{:S(2)}) collective-permute-start(bf16[512,256]{1,0:T(8,128)(2,1)} %get-tuple-element.114), channel_id=1, source_target_pairs={{0,1},{1,0},{2,3},{3,2},{4,5},{5,4},{6,7},{7,6},{8,9},{9,8},{10,11... | collective-permute-start | bytes 786440 | tf_op jit(solution)/shard_map/ppermute | solution.py:739
  513.6 73.6 %collective-permute-start.19 = (bf16[512,256]{1,0:T(8,128)(2,1)}, bf16[512,256]{1,0:T(8,128)(2,1)S(1)}, u32[]{:S(2)}, u32[]{:S(2)}) collective-permute-start(bf16[512,256]{1,0:T(8,128)(2,1)} %get-tuple-element.115), channel_id=1, source_target_pairs={{0,2},{1,3},{2,0},{3,1},{4,6},{5,7},{6,4},{7,5},{8,10},{9,11},{10,... | collective-permute-start | bytes 786440 | tf_op jit(solution)/shard_map/ppermute | solution.py:739
  514.2 73.0 %collective-permute-start.20 = (bf16[512,256]{1,0:T(8,128)(2,1)}, bf16[512,256]{1,0:T(8,128)(2,1)}, u32[]{:S(2)}, u32[]{:S(2)}) collective-permute-start(bf16[512,256]{1,0:T(8,128)(2,1)} %get-tuple-element.116), channel_id=1, source_target_pairs={{0,3},{1,2},{2,1},{3,0},{4,7},{5,6},{6,5},{7,4},{8,11},{9,10},{10,... | collective-permute-start | bytes 786440 | tf_op jit(solution)/shard_map/ppermute | solution.py:739
  549.2 92.2 %collective-permute-start.12 = (bf16[512,256]{1,0:T(8,128)(2,1)}, bf16[512,256]{1,0:T(8,128)(2,1)S(1)}, u32[]{:S(2)}, u32[]{:S(2)}) collective-permute-start(bf16[512,256]{1,0:T(8,128)(2,1)} %get-tuple-element.102), channel_id=1, source_target_pairs={{0,1},{1,0},{2,3},{3,2},{4,5},{5,4},{6,7},{7,6},{8,9},{9,8},{10,11... | collective-permute-start | bytes 786440 | tf_op jit(solution)/shard_map/ppermute | solution.py:739
  550.7 91.3 %collective-permute-start.13 = (bf16[512,256]{1,0:T(8,128)(2,1)}, bf16[512,256]{1,0:T(8,128)(2,1)S(1)}, u32[]{:S(2)}, u32[]{:S(2)}) collective-permute-start(bf16[512,256]{1,0:T(8,128)(2,1)} %get-tuple-element.103), channel_id=1, source_target_pairs={{0,2},{1,3},{2,0},{3,1},{4,6},{5,7},{6,4},{7,5},{8,10},{9,11},{10,... | collective-permute-start | bytes 786440 | tf_op jit(solution)/shard_map/ppermute | solution.py:739
  585.7 57.7 %collective-permute-start.14 = (bf16[512,256]{1,0:T(8,128)(2,1)S(1)}, bf16[512,256]{1,0:T(8,128)(2,1)S(1)}, u32[]{:S(2)}, u32[]{:S(2)}) collective-permute-start(bf16[512,256]{1,0:T(8,128)(2,1)S(1)} %copy-done.86), channel_id=1, source_target_pairs={{0,3},{1,2},{2,1},{3,0},{4,7},{5,6},{6,5},{7,4},{8,11},{9,10},{10,... | collective-permute-start | bytes 786440 | tf_op jit(solution)/shard_map/ppermute | solution.py:739
  587.2 165.3 %collective-permute-start.31 = (bf16[4,4,288,1024]{3,2,1,0:T(8,128)(2,1)}, bf16[4,4,288,1024]{3,2,1,0:T(8,128)(2,1)}, u32[]{:S(2)}, u32[]{:S(2)}) collective-permute-start(bf16[4,4,288,1024]{3,2,1,0:T(8,128)(2,1)} %early_send.1), channel_id=1, source_target_pairs={{0,4},{4,0},{8,12},{12,8},{16,20},{20,16},{24,28},{28,24},{1,5},{5... | collective-permute-start | bytes 28311560 | tf_op jit(solution)/shard_map/ppermute | solution.py:84
  639.9 57.5 %collective-permute-start.21 = (bf16[3,512,256]{2,1,0:T(8,128)(2,1)S(1)}, bf16[3,512,256]{2,1,0:T(8,128)(2,1)S(1)}, u32[]{:S(2)}, u32[]{:S(2)}) collective-permute-start(bf16[3,512,256]{2,1,0:T(8,128)(2,1)S(1)} %get-tuple-element.120), channel_id=1, source_target_pairs={{0,1},{1,0},{2,3},{3,2},{4,5},{5,4},{6,7},{7,6},{8,9},{9,8},{10,11... | collective-permute-start | bytes 2359304 | tf_op jit(solution)/shard_map/ppermute | solution.py:739
  641.3 57.5 %collective-permute-start.22 = (bf16[3,512,256]{2,1,0:T(8,128)(2,1)S(1)}, bf16[3,512,256]{2,1,0:T(8,128)(2,1)S(1)}, u32[]{:S(2)}, u32[]{:S(2)}) collective-permute-start(bf16[3,512,256]{2,1,0:T(8,128)(2,1)S(1)} %get-tuple-element.121), channel_id=1, source_target_pairs={{0,2},{1,3},{2,0},{3,1},{4,6},{5,7},{6,4},{7,5},{8,10},{9,11},{10,... | collective-permute-start | bytes 2359304 | tf_op jit(solution)/shard_map/ppermute | solution.py:739
  641.9 72.4 %collective-permute-start.23 = (bf16[3,512,256]{2,1,0:T(8,128)(2,1)}, bf16[3,512,256]{2,1,0:T(8,128)(2,1)}, u32[]{:S(2)}, u32[]{:S(2)}) collective-permute-start(bf16[3,512,256]{2,1,0:T(8,128)(2,1)} %get-tuple-element.122), channel_id=1, source_target_pairs={{0,3},{1,2},{2,1},{3,0},{4,7},{5,6},{6,5},{7,4},{8,11},{9,10},{10,... | collective-permute-start | bytes 2359304 | tf_op jit(solution)/shard_map/ppermute | solution.py:739
  752.4 82.4 %collective-permute-start.24 = (bf16[4,4,96,1024]{3,2,1,0:T(8,128)(2,1)}, bf16[4,4,96,1024]{3,2,1,0:T(8,128)(2,1)}, u32[]{:S(2)}, u32[]{:S(2)}) collective-permute-start(bf16[4,4,96,1024]{3,2,1,0:T(8,128)(2,1)} %late_send.1), channel_id=1, source_target_pairs={{0,4},{4,0},{8,12},{12,8},{16,20},{20,16},{24,28},{28,24},{1,5},{5... | collective-permute-start | bytes 9437192 | tf_op jit(solution)/shard_map/ppermute | solution.py:84
  774.3 68.4 %collective-permute-start.32 = (bf16[2,2,2,288,512]{4,3,0,1,2:T(8,128)(2,1)}, bf16[2,2,2,288,512]{4,3,0,1,2:T(8,128)(2,1)}, u32[]{:S(2)}, u32[]{:S(2)}) collective-permute-start(bf16[2,2,2,288,512]{4,3,0,1,2:T(8,128)(2,1)} %fusion.2), channel_id=1, source_target_pairs={{0,1},{1,0},{2,3},{3,2},{4,5},{5,4},{6,7},{7,6},{8,9},{9,8},{10,11... | collective-permute-start | bytes 7077896 | tf_op jit(solution)/shard_map/ppermute | solution.py:65
  776.3 57.4 %all-to-all-start = ((f32[32,16,192]{2,1,0:T(8,128)}), f32[32,16,192]{2,1,0:T(8,128)}, u32[]{:S(2)}, u32[]{:S(2)}) async-start(f32[32,16,192]{2,1,0:T(8,128)} %copy.87), calls=%async_computation | async-start | bytes 1048576 | tf_op jit(solution)/shard_map/all_to_all | solution.py:866
  779.8 256.0 %all-reduce.6.cloned.1.call-start = ((), (), s32[]{:S(2)}) async-start(), calls=%async_computation.9 | async-start | bytes 1048576 | tf_op jit(solution)/shard_map/psum | solution.py:880
  784.2 64.1 %collective-permute-start.34 = (bf16[2,2,2,288,512]{4,3,0,1,2:T(8,128)(2,1)}, bf16[2,2,2,288,512]{4,3,0,1,2:T(8,128)(2,1)}, u32[]{:S(2)}, u32[]{:S(2)}) collective-permute-start(bf16[2,2,2,288,512]{4,3,0,1,2:T(8,128)(2,1)} %fusion.3), channel_id=1, source_target_pairs={{0,2},{1,3},{2,0},{3,1},{4,6},{5,7},{6,4},{7,5},{8,10},{9,11},{10,... | collective-permute-start | bytes 7077896 | tf_op jit(solution)/shard_map/ppermute | solution.py:65
  897.5 291.5 %all-gather.20.cloned.1.call-start = ((), (), s32[]{:S(2)}) async-start(), calls=%async_computation.10 | async-start | bytes 9437184 | tf_op jit(solution)/shard_map/all_gather | solution.py:922
  922.1 119.3 %collective-permute-start.37 = (bf16[288,1024]{1,0:T(8,128)(2,1)}, bf16[288,1024]{1,0:T(8,128)(2,1)}, u32[]{:S(2)}, u32[]{:S(2)}) collective-permute-start(bf16[288,1024]{1,0:T(8,128)(2,1)} %fusion.22), channel_id=1, source_target_pairs={{0,16},{4,20},{8,24},{12,28},{16,0},{20,4},{24,8},{28,12},{1,17},{... | collective-permute-start | bytes 1769480 | tf_op jit(solution)/shard_map/ppermute | solution.py:65
  930.5 110.2 %collective-permute-start.30 = (bf16[96,1024]{1,0:T(8,128)(2,1)S(1)}, bf16[96,1024]{1,0:T(8,128)(2,1)S(1)}, u32[]{:S(2)}, u32[]{:S(2)}) collective-permute-start(bf16[96,1024]{1,0:T(8,128)(2,1)S(1)} %fusion.43), channel_id=1, source_target_pairs={{0,16},{4,20},{8,24},{12,28},{16,0},{20,4},{24,8},{28,12},{1,17},{... | collective-permute-start | bytes 589832 | tf_op jit(solution)/shard_map/ppermute | solution.py:65
  (112 other events, 3644.4 us)
Sparse Core Ops, SparseCore 0:
  11.5 56.7 all-gather.7
  71.7 95.1 all-gather.9
  170.4 68.4 all-gather.17
  242.2 73.1 all-gather.11
  318.6 79.4 all-gather.13
  401.5 77.5 all-gather.15
  897.6 138.1 all-reduce.5
  1111.1 77.8 all-gather.19

commit v3 on v2

--- a/solution.py
+++ b/solution.py
@@ -56,44 +56,75 @@
     return (first_new, second_new, master_new)
 
 
-def halve(value, dim, axis, bit):
+def halves(value, dim, axis, bit):
     mine = (lax.axis_index(axis) >> bit) & 1
     keep = lax.dynamic_index_in_dim(value, mine, dim, keepdims=False)
     send = lax.dynamic_index_in_dim(value, 1 - mine, dim, keepdims=False)
+    return keep, send.astype(jnp.bfloat16)
+
+
+def joined(keep, send, axis, bit):
     size = lax.axis_size(axis)
-    pairs = [(index, index ^ (1 << bit)) for index in range(size)]
-    came = lax.ppermute(send.astype(jnp.bfloat16), axis, pairs)
-    return keep.astype(jnp.float32) + came.astype(jnp.float32)
-
-
-def halve_all(value, names, order):
-    names = list(names)
-    for name in order:
-        dim = names.index(name)
-        value = halve(value, dim, name[0], name[1])
-        names.pop(dim)
-    return value
-
-
-def scatter_sum(pairs, name):
+    came = lax.ppermute(send, axis, [(index, index ^ (1 << bit)) for index in range(size)])
+    return keep + came.astype(jnp.float32)
+
+
+def held(value, *others):
+    if not others:
+        return value
+    return lax.optimization_barrier((value, *others))[0]
+
+
+def scatter_steps(groups, name):
     frame_bits = lax.axis_size("frame").bit_length() - 1
     row_bits = lax.axis_size("row").bit_length() - 1
-    parity = (lax.axis_index("frame") & 1).astype(jnp.int32).reshape(1)
-    send = weight_sums(1 - parity, pairs, jnp.bfloat16, name + "_send")
+    row = lax.axis_index("row")
+    numbers = jnp.stack([lax.axis_index("frame") & 1, row & 1, row >> (row_bits - 1)]).astype(jnp.int32)
     size = lax.axis_size("frame")
-    came = lax.ppermute(send, "frame", [(index, index ^ 1) for index in range(size)])
-    keep = weight_sums(parity, pairs, jnp.float32, name + "_keep")
-    value = keep + came.astype(jnp.float32)
+    came = []
+    for at, group in enumerate(groups):
+        send = send_sums(numbers, group, f"{name}_send_{at}")
+        came.append(lax.ppermute(send, "frame", [(index, index ^ 1) for index in range(size)]))
+        numbers = held(numbers, send)
+    keep, send = keep_sums(numbers, groups, came, name + "_keep")
     names = [("frame", bit) for bit in reversed(range(1, frame_bits))]
     names += [("row", bit) for bit in reversed(range(row_bits))]
-    value = value.reshape((2,) * len(names) + value.shape[2:])
-    upward = [("row", bit) for bit in range(row_bits)]
-    width = value.shape[-1] // 2
-    left = halve_all(value[..., :width], names, upward)
-    right = halve_all(value[..., width:], names, upward[::-1])
+    side_names = []
+    for side in range(2):
+        bit = 0 if side == 0 else row_bits - 1
+        side_names.append([item for item in names if item != ("row", bit)])
+        shape = (2,) * (len(names) - 1) + keep[side].shape[2:]
+        keep[side] = keep[side].reshape(shape)
+        send[side] = send[side].reshape(shape)
+    hold = yield send
+    for step in range(row_bits):
+        parts = []
+        for side in range(2):
+            bit = step if side == 0 else row_bits - 1 - step
+            parts.append(joined(held(keep[side], *hold), send[side], "row", bit))
+        if step == row_bits - 1:
+            break
+        for side in range(2):
+            bit = step + 1 if side == 0 else row_bits - 2 - step
+            dim = side_names[side].index(("row", bit))
+            side_names[side].pop(dim)
+            keep[side], send[side] = halves(parts[side], dim, "row", bit)
+        hold = yield send
+    value = jnp.concatenate(parts, axis=-1)
     names = names[: frame_bits - 1]
-    value = jnp.concatenate([left, right], axis=-1)
-    return halve_all(value, names, [("frame", bit) for bit in range(1, frame_bits)])
+    for bit in range(1, frame_bits):
+        dim = names.index(("frame", bit))
+        names.pop(dim)
+        keep, send = halves(value, dim, "frame", bit)
+        hold = yield [send]
+        value = joined(held(keep, *hold), send, "frame", bit)
+    yield value
+
+
+def finished(steps, state):
+    while isinstance(state, list):
+        state = steps.send([])
+    return state
 
 
 def split_two(value):
@@ -103,139 +134,6 @@
 
 def dot_low(left, right):
     return lax.dot_general(left, right, (((1,), (0,)), ((), ())), preferred_element_type=jnp.float32)
-
-
-def newton_kernel(all_ref, mine_ref, out_ref, a_ref, q_ref, t_ref, ah, al, nh, nl, th, tl, qh, ql):
-    width = a_ref.shape[0]
-    rows = 256
-    steps = width // rows
-    depth = all_ref.shape[0]
-
-    def block(index):
-        return pl.ds(pl.multiple_of(index * rows, rows), rows)
-
-    def gram(index, total):
-        columns = block(index)
-
-        def part(k, value):
-            deep = pl.ds(pl.multiple_of(k * 1024, 1024), 1024)
-            return value + lax.dot_general(
-                all_ref[deep, columns],
-                all_ref[deep, :],
-                (((0,), (0,)), ((), ())),
-                preferred_element_type=jnp.float32,
-            )
-
-        value = lax.fori_loop(0, depth // 1024, part, jnp.zeros((rows, width), jnp.float32))
-        a_ref[columns, :] = value
-        row_at = lax.broadcasted_iota(jnp.int32, (rows, width), 0) + index * rows
-        column_at = lax.broadcasted_iota(jnp.int32, (rows, width), 1)
-        return total + jnp.sum(jnp.where(row_at == column_at, value, 0.0))
-
-    squares = 0.0
-    for index in range(steps):
-        squares = gram(index, squares)
-    squares = jnp.full((1, 1), squares, jnp.float32)
-    inverse = 1.0 / (jnp.sqrt(squares) + 1e-07)
-
-    def first_split(index, carry):
-        at = block(index)
-        value = a_ref[at, :] * inverse * inverse
-        a_ref[at, :] = value
-        high, rest = split_two(value)
-        ah[at, :] = high
-        al[at, :] = rest
-        return carry
-
-    lax.fori_loop(0, steps, first_split, 0)
-
-    def three(lh, ll, rh, rl):
-        return dot_low(lh, rh) + dot_low(lh, rl) + dot_low(ll, rh)
-
-    def one_step(number, exact, last):
-        def make_n(index, carry):
-            at = block(index)
-            if exact:
-                square = three(ah[at, :], al[at, :], ah[...], al[...])
-            else:
-                square = dot_low(ah[at, :], ah[...])
-            value = newton_two * a_ref[at, :] + newton_three * square
-            high, rest = split_two(value)
-            nh[at, :] = high
-            if exact:
-                nl[at, :] = rest
-            return carry
-
-        lax.fori_loop(0, steps, make_n, 0)
-
-        def make_q(index, carry):
-            at = block(index)
-            if number == 0:
-                row_at = lax.broadcasted_iota(jnp.int32, (rows, width), 0) + index * rows
-                column_at = lax.broadcasted_iota(jnp.int32, (rows, width), 1)
-                value = nh[at, :].astype(jnp.float32) + jnp.where(row_at == column_at, newton_one, 0.0)
-            elif exact:
-                value = newton_one * q_ref[at, :] + three(qh[at, :], ql[at, :], nh[...], nl[...])
-            else:
-                value = newton_one * q_ref[at, :] + dot_low(qh[at, :], nh[...]) + dot_low(ql[at, :], nh[...])
-            q_ref[at, :] = value
-            high, rest = split_two(value)
-            qh[at, :] = high
-            ql[at, :] = rest
-            return carry
-
-        lax.fori_loop(0, steps, make_q, 0)
-        if last:
-            return
-
-        def make_t(index, carry):
-            at = block(index)
-            if exact:
-                value = newton_one * a_ref[at, :] + three(ah[at, :], al[at, :], nh[...], nl[...])
-            else:
-                value = newton_one * a_ref[at, :] + dot_low(ah[at, :], nh[...]) + dot_low(al[at, :], nh[...])
-            t_ref[at, :] = value
-            high, rest = split_two(value)
-            th[at, :] = high
-            tl[at, :] = rest
-            return carry
-
-        lax.fori_loop(0, steps, make_t, 0)
-
-        def make_a(index, carry):
-            at = block(index)
-            if exact:
-                value = newton_one * t_ref[at, :] + three(nh[at, :], nl[at, :], th[...], tl[...])
-            else:
-                value = newton_one * t_ref[at, :] + dot_low(nh[at, :], th[...]) + dot_low(nh[at, :], tl[...])
-            a_ref[at, :] = value
-            high, rest = split_two(value)
-            ah[at, :] = high
-            al[at, :] = rest
-            return carry
-
-        lax.fori_loop(0, steps, make_a, 0)
-
-    for number in range(5):
-        one_step(number, number >= 2, number == 4)
-
-    mine = mine_ref[...]
-    out_ref[...] = ((dot_low(mine, qh[...]) + dot_low(mine, ql[...])) * inverse).astype(out_ref.dtype)
-
-
-def newton(everything, mine):
-    width = everything.shape[1]
-    full = pltpu.VMEM((width, width), jnp.float32)
-    low = pltpu.VMEM((width, width), jnp.bfloat16)
-    return pl.pallas_call(
-        newton_kernel,
-        out_shape=jax.ShapeDtypeStruct(mine.shape, jnp.bfloat16),
-        in_specs=[pl.BlockSpec(memory_space=pltpu.VMEM)] * 2,
-        out_specs=pl.BlockSpec(memory_space=pltpu.VMEM),
-        scratch_shapes=[full] * 3 + [low] * 8,
-        compiler_params=pltpu.CompilerParams(vmem_limit_bytes=52 * 1024 * 1024),
-        cost_estimate=pl.CostEstimate(flops=110 * 10**9, bytes_accessed=12 * 10**6, transcendentals=0),
-    )(everything, mine)
 
 
 def dot_nt(left, right):
@@ -325,7 +223,7 @@
         out_specs=[pl.BlockSpec((1, tile, D), lambda i: (0, i, 0))]
         + [pl.BlockSpec((3, tile, group), lambda i: (0, i, 0))] * slots,
         out_shape=out_shape,
-        compiler_params=vmem_params(48),
+        compiler_params=vmem_params(60),
         cost_estimate=pl.CostEstimate(
             flops=6 * tall_rows * D * D, bytes_accessed=10 * MIB, transcendentals=0
         ),
@@ -385,7 +283,7 @@
         out_shape=[jax.ShapeDtypeStruct((length, group), jnp.bfloat16)] * slots
         + [jax.ShapeDtypeStruct((total, group), jnp.float32)] * 2,
         scratch_shapes=[scratch] * 3,
-        compiler_params=vmem_params(48),
+        compiler_params=vmem_params(60),
         cost_estimate=pl.CostEstimate(
             flops=16 * total * total * group, bytes_accessed=8 * MIB, transcendentals=total * total * 4
         ),
@@ -472,12 +370,17 @@
         out_specs=[pl.BlockSpec((3, length, 128), lambda i: (0, 0, i))] * slots,
         out_shape=[jax.ShapeDtypeStruct((3, length, group), jnp.bfloat16)] * slots,
         scratch_shapes=[low] * 4 + [low_t] * 2 + [low] + [full_t] * 2,
-        compiler_params=vmem_params(48),
+        compiler_params=vmem_params(60),
         cost_estimate=pl.CostEstimate(
             flops=40 * total * total * group, bytes_accessed=12 * MIB, transcendentals=total * total * 4
         ),
         name="attend_back",
     )(*pieces, *grads, full, logs)
+
+
+def part_of(ref, index, size):
+    count = size // ref.shape[1]
+    return ref[pl.ds(index * count, count)].reshape(size, ref.shape[2])
 
 
 def middle_kernel(slots, me_ref, x_ref, cot_ref, mod_ref, wo_ref, wu_ref, wd_ref, *refs):
@@ -514,7 +417,7 @@
         at = pl.ds(pl.multiple_of((me ^ slot) * group, group), group)
         piece = att_refs[slot][...]
         att_ref[:, at] = piece
-        branch += dot_low(piece, wo_ref[at, :])
+        branch += dot_low(piece, part_of(wo_ref, me ^ slot, group))
     middle = x_ref[0].astype(jnp.float32) + spread(branch, 2)
     normed, root = norm_parts(middle)
     hidden = (framed(spread(normed, 4, 1.0), frames) + mod(3)).reshape(rows, D).astype(jnp.bfloat16)
@@ -524,14 +427,14 @@
     branch_two = jnp.zeros((rows, D), jnp.float32)
     for first in range(0, FF, wide):
         cut = slice(first, first + wide)
-        up = dot_nt(hidden, wu_ref[cut, :])
+        up = dot_nt(hidden, part_of(wu_ref, first // wide, wide))
         square = up * up
         bent = jnp.tanh(curve * up * (1.0 + 0.044715 * square))
         half = 0.5 * (1.0 + bent)
         active = (up * half).astype(jnp.bfloat16)
         slope[:, cut] = half + 0.5 * up * (1.0 - bent * bent) * (curve * (1.0 + 3 * 0.044715 * square))
         act_ref[:, cut] = active
-        branch_two += dot_low(active, wd_ref[cut, :])
+        branch_two += dot_low(active, part_of(wd_ref, first // wide, wide))
     cot = cot_ref[0].astype(jnp.float32)
     out_ref[0] = (middle + spread(branch_two, 5)).astype(jnp.bfloat16)
     sums_ref[0, 3] = frame_sum(cot * branch_two)
@@ -540,9 +443,9 @@
     d_hidden = jnp.zeros((rows, D), jnp.float32)
     for first in range(0, FF, wide):
         cut = slice(first, first + wide)
-        d_up = (dot_nt(d_branch_two, wd_ref[cut, :]) * slope[:, cut]).astype(jnp.bfloat16)
+        d_up = (dot_nt(d_branch_two, part_of(wd_ref, first // wide, wide)) * slope[:, cut]).astype(jnp.bfloat16)
         dup_ref[:, cut] = d_up
-        d_hidden += dot_low(d_up, wu_ref[cut, :])
+        d_hidden += dot_low(d_up, part_of(wu_ref, first // wide, wide))
     sums_ref[0, 1] = frame_sum(d_hidden)
     sums_ref[0, 2] = frame_sum(d_hidden * normed)
     inner = spread(d_hidden, 4, 1.0)
@@ -556,8 +459,7 @@
     d_branch = spread(d_middle, 2).astype(jnp.bfloat16)
     db1_ref[...] = d_branch
     for slot in range(slots):
-        at = pl.ds(pl.multiple_of((me ^ slot) * group, group), group)
-        datt_refs[slot][...] = dot_nt(d_branch, wo_ref[at, :]).astype(jnp.bfloat16)
+        datt_refs[slot][...] = dot_nt(d_branch, part_of(wo_ref, me ^ slot, group)).astype(jnp.bfloat16)
 
 
 def middle(me, clip, tokens, cotangent, mod, w_out, w_up, w_down, attended):
@@ -583,9 +485,7 @@
             pl.BlockSpec((1, tile, D), lambda i: (clip, i, 0)),
             pl.BlockSpec((1, tile, D), lambda i: (clip, i, 0)),
             pl.BlockSpec((1, frames, 6 * D), lambda i: (clip * steps + i, 0, 0)),
-            whole_spec(w_out),
-            whole_spec(w_up),
-            whole_spec(w_down),
+            *(item[1] for item in (w_out, w_up, w_down)),
         ]
         + [flat_spec(group)] * slots,
         out_specs=[flat_spec(group)] * slots
@@ -597,12 +497,12 @@
         + [flat(D), flat(D), flat(FF), flat(D), flat(FF), flat(D), flat(D, jnp.float32)]
         + [jax.ShapeDtypeStruct((steps, 4, frames, D), jnp.float32)],
         scratch_shapes=[pltpu.VMEM((tile, FF), jnp.float32)],
-        compiler_params=vmem_params(58),
+        compiler_params=vmem_params(60),
         cost_estimate=pl.CostEstimate(
             flops=2 * length * D * (2 * D + 4 * FF), bytes_accessed=40 * MIB, transcendentals=length * FF
         ),
         name="middle",
-    )(me, tokens, cotangent, mod, w_out, w_up, w_down, *attended)
+    )(me, tokens, cotangent, mod, *(item[0] for item in (w_out, w_up, w_down)), *attended)
     return outs[:slots], outs[slots:]
 
 
@@ -674,7 +574,7 @@
             jax.ShapeDtypeStruct((1, length, D), jnp.float32),
             jax.ShapeDtypeStruct((steps, 2, frames, D), jnp.float32),
         ],
-        compiler_params=vmem_params(48),
+        compiler_params=vmem_params(60),
         cost_estimate=pl.CostEstimate(
             flops=6 * length * D * D, bytes_accessed=20 * MIB, transcendentals=0
         ),
@@ -682,54 +582,285 @@
     )(me, tokens, mod, cosine, sine, w_qkv, d_middle, *pieces)
 
 
-def weight_kernel(doubled, split_ref, *refs):
+def member_value(refs, member, doubled, parity):
+    left = refs[4 * member : 4 * member + 2]
+    right = refs[4 * member + 2 : 4 * member + 4]
+    value = dot_tn(left[0][...], right[0][...]) + dot_tn(left[1][...], right[1][...])
+    if doubled:
+        half = value.shape[0] // 2
+        value = jnp.where(parity == 0, value[:half], value[half:])
+    return value
+
+
+def send_kernel(doubled, number_ref, *refs):
+    out_ref = refs[-1]
+    rows = out_ref.shape[1]
+    first = 0
+    for member in range(len(doubled)):
+        value = member_value(refs, member, doubled[member], 1 - number_ref[0])
+        height = value.shape[0] // rows
+        out_ref[0, :, first : first + height, :] = value.reshape(rows, height, D).astype(out_ref.dtype)
+        first += height
+
+
+def keep_kernel(doubled, counts, number_ref, *refs):
     members = len(doubled)
-    out_ref = refs[-1]
+    came_refs = refs[4 * members : 4 * members + len(counts)]
+    keep_refs, send_refs = refs[-4:-2], refs[-2:]
+    half_rows = keep_refs[0].shape[1]
+    width = D // 2
     first = 0
-    for member in range(members):
-        left = refs[4 * member : 4 * member + 2]
-        right = refs[4 * member + 2 : 4 * member + 4]
-        value = dot_tn(left[0][...], right[0][...]) + dot_tn(left[1][...], right[1][...])
-        if doubled[member]:
-            half = value.shape[0] // 2
-            value = jnp.where(split_ref[0] == 0, value[:half], value[half:])
-        height = value.shape[0] // out_ref.shape[1]
-        out_ref[0, :, first : first + height, :] = value.reshape(
-            out_ref.shape[1], height, value.shape[1]
-        ).astype(out_ref.dtype)
-        first += height
-
-
-def weight_sums(keep, pairs, kind, name):
+    member = 0
+    for came_ref, count in zip(came_refs, counts):
+        inside = 0
+        for _ in range(count):
+            value = member_value(refs, member, doubled[member], number_ref[0])
+            height = value.shape[0] // (2 * half_rows)
+            rows = slice(first, first + height)
+            parts = [
+                value[row * height : (row + 1) * height]
+                + came_ref[0, row, inside : inside + height, :].astype(jnp.float32)
+                for row in range(2 * half_rows)
+            ]
+            for place in range(half_rows):
+                for side in range(2):
+                    cut = slice(side * width, (side + 1) * width)
+                    low = 2 * place if side == 0 else place
+                    high = low + (1 if side == 0 else half_rows)
+                    upper = number_ref[1 + side] == 1
+                    zero, one = parts[low][:, cut], parts[high][:, cut]
+                    keep_refs[side][0, place, rows, :] = jnp.where(upper, one, zero)
+                    send_refs[side][0, place, rows, :] = jnp.where(upper, zero, one).astype(jnp.bfloat16)
+            first += height
+            inside += height
+            member += 1
+
+
+def weight_specs(pairs, other):
     frame_devices = lax.axis_size("frame")
-    row_devices = lax.axis_size("row")
     specs, operands, doubled = [], [], []
     height = 0
     for left, right in pairs:
         width = left[0].shape[1] // frame_devices
-        height += width // row_devices
+        height += width // lax.axis_size("row")
         doubled.append(width % 128 != 0)
         if doubled[-1]:
             spec = pl.BlockSpec((left[0].shape[0], 2 * width), lambda i, s: (0, i))
+        elif other:
+            spec = pl.BlockSpec((left[0].shape[0], width), lambda i, s: (0, 2 * i + 1 - s[0]))
         else:
             spec = pl.BlockSpec((left[0].shape[0], width), lambda i, s: (0, 2 * i + s[0]))
         specs += [spec] * 2
         specs += [pl.BlockSpec(right[0].shape, lambda i, s: (0, 0))] * 2
         operands += [*left, *right]
     flops = sum(4 * left[0].shape[0] * left[0].shape[1] * D // 2 for left, _ in pairs)
+    return specs, operands, tuple(doubled), height, flops
+
+
+def send_sums(numbers, pairs, name):
+    specs, operands, doubled, height, flops = weight_specs(pairs, True)
+    frames, rows = lax.axis_size("frame") // 2, lax.axis_size("row")
     return pl.pallas_call(
-        functools.partial(weight_kernel, tuple(doubled)),
+        functools.partial(send_kernel, doubled),
         grid_spec=pltpu.PrefetchScalarGridSpec(
             num_scalar_prefetch=1,
-            grid=(frame_devices // 2,),
+            grid=(frames,),
             in_specs=specs,
-            out_specs=pl.BlockSpec((1, row_devices, height, D), lambda i, s: (i, 0, 0, 0)),
+            out_specs=pl.BlockSpec((1, rows, height, D), lambda i, s: (i, 0, 0, 0)),
         ),
-        out_shape=jax.ShapeDtypeStruct((frame_devices // 2, row_devices, height, D), kind),
-        compiler_params=vmem_params(48),
-        cost_estimate=pl.CostEstimate(flops=flops, bytes_accessed=30 * MIB, transcendentals=0),
+        out_shape=jax.ShapeDtypeStruct((frames, rows, height, D), jnp.bfloat16),
+        compiler_params=vmem_params(60),
+        cost_estimate=pl.CostEstimate(flops=flops, bytes_accessed=20 * MIB, transcendentals=0),
         name=name,
-    )(keep, *operands)
+    )(numbers, *operands)
+
+
+def keep_sums(numbers, groups, came, name):
+    pairs = [pair for group in groups for pair in group]
+    specs, operands, doubled, height, flops = weight_specs(pairs, False)
+    frames, rows = lax.axis_size("frame") // 2, lax.axis_size("row")
+    specs += [pl.BlockSpec((1,) + item.shape[1:], lambda i, s: (i, 0, 0, 0)) for item in came]
+    shape = (frames, rows // 2, height, D // 2)
+    out_spec = pl.BlockSpec((1,) + shape[1:], lambda i, s: (i, 0, 0, 0))
+    outs = pl.pallas_call(
+        functools.partial(keep_kernel, doubled, tuple(len(group) for group in groups)),
+        grid_spec=pltpu.PrefetchScalarGridSpec(
+            num_scalar_prefetch=1, grid=(frames,), in_specs=specs, out_specs=[out_spec] * 4
+        ),
+        out_shape=[jax.ShapeDtypeStruct(shape, jnp.float32)] * 2
+        + [jax.ShapeDtypeStruct(shape, jnp.bfloat16)] * 2,
+        compiler_params=vmem_params(60),
+        cost_estimate=pl.CostEstimate(flops=flops, bytes_accessed=40 * MIB, transcendentals=0),
+        name=name,
+    )(numbers, *operands, *came)
+    return list(outs[:2]), list(outs[2:])
+
+
+def newton_kernel(rows, *refs):
+    all_refs, mine_ref, out_ref = refs[:-11], refs[-11], refs[-10]
+    a_ref, ah, al, nh, th, tl, qh, ql, num_ref = refs[-9:]
+    width = a_ref.shape[0]
+    steps = width // rows
+    deep = min(1024, all_refs[0].shape[0])
+    a_at, m_at, t_at = 0, 1, 2
+
+    def block(index):
+        return pl.ds(pl.multiple_of(index * rows, rows), rows)
+
+    def on_diagonal(index):
+        row_at = lax.broadcasted_iota(jnp.int32, (rows, width), 0) + index * rows
+        return row_at == lax.broadcasted_iota(jnp.int32, (rows, width), 1)
+
+    def each(make):
+        def one(index, carry):
+            make(index)
+            return carry
+
+        lax.fori_loop(0, steps, one, 0)
+
+    def put(index, value, base, number_at, high, low=None):
+        diagonal = on_diagonal(index)
+
+        @pl.when(index == 0)
+        def _():
+            num_ref[3] = jnp.sum(jnp.where(diagonal, value, 0.0)) * (1.0 / rows)
+            num_ref[4 + number_at] = base + num_ref[3]
+
+        rest = value - jnp.where(diagonal, num_ref[3], 0.0)
+        first, second = split_two(rest)
+        high[block(index), :] = first
+        if low is not None:
+            low[block(index), :] = second
+
+    def commit(number_at):
+        num_ref[number_at] = num_ref[4 + number_at]
+
+    def wide(high, low, at):
+        return high[at, :].astype(jnp.float32) + low[at, :].astype(jnp.float32)
+
+    squares = 0.0
+    for index in range(steps):
+        columns = slice(index * rows, (index + 1) * rows)
+        value = jnp.zeros((rows, width), jnp.float32)
+        for ref in all_refs:
+
+            def part(k, total, ref=ref, columns=columns):
+                at = pl.ds(pl.multiple_of(k * deep, deep), deep)
+                return total + dot_tn(ref[at, columns], ref[at, :])
+
+            value = lax.fori_loop(0, ref.shape[0] // deep, part, value)
+        a_ref[columns, :] = value
+        squares += jnp.sum(jnp.where(on_diagonal(index), value, 0.0))
+    squares = jnp.full((1, 1), squares, jnp.float32)
+    inverse = 1.0 / (jnp.sqrt(squares) + 1e-07)
+    each(lambda index: put(index, a_ref[block(index), :] * inverse * inverse, 0.0, a_at, ah, al))
+    commit(a_at)
+
+    for number in range(5):
+        two = number < 2
+
+        def make_n(index):
+            at = block(index)
+            shift = num_ref[a_at]
+            value = newton_three * dot_low(ah[at, :], ah[...])
+            value += (newton_two + 2.0 * newton_three * shift) * wide(ah, al, at)
+            base = newton_one + newton_two * shift + newton_three * shift * shift
+            put(index, value, base, m_at, nh)
+
+        each(make_n)
+        commit(m_at)
+        if number == 0:
+
+            def first_q(index):
+                at = block(index)
+                value = nh[at, :].astype(jnp.float32) + jnp.where(on_diagonal(index), num_ref[m_at], 0.0)
+                qh[at, :], ql[at, :] = split_two(value)
+
+            each(first_q)
+        else:
+
+            def next_q(index):
+                at = block(index)
+                value = num_ref[m_at] * wide(qh, ql, at) + dot_low(qh[at, :], nh[...])
+                if number >= 3:
+                    value += dot_low(ql[at, :], nh[...])
+                qh[at, :], ql[at, :] = split_two(value)
+
+            each(next_q)
+        if number == 4:
+            break
+
+        def make_t(index):
+            at = block(index)
+            shift, much = num_ref[a_at], num_ref[m_at]
+            value = dot_low(ah[at, :], nh[...])
+            if two:
+                value += dot_low(al[at, :], nh[...])
+            value += shift * nh[at, :].astype(jnp.float32) + much * wide(ah, al, at)
+            put(index, value, shift * much, t_at, th, tl)
+
+        each(make_t)
+        commit(t_at)
+
+        def make_a(index):
+            at = block(index)
+            shift, much = num_ref[t_at], num_ref[m_at]
+            value = dot_low(nh[at, :], th[...])
+            if two:
+                value += dot_low(nh[at, :], tl[...])
+            value += shift * nh[at, :].astype(jnp.float32) + much * wide(th, tl, at)
+            put(index, value, shift * much, a_at, ah, al)
+
+        each(make_a)
+        commit(a_at)
+
+    mine = mine_ref[...]
+    out_ref[...] = ((dot_low(mine, qh[...]) + dot_low(mine, ql[...])) * inverse).astype(out_ref.dtype)
+
+
+def newton(everything, mine, rows=256):
+    width = mine.shape[1]
+    low = pltpu.VMEM((width, width), jnp.bfloat16)
+    return pl.pallas_call(
+        functools.partial(newton_kernel, rows),
+        out_shape=jax.ShapeDtypeStruct(mine.shape, jnp.bfloat16),
+        in_specs=[pl.BlockSpec(memory_space=pltpu.VMEM)] * (len(everything) + 1),
+        out_specs=pl.BlockSpec(memory_space=pltpu.VMEM),
+        scratch_shapes=[pltpu.VMEM((width, width), jnp.float32)]
+        + [low] * 7
+        + [pltpu.SMEM((8,), jnp.float32)],
+        compiler_params=pltpu.CompilerParams(vmem_limit_bytes=60 * 1024 * 1024),
+        cost_estimate=pl.CostEstimate(flops=60 * 10**9, bytes_accessed=12 * 10**6, transcendentals=0),
+        name="newton",
+    )(*everything, mine)
+
+
+def frame_sums_kernel(count, *refs):
+    out_ref = refs[-1]
+    ones, twos = refs[:count], refs[count : 2 * count]
+    steps, _, frames, _ = ones[0].shape
+    at = 0
+    for clip in range(count):
+        for step in range(steps):
+            rows = slice(at, at + frames)
+            for index in range(2):
+                out_ref[rows, index * D : (index + 1) * D] = ones[clip][step, index]
+            for index in range(4):
+                out_ref[rows, (index + 2) * D : (index + 3) * D] = twos[clip][step, index]
+            at += frames
+
+
+def frame_sums(ones, twos):
+    steps, _, frames, _ = ones[0].shape
+    return pl.pallas_call(
+        functools.partial(frame_sums_kernel, len(ones)),
+        out_shape=jax.ShapeDtypeStruct((len(ones) * steps * frames, 6 * D), jnp.float32),
+        in_specs=[pl.BlockSpec(memory_space=pltpu.VMEM)] * (2 * len(ones)),
+        out_specs=pl.BlockSpec(memory_space=pltpu.VMEM),
+        compiler_params=vmem_params(60),
+        cost_estimate=pl.CostEstimate(flops=0, bytes_accessed=MIB, transcendentals=0),
+        name="frame_sums",
+    )(*ones, *twos)
 
 
 def swap(slots):
@@ -772,24 +903,65 @@
     token_total = clip_count * seq_local
     frame_total = clip_count * frames
     shape_five = (clip_count, frames, rows_dev, columns, model_width)
-    w_table, w_ada, w_bias = (
-        lax.all_gather(table_master.astype(low_type), ("frame", "row"), axis=0, tiled=True),
-        lax.all_gather(ada_master.astype(low_type), ("frame", "row"), axis=1, tiled=True),
-        lax.all_gather(bias_master.astype(low_type), ("frame", "row"), axis=0, tiled=True),
-    )
-    w_qkv, w_out, w_up, w_down = (
-        lax.all_gather(item.astype(low_type), ("frame", "row"), axis=0, tiled=True)
-        for item in (qkv_master.T, out_master, up_master.T, down_master)
-    )
+    both = ("frame", "row")
+    frame_devices = lax.axis_size("frame")
+    device_total = frame_devices * row_devices
+    device_index = lax.axis_index("frame") * row_devices + lax.axis_index("row")
+    heights = (qkv_master.shape[1], out_master.shape[0], up_master.shape[1], down_master.shape[0])
+    w_qkv = lax.all_gather(qkv_master.T.astype(low_type), both, axis=0, tiled=True)
+    shards = jnp.concatenate([down_master, up_master.T, out_master], axis=0).astype(low_type)
+    gathered = lax.all_gather(shards, both, axis=0)
+    if heights[1] % 16 == 0:
+
+        def from_slab(first, height):
+            return gathered, pl.BlockSpec(
+                (device_total, height, model_width),
+                lambda *_: (0, first // height, 0),
+                pipeline_mode=pl.Buffered(1),
+            )
+
+    else:
+
+        def from_slab(first, height):
+            part = gathered[:, first : first + height].reshape(-1, model_width // row_devices, model_width)
+            return part, whole_spec(part)
+
+    w_down = from_slab(0, heights[3])
+    w_up = from_slab(heights[3], heights[2])
+    w_out = from_slab(heights[3] + heights[2], heights[1])
     level_flat = noise_levels.reshape(frame_total)
-    level_hot = (
-        level_flat[:, None] == jnp.arange(w_table.shape[0], dtype=jnp.int32)[None, :]
-    ).astype(low_type)
-    embedded = jnp.dot(level_hot, w_table, preferred_element_type=full_type)
-    cond_low = jax.nn.silu(embedded).astype(low_type)
-    modulation = jnp.dot(cond_low, w_ada, preferred_element_type=full_type) + w_bias.astype(
-        full_type
-    )
+    levels_all = lax.all_gather(level_flat, "frame", axis=0, tiled=True)
+    frames_all = frame_devices * frame_total
+    frames_each = frames_all // device_total
+    level_rows = table_master.shape[0]
+    my_levels = device_index * level_rows + jnp.arange(level_rows, dtype=jnp.int32)
+    level_hot = levels_all[:, None] == my_levels[None, :]
+    found = jnp.dot(
+        level_hot.astype(low_type),
+        lax.optimization_barrier(table_master.astype(low_type)),
+        preferred_element_type=full_type,
+    )
+
+    def to_all(value):
+        return lax.all_to_all(value, both, split_axis=0, concat_axis=0, tiled=True)
+
+    def from_all(value):
+        return to_all(jnp.broadcast_to(value[None], (device_total,) + value.shape))
+
+    embedded_mine = jnp.sum(
+        to_all(found.reshape(device_total, frames_each, model_width)), axis=0
+    )
+    embedded_all = from_all(embedded_mine).reshape(frames_all, model_width)
+    cond_all = jax.nn.silu(embedded_all).astype(low_type)
+    ada_low = lax.optimization_barrier(ada_master.astype(low_type))
+    bias_low = lax.optimization_barrier(bias_master.astype(low_type))
+    ada_width = ada_master.shape[1]
+    mod_columns = jnp.dot(cond_all, ada_low, preferred_element_type=full_type) + bias_low.astype(full_type)
+    mod_columns = mod_columns.reshape(frame_devices, 1, frame_total, ada_width)
+    mod_columns = jnp.broadcast_to(
+        mod_columns, (frame_devices, row_devices, frame_total, ada_width)
+    ).reshape(device_total, frame_total, ada_width)
+    modulation = jnp.moveaxis(to_all(mod_columns), 0, 1).reshape(frame_total, 6 * model_width)
     grid_shape = (clip_count, frames, rows_dev, columns)
     row_first = lax.axis_index("row") * rows_dev
     time_grid = jnp.broadcast_to(frame_times.astype(full_type)[:, :, None, None], grid_shape)
@@ -833,66 +1005,53 @@
     att_low, hidden_two, activated, d_branch_two, d_up, d_branch_one, d_middle, two_sums = (
         [item[index] for item in middles] for index in range(1, 9)
     )
-    early = scatter_sum(
-        [(activated, d_branch_two), (d_up, hidden_two), (att_low, d_branch_one)], "early"
-    )
-    d_pieces = [
-        swap(attend_back(pieces[clip], d_attended[clip], full[clip], logs[clip])) for clip in clips
-    ]
-    lasts = [
-        last(me, clip, tokens_flat, mod, cosine, sine, w_qkv, d_middle[clip], d_pieces[clip])
-        for clip in clips
-    ]
+    early = scatter_steps(
+        [[(activated, d_branch_two)], [(d_up, hidden_two), (att_low, d_branch_one)]], "early"
+    )
+
+    def after(value, state):
+        return [held(value[0], *state), *value[1:]]
+
+    state = next(early)
+    d_pieces = []
+    for clip in clips:
+        slots = attend_back(pieces[clip], after(d_attended[clip], state), full[clip], logs[clip])
+        d_pieces.append(swap(slots))
+        state = early.send([slots[0]])
+    lasts = []
+    for clip in clips:
+        lasts.append(
+            last(
+                me, clip, tokens_flat, mod, cosine, sine, w_qkv, d_middle[clip],
+                after(d_pieces[clip], state),
+            )
+        )
+        state = early.send([lasts[clip][2]])
+    early_sum = finished(early, state)
     input_grad = jnp.concatenate([item[1] for item in lasts], axis=0).reshape(shape_five)
-    g_qkv = scatter_sum([([item[0] for item in lasts], hidden_one)], "late")
-
-    def frames_of(sums, index):
-        return jnp.concatenate([item[:, index].reshape(frames, model_width) for item in sums], axis=0)
-
+    late = scatter_steps([[([item[0] for item in lasts], hidden_one)]], "late")
+    state = next(late)
     one_sums = [item[2] for item in lasts]
-    d_modulation = jnp.concatenate(
-        [frames_of(one_sums, 0), frames_of(one_sums, 1)] + [frames_of(two_sums, index) for index in range(4)],
-        axis=1,
-    )
-    frame_devices = lax.axis_size("frame")
-    device_total = frame_devices * row_devices
-    both = ("frame", "row")
-    levels_all = lax.all_gather(level_flat, "frame", axis=0, tiled=True)
-    embedded_all = lax.all_gather(embedded.astype(low_type), "frame", axis=0, tiled=True).astype(
-        full_type
-    )
-    cond_all = jax.nn.silu(embedded_all).astype(low_type)
-    ada_width = ada_master.shape[1]
-    mod_parts = lax.all_to_all(
-        jnp.moveaxis(d_modulation.reshape(frame_total, device_total, ada_width), 1, 0),
-        both,
-        split_axis=0,
-        concat_axis=0,
-        tiled=True,
-    )
+    one_sums[0] = held(one_sums[0], *state)
+    d_modulation = frame_sums(one_sums, two_sums)
+    g_qkv = finished(late, state)
+
+    mod_parts = to_all(jnp.moveaxis(d_modulation.reshape(frame_total, device_total, ada_width), 1, 0))
     mod_mine = (
         jnp.sum(mod_parts.reshape(frame_devices, row_devices, frame_total, ada_width), axis=1)
-        .reshape(frame_devices * frame_total, ada_width)
+        .reshape(frames_all, ada_width)
         .astype(low_type)
     )
     g_ada = jnp.einsum("fd,fe->de", cond_all, mod_mine, preferred_element_type=full_type)
     g_bias = jnp.sum(mod_mine.astype(full_type), axis=0)
-    d_cond = lax.psum(
-        jnp.einsum("fe,de->fd", mod_mine, ada_master.astype(low_type), preferred_element_type=full_type),
-        both,
-    )
-    d_embedded = jax.vjp(jax.nn.silu, embedded_all)[1](d_cond)[0]
-    device_index = lax.axis_index("frame") * row_devices + lax.axis_index("row")
-    level_rows = table_master.shape[0]
-    hot_mine = (
-        levels_all[None, :]
-        == (device_index * level_rows + jnp.arange(level_rows, dtype=jnp.int32))[:, None]
-    ).astype(full_type)
-    g_table = jnp.dot(hot_mine, d_embedded, precision=highest)
-    heights = (qkv_master.shape[1], out_master.shape[0], up_master.shape[1], down_master.shape[0])
-    g_down = early[: heights[3]]
-    g_up = early[heights[3] : heights[3] + heights[2]]
-    g_out = early[heights[3] + heights[2] :]
+    d_cond_parts = jnp.einsum("fe,de->fd", mod_mine, ada_low, preferred_element_type=full_type)
+    d_cond = jnp.sum(to_all(d_cond_parts.reshape(device_total, frames_each, model_width)), axis=0)
+    d_embedded_mine = jax.vjp(jax.nn.silu, embedded_mine)[1](d_cond)[0]
+    d_embedded = from_all(d_embedded_mine).reshape(frames_all, model_width)
+    g_table = jnp.dot(level_hot.astype(full_type).T, d_embedded, precision=highest)
+    g_down = early_sum[: heights[3]]
+    g_up = early_sum[heights[3] : heights[3] + heights[2]]
+    g_out = early_sum[heights[3] + heights[2] :]
     muon_grads = (g_qkv, g_out, g_up, g_down)
     flipped = (True, False, True, False)
 
@@ -904,25 +1063,59 @@
     factors = (math.sqrt(3.0), 1.0, math.sqrt(FF / D), math.sqrt(FF / D))
     adam_local = jnp.sum(g_ada * g_ada) + jnp.sum(g_table * g_table) + jnp.sum(g_bias * g_bias)
     local_total = adam_local + sum((jnp.sum(item * item) for item in muon_grads))
-    norm_value = jnp.sqrt(lax.psum(local_total, both))
+    norm_value = jnp.sqrt(jnp.sum(from_all(jnp.full((1, 128), local_total))[:, 0, 0]))
     clip_factor = jnp.minimum(1.0, clip_limit / (norm_value + 1e-06))
     moments_new = []
-    pieces = []
-    slot = max(heights)
+    updates = []
+    slot_rows = max(heights)
     for member in range(4):
         clipped = clip_factor * muon_grads[member]
         moment = momentum_decay * tall(muon_moments[member], member) + clipped
         update = (clipped + momentum_decay * moment).astype(low_type)
         moments_new.append(tall(moment, member))
-        pieces.append(jnp.pad(update, ((0, slot - heights[member]), (0, 0))))
-    slab = jnp.stack(pieces * (row_devices // 4))
-    updates = lax.all_to_all(slab, "row", split_axis=0, concat_axis=0, tiled=True).reshape(
-        row_devices * slot, model_width
-    )
-    everything = lax.all_gather(updates, "frame", axis=0, tiled=True)
-    ortho_rows = newton(everything, updates).reshape(row_devices, slot, model_width)
-    ortho_mine = lax.all_to_all(ortho_rows, "row", split_axis=0, concat_axis=0, tiled=True)
-    blocks = [tall(ortho_mine[member, : heights[member]].astype(full_type), member) for member in range(4)]
+        updates.append(jnp.pad(update, ((0, slot_rows - heights[member]), (0, 0))))
+    slab = jnp.stack(updates)
+    groups = frame_devices // 2
+    group_index = lax.axis_index("frame") >> 1
+
+    def frame_swap(slots):
+        out = [slots[0]]
+        for slot in range(1, groups):
+            pairs = [(index, index ^ (2 * slot)) for index in range(frame_devices)]
+            out.append(lax.ppermute(slots[slot], "frame", pairs))
+        return out
+
+    mine = jnp.concatenate(
+        frame_swap(
+            [
+                lax.dynamic_index_in_dim(slab, (group_index ^ slot) & 3, 0, keepdims=False)
+                for slot in range(groups)
+            ]
+        ),
+        axis=0,
+    )
+
+    def row_partner(value, bit):
+        return lax.ppermute(value, "row", [(index, index ^ (1 << bit)) for index in range(row_devices)])
+
+    row_bits = row_devices.bit_length() - 1
+    cut = mine.shape[0] // 2
+    grown = [mine[:cut], mine[cut:]]
+    for step in range(row_bits):
+        grown = [
+            jnp.concatenate([grown[0], row_partner(grown[0], step)], axis=0),
+            jnp.concatenate([grown[1], row_partner(grown[1], row_bits - 1 - step)], axis=0),
+        ]
+    others = [
+        lax.ppermute(item, "frame", [(index, index ^ 1) for index in range(frame_devices)]) for item in grown
+    ]
+    ortho_rows = newton([*grown, *others], mine).reshape(groups, slot_rows, model_width)
+    ortho_slots = jnp.stack(frame_swap([ortho_rows[slot] for slot in range(groups)]))
+    ortho_mine = [
+        lax.dynamic_index_in_dim(ortho_slots, (group_index & 3) ^ member, 0, keepdims=False)
+        for member in range(4)
+    ]
+    blocks = [tall(ortho_mine[member][: heights[member]].astype(full_type), member) for member in range(4)]
     masters_new = []
     for member in range(4):
         ortho = blocks[member]

time: 1360 us -> 972 us (0.71)
  waiting for transfers between devices: 574 us -> 289 us
  blocking collectives: 118 us -> 29.7 us
  starting transfers between devices: 50.6 us -> 86.6 us
  local copies, waits for them, and re-layouts: 64.5 us -> 49.2 us
    all_gather x7 -> x2, waiting for transfers between devices: 359 us -> 14 us  [the longest x1 14 us: per_device(): gathered = lax.all_gather(shards, both, axis=0)]
    psum x1 -> x0, waiting for transfers between devices: 102 us -> none  [per_device(): lax.psum(jnp.einsum('fe,de->fd', mod_mine, ada_master.astype(low_type), p...]
    ppermute x24, waiting for transfers between devices: 31.4 us -> 101 us  [swap(): lax.ppermute(slots[slot], 'row', [(index, index ^ slot) for index in rang...]
    ppermute x14 -> x27, waiting for transfers between devices: 57.4 us -> 118 us  [the longest x6 41.7 us: frame_swap(): out.append(lax.ppermute(slots[slot], 'frame', pairs))]
    unnamed x2 -> x1, blocking collectives: 49.1 us -> 8.45 us
    psum x1 -> x0, blocking collectives: 39.2 us -> none  [per_device(): norm_value = jnp.sqrt(lax.psum(local_total, both))]
    all_to_all x2 -> x6, waiting for transfers between devices: 24.5 us -> 55.6 us  [to_all(): return lax.all_to_all(value, both, split_axis=0, concat_axis=0, tiled=True)]
    all_to_all x2 -> x6, starting transfers between devices: 7.52 us -> 29.7 us  [to_all(): return lax.all_to_all(value, both, split_axis=0, concat_axis=0, tiled=True)]
  transfers between devices with their start and end apart: 48 -> 59, of which waited for: 22 -> 29; matrix products, arithmetic and copies ran while one was open for 8% -> 7% of each run, Pallas kernels for 23% -> 26%
where the time goes in v3:
time: 972 us; the launch traced here: 965 us
  Pallas kernels  433 us (45%)
  waiting for transfers between devices  289 us (30%)
  starting transfers between devices  86.6 us (9%)
  other arithmetic  50.3 us (5%)
  local copies, waits for them, and re-layouts  49.2 us (5%)
  blocking collectives  29.7 us (3%)
  between operations  23.3 us (2%)
    pallas_call x2, Pallas kernels, attend_back(): pl.pallas_call(functools.partial(attend_back_kernel, slots, 512), grid=(g...  104 us
    pallas_call x1, Pallas kernels, newton(): pl.pallas_call(functools.partial(newton_kernel, rows), out_shape=jax.Shap...  102 us
    ppermute x24, waiting for transfers between devices, swap(): lax.ppermute(slots[slot], 'row', [(index, index ^ slot) for index in rang...  101 us
    pallas_call x2, Pallas kernels, middle(): pl.pallas_call(functools.partial(middle_kernel, slots), grid=(steps,), in...  66.5 us
    pallas_call x2, Pallas kernels, attend(): pl.pallas_call(functools.partial(attend_kernel, slots, 256), grid=(group...  64.3 us
    all_to_all x6, waiting for transfers between devices, to_all(): return lax.all_to_all(value, both, split_axis=0, concat_axis=0, tiled=True)  55.6 us
    ppermute x6, waiting for transfers between devices, frame_swap(): out.append(lax.ppermute(slots[slot], 'frame', pairs))  41.7 us
    ppermute x4, waiting for transfers between devices, row_partner(): lax.ppermute(value, 'row', [(index, index ^ 1 << bit) for index in range(...  32.5 us
  transfers between devices with their start and end apart: 59, of which 29 were waited for; matrix products, arithmetic and copies ran while one was open for 7% of the time, Pallas kernels for 26%

profile of v3, /device:TPU:8, one launch (start us, length us, event | category | flops | bytes accessed | tf_op | source)
XLA Modules:
  0.0 965.5 jit_solution(9023678439269860523)
XLA Ops:
  24.1 21.3 %all_to_all.35 = f32[32,4,1024]{2,1,0:T(4,128)S(1)} all-to-all(f32[32,4,1024]{2,1,0:T(4,128)S(1)} %reshape.254), channel_id=1, replica_groups=mesh['frame'=8,'row'=4] {'frame','row'}, dimensions={0} | all-to-all | bytes 1048576 | tf_op jit(solution)/shard_map/all_to_all | solution.py:946
  51.7 20.6 %all-to-all-done.1 = f32[32,4,1024]{2,1,0:T(4,128)S(1)} async-done(((f32[32,4,1024]{2,1,0:T(4,128)}), f32[32,4,1024]{2,1,0:T(4,128)S(1)}, u32[]{:S(2)}, u32[]{:S(2)}) %all-to-all-start.1) | async-done | bytes 524320 | tf_op jit(solution)/shard_map/all_to_all | solution.py:946
  82.2 12.6 %all-to-all-done.2 = f32[32,16,192]{2,1,0:T(8,128)S(1)} async-done(((f32[32,16,192]{2,1,0:T(8,128)}), f32[32,16,192]{2,1,0:T(8,128)S(1)}, u32[]{:S(2)}, u32[]{:S(2)}) %all-to-all-start.2) | async-done | bytes 393248 | tf_op jit(solution)/shard_map/all_to_all | solution.py:946
  96.1 9.1 project.2
  109.4 9.1 project.3
  134.4 25.7 %collective-permute-done.2.refs_3_ = bf16[3,512,256]{2,1,0:T(8,128)(2,1)} collective-permute-done((bf16[3,512,256]{2,1,0:T(8,128)(2,1)}, bf16[3,512,256]{2,1,0:T(8,128)(2,1)}, u32[]{:S(2)}, u32[]{:S(2)}) %collective-permute-start.2) | collective-permute-done | bytes 786464 | tf_op jit(solution)/shard_map/ppermute | solution.py:870
  160.1 32.2 %attend.2 = (bf16[512,256]{1,0:T(8,128)(2,1)}, bf16[512,256]{1,0:T(8,128)(2,1)}, bf16[512,256]{1,0:T(8,128)(2,1)}, bf16[512,256]{1,0:T(8,128)(2,1)}, f32[2048,256]{1,0:T(8,128)}, /*index=5*/f32[2048,256]{1,0:T(8,128)}) custom-call(bf16[3,512,256]{2,1,0:T(8,128)(2,1)} %get-tuple-element.104.refs_0_, bf16[3,512,256]{2,1,0:T(8,128)(2,1)} %copy-done.51, ...), custom_call_target="tpu_custom_call" | custom-call | flops 17179869184 | bytes 8388608 | tf_op jit(solution)/shard_map/attend/pallas_call | solution.py:277
  195.9 13.6 %collective-permute-done.8.refs_3_ = bf16[3,512,256]{2,1,0:T(8,128)(2,1)S(1)} collective-permute-done((bf16[3,512,256]{2,1,0:T(8,128)(2,1)}, bf16[3,512,256]{2,1,0:T(8,128)(2,1)S(1)}, u32[]{:S(2)}, u32[]{:S(2)}) %collective-permute-start.8) | collective-permute-done | bytes 786464 | tf_op jit(solution)/shard_map/ppermute | solution.py:870
  210.3 32.1 %attend.3 = (bf16[512,256]{1,0:T(8,128)(2,1)}, bf16[512,256]{1,0:T(8,128)(2,1)}, bf16[512,256]{1,0:T(8,128)(2,1)}, bf16[512,256]{1,0:T(8,128)(2,1)}, f32[2048,256]{1,0:T(8,128)}, /*index=5*/f32[2048,256]{1,0:T(8,128)}) custom-call(bf16[3,512,256]{2,1,0:T(8,128)(2,1)} %get-tuple-element.113.refs_0_, bf16[3,512,256]{2,1,0:T(8,128)(2,1)} %copy-done.48, ...), custom_call_target="tpu_custom_call" | custom-call | flops 17179869184 | bytes 8388608 | tf_op jit(solution)/shard_map/attend/pallas_call | solution.py:277
  246.0 14.0 %all-gather.3.cloned.1.call-done.wo_ref.wu_ref.wd_ref = bf16[32,288,1024]{2,1,0:T(8,128)(2,1)} async-done(((bf16[1,288,1024]{2,1,0:T(8,128)(2,1)}), bf16[32,288,1024]{2,1,0:T(8,128)(2,1)}) %all-gather.3.cloned.1.call-update) | async-done | bytes 18874384 | tf_op jit(solution)/shard_map/all_gather | solution.py:913
  260.0 33.3 %middle.2 = (bf16[512,256]{1,0:T(8,128)(2,1)}, bf16[512,256]{1,0:T(8,128)(2,1)}, bf16[512,256]{1,0:T(8,128)(2,1)}, bf16[512,256]{1,0:T(8,128)(2,1)}, bf16[1,512,...) custom-call(s32[1]{0:T(128)} %bitcast.me_ref, ...), custom_call_target="tpu_custom_call" | custom-call | flops 19327352832 | bytes 41943040 | tf_op jit(solution)/shard_map/middle/pallas_call | solution.py:480
  294.3 33.2 %middle.3 = (bf16[512,256]{1,0:T(8,128)(2,1)}, bf16[512,256]{1,0:T(8,128)(2,1)}, bf16[512,256]{1,0:T(8,128)(2,1)}, bf16[512,256]{1,0:T(8,128)(2,1)}, bf16[1,512,...) custom-call(s32[1]{0:T(128)} %bitcast.me_ref, ...), custom_call_target="tpu_custom_call" | custom-call | flops 19327352832 | bytes 41943040 | tf_op jit(solution)/shard_map/middle/pallas_call | solution.py:480
  327.5 9.1 early_send_0.1
  336.6 11.6 %early_send_1.1 = bf16[4,4,160,1024]{3,2,1,0:T(8,128)(2,1)} custom-call(s32[3]{0:T(128)} %pad_add_fusion.number_ref, bf16[512,4096]{1,0:T(8,128)(2,1)} %get-tuple-element.129.refs_0_.refs_4_, bf16[512,4096]{1,0:T(8,128)(2,1)} %get-tuple-element.130.refs_1_.refs_5_, bf16[512,1024]{1,0:T(8,128)(2,1)} %get-tuple-element.131.refs_2_.refs_6_, ...), custom_call_target="tpu_custom_call" | custom-call | flops 5368709120 | bytes 20971520 | tf_op jit(solution)/shard_map/early_send_1/pallas_call | solution.py:663
  352.1 11.0 %collective-permute-done.12.refs_12_ = bf16[4,4,128,1024]{3,2,1,0:T(8,128)(2,1)} collective-permute-done((bf16[4,4,128,1024]{3,2,1,0:T(8,128)(2,1)}, bf16[4,4,128,1024]{3,2,1,0:T(8,128)(2,1)}, u32[]{:S(2)}, u32[]{:S(2)}) %collective-permute-start.12) | collective-permute-done | bytes 4194336 | tf_op jit(solution)/shard_map/ppermute | solution.py:87
  365.1 19.5 %early_keep.1 = (f32[4,2,288,512]{3,2,1,0:T(8,128)}, f32[4,2,288,512]{3,2,1,0:T(8,128)}, bf16[4,2,288,512]{3,2,1,0:T(8,128)(2,1)}, bf16[4,2,288,512]{3,2,1,0:T(8,128)(2,1)}) custom-call(s32[3]{0:T(128)} %pad_add_fusion.number_ref, bf16[512,4096]{1,0:T(8,128)(2,1)} %get-tuple-element.124.refs_0_, bf16[512,4096]{1,0:T(8,128)(2,1)} %get-tuple-element.125.refs_1_, ...), custom_call_target="tpu_custom_call" | custom-call | flops 9663676416 | bytes 41943040 | tf_op jit(solution)/shard_map/early_keep/pallas_call | solution.py:685
  392.4 51.8 %attend_back.2 = (bf16[3,512,256]{2,1,0:T(8,128)(2,1)}, bf16[3,512,256]{2,1,0:T(8,128)(2,1)}, bf16[3,512,256]{2,1,0:T(8,128)(2,1)}, bf16[3,512,256]{2,1,0:T(8,128)(2,1)}) custom-call(bf16[3,512,256]{2,1,0:T(8,128)(2,1)} %get-tuple-element.104.refs_0_, bf16[3,512,256]{2,1,0:T(8,128)(2,1)} %copy-done.51, bf16[3,512,256]{2,1,0:T(8,128)(2,1)} %copy-done.52, ...), custom_call_target="tpu_custom_call" | custom-call | flops 42949672960 | bytes 12582912 | tf_op jit(solution)/shard_map/attend_back/pallas_call | solution.py:364
  460.6 52.0 %attend_back.3 = (bf16[3,512,256]{2,1,0:T(8,128)(2,1)}, bf16[3,512,256]{2,1,0:T(8,128)(2,1)}, bf16[3,512,256]{2,1,0:T(8,128)(2,1)}, bf16[3,512,256]{2,1,0:T(8,128)(2,1)}) custom-call(bf16[3,512,256]{2,1,0:T(8,128)(2,1)} %get-tuple-element.113.refs_0_, bf16[3,512,256]{2,1,0:T(8,128)(2,1)} %copy-done.48, bf16[3,512,256]{2,1,0:T(8,128)(2,1)} %copy-done.49, ...), custom_call_target="tpu_custom_call" | custom-call | flops 42949672960 | bytes 12582912 | tf_op jit(solution)/shard_map/attend_back/pallas_call | solution.py:364
  528.7 13.0 %collective-permute-done.24.refs_1_ = bf16[3,512,256]{2,1,0:T(8,128)(2,1)} collective-permute-done((bf16[3,512,256]{2,1,0:T(8,128)(2,1)}, bf16[3,512,256]{2,1,0:T(8,128)(2,1)}, u32[]{:S(2)}, u32[]{:S(2)}) %collective-permute-start.24) | collective-permute-done | bytes 786464 | tf_op jit(solution)/shard_map/ppermute | solution.py:870
  542.5 15.0 %collective-permute-done.25.refs_2_ = bf16[3,512,256]{2,1,0:T(8,128)(2,1)} collective-permute-done((bf16[3,512,256]{2,1,0:T(8,128)(2,1)}, bf16[3,512,256]{2,1,0:T(8,128)(2,1)}, u32[]{:S(2)}, u32[]{:S(2)}) %collective-permute-start.25) | collective-permute-done | bytes 786464 | tf_op jit(solution)/shard_map/ppermute | solution.py:870
  558.9 9.9 %last.2 = (bf16[512,3072]{1,0:T(8,128)(2,1)}, f32[1,512,1024]{2,1,0:T(8,128)}, f32[2,2,4,1024]{3,2,1,0:T(4,128)}) custom-call(s32[1]{0:T(128)} %bitcast.me_ref, bf16[2,512,1024]{2,1,0:T(8,128)(2,1)} %bitcast.148, f32[4,4,6144]{2,1,0:T(4,128)} %reshape_reshape.4.mod_ref, f32[1024,128]{1,0:T(8,128)} %copy.159.cos_ref, ...), custom_call_target="tpu_custom_call" | custom-call | flops 3221225472 | bytes 20971520 | tf_op jit(solution)/shard_map/last/pallas_call | solution.py:554
  575.4 16.1 %collective-permute-done.29.refs_2_ = bf16[3,512,256]{2,1,0:T(8,128)(2,1)} collective-permute-done((bf16[3,512,256]{2,1,0:T(8,128)(2,1)}, bf16[3,512,256]{2,1,0:T(8,128)(2,1)}, u32[]{:S(2)}, u32[]{:S(2)}) %collective-permute-start.29) | collective-permute-done | bytes 786464 | tf_op jit(solution)/shard_map/ppermute | solution.py:870
  591.6 9.9 %last.3 = (bf16[512,3072]{1,0:T(8,128)(2,1)}, f32[1,512,1024]{2,1,0:T(8,128)}, f32[2,2,4,1024]{3,2,1,0:T(4,128)}) custom-call(s32[1]{0:T(128)} %bitcast.me_ref, bf16[2,512,1024]{2,1,0:T(8,128)(2,1)} %bitcast.149, f32[4,4,6144]{2,1,0:T(4,128)} %reshape_reshape.4.mod_ref, f32[1024,128]{1,0:T(8,128)} %copy.159.cos_ref, ...), custom_call_target="tpu_custom_call" | custom-call | flops 3221225472 | bytes 20971520 | tf_op jit(solution)/shard_map/last/pallas_call | solution.py:554
  616.9 8.7 late_keep.1
  644.5 18.5 %all-to-all-done.3 = f32[32,16,192]{2,1,0:T(8,128)} async-done(((f32[32,16,192]{2,1,0:T(8,128)}), f32[32,16,192]{2,1,0:T(8,128)}, u32[]{:S(2)}, u32[]{:S(2)}) %all-to-all-start.3) | async-done | bytes 393248 | tf_op jit(solution)/shard_map/all_to_all | solution.py:946
  679.8 9.1 collective-permute-done.35
  709.2 9.0 collective-permute-done.37
  751.9 13.9 %collective-permute-done.42 = bf16[128,1024]{1,0:T(8,128)(2,1)S(1)} collective-permute-done((bf16[128,1024]{1,0:T(8,128)(2,1)S(1)}, bf16[128,1024]{1,0:T(8,128)(2,1)S(1)}, u32[]{:S(2)}, u32[]{:S(2)}) %collective-permute-start.42) | collective-permute-done | bytes 262176 | tf_op jit(solution)/shard_map/ppermute | solution.py:1085
  774.7 12.5 %collective-permute-done.44 = bf16[256,1024]{1,0:T(8,128)(2,1)S(1)} collective-permute-done((bf16[256,1024]{1,0:T(8,128)(2,1)S(1)}, bf16[256,1024]{1,0:T(8,128)(2,1)S(1)}, u32[]{:S(2)}, u32[]{:S(2)}) %collective-permute-start.44) | collective-permute-done | bytes 524320 | tf_op jit(solution)/shard_map/ppermute | solution.py:1099
  793.2 19.5 %collective-permute-done.45 = bf16[512,1024]{1,0:T(8,128)(2,1)S(1)} collective-permute-done((bf16[512,1024]{1,0:T(8,128)(2,1)S(1)}, bf16[512,1024]{1,0:T(8,128)(2,1)S(1)}, u32[]{:S(2)}, u32[]{:S(2)}) %collective-permute-start.45) | collective-permute-done | bytes 1048608 | tf_op jit(solution)/shard_map/ppermute | solution.py:1099
  824.0 101.9 %newton.1 = bf16[512,1024]{1,0:T(8,128)(2,1)} custom-call(bf16[1024,1024]{1,0:T(8,128)(2,1)} %pad_maximum_fusion.2.refs_0_, bf16[1024,1024]{1,0:T(8,128)(2,1)} %constant_dynamic-update-slice_fusion.refs_1_, bf16[1024,1024]{1,0:T(8,128)(2,1)} %collective-permute-done.46.refs_2_, bf16[1024,1024]{1,0:T(8,128)(2,1)} %collective-permute-done.47.refs_3_, ...), custom_call_target="tpu_custom_call" | custom-call | flops 60000002048 | bytes 12000000 | tf_op jit(solution)/shard_map/newton/pallas_call | solution.py:824
  941.0 12.6 %collective-permute-done.50 = bf16[128,1024]{1,0:T(8,128)(2,1)S(1)} collective-permute-done((bf16[128,1024]{1,0:T(8,128)(2,1)S(1)}, bf16[128,1024]{1,0:T(8,128)(2,1)S(1)}, u32[]{:S(2)}, u32[]{:S(2)}) %collective-permute-start.50) | collective-permute-done | bytes 262176 | tf_op jit(solution)/shard_map/ppermute | solution.py:1085
  (374 shorter events, 260.7 us)
Async XLA Ops:
  7.2 88.9 %all-gather.5.cloned.1.call-start = ((), (), s32[]{:S(2)}) async-start(), calls=%async_computation.8 | async-start | bytes 6488064 | tf_op jit(solution)/shard_map/all_gather | solution.py:911
  9.0 251.0 %all-gather.3.cloned.1.call-start = ((), (), s32[]{:S(2)}) async-start(), calls=%async_computation.7 | async-start | bytes 19464192 | tf_op jit(solution)/shard_map/all_gather | solution.py:913
  107.2 52.9 %collective-permute-start.2 = (bf16[3,512,256]{2,1,0:T(8,128)(2,1)}, bf16[3,512,256]{2,1,0:T(8,128)(2,1)}, u32[]{:S(2)}, u32[]{:S(2)}) collective-permute-start(bf16[3,512,256]{2,1,0:T(8,128)(2,1)} %get-tuple-element.107), channel_id=1, source_target_pairs={{0,3},{1,2},{2,1},{3,0},{4,7},{5,6},{6,5},{7,4},{8,11},{9,10},{10,... | collective-permute-start | bytes 2359304 | tf_op jit(solution)/shard_map/ppermute | solution.py:870
  118.5 75.6 %collective-permute-start.6 = (bf16[3,512,256]{2,1,0:T(8,128)(2,1)}, bf16[3,512,256]{2,1,0:T(8,128)(2,1)S(1)}, u32[]{:S(2)}, u32[]{:S(2)}) collective-permute-start(bf16[3,512,256]{2,1,0:T(8,128)(2,1)} %get-tuple-element.114), channel_id=1, source_target_pairs={{0,1},{1,0},{2,3},{3,2},{4,5},{5,4},{6,7},{7,6},{8,9},{9,8},{10,11... | collective-permute-start | bytes 2359304 | tf_op jit(solution)/shard_map/ppermute | solution.py:870
  119.1 76.7 %collective-permute-start.7 = (bf16[3,512,256]{2,1,0:T(8,128)(2,1)}, bf16[3,512,256]{2,1,0:T(8,128)(2,1)S(1)}, u32[]{:S(2)}, u32[]{:S(2)}) collective-permute-start(bf16[3,512,256]{2,1,0:T(8,128)(2,1)} %get-tuple-element.115), channel_id=1, source_target_pairs={{0,2},{1,3},{2,0},{3,1},{4,6},{5,7},{6,4},{7,5},{8,10},{9,11},{10,... | collective-permute-start | bytes 2359304 | tf_op jit(solution)/shard_map/ppermute | solution.py:870
  128.3 81.1 %collective-permute-start.8 = (bf16[3,512,256]{2,1,0:T(8,128)(2,1)}, bf16[3,512,256]{2,1,0:T(8,128)(2,1)S(1)}, u32[]{:S(2)}, u32[]{:S(2)}) collective-permute-start(bf16[3,512,256]{2,1,0:T(8,128)(2,1)} %get-tuple-element.116), channel_id=1, source_target_pairs={{0,3},{1,2},{2,1},{3,0},{4,7},{5,6},{6,5},{7,4},{8,11},{9,10},{10,... | collective-permute-start | bytes 2359304 | tf_op jit(solution)/shard_map/ppermute | solution.py:870
  192.3 53.2 %collective-permute-start.3 = (bf16[512,256]{1,0:T(8,128)(2,1)}, bf16[512,256]{1,0:T(8,128)(2,1)S(1)}, u32[]{:S(2)}, u32[]{:S(2)}) collective-permute-start(bf16[512,256]{1,0:T(8,128)(2,1)} %get-tuple-element.109), channel_id=1, source_target_pairs={{0,1},{1,0},{2,3},{3,2},{4,5},{5,4},{6,7},{7,6},{8,9},{9,8},{10,11... | collective-permute-start | bytes 786440 | tf_op jit(solution)/shard_map/ppermute | solution.py:870
  193.4 52.6 %collective-permute-start.4 = (bf16[512,256]{1,0:T(8,128)(2,1)}, bf16[512,256]{1,0:T(8,128)(2,1)S(1)}, u32[]{:S(2)}, u32[]{:S(2)}) collective-permute-start(bf16[512,256]{1,0:T(8,128)(2,1)} %get-tuple-element.110), channel_id=1, source_target_pairs={{0,2},{1,3},{2,0},{3,1},{4,6},{5,7},{6,4},{7,5},{8,10},{9,11},{10,... | collective-permute-start | bytes 786440 | tf_op jit(solution)/shard_map/ppermute | solution.py:870
  194.1 51.9 %collective-permute-start.5 = (bf16[512,256]{1,0:T(8,128)(2,1)}, bf16[512,256]{1,0:T(8,128)(2,1)S(1)}, u32[]{:S(2)}, u32[]{:S(2)}) collective-permute-start(bf16[512,256]{1,0:T(8,128)(2,1)} %get-tuple-element.111), channel_id=1, source_target_pairs={{0,3},{1,2},{2,1},{3,0},{4,7},{5,6},{6,5},{7,4},{8,11},{9,10},{10,... | collective-permute-start | bytes 786440 | tf_op jit(solution)/shard_map/ppermute | solution.py:870
  242.4 51.0 %collective-permute-start.10 = (bf16[512,256]{1,0:T(8,128)(2,1)}, bf16[512,256]{1,0:T(8,128)(2,1)S(1)}, u32[]{:S(2)}, u32[]{:S(2)}) collective-permute-start(bf16[512,256]{1,0:T(8,128)(2,1)} %get-tuple-element.119), channel_id=1, source_target_pairs={{0,2},{1,3},{2,0},{3,1},{4,6},{5,7},{6,4},{7,5},{8,10},{9,11},{10,... | collective-permute-start | bytes 786440 | tf_op jit(solution)/shard_map/ppermute | solution.py:870
  244.1 49.3 %collective-permute-start.11 = (bf16[512,256]{1,0:T(8,128)(2,1)}, bf16[512,256]{1,0:T(8,128)(2,1)S(1)}, u32[]{:S(2)}, u32[]{:S(2)}) collective-permute-start(bf16[512,256]{1,0:T(8,128)(2,1)} %get-tuple-element.120), channel_id=1, source_target_pairs={{0,3},{1,2},{2,1},{3,0},{4,7},{5,6},{6,5},{7,4},{8,11},{9,10},{10,... | collective-permute-start | bytes 786440 | tf_op jit(solution)/shard_map/ppermute | solution.py:870
  245.5 48.0 %collective-permute-start.9 = (bf16[512,256]{1,0:T(8,128)(2,1)}, bf16[512,256]{1,0:T(8,128)(2,1)S(1)}, u32[]{:S(2)}, u32[]{:S(2)}) collective-permute-start(bf16[512,256]{1,0:T(8,128)(2,1)} %get-tuple-element.118), channel_id=1, source_target_pairs={{0,1},{1,0},{2,3},{3,2},{4,5},{5,4},{6,7},{7,6},{8,9},{9,8},{10,11... | collective-permute-start | bytes 786440 | tf_op jit(solution)/shard_map/ppermute | solution.py:870
  348.6 39.5 %collective-permute-start.14 = (bf16[512,256]{1,0:T(8,128)(2,1)S(1)}, bf16[512,256]{1,0:T(8,128)(2,1)S(1)}, u32[]{:S(2)}, u32[]{:S(2)}) collective-permute-start(bf16[512,256]{1,0:T(8,128)(2,1)S(1)} %copy-done.57), channel_id=1, source_target_pairs={{0,1},{1,0},{2,3},{3,2},{4,5},{5,4},{6,7},{7,6},{8,9},{9,8},{10,11... | collective-permute-start | bytes 786440 | tf_op jit(solution)/shard_map/ppermute | solution.py:870
  350.0 40.4 %collective-permute-start.15 = (bf16[512,256]{1,0:T(8,128)(2,1)S(1)}, bf16[512,256]{1,0:T(8,128)(2,1)}, u32[]{:S(2)}, u32[]{:S(2)}) collective-permute-start(bf16[512,256]{1,0:T(8,128)(2,1)S(1)} %copy-done.56), channel_id=1, source_target_pairs={{0,2},{1,3},{2,0},{3,1},{4,6},{5,7},{6,4},{7,5},{8,10},{9,11},{10,... | collective-permute-start | bytes 786440 | tf_op jit(solution)/shard_map/ppermute | solution.py:870
  350.6 40.9 %collective-permute-start.16 = (bf16[512,256]{1,0:T(8,128)(2,1)S(1)}, bf16[512,256]{1,0:T(8,128)(2,1)}, u32[]{:S(2)}, u32[]{:S(2)}) collective-permute-start(bf16[512,256]{1,0:T(8,128)(2,1)S(1)} %copy-done.55), channel_id=1, source_target_pairs={{0,3},{1,2},{2,1},{3,0},{4,7},{5,6},{6,5},{7,4},{8,11},{9,10},{10,... | collective-permute-start | bytes 786440 | tf_op jit(solution)/shard_map/ppermute | solution.py:870
  363.1 97.4 %collective-permute-start.19 = (bf16[512,256]{1,0:T(8,128)(2,1)}, bf16[512,256]{1,0:T(8,128)(2,1)}, u32[]{:S(2)}, u32[]{:S(2)}) collective-permute-start(bf16[512,256]{1,0:T(8,128)(2,1)} %get-tuple-element.153), channel_id=1, source_target_pairs={{0,1},{1,0},{2,3},{3,2},{4,5},{5,4},{6,7},{7,6},{8,9},{9,8},{10,11... | collective-permute-start | bytes 786440 | tf_op jit(solution)/shard_map/ppermute | solution.py:870
  364.5 96.0 %collective-permute-start.20 = (bf16[512,256]{1,0:T(8,128)(2,1)S(1)}, bf16[512,256]{1,0:T(8,128)(2,1)}, u32[]{:S(2)}, u32[]{:S(2)}) collective-permute-start(bf16[512,256]{1,0:T(8,128)(2,1)S(1)} %copy-done.54), channel_id=1, source_target_pairs={{0,2},{1,3},{2,0},{3,1},{4,6},{5,7},{6,4},{7,5},{8,10},{9,11},{10,... | collective-permute-start | bytes 786440 | tf_op jit(solution)/shard_map/ppermute | solution.py:870
  388.9 71.6 %collective-permute-start.21 = (bf16[512,256]{1,0:T(8,128)(2,1)S(1)}, bf16[512,256]{1,0:T(8,128)(2,1)}, u32[]{:S(2)}, u32[]{:S(2)}) collective-permute-start(bf16[512,256]{1,0:T(8,128)(2,1)S(1)} %copy-done.53), channel_id=1, source_target_pairs={{0,3},{1,2},{2,1},{3,0},{4,7},{5,6},{6,5},{7,4},{8,11},{9,10},{10,... | collective-permute-start | bytes 786440 | tf_op jit(solution)/shard_map/ppermute | solution.py:870
  390.4 58.0 %collective-permute-start.18 = (bf16[2,2,2,288,512]{4,3,0,1,2:T(8,128)(2,1)}, bf16[2,2,2,288,512]{4,3,0,1,2:T(8,128)(2,1)}, u32[]{:S(2)}, u32[]{:S(2)}) collective-permute-start(bf16[2,2,2,288,512]{4,3,0,1,2:T(8,128)(2,1)} %copy.163), channel_id=1, source_target_pairs={{0,2},{1,3},{2,0},{3,1},{4,6},{5,7},{6,4},{7,5},{8,10},{9,11},{10,... | collective-permute-start | bytes 7077896 | tf_op jit(solution)/shard_map/ppermute | solution.py:68
  391.6 62.1 %collective-permute-start.17 = (bf16[2,2,2,288,512]{4,3,0,1,2:T(8,128)(2,1)S(1)}, bf16[2,2,2,288,512]{4,3,0,1,2:T(8,128)(2,1)}, u32[]{:S(2)}, u32[]{:S(2)}) collective-permute-start(bf16[2,2,2,288,512]{4,3,0,1,2:T(8,128)(2,1)S(1)} %copy.161), channel_id=1, source_target_pairs={{0,1},{1,0},{2,3},{3,2},{4,5},{5,4},{6,7},{7,6},{8,9},{9,8},{10,11... | collective-permute-start | bytes 7077896 | tf_op jit(solution)/shard_map/ppermute | solution.py:68
  452.4 63.4 %collective-permute-start.23 = (bf16[2,2,288,512]{3,2,0,1:T(8,128)(2,1)S(1)}, bf16[2,2,288,512]{3,2,0,1:T(8,128)(2,1)}, u32[]{:S(2)}, u32[]{:S(2)}) collective-permute-start(bf16[2,2,288,512]{3,2,0,1:T(8,128)(2,1)S(1)} %fusion.5), channel_id=1, source_target_pairs={{0,1},{1,0},{2,3},{3,2},{4,5},{5,4},{6,7},{7,6},{8,9},{9,8},{10,11... | collective-permute-start | bytes 3538952 | tf_op jit(solution)/shard_map/ppermute | solution.py:68
  459.1 58.4 %collective-permute-start.22 = (bf16[2,2,288,512]{3,2,0,1:T(8,128)(2,1)}, bf16[2,2,288,512]{3,2,0,1:T(8,128)(2,1)}, u32[]{:S(2)}, u32[]{:S(2)}) collective-permute-start(bf16[2,2,288,512]{3,2,0,1:T(8,128)(2,1)} %fusion.4), channel_id=1, source_target_pairs={{0,2},{1,3},{2,0},{3,1},{4,6},{5,7},{6,4},{7,5},{8,10},{9,11},{10,... | collective-permute-start | bytes 3538952 | tf_op jit(solution)/shard_map/ppermute | solution.py:68
  520.9 47.9 %collective-permute-start.27 = (bf16[2,288,1024]{2,1,0:T(8,128)(2,1)}, bf16[2,288,1024]{2,1,0:T(8,128)(2,1)S(1)}, u32[]{:S(2)}, u32[]{:S(2)}) collective-permute-start(bf16[2,288,1024]{2,1,0:T(8,128)(2,1)} %fusion.6), channel_id=1, source_target_pairs={{0,8},{4,12},{8,0},{12,4},{16,24},{20,28},{24,16},{28,20},{1,9},{5... | collective-permute-start | bytes 3538952 | tf_op jit(solution)/shard_map/ppermute | solution.py:68
  522.2 35.4 %collective-permute-start.25 = (bf16[3,512,256]{2,1,0:T(8,128)(2,1)}, bf16[3,512,256]{2,1,0:T(8,128)(2,1)}, u32[]{:S(2)}, u32[]{:S(2)}) collective-permute-start(bf16[3,512,256]{2,1,0:T(8,128)(2,1)} %get-tuple-element.163), channel_id=1, source_target_pairs={{0,2},{1,3},{2,0},{3,1},{4,6},{5,7},{6,4},{7,5},{8,10},{9,11},{10,... | collective-permute-start | bytes 2359304 | tf_op jit(solution)/shard_map/ppermute | solution.py:870
  523.1 35.8 %collective-permute-start.26 = (bf16[3,512,256]{2,1,0:T(8,128)(2,1)}, bf16[3,512,256]{2,1,0:T(8,128)(2,1)}, u32[]{:S(2)}, u32[]{:S(2)}) collective-permute-start(bf16[3,512,256]{2,1,0:T(8,128)(2,1)} %get-tuple-element.164), channel_id=1, source_target_pairs={{0,3},{1,2},{2,1},{3,0},{4,7},{5,6},{6,5},{7,4},{8,11},{9,10},{10,... | collective-permute-start | bytes 2359304 | tf_op jit(solution)/shard_map/ppermute | solution.py:870
  524.4 51.0 %collective-permute-start.28 = (bf16[3,512,256]{2,1,0:T(8,128)(2,1)}, bf16[3,512,256]{2,1,0:T(8,128)(2,1)}, u32[]{:S(2)}, u32[]{:S(2)}) collective-permute-start(bf16[3,512,256]{2,1,0:T(8,128)(2,1)} %get-tuple-element.170), channel_id=1, source_target_pairs={{0,1},{1,0},{2,3},{3,2},{4,5},{5,4},{6,7},{7,6},{8,9},{9,8},{10,11... | collective-permute-start | bytes 2359304 | tf_op jit(solution)/shard_map/ppermute | solution.py:870
  541.7 49.9 %collective-permute-start.29 = (bf16[3,512,256]{2,1,0:T(8,128)(2,1)}, bf16[3,512,256]{2,1,0:T(8,128)(2,1)}, u32[]{:S(2)}, u32[]{:S(2)}) collective-permute-start(bf16[3,512,256]{2,1,0:T(8,128)(2,1)} %get-tuple-element.171), channel_id=1, source_target_pairs={{0,2},{1,3},{2,0},{3,1},{4,6},{5,7},{6,4},{7,5},{8,10},{9,11},{10,... | collective-permute-start | bytes 2359304 | tf_op jit(solution)/shard_map/ppermute | solution.py:870
  557.6 34.0 %collective-permute-start.30 = (bf16[3,512,256]{2,1,0:T(8,128)(2,1)}, bf16[3,512,256]{2,1,0:T(8,128)(2,1)}, u32[]{:S(2)}, u32[]{:S(2)}) collective-permute-start(bf16[3,512,256]{2,1,0:T(8,128)(2,1)} %get-tuple-element.172), channel_id=1, source_target_pairs={{0,3},{1,2},{2,1},{3,0},{4,7},{5,6},{6,5},{7,4},{8,11},{9,10},{10,... | collective-permute-start | bytes 2359304 | tf_op jit(solution)/shard_map/ppermute | solution.py:870
  629.9 33.1 %all-to-all-start.3 = ((f32[32,16,192]{2,1,0:T(8,128)}), f32[32,16,192]{2,1,0:T(8,128)}, u32[]{:S(2)}, u32[]{:S(2)}) async-start(f32[32,16,192]{2,1,0:T(8,128)} %bitcast.143), calls=%async_computation.3 | async-start | bytes 1048576 | tf_op jit(solution)/shard_map/all_to_all | solution.py:946
  636.5 35.8 %collective-permute-start.34 = (bf16[2,2,2,96,512]{4,3,0,1,2:T(8,128)(2,1)}, bf16[2,2,2,96,512]{4,3,0,1,2:T(8,128)(2,1)}, u32[]{:S(2)}, u32[]{:S(2)}) collective-permute-start(bf16[2,2,2,96,512]{4,3,0,1,2:T(8,128)(2,1)} %copy.175), channel_id=1, source_target_pairs={{0,2},{1,3},{2,0},{3,1},{4,6},{5,7},{6,4},{7,5},{8,10},{9,11},{10,... | collective-permute-start | bytes 2359304 | tf_op jit(solution)/shard_map/ppermute | solution.py:68
  639.1 39.5 %collective-permute-start.38 = (bf16[288,1024]{1,0:T(8,128)(2,1)}, bf16[288,1024]{1,0:T(8,128)(2,1)}, u32[]{:S(2)}, u32[]{:S(2)}) collective-permute-start(bf16[288,1024]{1,0:T(8,128)(2,1)} %fusion.13), channel_id=1, source_target_pairs={{0,16},{4,20},{8,24},{12,28},{16,0},{20,4},{24,8},{28,12},{1,17},{... | collective-permute-start | bytes 1769480 | tf_op jit(solution)/shard_map/ppermute | solution.py:68
  642.9 32.6 %collective-permute-start.32 = (bf16[2,2,2,96,512]{4,3,0,1,2:T(8,128)(2,1)S(1)}, bf16[2,2,2,96,512]{4,3,0,1,2:T(8,128)(2,1)}, u32[]{:S(2)}, u32[]{:S(2)}) collective-permute-start(bf16[2,2,2,96,512]{4,3,0,1,2:T(8,128)(2,1)S(1)} %copy.173), channel_id=1, source_target_pairs={{0,1},{1,0},{2,3},{3,2},{4,5},{5,4},{6,7},{7,6},{8,9},{9,8},{10,11... | collective-permute-start | bytes 2359304 | tf_op jit(solution)/shard_map/ppermute | solution.py:68
  (96 other events, 1114.4 us)
Sparse Core Ops, SparseCore 0:
  11.5 76.2 all-gather.4
  90.7 169.2 all-gather.2

commit v4 on v3

--- a/solution.py
+++ b/solution.py
@@ -75,28 +75,46 @@
     return lax.optimization_barrier((value, *others))[0]
 
 
-def scatter_steps(groups, name):
+def scatter_steps(groups, name, by_frame, ready):
     frame_bits = lax.axis_size("frame").bit_length() - 1
     row_bits = lax.axis_size("row").bit_length() - 1
-    row = lax.axis_index("row")
-    numbers = jnp.stack([lax.axis_index("frame") & 1, row & 1, row >> (row_bits - 1)]).astype(jnp.int32)
+    row, frame = lax.axis_index("row"), lax.axis_index("frame")
+    numbers = jnp.stack([frame & 1, row & 1, row >> (row_bits - 1), (frame >> 1) & 1]).astype(jnp.int32)
+    numbers = held(numbers, *ready)
     size = lax.axis_size("frame")
     came = []
     for at, group in enumerate(groups):
         send = send_sums(numbers, group, f"{name}_send_{at}")
         came.append(lax.ppermute(send, "frame", [(index, index ^ 1) for index in range(size)]))
         numbers = held(numbers, send)
-    keep, send = keep_sums(numbers, groups, came, name + "_keep")
+    keep, send = keep_sums(numbers, groups, came, name + "_keep", by_frame)
+    hold = yield send
     names = [("frame", bit) for bit in reversed(range(1, frame_bits))]
     names += [("row", bit) for bit in reversed(range(row_bits))]
+    rest = [("frame", bit) for bit in range(1, frame_bits)]
     side_names = []
-    for side in range(2):
-        bit = 0 if side == 0 else row_bits - 1
-        side_names.append([item for item in names if item != ("row", bit)])
-        shape = (2,) * (len(names) - 1) + keep[side].shape[2:]
-        keep[side] = keep[side].reshape(shape)
-        send[side] = send[side].reshape(shape)
-    hold = yield send
+    if by_frame:
+        names.remove(("frame", 1))
+        rest.remove(("frame", 1))
+        value = joined(held(keep[0], *hold), send[0], "frame", 1)
+        value = value.reshape((2,) * len(names) + value.shape[2:])
+        width = value.shape[-1] // 2
+        keep, send = [], []
+        for side in range(2):
+            bit = 0 if side == 0 else row_bits - 1
+            side_names.append([item for item in names if item != ("row", bit)])
+            part = value[..., side * width : (side + 1) * width]
+            kept, sent = halves(part, names.index(("row", bit)), "row", bit)
+            keep.append(kept)
+            send.append(sent)
+        hold = yield send
+    else:
+        for side in range(2):
+            bit = 0 if side == 0 else row_bits - 1
+            side_names.append([item for item in names if item != ("row", bit)])
+            shape = (2,) * (len(names) - 1) + keep[side].shape[2:]
+            keep[side] = keep[side].reshape(shape)
+            send[side] = send[side].reshape(shape)
     for step in range(row_bits):
         parts = []
         for side in range(2):
@@ -111,13 +129,13 @@
             keep[side], send[side] = halves(parts[side], dim, "row", bit)
         hold = yield send
     value = jnp.concatenate(parts, axis=-1)
-    names = names[: frame_bits - 1]
-    for bit in range(1, frame_bits):
-        dim = names.index(("frame", bit))
+    names = [item for item in names if item[0] == "frame"]
+    for item in rest:
+        dim = names.index(item)
         names.pop(dim)
-        keep, send = halves(value, dim, "frame", bit)
+        keep, send = halves(value, dim, *item)
         hold = yield [send]
-        value = joined(held(keep, *hold), send, "frame", bit)
+        value = joined(held(keep, *hold), send, *item)
     yield value
 
 
@@ -193,22 +211,25 @@
             rows = pl.ds(pl.multiple_of(part * D + peer * group, group), group)
             value = dot_nt(hidden, w_ref[rows, :])
             if part == 2:
-                out_refs[slot][part] = value.astype(jnp.bfloat16)
+                for pair in range(group // 128):
+                    out_refs[pair * slots + slot][part] = value[:, pair * 128 : (pair + 1) * 128].astype(
+                        jnp.bfloat16
+                    )
                 continue
-            for first in range(0, group, 128):
-                piece = turned(value[:, first : first + 128], cosine, sine)
+            for pair in range(group // 128):
+                piece = turned(value[:, pair * 128 : (pair + 1) * 128], cosine, sine)
                 if part == 0:
                     piece = piece * (1.0 / math.sqrt(HD))
-                out_refs[slot][part, :, first : first + 128] = piece.astype(jnp.bfloat16)
+                out_refs[pair * slots + slot][part] = piece.astype(jnp.bfloat16)
 
 
 def project(me, clip, tokens, mod, cosine, sine, w_qkv, slots):
-    count, tall_rows, _ = tokens.shape
+    _, tall_rows, _ = tokens.shape
     tile = 256
     steps = tall_rows // tile
-    group = D // slots
     out_shape = [jax.ShapeDtypeStruct((1, tall_rows, D), jnp.bfloat16)]
-    out_shape += [jax.ShapeDtypeStruct((3, tall_rows, group), jnp.bfloat16)] * slots
+    count = D // 128
+    out_shape += [jax.ShapeDtypeStruct((3, tall_rows, 128), jnp.bfloat16)] * count
     return pl.pallas_call(
         functools.partial(project_kernel, slots),
         grid=(steps,),
@@ -221,7 +242,7 @@
             whole_spec(w_qkv),
         ],
         out_specs=[pl.BlockSpec((1, tile, D), lambda i: (0, i, 0))]
-        + [pl.BlockSpec((3, tile, group), lambda i: (0, i, 0))] * slots,
+        + [pl.BlockSpec((3, tile, 128), lambda i: (0, i, 0))] * count,
         out_shape=out_shape,
         compiler_params=vmem_params(60),
         cost_estimate=pl.CostEstimate(
@@ -384,8 +405,10 @@
 
 
 def middle_kernel(slots, me_ref, x_ref, cot_ref, mod_ref, wo_ref, wu_ref, wd_ref, *refs):
-    att_refs = refs[:slots]
-    datt_refs = refs[slots : 2 * slots]
+    count = D // 128
+    pairs = count // slots
+    att_refs = refs[:count]
+    datt_refs = refs[count : 2 * count]
     (
         out_ref,
         att_ref,
@@ -397,7 +420,7 @@
         dmid_ref,
         sums_ref,
         slope,
-    ) = refs[2 * slots :]
+    ) = refs[2 * count :]
     frames = mod_ref.shape[1]
     rows = x_ref.shape[1]
     group = D // slots
@@ -415,7 +438,7 @@
     branch = jnp.zeros((rows, D), jnp.float32)
     for slot in range(slots):
         at = pl.ds(pl.multiple_of((me ^ slot) * group, group), group)
-        piece = att_refs[slot][...]
+        piece = jnp.concatenate([att_refs[pair * slots + slot][...] for pair in range(pairs)], axis=1)
         att_ref[:, at] = piece
         branch += dot_low(piece, part_of(wo_ref, me ^ slot, group))
     middle = x_ref[0].astype(jnp.float32) + spread(branch, 2)
@@ -459,15 +482,16 @@
     d_branch = spread(d_middle, 2).astype(jnp.bfloat16)
     db1_ref[...] = d_branch
     for slot in range(slots):
-        datt_refs[slot][...] = dot_nt(d_branch, part_of(wo_ref, me ^ slot, group)).astype(jnp.bfloat16)
-
-
-def middle(me, clip, tokens, cotangent, mod, w_out, w_up, w_down, attended):
-    slots = len(attended)
-    count, length, _ = tokens.shape
+        value = dot_nt(d_branch, part_of(wo_ref, me ^ slot, group)).astype(jnp.bfloat16)
+        for pair in range(pairs):
+            datt_refs[pair * slots + slot][...] = value[:, pair * 128 : (pair + 1) * 128]
+
+
+def middle(me, clip, tokens, cotangent, mod, w_out, w_up, w_down, attended, slots):
+    count = len(attended)
+    _, length, _ = tokens.shape
     tile = 256
     steps = length // tile
-    group = D // slots
     frames = mod.shape[1]
     low = jnp.bfloat16
 
@@ -487,12 +511,12 @@
             pl.BlockSpec((1, frames, 6 * D), lambda i: (clip * steps + i, 0, 0)),
             *(item[1] for item in (w_out, w_up, w_down)),
         ]
-        + [flat_spec(group)] * slots,
-        out_specs=[flat_spec(group)] * slots
+        + [flat_spec(128)] * count,
+        out_specs=[flat_spec(128)] * count
         + [pl.BlockSpec((1, tile, D), lambda i: (0, i, 0))]
         + [flat_spec(width) for width in (D, D, FF, D, FF, D, D)]
         + [pl.BlockSpec((1, 4, frames, D), lambda i: (i, 0, 0, 0))],
-        out_shape=[flat(group)] * slots
+        out_shape=[flat(128)] * count
         + [jax.ShapeDtypeStruct((1, length, D), low)]
         + [flat(D), flat(D), flat(FF), flat(D), flat(FF), flat(D), flat(D, jnp.float32)]
         + [jax.ShapeDtypeStruct((steps, 4, frames, D), jnp.float32)],
@@ -503,12 +527,14 @@
         ),
         name="middle",
     )(me, tokens, cotangent, mod, *(item[0] for item in (w_out, w_up, w_down)), *attended)
-    return outs[:slots], outs[slots:]
+    return outs[:count], outs[count:]
 
 
 def last_kernel(slots, me_ref, x_ref, mod_ref, cos_ref, sin_ref, w_ref, dmid_ref, *refs):
-    pieces = refs[:slots]
-    dproj_ref, grad_ref, sums_ref = refs[slots:]
+    count = D // 128
+    pairs = count // slots
+    pieces = refs[:count]
+    dproj_ref, grad_ref, sums_ref = refs[count:]
     frames = mod_ref.shape[1]
     rows = x_ref.shape[1]
     group = D // slots
@@ -521,12 +547,12 @@
         for part in range(3):
             base = pl.multiple_of(part * D + peer * group, group)
             if part == 2:
-                value = pieces[slot][part]
+                value = jnp.concatenate([pieces[pair * slots + slot][part] for pair in range(pairs)], axis=1)
             else:
                 value = jnp.concatenate(
                     [
-                        turned(pieces[slot][part, :, at : at + 128].astype(jnp.float32), cosine, sine)
-                        for at in range(0, group, 128)
+                        turned(pieces[pair * slots + slot][part].astype(jnp.float32), cosine, sine)
+                        for pair in range(pairs)
                     ],
                     axis=1,
                 ).astype(jnp.bfloat16)
@@ -544,12 +570,11 @@
     )
 
 
-def last(me, clip, tokens, mod, cosine, sine, w_qkv, d_middle, pieces):
-    slots = len(pieces)
-    count, length, _ = tokens.shape
+def last(me, clip, tokens, mod, cosine, sine, w_qkv, d_middle, pieces, slots):
+    count = len(pieces)
+    _, length, _ = tokens.shape
     tile = 256
     steps = length // tile
-    group = D // slots
     frames = mod.shape[1]
     return pl.pallas_call(
         functools.partial(last_kernel, slots),
@@ -563,7 +588,7 @@
             whole_spec(w_qkv),
             pl.BlockSpec((tile, D), lambda i: (i, 0)),
         ]
-        + [pl.BlockSpec((3, tile, group), lambda i: (0, i, 0))] * slots,
+        + [pl.BlockSpec((3, tile, 128), lambda i: (0, i, 0))] * count,
         out_specs=[
             pl.BlockSpec((tile, 3 * D), lambda i: (i, 0)),
             pl.BlockSpec((1, tile, D), lambda i: (0, i, 0)),
@@ -636,6 +661,36 @@
             member += 1
 
 
+def keep_frame_kernel(doubled, counts, number_ref, *refs):
+    members = len(doubled)
+    came_refs = refs[4 * members : 4 * members + len(counts)]
+    keep_ref, send_ref = refs[-2:]
+    rows = keep_ref.shape[1]
+    kept = lax.rem(pl.program_id(0), 2) == number_ref[3]
+    first = 0
+    member = 0
+    for came_ref, count in zip(came_refs, counts):
+        inside = 0
+        for _ in range(count):
+            value = member_value(refs, member, doubled[member], number_ref[0])
+            height = value.shape[0] // rows
+            value = value.reshape(rows, height, D)
+            value += came_ref[0, :, inside : inside + height, :].astype(jnp.float32)
+            at = slice(first, first + height)
+
+            @pl.when(kept)
+            def _(value=value, at=at):
+                keep_ref[0, :, at, :] = value
+
+            @pl.when(jnp.logical_not(kept))
+            def _(value=value, at=at):
+                send_ref[0, :, at, :] = value.astype(jnp.bfloat16)
+
+            first += height
+            inside += height
+            member += 1
+
+
 def weight_specs(pairs, other):
     frame_devices = lax.axis_size("frame")
     specs, operands, doubled = [], [], []
@@ -675,164 +730,229 @@
     )(numbers, *operands)
 
 
-def keep_sums(numbers, groups, came, name):
+def keep_sums(numbers, groups, came, name, by_frame):
     pairs = [pair for group in groups for pair in group]
     specs, operands, doubled, height, flops = weight_specs(pairs, False)
     frames, rows = lax.axis_size("frame") // 2, lax.axis_size("row")
     specs += [pl.BlockSpec((1,) + item.shape[1:], lambda i, s: (i, 0, 0, 0)) for item in came]
-    shape = (frames, rows // 2, height, D // 2)
-    out_spec = pl.BlockSpec((1,) + shape[1:], lambda i, s: (i, 0, 0, 0))
+    if by_frame:
+        kernel = keep_frame_kernel
+        shape = (frames // 2, rows, height, D)
+        out_spec = pl.BlockSpec((1,) + shape[1:], lambda i, s: (i // 2, 0, 0, 0))
+    else:
+        kernel = keep_kernel
+        shape = (frames, rows // 2, height, D // 2)
+        out_spec = pl.BlockSpec((1,) + shape[1:], lambda i, s: (i, 0, 0, 0))
+    each = 1 if by_frame else 2
     outs = pl.pallas_call(
-        functools.partial(keep_kernel, doubled, tuple(len(group) for group in groups)),
+        functools.partial(kernel, doubled, tuple(len(group) for group in groups)),
         grid_spec=pltpu.PrefetchScalarGridSpec(
-            num_scalar_prefetch=1, grid=(frames,), in_specs=specs, out_specs=[out_spec] * 4
+            num_scalar_prefetch=1, grid=(frames,), in_specs=specs, out_specs=[out_spec] * (2 * each)
         ),
-        out_shape=[jax.ShapeDtypeStruct(shape, jnp.float32)] * 2
-        + [jax.ShapeDtypeStruct(shape, jnp.bfloat16)] * 2,
+        out_shape=[jax.ShapeDtypeStruct(shape, jnp.float32)] * each
+        + [jax.ShapeDtypeStruct(shape, jnp.bfloat16)] * each,
         compiler_params=vmem_params(60),
         cost_estimate=pl.CostEstimate(flops=flops, bytes_accessed=40 * MIB, transcendentals=0),
         name=name,
     )(numbers, *operands, *came)
-    return list(outs[:2]), list(outs[2:])
-
-
-def newton_kernel(rows, *refs):
-    all_refs, mine_ref, out_ref = refs[:-11], refs[-11], refs[-10]
-    a_ref, ah, al, nh, th, tl, qh, ql, num_ref = refs[-9:]
+    return list(outs[:each]), list(outs[each:])
+
+
+def newton_kernel(rows, unroll, pieces, scale_ref, *refs):
+    g_refs, m_refs, out_ref = refs[:pieces], refs[pieces : 2 * pieces], refs[2 * pieces]
+    x_ref, a_ref, t_ref, q_ref, eye_ref, ah, al, nh, th, tl, qh, ql, num_ref = refs[2 * pieces + 1 :]
     width = a_ref.shape[0]
     steps = width // rows
-    deep = min(1024, all_refs[0].shape[0])
-    a_at, m_at, t_at = 0, 1, 2
+    deep = g_refs[0].shape[0]
+    a_at, m_at, t_at, shift_at, sum_at = 0, 1, 2, 3, 8
 
     def block(index):
         return pl.ds(pl.multiple_of(index * rows, rows), rows)
-
-    def on_diagonal(index):
-        row_at = lax.broadcasted_iota(jnp.int32, (rows, width), 0) + index * rows
-        return row_at == lax.broadcasted_iota(jnp.int32, (rows, width), 1)
 
     def each(make):
         def one(index, carry):
             make(index)
             return carry
 
-        lax.fori_loop(0, steps, one, 0)
-
-    def put(index, value, base, number_at, high, low=None):
-        diagonal = on_diagonal(index)
-
-        @pl.when(index == 0)
-        def _():
-            num_ref[3] = jnp.sum(jnp.where(diagonal, value, 0.0)) * (1.0 / rows)
-            num_ref[4 + number_at] = base + num_ref[3]
-
-        rest = value - jnp.where(diagonal, num_ref[3], 0.0)
-        first, second = split_two(rest)
-        high[block(index), :] = first
-        if low is not None:
-            low[block(index), :] = second
-
-    def commit(number_at):
-        num_ref[number_at] = num_ref[4 + number_at]
-
-    def wide(high, low, at):
-        return high[at, :].astype(jnp.float32) + low[at, :].astype(jnp.float32)
-
+        lax.fori_loop(0, steps, one, 0, unroll=unroll)
+
+    def mean():
+        total = num_ref[sum_at]
+        for index in range(1, steps):
+            total += num_ref[sum_at + index]
+        return total * (1.0 / width)
+
+    for piece in range(pieces):
+
+        def mix(index, carry, piece=piece):
+            at = pl.ds(pl.multiple_of(index * 128, 128), 128)
+            to = pl.ds(pl.multiple_of(piece * deep + index * 128, 128), 128)
+            value = scale_ref[0] * g_refs[piece][at, :].astype(jnp.float32)
+            value += scale_ref[1] * m_refs[piece][at, :].astype(jnp.float32)
+            x_ref[to, :] = value.astype(jnp.bfloat16)
+            return carry
+
+        lax.fori_loop(0, deep // 128, mix, 0)
+    eye_ref[...] = jnp.where(
+        lax.broadcasted_iota(jnp.int32, (rows, rows), 0) == lax.broadcasted_iota(jnp.int32, (rows, rows), 1),
+        1.0,
+        0.0,
+    )
     squares = 0.0
     for index in range(steps):
         columns = slice(index * rows, (index + 1) * rows)
-        value = jnp.zeros((rows, width), jnp.float32)
-        for ref in all_refs:
-
-            def part(k, total, ref=ref, columns=columns):
-                at = pl.ds(pl.multiple_of(k * deep, deep), deep)
-                return total + dot_tn(ref[at, columns], ref[at, :])
-
-            value = lax.fori_loop(0, ref.shape[0] // deep, part, value)
-        a_ref[columns, :] = value
-        squares += jnp.sum(jnp.where(on_diagonal(index), value, 0.0))
-    squares = jnp.full((1, 1), squares, jnp.float32)
-    inverse = 1.0 / (jnp.sqrt(squares) + 1e-07)
-    each(lambda index: put(index, a_ref[block(index), :] * inverse * inverse, 0.0, a_at, ah, al))
-    commit(a_at)
+        value = dot_tn(x_ref[:, columns], x_ref[:, index * rows :])
+        t_ref[columns, index * rows :] = value
+        for other in range(index + 1, steps):
+            there = slice(other * rows, (other + 1) * rows)
+            t_ref[there, columns] = t_ref[columns, there].T
+        squares += jnp.sum(value[:, :rows] * eye_ref[...])
+    inverse = 1.0 / (jnp.sqrt(jnp.full((1, 1), squares, jnp.float32)) + 1e-07)
+    scale = jnp.sum(inverse)
+    scale = scale * scale
+    num_ref[a_at] = squares * scale * (1.0 / width)
+
+    def chunks(index):
+        for chunk in range(steps):
+            yield chunk, slice(chunk * rows, (chunk + 1) * rows), jnp.where(index == chunk, 1.0, 0.0)
+
+    def first_split(index):
+        at = block(index)
+        total = 0.0
+        for _, cut, here in chunks(index):
+            value = t_ref[at, cut] * scale - (here * num_ref[a_at]) * eye_ref[...]
+            a_ref[at, cut] = value
+            ah[at, cut], al[at, cut] = split_two(value)
+            total += jnp.sum(value * value)
+        num_ref[sum_at + index] = total
+
+    each(first_split)
 
     for number in range(5):
         two = number < 2
+        shift = num_ref[a_at]
+        fix = newton_three * mean()
+        num_ref[m_at] = newton_one + newton_two * shift + newton_three * shift * shift + fix
+        slope = newton_two + 2.0 * newton_three * shift
 
         def make_n(index):
             at = block(index)
-            shift = num_ref[a_at]
-            value = newton_three * dot_low(ah[at, :], ah[...])
-            value += (newton_two + 2.0 * newton_three * shift) * wide(ah, al, at)
-            base = newton_one + newton_two * shift + newton_three * shift * shift
-            put(index, value, base, m_at, nh)
+            total = 0.0
+            for _, cut, here in chunks(index):
+                value = newton_three * dot_low(ah[at, :], ah[:, cut])
+                value += slope * a_ref[at, cut] - (here * fix) * eye_ref[...]
+                nh[at, cut] = value.astype(jnp.bfloat16)
+                total += jnp.sum(value * a_ref[at, cut])
+            num_ref[sum_at + index] = total
 
         each(make_n)
-        commit(m_at)
+        much = num_ref[m_at]
+        keep_low = number < 4 and number >= 2
         if number == 0:
 
             def first_q(index):
                 at = block(index)
-                value = nh[at, :].astype(jnp.float32) + jnp.where(on_diagonal(index), num_ref[m_at], 0.0)
-                qh[at, :], ql[at, :] = split_two(value)
+                for _, cut, here in chunks(index):
+                    value = nh[at, cut].astype(jnp.float32) + (here * much) * eye_ref[...]
+                    q_ref[at, cut] = value
+                    qh[at, cut] = value.astype(jnp.bfloat16)
 
             each(first_q)
         else:
 
             def next_q(index):
                 at = block(index)
-                value = num_ref[m_at] * wide(qh, ql, at) + dot_low(qh[at, :], nh[...])
-                if number >= 3:
-                    value += dot_low(ql[at, :], nh[...])
-                qh[at, :], ql[at, :] = split_two(value)
+                high = qh[at, :]
+                rest = ql[at, :] if number >= 3 else None
+                for _, cut, _ in chunks(index):
+                    value = much * q_ref[at, cut] + dot_low(high, nh[:, cut])
+                    if number >= 3:
+                        value += dot_low(rest, nh[:, cut])
+                    t_ref[at, cut] = value
+                for _, cut, _ in chunks(index):
+                    value = t_ref[at, cut]
+                    first, second = split_two(value)
+                    qh[at, cut] = first
+                    if number >= 2:
+                        ql[at, cut] = second
+                    if number < 4:
+                        q_ref[at, cut] = value
 
             each(next_q)
         if number == 4:
             break
+        fix_t = mean()
+        num_ref[t_at] = shift * much + fix_t
 
         def make_t(index):
             at = block(index)
-            shift, much = num_ref[a_at], num_ref[m_at]
-            value = dot_low(ah[at, :], nh[...])
-            if two:
-                value += dot_low(al[at, :], nh[...])
-            value += shift * nh[at, :].astype(jnp.float32) + much * wide(ah, al, at)
-            put(index, value, shift * much, t_at, th, tl)
+            total = 0.0
+            for _, cut, here in chunks(index):
+                value = dot_low(ah[at, :], nh[:, cut])
+                if two:
+                    value += dot_low(al[at, :], nh[:, cut])
+                near = nh[at, cut].astype(jnp.float32)
+                value += shift * near + much * a_ref[at, cut] - (here * fix_t) * eye_ref[...]
+                t_ref[at, cut] = value
+                if two:
+                    th[at, cut], tl[at, cut] = split_two(value)
+                else:
+                    th[at, cut] = value.astype(jnp.bfloat16)
+                total += jnp.sum(value * near)
+            num_ref[sum_at + index] = total
 
         each(make_t)
-        commit(t_at)
+        fix_a = mean()
+        t_shift = num_ref[t_at]
+        num_ref[a_at] = t_shift * much + fix_a
 
         def make_a(index):
             at = block(index)
-            shift, much = num_ref[t_at], num_ref[m_at]
-            value = dot_low(nh[at, :], th[...])
-            if two:
-                value += dot_low(nh[at, :], tl[...])
-            value += shift * nh[at, :].astype(jnp.float32) + much * wide(th, tl, at)
-            put(index, value, shift * much, a_at, ah, al)
+            total = 0.0
+            for _, cut, here in chunks(index):
+                value = dot_low(nh[at, :], th[:, cut])
+                if two:
+                    value += dot_low(nh[at, :], tl[:, cut])
+                near = nh[at, cut].astype(jnp.float32)
+                value += t_shift * near + much * t_ref[at, cut] - (here * fix_a) * eye_ref[...]
+                a_ref[at, cut] = value
+                if number == 0:
+                    ah[at, cut], al[at, cut] = split_two(value)
+                else:
+                    ah[at, cut] = value.astype(jnp.bfloat16)
+                total += jnp.sum(value * value)
+            num_ref[sum_at + index] = total
 
         each(make_a)
-        commit(a_at)
-
-    mine = mine_ref[...]
-    out_ref[...] = ((dot_low(mine, qh[...]) + dot_low(mine, ql[...])) * inverse).astype(out_ref.dtype)
-
-
-def newton(everything, mine, rows=256):
-    width = mine.shape[1]
+
+    half = out_ref.shape[0] // 2
+    for side in range(2):
+        mine = x_ref[side * deep : side * deep + half, :]
+        out_ref[side * half : (side + 1) * half, :] = (
+            (dot_low(mine, qh[...]) + dot_low(mine, ql[...])) * inverse
+        ).astype(out_ref.dtype)
+
+
+def newton(scales, grads, moments, mine_rows, rows=256, unroll=4):
+    width = grads[0].shape[1]
+    pieces = len(grads)
     low = pltpu.VMEM((width, width), jnp.bfloat16)
+    full = pltpu.VMEM((width, width), jnp.float32)
+    vmem = pl.BlockSpec(memory_space=pltpu.VMEM)
     return pl.pallas_call(
-        functools.partial(newton_kernel, rows),
-        out_shape=jax.ShapeDtypeStruct(mine.shape, jnp.bfloat16),
-        in_specs=[pl.BlockSpec(memory_space=pltpu.VMEM)] * (len(everything) + 1),
-        out_specs=pl.BlockSpec(memory_space=pltpu.VMEM),
-        scratch_shapes=[pltpu.VMEM((width, width), jnp.float32)]
+        functools.partial(newton_kernel, rows, unroll, pieces),
+        out_shape=jax.ShapeDtypeStruct((mine_rows, width), jnp.bfloat16),
+        in_specs=[pl.BlockSpec(memory_space=pltpu.SMEM)] + [vmem] * (2 * pieces),
+        out_specs=vmem,
+        scratch_shapes=[pltpu.VMEM((pieces * grads[0].shape[0], width), jnp.bfloat16)]
+        + [full] * 3
+        + [pltpu.VMEM((rows, rows), jnp.float32)]
         + [low] * 7
-        + [pltpu.SMEM((8,), jnp.float32)],
-        compiler_params=pltpu.CompilerParams(vmem_limit_bytes=60 * 1024 * 1024),
-        cost_estimate=pl.CostEstimate(flops=60 * 10**9, bytes_accessed=12 * 10**6, transcendentals=0),
+        + [pltpu.SMEM((16,), jnp.float32)],
+        compiler_params=vmem_params(60),
+        cost_estimate=pl.CostEstimate(flops=60 * 10**9, bytes_accessed=20 * 10**6, transcendentals=0),
         name="newton",
-    )(*everything, mine)
+    )(scales, *grads, *moments)
 
 
 def frame_sums_kernel(count, *refs):
@@ -869,6 +989,43 @@
     for slot in range(1, size):
         out.append(lax.ppermute(slots[slot], "row", [(index, index ^ slot) for index in range(size)]))
     return out
+
+
+def frame_swap(slots):
+    size = lax.axis_size("frame")
+    out = [slots[0]]
+    for slot in range(1, size // 2):
+        pairs = [(index, index ^ (2 * slot)) for index in range(size)]
+        out.append(lax.ppermute(slots[slot], "frame", pairs))
+    return out
+
+
+def plane_steps(members):
+    size = lax.axis_size("row")
+    row_bits = size.bit_length() - 1
+    groups = lax.axis_size("frame") // 2
+    group_index = lax.axis_index("frame") >> 1
+    height = max(item.shape[0] for item in members)
+    slab = jnp.stack([jnp.pad(item, ((0, height - item.shape[0]), (0, 0))) for item in members])
+    slots = [
+        lax.dynamic_index_in_dim(slab, (group_index ^ slot) & 3, 0, keepdims=False) for slot in range(groups)
+    ]
+    hold = yield slots
+    slots = frame_swap(slots)
+    slots[0] = held(slots[0], *hold)
+    mine = jnp.concatenate(slots, axis=0)
+    cut = mine.shape[0] // 2
+    grown = [mine[:cut], mine[cut:]]
+    for step in range(row_bits):
+        hold = yield grown
+        for side in range(2):
+            bit = step if side == 0 else row_bits - 1 - step
+            pairs = [(index, index ^ (1 << bit)) for index in range(size)]
+            came = lax.ppermute(grown[side], "row", pairs)
+            grown[side] = jnp.concatenate([held(grown[side], *hold), came], axis=0)
+    frame_size = lax.axis_size("frame")
+    pairs = [(index, index ^ 1) for index in range(frame_size)]
+    yield (*grown, *(lax.ppermute(item, "frame", pairs) for item in grown))
 
 
 def per_device(
@@ -983,54 +1140,81 @@
     tokens_flat = tokens.reshape(clip_count, seq_local, model_width)
     cotangent_flat = cotangent.reshape(clip_count, seq_local, model_width)
     clips = range(clip_count)
-    hidden_one, pieces = [], []
+    pair_count = D // 128 // row_devices
+    units = [(clip, pair) for clip in clips for pair in range(pair_count)]
+
+    def of_unit(slots, pair):
+        return slots[pair * row_devices : (pair + 1) * row_devices]
+
+    def after(value, state):
+        return [held(value[0], *state), *value[1:]]
+
+    def of_clip(by_unit, clip):
+        return [item for pair in range(pair_count) for item in by_unit[clip, pair]]
+
+    hidden_one, pieces = [], {}
     for clip in clips:
         hidden, *slots = project(me, clip, tokens_flat, mod, cosine, sine, w_qkv, row_devices)
         hidden_one.append(hidden[0])
-        pieces.append(swap(slots))
-    attended, full, logs = [], [], []
-    for clip in clips:
-        slots, full_clip, log_clip = attend(pieces[clip])
-        attended.append(swap(slots))
-        full.append(full_clip)
-        logs.append(log_clip)
-    d_attended, middles = [], []
+        for pair in range(pair_count):
+            pieces[clip, pair] = swap(of_unit(slots, pair))
+    attended, full, logs = {}, {}, {}
+    for at, unit in enumerate(units):
+        ready = list(attended[units[at - 2]][1:]) if at >= 2 else []
+        if at >= 1:
+            ready.append(slots[0])
+        slots, full[unit], logs[unit] = attend(after(pieces[unit], ready))
+        attended[unit] = swap(slots)
+    moments_tall = [
+        item.astype(low_type) for item in (qkv_momentum.T, out_momentum, up_momentum.T, down_momentum)
+    ]
+    moments_tall[0] = held(moments_tall[0], attended[units[pair_count - 1]][-1])
+    moment_steps = plane_steps(moments_tall)
+    moment_rows = next(moment_steps)
+    d_attended, middles = {}, []
     for clip in clips:
         slots, others = middle(
-            me, clip, tokens_flat, cotangent_flat, mod, w_out, w_up, w_down, attended[clip]
+            me, clip, tokens_flat, cotangent_flat, mod, w_out, w_up, w_down,
+            after(of_clip(attended, clip), moment_rows), row_devices,
         )
-        d_attended.append(swap(slots))
+        for pair in range(pair_count):
+            d_attended[clip, pair] = swap(of_unit(slots, pair))
         middles.append(others)
+        moment_rows = moment_steps.send([others[0]])
     block_out = jnp.concatenate([item[0] for item in middles], axis=0).reshape(shape_five)
     att_low, hidden_two, activated, d_branch_two, d_up, d_branch_one, d_middle, two_sums = (
         [item[index] for item in middles] for index in range(1, 9)
     )
     early = scatter_steps(
-        [[(activated, d_branch_two)], [(d_up, hidden_two), (att_low, d_branch_one)]], "early"
-    )
-
-    def after(value, state):
-        return [held(value[0], *state), *value[1:]]
-
+        [[(activated, d_branch_two)], [(d_up, hidden_two), (att_low, d_branch_one)]], "early", True, moment_rows
+    )
     state = next(early)
-    d_pieces = []
-    for clip in clips:
-        slots = attend_back(pieces[clip], after(d_attended[clip], state), full[clip], logs[clip])
-        d_pieces.append(swap(slots))
-        state = early.send([slots[0]])
+    d_pieces = {}
+    while not isinstance(moment_rows, tuple):
+        moment_rows = moment_steps.send(list(state))
+    for at, unit in enumerate(units):
+        ready = list(d_pieces[units[at - 2]][1:]) if at >= 2 else list(state)
+        if at >= 1:
+            ready.append(slots[0])
+        if at == 1:
+            ready += moment_rows
+        slots = attend_back(pieces[unit], after(d_attended[unit], ready), full[unit], logs[unit])
+        d_pieces[unit] = swap(slots)
+    state = early.send([slots[0]])
     lasts = []
     for clip in clips:
         lasts.append(
             last(
                 me, clip, tokens_flat, mod, cosine, sine, w_qkv, d_middle[clip],
-                after(d_pieces[clip], state),
+                after(of_clip(d_pieces, clip), state), row_devices,
             )
         )
         state = early.send([lasts[clip][2]])
+    input_grad = jnp.concatenate([item[1] for item in lasts], axis=0).reshape(shape_five)
+    late = scatter_steps([[([item[0] for item in lasts], hidden_one)]], "late", False, [])
+    late_state = next(late)
     early_sum = finished(early, state)
-    input_grad = jnp.concatenate([item[1] for item in lasts], axis=0).reshape(shape_five)
-    late = scatter_steps([[([item[0] for item in lasts], hidden_one)]], "late")
-    state = next(late)
+    state = late_state
     one_sums = [item[2] for item in lasts]
     one_sums[0] = held(one_sums[0], *state)
     d_modulation = frame_sums(one_sums, two_sums)
@@ -1065,52 +1249,25 @@
     local_total = adam_local + sum((jnp.sum(item * item) for item in muon_grads))
     norm_value = jnp.sqrt(jnp.sum(from_all(jnp.full((1, 128), local_total))[:, 0, 0]))
     clip_factor = jnp.minimum(1.0, clip_limit / (norm_value + 1e-06))
+    grad_steps = plane_steps([item.astype(low_type) for item in muon_grads])
+    grad_rows = next(grad_steps)
+    while not isinstance(grad_rows, tuple):
+        grad_rows = grad_steps.send([])
     moments_new = []
-    updates = []
-    slot_rows = max(heights)
     for member in range(4):
         clipped = clip_factor * muon_grads[member]
-        moment = momentum_decay * tall(muon_moments[member], member) + clipped
-        update = (clipped + momentum_decay * moment).astype(low_type)
-        moments_new.append(tall(moment, member))
-        updates.append(jnp.pad(update, ((0, slot_rows - heights[member]), (0, 0))))
-    slab = jnp.stack(updates)
+        moments_new.append(
+            tall(momentum_decay * tall(muon_moments[member], member) + clipped, member)
+        )
+    scales = jnp.stack(
+        [clip_factor * (1.0 + momentum_decay), jnp.full((), momentum_decay * momentum_decay, full_type)]
+    )
+    slot_rows = max(heights)
     groups = frame_devices // 2
+    ortho_rows = newton(scales, grad_rows, moment_rows, groups * slot_rows)
+    ortho_rows = ortho_rows.reshape(groups, slot_rows, model_width)
+    ortho_slots = jnp.stack(frame_swap([ortho_rows[slot] for slot in range(groups)]))
     group_index = lax.axis_index("frame") >> 1
-
-    def frame_swap(slots):
-        out = [slots[0]]
-        for slot in range(1, groups):
-            pairs = [(index, index ^ (2 * slot)) for index in range(frame_devices)]
-            out.append(lax.ppermute(slots[slot], "frame", pairs))
-        return out
-
-    mine = jnp.concatenate(
-        frame_swap(
-            [
-                lax.dynamic_index_in_dim(slab, (group_index ^ slot) & 3, 0, keepdims=False)
-                for slot in range(groups)
-            ]
-        ),
-        axis=0,
-    )
-
-    def row_partner(value, bit):
-        return lax.ppermute(value, "row", [(index, index ^ (1 << bit)) for index in range(row_devices)])
-
-    row_bits = row_devices.bit_length() - 1
-    cut = mine.shape[0] // 2
-    grown = [mine[:cut], mine[cut:]]
-    for step in range(row_bits):
-        grown = [
-            jnp.concatenate([grown[0], row_partner(grown[0], step)], axis=0),
-            jnp.concatenate([grown[1], row_partner(grown[1], row_bits - 1 - step)], axis=0),
-        ]
-    others = [
-        lax.ppermute(item, "frame", [(index, index ^ 1) for index in range(frame_devices)]) for item in grown
-    ]
-    ortho_rows = newton([*grown, *others], mine).reshape(groups, slot_rows, model_width)
-    ortho_slots = jnp.stack(frame_swap([ortho_rows[slot] for slot in range(groups)]))
     ortho_mine = [
         lax.dynamic_index_in_dim(ortho_slots, (group_index & 3) ^ member, 0, keepdims=False)
         for member in range(4)

time: 972 us -> 994 us (1.023)
  starting transfers between devices: 86.6 us -> 122 us
  waiting for transfers between devices: 289 us -> 273 us
    ppermute x12, waiting for transfers between devices: 27.1 us -> 58 us  [joined(): lax.ppermute(send, axis, [(index, index ^ 1 << bit) for index in range(si...]
    ppermute x24 -> x48, starting transfers between devices: 26.7 us -> 56.6 us  [swap(): lax.ppermute(slots[slot], 'row', [(index, index ^ slot) for index in rang...]
    ppermute x24 -> x48, waiting for transfers between devices: 101 us -> 78.7 us  [swap(): lax.ppermute(slots[slot], 'row', [(index, index ^ slot) for index in rang...]
    pallas_call x3, Pallas kernels: 130 us -> 108 us  [the longest x1 76.6 us: newton(): pl.pallas_call(functools.partial(newton_kernel, rows, unroll, pieces), ou...]
    pallas_call x2 -> x4, Pallas kernels: 64.3 us -> 80.8 us  [attend(): pl.pallas_call(functools.partial(attend_kernel, slots, 256), grid=(group...]
    all_gather x1, waiting for transfers between devices: 14 us -> 0.02 us  [per_device(): gathered = lax.all_gather(shards, both, axis=0)]
    all_to_all x6, waiting for transfers between devices: 55.6 us -> 44.6 us  [to_all(): return lax.all_to_all(value, both, split_axis=0, concat_axis=0, tiled=True)]
    pallas_call x2 -> x4, Pallas kernels: 104 us -> 110 us  [attend_back(): pl.pallas_call(functools.partial(attend_back_kernel, slots, 512), grid=(g...]
  transfers between devices with their start and end apart: 59 -> 92, of which waited for: 29 -> 35; matrix products, arithmetic and copies ran while one was open for 7% -> 7% of each run, Pallas kernels for 26% -> 32%
where the time goes in v4:
time: 994 us; the launch traced here: 989 us
  Pallas kernels  435 us (44%)
  waiting for transfers between devices  273 us (27%)
  starting transfers between devices  122 us (12%)
  local copies, waits for them, and re-layouts  54.1 us (5%)
  other arithmetic  47.9 us (5%)
  blocking collectives  28.8 us (3%)
  between operations  23.8 us (2%)
    pallas_call x4, Pallas kernels, attend_back(): pl.pallas_call(functools.partial(attend_back_kernel, slots, 512), grid=(g...  110 us
    pallas_call x4, Pallas kernels, attend(): pl.pallas_call(functools.partial(attend_kernel, slots, 256), grid=(group...  80.8 us
    ppermute x48, waiting for transfers between devices, swap(): lax.ppermute(slots[slot], 'row', [(index, index ^ slot) for index in rang...  78.7 us
    pallas_call x1, Pallas kernels, newton(): pl.pallas_call(functools.partial(newton_kernel, rows, unroll, pieces), ou...  76.6 us
    pallas_call x2, Pallas kernels, middle(): pl.pallas_call(functools.partial(middle_kernel, slots), grid=(steps,), in...  66.8 us
    ppermute x12, waiting for transfers between devices, joined(): lax.ppermute(send, axis, [(index, index ^ 1 << bit) for index in range(si...  58 us
    ppermute x48, starting transfers between devices, swap(): lax.ppermute(slots[slot], 'row', [(index, index ^ slot) for index in rang...  56.6 us
    ppermute x9, waiting for transfers between devices, frame_swap(): out.append(lax.ppermute(slots[slot], 'frame', pairs))  47.5 us
  transfers between devices with their start and end apart: 92, of which 35 were waited for; matrix products, arithmetic and copies ran while one was open for 7% of the time, Pallas kernels for 32%

profile of v4, /device:TPU:8, one launch (start us, length us, event | category | flops | bytes accessed | tf_op | source)
XLA Modules:
  0.0 989.3 jit_solution(18296906854330134286)
XLA Ops:
  24.0 20.4 %all_to_all.35 = f32[32,4,1024]{2,1,0:T(4,128)S(1)} all-to-all(f32[32,4,1024]{2,1,0:T(4,128)S(1)} %reshape.246), channel_id=1, replica_groups=mesh['frame'=8,'row'=4] {'frame','row'}, dimensions={0} | all-to-all | bytes 1048576 | tf_op jit(solution)/shard_map/all_to_all | solution.py:1103
  50.6 15.6 %all-to-all-done.1 = f32[32,4,1024]{2,1,0:T(4,128)S(1)} async-done(((f32[32,4,1024]{2,1,0:T(4,128)}), f32[32,4,1024]{2,1,0:T(4,128)S(1)}, u32[]{:S(2)}, u32[]{:S(2)}) %all-to-all-start.1) | async-done | bytes 524320 | tf_op jit(solution)/shard_map/all_to_all | solution.py:1103
  76.2 18.6 %all-to-all-done.2 = f32[32,16,192]{2,1,0:T(8,128)S(1)} async-done(((f32[32,16,192]{2,1,0:T(8,128)}), f32[32,16,192]{2,1,0:T(8,128)S(1)}, u32[]{:S(2)}, u32[]{:S(2)}) %all-to-all-start.2) | async-done | bytes 393248 | tf_op jit(solution)/shard_map/all_to_all | solution.py:1103
  96.2 9.1 project.2
  110.8 10.6 %collective-permute-done.refs_1_ = bf16[3,512,128]{2,1,0:T(8,128)(2,1)S(1)} collective-permute-done((bf16[3,512,128]{2,1,0:T(8,128)(2,1)}, bf16[3,512,128]{2,1,0:T(8,128)(2,1)S(1)}, u32[]{:S(2)}, u32[]{:S(2)}) %collective-permute-start) | collective-permute-done | bytes 393248 | tf_op jit(solution)/shard_map/ppermute | solution.py:990
  130.7 17.6 %attend.4 = (bf16[512,128]{1,0:T(8,128)(2,1)}, bf16[512,128]{1,0:T(8,128)(2,1)}, bf16[512,128]{1,0:T(8,128)(2,1)}, bf16[512,128]{1,0:T(8,128)(2,1)}, f32[2048,128]{1,0:T(8,128)}, /*index=5*/f32[2048,128]{1,0:T(8,128)}) custom-call(bf16[3,512,128]{2,1,0:T(8,128)(2,1)} %get-tuple-element.151.refs_0_, bf16[3,512,128]{2,1,0:T(8,128)(2,1)} %copy-done.72, ...), custom_call_target="tpu_custom_call" | custom-call | flops 8589934592 | bytes 8388608 | tf_op jit(solution)/shard_map/attend/pallas_call | solution.py:298
  150.0 9.1 project.3
  166.2 28.8 %attend.5 = (bf16[512,128]{1,0:T(8,128)(2,1)}, bf16[512,128]{1,0:T(8,128)(2,1)}, bf16[512,128]{1,0:T(8,128)(2,1)}, bf16[512,128]{1,0:T(8,128)(2,1)}, f32[2048,128]{1,0:T(8,128)}, /*index=5*/f32[2048,128]{1,0:T(8,128)}) custom-call(bf16[3,512,128]{2,1,0:T(8,128)(2,1)} %get-tuple-element.157.refs_0_, bf16[3,512,128]{2,1,0:T(8,128)(2,1)} %copy-done.73, ...), custom_call_target="tpu_custom_call" | custom-call | flops 8589934592 | bytes 8388608 | tf_op jit(solution)/shard_map/attend/pallas_call | solution.py:298
  201.7 17.2 %attend.6 = (bf16[512,128]{1,0:T(8,128)(2,1)}, bf16[512,128]{1,0:T(8,128)(2,1)}, bf16[512,128]{1,0:T(8,128)(2,1)}, bf16[512,128]{1,0:T(8,128)(2,1)}, f32[2048,128]{1,0:T(8,128)}, /*index=5*/f32[2048,128]{1,0:T(8,128)}) custom-call(bf16[3,512,128]{2,1,0:T(8,128)(2,1)} %get-tuple-element.172.refs_0_, bf16[3,512,128]{2,1,0:T(8,128)(2,1)} %copy-done.67, ...), custom_call_target="tpu_custom_call" | custom-call | flops 8589934592 | bytes 8388608 | tf_op jit(solution)/shard_map/attend/pallas_call | solution.py:298
  231.1 11.4 %collective-permute-done.23.refs_3_ = bf16[3,512,128]{2,1,0:T(8,128)(2,1)S(1)} collective-permute-done((bf16[3,512,128]{2,1,0:T(8,128)(2,1)S(1)}, bf16[3,512,128]{2,1,0:T(8,128)(2,1)S(1)}, u32[]{:S(2)}, u32[]{:S(2)}) %collective-permute-start.23) | collective-permute-done | bytes 393248 | tf_op jit(solution)/shard_map/ppermute | solution.py:990
  243.3 17.2 %attend.7 = (bf16[512,128]{1,0:T(8,128)(2,1)}, bf16[512,128]{1,0:T(8,128)(2,1)}, bf16[512,128]{1,0:T(8,128)(2,1)}, bf16[512,128]{1,0:T(8,128)(2,1)}, f32[2048,128]{1,0:T(8,128)}, /*index=5*/f32[2048,128]{1,0:T(8,128)}) custom-call(bf16[3,512,128]{2,1,0:T(8,128)(2,1)} %get-tuple-element.183.refs_0_, bf16[3,512,128]{2,1,0:T(8,128)(2,1)} %copy-done.70, ...), custom_call_target="tpu_custom_call" | custom-call | flops 8589934592 | bytes 8388608 | tf_op jit(solution)/shard_map/attend/pallas_call | solution.py:298
  270.7 33.3 %middle.2 = (bf16[512,128]{1,0:T(8,128)(2,1)}, bf16[512,128]{1,0:T(8,128)(2,1)}, bf16[512,128]{1,0:T(8,128)(2,1)}, bf16[512,128]{1,0:T(8,128)(2,1)}, bf16[512,12...) custom-call(s32[1]{0:T(128)} %bitcast.me_ref, ...), custom_call_target="tpu_custom_call" | custom-call | flops 19327352832 | bytes 41943040 | tf_op jit(solution)/shard_map/middle/pallas_call | solution.py:504
  314.7 33.5 %middle.3 = (bf16[512,128]{1,0:T(8,128)(2,1)}, bf16[512,128]{1,0:T(8,128)(2,1)}, bf16[512,128]{1,0:T(8,128)(2,1)}, bf16[512,128]{1,0:T(8,128)(2,1)}, bf16[512,12...) custom-call(s32[1]{0:T(128)} %bitcast.me_ref, ...), custom_call_target="tpu_custom_call" | custom-call | flops 19327352832 | bytes 41943040 | tf_op jit(solution)/shard_map/middle/pallas_call | solution.py:504
  358.6 11.4 %early_send_1.1 = bf16[4,4,160,1024]{3,2,1,0:T(8,128)(2,1)} custom-call(s32[4]{0:T(128)} %pad_add_fusion.number_ref, bf16[512,4096]{1,0:T(8,128)(2,1)} %get-tuple-element.202.refs_0_.refs_4_, bf16[512,4096]{1,0:T(8,128)(2,1)} %get-tuple-element.203.refs_1_.refs_5_, bf16[512,1024]{1,0:T(8,128)(2,1)} %get-tuple-element.204.refs_2_.refs_6_, ...), custom_call_target="tpu_custom_call" | custom-call | flops 5368709120 | bytes 20971520 | tf_op jit(solution)/shard_map/early_send_1/pallas_call | solution.py:718
  374.4 10.2 %collective-permute-done.29.refs_12_ = bf16[4,4,128,1024]{3,2,1,0:T(8,128)(2,1)S(1)} collective-permute-done((bf16[4,4,128,1024]{3,2,1,0:T(8,128)(2,1)}, bf16[4,4,128,1024]{3,2,1,0:T(8,128)(2,1)S(1)}, u32[]{:S(2)}, u32[]{:S(2)}) %collective-permute-start.29) | collective-permute-done | bytes 4194336 | tf_op jit(solution)/shard_map/ppermute | solution.py:88
  388.4 22.9 %early_keep.1 = (f32[2,4,288,1024]{3,2,1,0:T(8,128)}, bf16[2,4,288,1024]{3,2,1,0:T(8,128)(2,1)}) custom-call(s32[4]{0:T(128)} %pad_add_fusion.number_ref, bf16[512,4096]{1,0:T(8,128)(2,1)} %get-tuple-element.197.refs_0_, bf16[512,4096]{1,0:T(8,128)(2,1)} %get-tuple-element.198.refs_1_, bf16[512,1024]{1,0:T(8,128)(2,1)} %get-tuple-element.199.refs_2_, ...), custom_call_target="tpu_custom_call" | custom-call | flops 9663676416 | bytes 41943040 | tf_op jit(solution)/shard_map/early_keep/pallas_call | solution.py:747
  420.0 27.5 %attend_back.4 = (bf16[3,512,128]{2,1,0:T(8,128)(2,1)}, bf16[3,512,128]{2,1,0:T(8,128)(2,1)}, bf16[3,512,128]{2,1,0:T(8,128)(2,1)}, bf16[3,512,128]{2,1,0:T(8,128)(2,1)}) custom-call(bf16[3,512,128]{2,1,0:T(8,128)(2,1)} %get-tuple-element.151.refs_0_, bf16[3,512,128]{2,1,0:T(8,128)(2,1)} %copy-done.72, bf16[3,512,128]{2,1,0:T(8,128)(2,1)} %copy-done.74, ...), custom_call_target="tpu_custom_call" | custom-call | flops 21474836480 | bytes 12582912 | tf_op jit(solution)/shard_map/attend_back/pallas_call | solution.py:385
  454.7 27.5 %attend_back.5 = (bf16[3,512,128]{2,1,0:T(8,128)(2,1)}, bf16[3,512,128]{2,1,0:T(8,128)(2,1)}, bf16[3,512,128]{2,1,0:T(8,128)(2,1)}, bf16[3,512,128]{2,1,0:T(8,128)(2,1)}) custom-call(bf16[3,512,128]{2,1,0:T(8,128)(2,1)} %get-tuple-element.157.refs_0_, bf16[3,512,128]{2,1,0:T(8,128)(2,1)} %copy-done.73, bf16[3,512,128]{2,1,0:T(8,128)(2,1)} %copy-done.75, ...), custom_call_target="tpu_custom_call" | custom-call | flops 21474836480 | bytes 12582912 | tf_op jit(solution)/shard_map/attend_back/pallas_call | solution.py:385
  487.6 10.8 %collective-permute-done.48.refs_6_ = bf16[512,128]{1,0:T(8,128)(2,1)S(1)} collective-permute-done((bf16[512,128]{1,0:T(8,128)(2,1)S(1)}, bf16[512,128]{1,0:T(8,128)(2,1)S(1)}, u32[]{:S(2)}, u32[]{:S(2)}) %collective-permute-start.48) | collective-permute-done | bytes 131104 | tf_op jit(solution)/shard_map/ppermute | solution.py:990
  503.9 27.8 %attend_back.6 = (bf16[3,512,128]{2,1,0:T(8,128)(2,1)}, bf16[3,512,128]{2,1,0:T(8,128)(2,1)}, bf16[3,512,128]{2,1,0:T(8,128)(2,1)}, bf16[3,512,128]{2,1,0:T(8,128)(2,1)}) custom-call(bf16[3,512,128]{2,1,0:T(8,128)(2,1)} %get-tuple-element.172.refs_0_, bf16[3,512,128]{2,1,0:T(8,128)(2,1)} %copy-done.67, bf16[3,512,128]{2,1,0:T(8,128)(2,1)} %copy-done.68, ...), custom_call_target="tpu_custom_call" | custom-call | flops 21474836480 | bytes 12582912 | tf_op jit(solution)/shard_map/attend_back/pallas_call | solution.py:385
  532.6 27.4 %attend_back.7 = (bf16[3,512,128]{2,1,0:T(8,128)(2,1)}, bf16[3,512,128]{2,1,0:T(8,128)(2,1)}, bf16[3,512,128]{2,1,0:T(8,128)(2,1)}, bf16[3,512,128]{2,1,0:T(8,128)(2,1)}) custom-call(bf16[3,512,128]{2,1,0:T(8,128)(2,1)} %get-tuple-element.183.refs_0_, bf16[3,512,128]{2,1,0:T(8,128)(2,1)} %copy-done.70, bf16[3,512,128]{2,1,0:T(8,128)(2,1)} %copy-done.71, ...), custom_call_target="tpu_custom_call" | custom-call | flops 21474836480 | bytes 12582912 | tf_op jit(solution)/shard_map/attend_back/pallas_call | solution.py:385
  582.1 10.1 %last.2 = (bf16[512,3072]{1,0:T(8,128)(2,1)}, f32[1,512,1024]{2,1,0:T(8,128)}, f32[2,2,4,1024]{3,2,1,0:T(4,128)}) custom-call(s32[1]{0:T(128)} %bitcast.me_ref, bf16[2,512,1024]{2,1,0:T(8,128)(2,1)} %bitcast.170, f32[4,4,6144]{2,1,0:T(4,128)} %reshape_reshape.4.mod_ref, f32[1024,128]{1,0:T(8,128)} %copy.154.cos_ref, ...), custom_call_target="tpu_custom_call" | custom-call | flops 3221225472 | bytes 20971520 | tf_op jit(solution)/shard_map/last/pallas_call | solution.py:579
  634.7 9.9 last.3
  655.4 13.1 %collective-permute-done.70 = bf16[2,288,512]{2,1,0:T(8,128)(2,1)} collective-permute-done((bf16[2,288,512]{2,1,0:T(8,128)(2,1)S(1)}, bf16[2,288,512]{2,1,0:T(8,128)(2,1)}, u32[]{:S(2)}, u32[]{:S(2)}) %collective-permute-start.70) | collective-permute-done | bytes 589856 | tf_op jit(solution)/shard_map/ppermute | solution.py:68
  694.2 9.3 collective-permute-done.71
  721.1 9.6 collective-permute-done.63
  759.1 10.5 %collective-permute-done.68 = bf16[96,1024]{1,0:T(8,128)(2,1)S(1)} collective-permute-done((bf16[96,1024]{1,0:T(8,128)(2,1)S(1)}, bf16[96,1024]{1,0:T(8,128)(2,1)S(1)}, u32[]{:S(2)}, u32[]{:S(2)}) %collective-permute-start.68) | collective-permute-done | bytes 196640 | tf_op jit(solution)/shard_map/ppermute | solution.py:68
  799.0 14.0 %collective-permute-done.75 = bf16[128,1024]{1,0:T(8,128)(2,1)S(1)} collective-permute-done((bf16[128,1024]{1,0:T(8,128)(2,1)S(1)}, bf16[128,1024]{1,0:T(8,128)(2,1)S(1)}, u32[]{:S(2)}, u32[]{:S(2)}) %collective-permute-start.75) | collective-permute-done | bytes 262176 | tf_op jit(solution)/shard_map/ppermute | solution.py:999
  821.7 12.5 %collective-permute-done.77 = bf16[256,1024]{1,0:T(8,128)(2,1)S(1)} collective-permute-done((bf16[256,1024]{1,0:T(8,128)(2,1)S(1)}, bf16[256,1024]{1,0:T(8,128)(2,1)S(1)}, u32[]{:S(2)}, u32[]{:S(2)}) %collective-permute-start.77) | collective-permute-done | bytes 524320 | tf_op jit(solution)/shard_map/ppermute | solution.py:1024
  838.5 20.1 %collective-permute-done.78 = bf16[512,1024]{1,0:T(8,128)(2,1)S(1)} collective-permute-done((bf16[512,1024]{1,0:T(8,128)(2,1)S(1)}, bf16[512,1024]{1,0:T(8,128)(2,1)S(1)}, u32[]{:S(2)}, u32[]{:S(2)}) %collective-permute-start.78) | collective-permute-done | bytes 1048608 | tf_op jit(solution)/shard_map/ppermute | solution.py:1024
  873.1 76.6 %newton.1 = bf16[512,1024]{1,0:T(8,128)(2,1)} custom-call(f32[2]{0:T(128)} %pad_maximum_fusion.12.scale_ref, bf16[1024,1024]{1,0:T(8,128)(2,1)} %pad_maximum_fusion.2.refs_0_, bf16[1024,1024]{1,0:T(8,128)(2,1)} %constant_dynamic-update-slice_fusion.12.refs_1_, bf16[1024,1024]{1,0:T(8,128)(2,1)} %collective-permute-done.79.refs_2_, ...), custom_call_target="tpu_custom_call" | custom-call | flops 60000002048 | bytes 20000000 | tf_op jit(solution)/shard_map/newton/pallas_call | solution.py:942
  964.9 12.5 %collective-permute-done.83 = bf16[128,1024]{1,0:T(8,128)(2,1)S(1)} collective-permute-done((bf16[128,1024]{1,0:T(8,128)(2,1)S(1)}, bf16[128,1024]{1,0:T(8,128)(2,1)S(1)}, u32[]{:S(2)}, u32[]{:S(2)}) %collective-permute-start.83) | collective-permute-done | bytes 262176 | tf_op jit(solution)/shard_map/ppermute | solution.py:999
  (571 shorter events, 359.4 us)
Async XLA Ops:
  7.2 89.0 %all-gather.5.cloned.1.call-start = ((), (), s32[]{:S(2)}) async-start(), calls=%async_computation.8 | async-start | bytes 6488064 | tf_op jit(solution)/shard_map/all_gather | solution.py:1068
  9.0 261.6 %all-gather.3.cloned.1.call-start = ((), (), s32[]{:S(2)}) async-start(), calls=%async_computation.7 | async-start | bytes 19464192 | tf_op jit(solution)/shard_map/all_gather | solution.py:1070
  109.7 49.9 %collective-permute-start.3 = (bf16[3,512,128]{2,1,0:T(8,128)(2,1)}, bf16[3,512,128]{2,1,0:T(8,128)(2,1)S(1)}, u32[]{:S(2)}, u32[]{:S(2)}) collective-permute-start(bf16[3,512,128]{2,1,0:T(8,128)(2,1)} %get-tuple-element.158), channel_id=1, source_target_pairs={{0,1},{1,0},{2,3},{3,2},{4,5},{5,4},{6,7},{7,6},{8,9},{9,8},{10,11... | collective-permute-start | bytes 1179656 | tf_op jit(solution)/shard_map/ppermute | solution.py:990
  109.8 50.1 %collective-permute-start.4 = (bf16[3,512,128]{2,1,0:T(8,128)(2,1)}, bf16[3,512,128]{2,1,0:T(8,128)(2,1)S(1)}, u32[]{:S(2)}, u32[]{:S(2)}) collective-permute-start(bf16[3,512,128]{2,1,0:T(8,128)(2,1)} %get-tuple-element.159), channel_id=1, source_target_pairs={{0,2},{1,3},{2,0},{3,1},{4,6},{5,7},{6,4},{7,5},{8,10},{9,11},{10,... | collective-permute-start | bytes 1179656 | tf_op jit(solution)/shard_map/ppermute | solution.py:990
  121.4 41.3 %collective-permute-start.5 = (bf16[3,512,128]{2,1,0:T(8,128)(2,1)}, bf16[3,512,128]{2,1,0:T(8,128)(2,1)}, u32[]{:S(2)}, u32[]{:S(2)}) collective-permute-start(bf16[3,512,128]{2,1,0:T(8,128)(2,1)} %get-tuple-element.160), channel_id=1, source_target_pairs={{0,3},{1,2},{2,1},{3,0},{4,7},{5,6},{6,5},{7,4},{8,11},{9,10},{10,... | collective-permute-start | bytes 1179656 | tf_op jit(solution)/shard_map/ppermute | solution.py:990
  159.1 39.0 %collective-permute-start.12 = (bf16[3,512,128]{2,1,0:T(8,128)(2,1)}, bf16[3,512,128]{2,1,0:T(8,128)(2,1)S(1)}, u32[]{:S(2)}, u32[]{:S(2)}) collective-permute-start(bf16[3,512,128]{2,1,0:T(8,128)(2,1)} %get-tuple-element.173), channel_id=1, source_target_pairs={{0,1},{1,0},{2,3},{3,2},{4,5},{5,4},{6,7},{7,6},{8,9},{9,8},{10,11... | collective-permute-start | bytes 1179656 | tf_op jit(solution)/shard_map/ppermute | solution.py:990
  159.6 39.0 %collective-permute-start.13 = (bf16[3,512,128]{2,1,0:T(8,128)(2,1)}, bf16[3,512,128]{2,1,0:T(8,128)(2,1)S(1)}, u32[]{:S(2)}, u32[]{:S(2)}) collective-permute-start(bf16[3,512,128]{2,1,0:T(8,128)(2,1)} %get-tuple-element.174), channel_id=1, source_target_pairs={{0,2},{1,3},{2,0},{3,1},{4,6},{5,7},{6,4},{7,5},{8,10},{9,11},{10,... | collective-permute-start | bytes 1179656 | tf_op jit(solution)/shard_map/ppermute | solution.py:990
  159.9 39.8 %collective-permute-start.14 = (bf16[3,512,128]{2,1,0:T(8,128)(2,1)}, bf16[3,512,128]{2,1,0:T(8,128)(2,1)S(1)}, u32[]{:S(2)}, u32[]{:S(2)}) collective-permute-start(bf16[3,512,128]{2,1,0:T(8,128)(2,1)} %get-tuple-element.175), channel_id=1, source_target_pairs={{0,3},{1,2},{2,1},{3,0},{4,7},{5,6},{6,5},{7,4},{8,11},{9,10},{10,... | collective-permute-start | bytes 1179656 | tf_op jit(solution)/shard_map/ppermute | solution.py:990
  195.0 36.1 %collective-permute-start.21 = (bf16[3,512,128]{2,1,0:T(8,128)(2,1)}, bf16[3,512,128]{2,1,0:T(8,128)(2,1)S(1)}, u32[]{:S(2)}, u32[]{:S(2)}) collective-permute-start(bf16[3,512,128]{2,1,0:T(8,128)(2,1)} %get-tuple-element.184), channel_id=1, source_target_pairs={{0,1},{1,0},{2,3},{3,2},{4,5},{5,4},{6,7},{7,6},{8,9},{9,8},{10,11... | collective-permute-start | bytes 1179656 | tf_op jit(solution)/shard_map/ppermute | solution.py:990
  195.4 35.7 %collective-permute-start.22 = (bf16[3,512,128]{2,1,0:T(8,128)(2,1)}, bf16[3,512,128]{2,1,0:T(8,128)(2,1)S(1)}, u32[]{:S(2)}, u32[]{:S(2)}) collective-permute-start(bf16[3,512,128]{2,1,0:T(8,128)(2,1)} %get-tuple-element.185), channel_id=1, source_target_pairs={{0,2},{1,3},{2,0},{3,1},{4,6},{5,7},{6,4},{7,5},{8,10},{9,11},{10,... | collective-permute-start | bytes 1179656 | tf_op jit(solution)/shard_map/ppermute | solution.py:990
  227.8 34.9 %collective-permute-start.16 = (bf16[128,1024]{1,0:T(8,128)(2,1)S(1)}, bf16[128,1024]{1,0:T(8,128)(2,1)S(1)}, u32[]{:S(2)}, u32[]{:S(2)}) collective-permute-start(bf16[128,1024]{1,0:T(8,128)(2,1)S(1)} %get-tuple-element.430), channel_id=1, source_target_pairs={{0,16},{4,20},{8,24},{12,28},{16,0},{20,4},{24,8},{28,12},{1,17},{... | collective-permute-start | bytes 786440 | tf_op jit(solution)/shard_map/ppermute | solution.py:999
  228.8 41.8 %collective-permute-start.17 = (bf16[128,1024]{1,0:T(8,128)(2,1)S(1)}, bf16[128,1024]{1,0:T(8,128)(2,1)S(1)}, u32[]{:S(2)}, u32[]{:S(2)}) collective-permute-start(bf16[128,1024]{1,0:T(8,128)(2,1)S(1)} %get-tuple-element.429), channel_id=1, source_target_pairs={{0,24},{4,28},{8,16},{12,20},{16,8},{20,12},{24,0},{28,4},{1,25},{... | collective-permute-start | bytes 786440 | tf_op jit(solution)/shard_map/ppermute | solution.py:999
  260.5 43.5 %collective-permute-start.24 = (bf16[512,128]{1,0:T(8,128)(2,1)}, bf16[512,128]{1,0:T(8,128)(2,1)S(1)}, u32[]{:S(2)}, u32[]{:S(2)}) collective-permute-start(bf16[512,128]{1,0:T(8,128)(2,1)} %get-tuple-element.188), channel_id=1, source_target_pairs={{0,1},{1,0},{2,3},{3,2},{4,5},{5,4},{6,7},{7,6},{8,9},{9,8},{10,11... | collective-permute-start | bytes 393224 | tf_op jit(solution)/shard_map/ppermute | solution.py:990
  261.1 46.4 %collective-permute-start.25 = (bf16[512,128]{1,0:T(8,128)(2,1)}, bf16[512,128]{1,0:T(8,128)(2,1)S(1)}, u32[]{:S(2)}, u32[]{:S(2)}) collective-permute-start(bf16[512,128]{1,0:T(8,128)(2,1)} %get-tuple-element.189), channel_id=1, source_target_pairs={{0,2},{1,3},{2,0},{3,1},{4,6},{5,7},{6,4},{7,5},{8,10},{9,11},{10,... | collective-permute-start | bytes 393224 | tf_op jit(solution)/shard_map/ppermute | solution.py:990
  261.9 44.9 %collective-permute-start.15 = (bf16[128,1024]{1,0:T(8,128)(2,1)S(1)}, bf16[128,1024]{1,0:T(8,128)(2,1)S(1)}, u32[]{:S(2)}, u32[]{:S(2)}) collective-permute-start(bf16[128,1024]{1,0:T(8,128)(2,1)S(1)} %get-tuple-element.431), channel_id=1, source_target_pairs={{0,8},{4,12},{8,0},{12,4},{16,24},{20,28},{24,16},{28,20},{1,9},{5... | collective-permute-start | bytes 786440 | tf_op jit(solution)/shard_map/ppermute | solution.py:999
  262.7 46.0 %collective-permute-start.26 = (bf16[512,128]{1,0:T(8,128)(2,1)}, bf16[512,128]{1,0:T(8,128)(2,1)S(1)}, u32[]{:S(2)}, u32[]{:S(2)}) collective-permute-start(bf16[512,128]{1,0:T(8,128)(2,1)} %get-tuple-element.190), channel_id=1, source_target_pairs={{0,3},{1,2},{2,1},{3,0},{4,7},{5,6},{6,5},{7,4},{8,11},{9,10},{10,... | collective-permute-start | bytes 393224 | tf_op jit(solution)/shard_map/ppermute | solution.py:990
  270.6 39.8 %collective-permute-start.18 = (bf16[512,128]{1,0:T(8,128)(2,1)S(1)}, bf16[512,128]{1,0:T(8,128)(2,1)S(1)}, u32[]{:S(2)}, u32[]{:S(2)}) collective-permute-start(bf16[512,128]{1,0:T(8,128)(2,1)S(1)} %copy-done.98), channel_id=1, source_target_pairs={{0,1},{1,0},{2,3},{3,2},{4,5},{5,4},{6,7},{7,6},{8,9},{9,8},{10,11... | collective-permute-start | bytes 393224 | tf_op jit(solution)/shard_map/ppermute | solution.py:990
  307.5 40.8 %collective-permute-start.28 = (bf16[256,1024]{1,0:T(8,128)(2,1)S(1)}, bf16[256,1024]{1,0:T(8,128)(2,1)S(1)}, u32[]{:S(2)}, u32[]{:S(2)}) collective-permute-start(bf16[256,1024]{1,0:T(8,128)(2,1)S(1)} %constant_dynamic-update-slice_fusion.2), channel_id=1, source_target_pairs={{0,2},{1,3},{2,0},{3,1},{4,6},{5,7},{6,4},{7,5},{8,10},{9,11},{10,... | collective-permute-start | bytes 1572872 | tf_op jit(solution)/shard_map/ppermute | solution.py:1024
  308.7 39.7 %collective-permute-start.27 = (bf16[256,1024]{1,0:T(8,128)(2,1)S(1)}, bf16[256,1024]{1,0:T(8,128)(2,1)}, u32[]{:S(2)}, u32[]{:S(2)}) collective-permute-start(bf16[256,1024]{1,0:T(8,128)(2,1)S(1)} %constant_dynamic-update-slice_fusion), channel_id=1, source_target_pairs={{0,1},{1,0},{2,3},{3,2},{4,5},{5,4},{6,7},{7,6},{8,9},{9,8},{10,11... | collective-permute-start | bytes 1572872 | tf_op jit(solution)/shard_map/ppermute | solution.py:1024
  370.6 41.8 %collective-permute-start.35 = (bf16[512,1024]{1,0:T(8,128)(2,1)S(1)}, bf16[512,1024]{1,0:T(8,128)(2,1)S(1)}, u32[]{:S(2)}, u32[]{:S(2)}) collective-permute-start(bf16[512,1024]{1,0:T(8,128)(2,1)S(1)} %constant_dynamic-update-slice_fusion.6), channel_id=1, source_target_pairs={{0,1},{1,0},{2,3},{3,2},{4,5},{5,4},{6,7},{7,6},{8,9},{9,8},{10,11... | collective-permute-start | bytes 3145736 | tf_op jit(solution)/shard_map/ppermute | solution.py:1024
  371.1 45.2 %collective-permute-start.31 = (bf16[512,128]{1,0:T(8,128)(2,1)S(1)}, bf16[512,128]{1,0:T(8,128)(2,1)S(1)}, u32[]{:S(2)}, u32[]{:S(2)}) collective-permute-start(bf16[512,128]{1,0:T(8,128)(2,1)S(1)} %copy-done.93), channel_id=1, source_target_pairs={{0,1},{1,0},{2,3},{3,2},{4,5},{5,4},{6,7},{7,6},{8,9},{9,8},{10,11... | collective-permute-start | bytes 393224 | tf_op jit(solution)/shard_map/ppermute | solution.py:990
  372.6 44.8 %collective-permute-start.32 = (bf16[512,128]{1,0:T(8,128)(2,1)S(1)}, bf16[512,128]{1,0:T(8,128)(2,1)}, u32[]{:S(2)}, u32[]{:S(2)}) collective-permute-start(bf16[512,128]{1,0:T(8,128)(2,1)S(1)} %copy-done.92), channel_id=1, source_target_pairs={{0,2},{1,3},{2,0},{3,1},{4,6},{5,7},{6,4},{7,5},{8,10},{9,11},{10,... | collective-permute-start | bytes 393224 | tf_op jit(solution)/shard_map/ppermute | solution.py:990
  384.6 34.1 %collective-permute-start.33 = (bf16[512,128]{1,0:T(8,128)(2,1)S(1)}, bf16[512,128]{1,0:T(8,128)(2,1)}, u32[]{:S(2)}, u32[]{:S(2)}) collective-permute-start(bf16[512,128]{1,0:T(8,128)(2,1)S(1)} %copy-done.91), channel_id=1, source_target_pairs={{0,3},{1,2},{2,1},{3,0},{4,7},{5,6},{6,5},{7,4},{8,11},{9,10},{10,... | collective-permute-start | bytes 393224 | tf_op jit(solution)/shard_map/ppermute | solution.py:990
  416.4 34.7 %collective-permute-start.38 = (bf16[512,128]{1,0:T(8,128)(2,1)S(1)}, bf16[512,128]{1,0:T(8,128)(2,1)S(1)}, u32[]{:S(2)}, u32[]{:S(2)}) collective-permute-start(bf16[512,128]{1,0:T(8,128)(2,1)S(1)} %copy-done.88), channel_id=1, source_target_pairs={{0,1},{1,0},{2,3},{3,2},{4,5},{5,4},{6,7},{7,6},{8,9},{9,8},{10,11... | collective-permute-start | bytes 393224 | tf_op jit(solution)/shard_map/ppermute | solution.py:990
  417.4 35.0 %collective-permute-start.39 = (bf16[512,128]{1,0:T(8,128)(2,1)S(1)}, bf16[512,128]{1,0:T(8,128)(2,1)S(1)}, u32[]{:S(2)}, u32[]{:S(2)}) collective-permute-start(bf16[512,128]{1,0:T(8,128)(2,1)S(1)} %copy-done.87), channel_id=1, source_target_pairs={{0,2},{1,3},{2,0},{3,1},{4,6},{5,7},{6,4},{7,5},{8,10},{9,11},{10,... | collective-permute-start | bytes 393224 | tf_op jit(solution)/shard_map/ppermute | solution.py:990
  418.7 34.9 %collective-permute-start.40 = (bf16[512,128]{1,0:T(8,128)(2,1)S(1)}, bf16[512,128]{1,0:T(8,128)(2,1)S(1)}, u32[]{:S(2)}, u32[]{:S(2)}) collective-permute-start(bf16[512,128]{1,0:T(8,128)(2,1)S(1)} %copy-done.85), channel_id=1, source_target_pairs={{0,3},{1,2},{2,1},{3,0},{4,7},{5,6},{6,5},{7,4},{8,11},{9,10},{10,... | collective-permute-start | bytes 393224 | tf_op jit(solution)/shard_map/ppermute | solution.py:990
  447.4 34.8 %collective-permute-start.47 = (bf16[512,128]{1,0:T(8,128)(2,1)S(1)}, bf16[512,128]{1,0:T(8,128)(2,1)S(1)}, u32[]{:S(2)}, u32[]{:S(2)}) collective-permute-start(bf16[512,128]{1,0:T(8,128)(2,1)S(1)} %copy-done.90), channel_id=1, source_target_pairs={{0,1},{1,0},{2,3},{3,2},{4,5},{5,4},{6,7},{7,6},{8,9},{9,8},{10,11... | collective-permute-start | bytes 393224 | tf_op jit(solution)/shard_map/ppermute | solution.py:990
  448.4 111.7 %collective-permute-start.53 = (bf16[2,4,288,1024]{3,2,1,0:T(8,128)(2,1)}, bf16[2,4,288,1024]{3,2,1,0:T(8,128)(2,1)}, u32[]{:S(2)}, u32[]{:S(2)}) collective-permute-start(bf16[2,4,288,1024]{3,2,1,0:T(8,128)(2,1)} %get-tuple-element.211), channel_id=1, source_target_pairs={{0,8},{4,12},{8,0},{12,4},{16,24},{20,28},{24,16},{28,20},{1,9},{5... | collective-permute-start | bytes 14155784 | tf_op jit(solution)/shard_map/ppermute | solution.py:68
  575.4 39.2 %collective-permute-start.54 = (bf16[2,2,288,512]{3,2,0,1:T(8,128)(2,1)S(1)}, bf16[2,2,288,512]{3,2,0,1:T(8,128)(2,1)}, u32[]{:S(2)}, u32[]{:S(2)}) collective-permute-start(bf16[2,2,288,512]{3,2,0,1:T(8,128)(2,1)S(1)} %fusion), channel_id=1, source_target_pairs={{0,1},{1,0},{2,3},{3,2},{4,5},{5,4},{6,7},{7,6},{8,9},{9,8},{10,11... | collective-permute-start | bytes 3538952 | tf_op jit(solution)/shard_map/ppermute | solution.py:68
  576.7 36.2 %collective-permute-start.56 = (bf16[3,512,128]{2,1,0:T(8,128)(2,1)}, bf16[3,512,128]{2,1,0:T(8,128)(2,1)}, u32[]{:S(2)}, u32[]{:S(2)}) collective-permute-start(bf16[3,512,128]{2,1,0:T(8,128)(2,1)} %get-tuple-element.260), channel_id=1, source_target_pairs={{0,1},{1,0},{2,3},{3,2},{4,5},{5,4},{6,7},{7,6},{8,9},{9,8},{10,11... | collective-permute-start | bytes 1179656 | tf_op jit(solution)/shard_map/ppermute | solution.py:990
  577.5 41.2 %collective-permute-start.57 = (bf16[3,512,128]{2,1,0:T(8,128)(2,1)}, bf16[3,512,128]{2,1,0:T(8,128)(2,1)}, u32[]{:S(2)}, u32[]{:S(2)}) collective-permute-start(bf16[3,512,128]{2,1,0:T(8,128)(2,1)} %get-tuple-element.261), channel_id=1, source_target_pairs={{0,2},{1,3},{2,0},{3,1},{4,6},{5,7},{6,4},{7,5},{8,10},{9,11},{10,... | collective-permute-start | bytes 1179656 | tf_op jit(solution)/shard_map/ppermute | solution.py:990
  579.2 43.4 %collective-permute-start.58 = (bf16[3,512,128]{2,1,0:T(8,128)(2,1)}, bf16[3,512,128]{2,1,0:T(8,128)(2,1)}, u32[]{:S(2)}, u32[]{:S(2)}) collective-permute-start(bf16[3,512,128]{2,1,0:T(8,128)(2,1)} %get-tuple-element.262), channel_id=1, source_target_pairs={{0,3},{1,2},{2,1},{3,0},{4,7},{5,6},{6,5},{7,4},{8,11},{9,10},{10,... | collective-permute-start | bytes 1179656 | tf_op jit(solution)/shard_map/ppermute | solution.py:990
  (181 other events, 2765.7 us)
Sparse Core Ops, SparseCore 0:
  11.5 81.4 all-gather.4
  96.4 170.3 all-gather.2

commit v5 on v4

--- a/solution.py
+++ b/solution.py
@@ -129,14 +129,21 @@
             keep[side], send[side] = halves(parts[side], dim, "row", bit)
         hold = yield send
     value = jnp.concatenate(parts, axis=-1)
-    names = [item for item in names if item[0] == "frame"]
-    for item in rest:
-        dim = names.index(item)
-        names.pop(dim)
-        keep, send = halves(value, dim, *item)
-        hold = yield [send]
-        value = joined(held(keep, *hold), send, *item)
-    yield value
+    value = value.reshape((-1,) + value.shape[-2:])
+    count = value.shape[0]
+    low = rest[0][1] if rest else 0
+    mine = frame >> low
+    keep = lax.dynamic_index_in_dim(value, mine & (count - 1), 0, keepdims=False)
+    sends = [
+        lax.dynamic_index_in_dim(value, (mine ^ slot) & (count - 1), 0, keepdims=False).astype(jnp.bfloat16)
+        for slot in range(1, count)
+    ]
+    hold = yield sends
+    keep = held(keep, *hold)
+    for slot, send in enumerate(sends, 1):
+        pairs = [(index, index ^ (slot << low)) for index in range(size)]
+        keep = keep + lax.ppermute(send, "frame", pairs).astype(jnp.float32)
+    yield keep
 
 
 def finished(steps, state):
@@ -211,25 +218,22 @@
             rows = pl.ds(pl.multiple_of(part * D + peer * group, group), group)
             value = dot_nt(hidden, w_ref[rows, :])
             if part == 2:
-                for pair in range(group // 128):
-                    out_refs[pair * slots + slot][part] = value[:, pair * 128 : (pair + 1) * 128].astype(
-                        jnp.bfloat16
-                    )
+                out_refs[slot][part] = value.astype(jnp.bfloat16)
                 continue
-            for pair in range(group // 128):
-                piece = turned(value[:, pair * 128 : (pair + 1) * 128], cosine, sine)
+            for first in range(0, group, 128):
+                piece = turned(value[:, first : first + 128], cosine, sine)
                 if part == 0:
                     piece = piece * (1.0 / math.sqrt(HD))
-                out_refs[pair * slots + slot][part] = piece.astype(jnp.bfloat16)
+                out_refs[slot][part, :, first : first + 128] = piece.astype(jnp.bfloat16)
 
 
 def project(me, clip, tokens, mod, cosine, sine, w_qkv, slots):
-    _, tall_rows, _ = tokens.shape
+    count, tall_rows, _ = tokens.shape
     tile = 256
     steps = tall_rows // tile
+    group = D // slots
     out_shape = [jax.ShapeDtypeStruct((1, tall_rows, D), jnp.bfloat16)]
-    count = D // 128
-    out_shape += [jax.ShapeDtypeStruct((3, tall_rows, 128), jnp.bfloat16)] * count
+    out_shape += [jax.ShapeDtypeStruct((3, tall_rows, group), jnp.bfloat16)] * slots
     return pl.pallas_call(
         functools.partial(project_kernel, slots),
         grid=(steps,),
@@ -242,7 +246,7 @@
             whole_spec(w_qkv),
         ],
         out_specs=[pl.BlockSpec((1, tile, D), lambda i: (0, i, 0))]
-        + [pl.BlockSpec((3, tile, 128), lambda i: (0, i, 0))] * count,
+        + [pl.BlockSpec((3, tile, group), lambda i: (0, i, 0))] * slots,
         out_shape=out_shape,
         compiler_params=vmem_params(60),
         cost_estimate=pl.CostEstimate(
@@ -375,19 +379,22 @@
         outs[slot][2] = dv[:, rows].T.astype(jnp.bfloat16)
 
 
-def attend_back(pieces, grads, full, logs):
+def attend_back(pieces, grads, full, logs, pair=None):
     slots = len(pieces)
     _, length, group = pieces[0].shape
+    first = 0 if pair is None else pair
+    count = group // 128 if pair is None else 1
+    group = 128 * count
     total = slots * length
     low = pltpu.VMEM((total, 128), jnp.bfloat16)
     low_t = pltpu.VMEM((128, total), jnp.bfloat16)
     full_t = pltpu.VMEM((128, total), jnp.float32)
     return pl.pallas_call(
         functools.partial(attend_back_kernel, slots, 512),
-        grid=(group // 128,),
-        in_specs=[pl.BlockSpec((3, length, 128), lambda i: (0, 0, i))] * slots
-        + [pl.BlockSpec((length, 128), lambda i: (0, i))] * slots
-        + [pl.BlockSpec((total, 128), lambda i: (0, i))] * 2,
+        grid=(count,),
+        in_specs=[pl.BlockSpec((3, length, 128), lambda i: (0, 0, i + first))] * slots
+        + [pl.BlockSpec((length, 128), lambda i: (0, i + first))] * slots
+        + [pl.BlockSpec((total, 128), lambda i: (0, i + first))] * 2,
         out_specs=[pl.BlockSpec((3, length, 128), lambda i: (0, 0, i))] * slots,
         out_shape=[jax.ShapeDtypeStruct((3, length, group), jnp.bfloat16)] * slots,
         scratch_shapes=[low] * 4 + [low_t] * 2 + [low] + [full_t] * 2,
@@ -405,10 +412,8 @@
 
 
 def middle_kernel(slots, me_ref, x_ref, cot_ref, mod_ref, wo_ref, wu_ref, wd_ref, *refs):
-    count = D // 128
-    pairs = count // slots
-    att_refs = refs[:count]
-    datt_refs = refs[count : 2 * count]
+    att_refs = refs[:slots]
+    datt_refs = refs[slots : 2 * slots]
     (
         out_ref,
         att_ref,
@@ -420,7 +425,7 @@
         dmid_ref,
         sums_ref,
         slope,
-    ) = refs[2 * count :]
+    ) = refs[2 * slots :]
     frames = mod_ref.shape[1]
     rows = x_ref.shape[1]
     group = D // slots
@@ -438,7 +443,7 @@
     branch = jnp.zeros((rows, D), jnp.float32)
     for slot in range(slots):
         at = pl.ds(pl.multiple_of((me ^ slot) * group, group), group)
-        piece = jnp.concatenate([att_refs[pair * slots + slot][...] for pair in range(pairs)], axis=1)
+        piece = att_refs[slot][...]
         att_ref[:, at] = piece
         branch += dot_low(piece, part_of(wo_ref, me ^ slot, group))
     middle = x_ref[0].astype(jnp.float32) + spread(branch, 2)
@@ -482,16 +487,15 @@
     d_branch = spread(d_middle, 2).astype(jnp.bfloat16)
     db1_ref[...] = d_branch
     for slot in range(slots):
-        value = dot_nt(d_branch, part_of(wo_ref, me ^ slot, group)).astype(jnp.bfloat16)
-        for pair in range(pairs):
-            datt_refs[pair * slots + slot][...] = value[:, pair * 128 : (pair + 1) * 128]
-
-
-def middle(me, clip, tokens, cotangent, mod, w_out, w_up, w_down, attended, slots):
-    count = len(attended)
-    _, length, _ = tokens.shape
+        datt_refs[slot][...] = dot_nt(d_branch, part_of(wo_ref, me ^ slot, group)).astype(jnp.bfloat16)
+
+
+def middle(me, clip, tokens, cotangent, mod, w_out, w_up, w_down, attended):
+    slots = len(attended)
+    count, length, _ = tokens.shape
     tile = 256
     steps = length // tile
+    group = D // slots
     frames = mod.shape[1]
     low = jnp.bfloat16
 
@@ -511,12 +515,12 @@
             pl.BlockSpec((1, frames, 6 * D), lambda i: (clip * steps + i, 0, 0)),
             *(item[1] for item in (w_out, w_up, w_down)),
         ]
-        + [flat_spec(128)] * count,
-        out_specs=[flat_spec(128)] * count
+        + [flat_spec(group)] * slots,
+        out_specs=[flat_spec(group)] * slots
         + [pl.BlockSpec((1, tile, D), lambda i: (0, i, 0))]
         + [flat_spec(width) for width in (D, D, FF, D, FF, D, D)]
         + [pl.BlockSpec((1, 4, frames, D), lambda i: (i, 0, 0, 0))],
-        out_shape=[flat(128)] * count
+        out_shape=[flat(group)] * slots
         + [jax.ShapeDtypeStruct((1, length, D), low)]
         + [flat(D), flat(D), flat(FF), flat(D), flat(FF), flat(D), flat(D, jnp.float32)]
         + [jax.ShapeDtypeStruct((steps, 4, frames, D), jnp.float32)],
@@ -527,17 +531,17 @@
         ),
         name="middle",
     )(me, tokens, cotangent, mod, *(item[0] for item in (w_out, w_up, w_down)), *attended)
-    return outs[:count], outs[count:]
+    return outs[:slots], outs[slots:]
 
 
 def last_kernel(slots, me_ref, x_ref, mod_ref, cos_ref, sin_ref, w_ref, dmid_ref, *refs):
-    count = D // 128
-    pairs = count // slots
-    pieces = refs[:count]
-    dproj_ref, grad_ref, sums_ref = refs[count:]
+    pieces = refs[:-3]
+    dproj_ref, grad_ref, sums_ref = refs[-3:]
     frames = mod_ref.shape[1]
     rows = x_ref.shape[1]
     group = D // slots
+    pairs = len(pieces) // slots
+    narrow = group // pairs
     me = me_ref[0]
     cosine = cos_ref[...]
     sine = -sin_ref[...]
@@ -551,8 +555,14 @@
             else:
                 value = jnp.concatenate(
                     [
-                        turned(pieces[pair * slots + slot][part].astype(jnp.float32), cosine, sine)
-                        for pair in range(pairs)
+                        turned(
+                            pieces[at // narrow * slots + slot][
+                                part, :, at % narrow : at % narrow + 128
+                            ].astype(jnp.float32),
+                            cosine,
+                            sine,
+                        )
+                        for at in range(0, group, 128)
                     ],
                     axis=1,
                 ).astype(jnp.bfloat16)
@@ -571,10 +581,10 @@
 
 
 def last(me, clip, tokens, mod, cosine, sine, w_qkv, d_middle, pieces, slots):
-    count = len(pieces)
-    _, length, _ = tokens.shape
+    count, length, _ = tokens.shape
     tile = 256
     steps = length // tile
+    narrow = pieces[0].shape[2]
     frames = mod.shape[1]
     return pl.pallas_call(
         functools.partial(last_kernel, slots),
@@ -588,7 +598,7 @@
             whole_spec(w_qkv),
             pl.BlockSpec((tile, D), lambda i: (i, 0)),
         ]
-        + [pl.BlockSpec((3, tile, 128), lambda i: (0, i, 0))] * count,
+        + [pl.BlockSpec((3, tile, narrow), lambda i: (0, i, 0))] * len(pieces),
         out_specs=[
             pl.BlockSpec((tile, 3 * D), lambda i: (i, 0)),
             pl.BlockSpec((1, tile, D), lambda i: (0, i, 0)),
@@ -758,12 +768,11 @@
     return list(outs[:each]), list(outs[each:])
 
 
-def newton_kernel(rows, unroll, pieces, scale_ref, *refs):
-    g_refs, m_refs, out_ref = refs[:pieces], refs[pieces : 2 * pieces], refs[2 * pieces]
-    x_ref, a_ref, t_ref, q_ref, eye_ref, ah, al, nh, th, tl, qh, ql, num_ref = refs[2 * pieces + 1 :]
+def newton_kernel(rows, unroll, pieces, *refs):
+    x_refs, out_ref = refs[:pieces], refs[pieces]
+    a_ref, t_ref, q_ref, eye_ref, ah, al, nh, th, tl, qh, ql, num_ref = refs[pieces + 1 :]
     width = a_ref.shape[0]
     steps = width // rows
-    deep = g_refs[0].shape[0]
     a_at, m_at, t_at, shift_at, sum_at = 0, 1, 2, 3, 8
 
     def block(index):
@@ -782,17 +791,6 @@
             total += num_ref[sum_at + index]
         return total * (1.0 / width)
 
-    for piece in range(pieces):
-
-        def mix(index, carry, piece=piece):
-            at = pl.ds(pl.multiple_of(index * 128, 128), 128)
-            to = pl.ds(pl.multiple_of(piece * deep + index * 128, 128), 128)
-            value = scale_ref[0] * g_refs[piece][at, :].astype(jnp.float32)
-            value += scale_ref[1] * m_refs[piece][at, :].astype(jnp.float32)
-            x_ref[to, :] = value.astype(jnp.bfloat16)
-            return carry
-
-        lax.fori_loop(0, deep // 128, mix, 0)
     eye_ref[...] = jnp.where(
         lax.broadcasted_iota(jnp.int32, (rows, rows), 0) == lax.broadcasted_iota(jnp.int32, (rows, rows), 1),
         1.0,
@@ -801,7 +799,7 @@
     squares = 0.0
     for index in range(steps):
         columns = slice(index * rows, (index + 1) * rows)
-        value = dot_tn(x_ref[:, columns], x_ref[:, index * rows :])
+        value = sum(dot_tn(ref[:, columns], ref[:, index * rows :]) for ref in x_refs)
         t_ref[columns, index * rows :] = value
         for other in range(index + 1, steps):
             there = slice(other * rows, (other + 1) * rows)
@@ -927,13 +925,13 @@
 
     half = out_ref.shape[0] // 2
     for side in range(2):
-        mine = x_ref[side * deep : side * deep + half, :]
+        mine = x_refs[side][0:half, :]
         out_ref[side * half : (side + 1) * half, :] = (
             (dot_low(mine, qh[...]) + dot_low(mine, ql[...])) * inverse
         ).astype(out_ref.dtype)
 
 
-def newton(scales, grads, moments, mine_rows, rows=256, unroll=4):
+def newton(grads, mine_rows, rows=256, unroll=4):
     width = grads[0].shape[1]
     pieces = len(grads)
     low = pltpu.VMEM((width, width), jnp.bfloat16)
@@ -942,17 +940,16 @@
     return pl.pallas_call(
         functools.partial(newton_kernel, rows, unroll, pieces),
         out_shape=jax.ShapeDtypeStruct((mine_rows, width), jnp.bfloat16),
-        in_specs=[pl.BlockSpec(memory_space=pltpu.SMEM)] + [vmem] * (2 * pieces),
+        in_specs=[vmem] * pieces,
         out_specs=vmem,
-        scratch_shapes=[pltpu.VMEM((pieces * grads[0].shape[0], width), jnp.bfloat16)]
-        + [full] * 3
+        scratch_shapes=[full] * 3
         + [pltpu.VMEM((rows, rows), jnp.float32)]
         + [low] * 7
         + [pltpu.SMEM((16,), jnp.float32)],
         compiler_params=vmem_params(60),
         cost_estimate=pl.CostEstimate(flops=60 * 10**9, bytes_accessed=20 * 10**6, transcendentals=0),
         name="newton",
-    )(scales, *grads, *moments)
+    )(*grads)
 
 
 def frame_sums_kernel(count, *refs):
@@ -1140,87 +1137,72 @@
     tokens_flat = tokens.reshape(clip_count, seq_local, model_width)
     cotangent_flat = cotangent.reshape(clip_count, seq_local, model_width)
     clips = range(clip_count)
-    pair_count = D // 128 // row_devices
-    units = [(clip, pair) for clip in clips for pair in range(pair_count)]
-
-    def of_unit(slots, pair):
-        return slots[pair * row_devices : (pair + 1) * row_devices]
-
-    def after(value, state):
-        return [held(value[0], *state), *value[1:]]
-
-    def of_clip(by_unit, clip):
-        return [item for pair in range(pair_count) for item in by_unit[clip, pair]]
-
-    hidden_one, pieces = [], {}
+    hidden_one, pieces = [], []
     for clip in clips:
         hidden, *slots = project(me, clip, tokens_flat, mod, cosine, sine, w_qkv, row_devices)
         hidden_one.append(hidden[0])
-        for pair in range(pair_count):
-            pieces[clip, pair] = swap(of_unit(slots, pair))
-    attended, full, logs = {}, {}, {}
-    for at, unit in enumerate(units):
-        ready = list(attended[units[at - 2]][1:]) if at >= 2 else []
-        if at >= 1:
-            ready.append(slots[0])
-        slots, full[unit], logs[unit] = attend(after(pieces[unit], ready))
-        attended[unit] = swap(slots)
-    moments_tall = [
-        item.astype(low_type) for item in (qkv_momentum.T, out_momentum, up_momentum.T, down_momentum)
-    ]
-    moments_tall[0] = held(moments_tall[0], attended[units[pair_count - 1]][-1])
-    moment_steps = plane_steps(moments_tall)
-    moment_rows = next(moment_steps)
-    d_attended, middles = {}, []
+        pieces.append(swap(slots))
+    attended, full, logs = [], [], []
+    for clip in clips:
+        slots, full_clip, log_clip = attend(pieces[clip])
+        attended.append(swap(slots))
+        full.append(full_clip)
+        logs.append(log_clip)
+    d_attended, middles = [], []
     for clip in clips:
         slots, others = middle(
-            me, clip, tokens_flat, cotangent_flat, mod, w_out, w_up, w_down,
-            after(of_clip(attended, clip), moment_rows), row_devices,
+            me, clip, tokens_flat, cotangent_flat, mod, w_out, w_up, w_down, attended[clip]
         )
-        for pair in range(pair_count):
-            d_attended[clip, pair] = swap(of_unit(slots, pair))
+        d_attended.append(swap(slots))
         middles.append(others)
-        moment_rows = moment_steps.send([others[0]])
     block_out = jnp.concatenate([item[0] for item in middles], axis=0).reshape(shape_five)
     att_low, hidden_two, activated, d_branch_two, d_up, d_branch_one, d_middle, two_sums = (
         [item[index] for item in middles] for index in range(1, 9)
     )
     early = scatter_steps(
-        [[(activated, d_branch_two)], [(d_up, hidden_two), (att_low, d_branch_one)]], "early", True, moment_rows
-    )
-    state = next(early)
-    d_pieces = {}
-    while not isinstance(moment_rows, tuple):
-        moment_rows = moment_steps.send(list(state))
-    for at, unit in enumerate(units):
-        ready = list(d_pieces[units[at - 2]][1:]) if at >= 2 else list(state)
-        if at >= 1:
-            ready.append(slots[0])
-        if at == 1:
-            ready += moment_rows
-        slots = attend_back(pieces[unit], after(d_attended[unit], ready), full[unit], logs[unit])
-        d_pieces[unit] = swap(slots)
+        [[(activated, d_branch_two)], [(d_up, hidden_two), (att_low, d_branch_one)]], "early", True, []
+    )
+
+    def after(value, state):
+        return [held(value[0], *state), *value[1:]]
+
+    ready = next(early)
+    d_pieces = []
+    for clip in clips:
+        if clip < clip_count - 1:
+            slots = attend_back(pieces[clip], after(d_attended[clip], ready), full[clip], logs[clip])
+            before = swap(slots)
+            d_pieces.append(before)
+            ready = [slots[0]]
+            continue
+        parts = []
+        for pair in range(D // 128 // row_devices):
+            slots = attend_back(pieces[clip], after(d_attended[clip], ready), full[clip], logs[clip], pair)
+            parts += swap(slots)
+            ready = [slots[0], *before[1:]]
+        d_pieces.append(parts)
     state = early.send([slots[0]])
     lasts = []
     for clip in clips:
         lasts.append(
             last(
                 me, clip, tokens_flat, mod, cosine, sine, w_qkv, d_middle[clip],
-                after(of_clip(d_pieces, clip), state), row_devices,
+                after(d_pieces[clip], state), row_devices,
             )
         )
-        state = early.send([lasts[clip][2]])
+        if clip < clip_count - 1:
+            state = early.send([lasts[clip][2]])
     input_grad = jnp.concatenate([item[1] for item in lasts], axis=0).reshape(shape_five)
-    late = scatter_steps([[([item[0] for item in lasts], hidden_one)]], "late", False, [])
+    one_sums = [item[2] for item in lasts]
+    d_modulation = frame_sums(one_sums, two_sums)
+    late = scatter_steps([[([item[0] for item in lasts], hidden_one)]], "late", False, [d_modulation])
     late_state = next(late)
-    early_sum = finished(early, state)
+    early_sum = finished(early, early.send(late_state))
     state = late_state
-    one_sums = [item[2] for item in lasts]
-    one_sums[0] = held(one_sums[0], *state)
-    d_modulation = frame_sums(one_sums, two_sums)
     g_qkv = finished(late, state)
 
     mod_parts = to_all(jnp.moveaxis(d_modulation.reshape(frame_total, device_total, ada_width), 1, 0))
+    mod_parts = held(mod_parts, *late_state)
     mod_mine = (
         jnp.sum(mod_parts.reshape(frame_devices, row_devices, frame_total, ada_width), axis=1)
         .reshape(frames_all, ada_width)
@@ -1249,25 +1231,23 @@
     local_total = adam_local + sum((jnp.sum(item * item) for item in muon_grads))
     norm_value = jnp.sqrt(jnp.sum(from_all(jnp.full((1, 128), local_total))[:, 0, 0]))
     clip_factor = jnp.minimum(1.0, clip_limit / (norm_value + 1e-06))
-    grad_steps = plane_steps([item.astype(low_type) for item in muon_grads])
-    grad_rows = next(grad_steps)
-    while not isinstance(grad_rows, tuple):
-        grad_rows = grad_steps.send([])
     moments_new = []
+    updates = []
+    slot_rows = max(heights)
     for member in range(4):
         clipped = clip_factor * muon_grads[member]
-        moments_new.append(
-            tall(momentum_decay * tall(muon_moments[member], member) + clipped, member)
-        )
-    scales = jnp.stack(
-        [clip_factor * (1.0 + momentum_decay), jnp.full((), momentum_decay * momentum_decay, full_type)]
-    )
-    slot_rows = max(heights)
+        moment = momentum_decay * tall(muon_moments[member], member) + clipped
+        update = (clipped + momentum_decay * moment).astype(low_type)
+        moments_new.append(tall(moment, member))
+        updates.append(update)
+    row_steps = plane_steps(updates)
+    update_rows = next(row_steps)
+    while not isinstance(update_rows, tuple):
+        update_rows = row_steps.send([])
     groups = frame_devices // 2
-    ortho_rows = newton(scales, grad_rows, moment_rows, groups * slot_rows)
-    ortho_rows = ortho_rows.reshape(groups, slot_rows, model_width)
+    group_index = lax.axis_index("frame") >> 1
+    ortho_rows = newton(update_rows, groups * slot_rows).reshape(groups, slot_rows, model_width)
     ortho_slots = jnp.stack(frame_swap([ortho_rows[slot] for slot in range(groups)]))
-    group_index = lax.axis_index("frame") >> 1
     ortho_mine = [
         lax.dynamic_index_in_dim(ortho_slots, (group_index & 3) ^ member, 0, keepdims=False)
         for member in range(4)

time: 994 us -> 941 us (0.947)
  starting transfers between devices: 122 us -> 85.2 us
  Pallas kernels: 435 us -> 408 us
  waiting for transfers between devices: 273 us -> 286 us
    ppermute x48 -> x27, starting transfers between devices: 56.6 us -> 29.7 us  [swap(): lax.ppermute(slots[slot], 'row', [(index, index ^ slot) for index in rang...]
    ppermute x12 -> x9, waiting for transfers between devices: 58 us -> 32.7 us  [joined(): lax.ppermute(send, axis, [(index, index ^ 1 << bit) for index in range(si...]
    ppermute x0 -> x4, waiting for transfers between devices: none -> 24.6 us  [scatter_steps(): keep = keep + lax.ppermute(send, 'frame', pairs).astype(jnp.float32)]
    all_gather x1, waiting for transfers between devices: 0.02 us -> 18 us  [per_device(): gathered = lax.all_gather(shards, both, axis=0)]
    pallas_call x4 -> x2, Pallas kernels: 80.8 us -> 64.3 us  [attend(): pl.pallas_call(functools.partial(attend_kernel, slots, 256), grid=(group...]
    ppermute x9 -> x6, waiting for transfers between devices: 47.5 us -> 41.8 us  [frame_swap(): out.append(lax.ppermute(slots[slot], 'frame', pairs))]
    ppermute x48 -> x27, waiting for transfers between devices: 78.7 us -> 83.5 us  [swap(): lax.ppermute(slots[slot], 'row', [(index, index ^ slot) for index in rang...]
    pallas_call x4 -> x3, Pallas kernels: 110 us -> 108 us  [attend_back(): pl.pallas_call(functools.partial(attend_back_kernel, slots, 512), grid=(c...]
  transfers between devices with their start and end apart: 92 -> 63, of which waited for: 35 -> 30; matrix products, arithmetic and copies ran while one was open for 7% -> 7% of each run, Pallas kernels for 32% -> 28%
where the time goes in v5:
time: 941 us; the launch traced here: 937 us
  Pallas kernels  408 us (43%)
  waiting for transfers between devices  286 us (30%)
  starting transfers between devices  85.2 us (9%)
  local copies, waits for them, and re-layouts  52.4 us (6%)
  other arithmetic  47.5 us (5%)
  blocking collectives  28.8 us (3%)
  between operations  23.3 us (2%)
    pallas_call x3, Pallas kernels, attend_back(): pl.pallas_call(functools.partial(attend_back_kernel, slots, 512), grid=(c...  108 us
    ppermute x27, waiting for transfers between devices, swap(): lax.ppermute(slots[slot], 'row', [(index, index ^ slot) for index in rang...  83.5 us
    pallas_call x1, Pallas kernels, newton(): pl.pallas_call(functools.partial(newton_kernel, rows, unroll, pieces), ou...  70.1 us
    pallas_call x2, Pallas kernels, middle(): pl.pallas_call(functools.partial(middle_kernel, slots), grid=(steps,), in...  66.6 us
    pallas_call x2, Pallas kernels, attend(): pl.pallas_call(functools.partial(attend_kernel, slots, 256), grid=(group...  64.3 us
    ppermute x6, waiting for transfers between devices, frame_swap(): out.append(lax.ppermute(slots[slot], 'frame', pairs))  41.8 us
    all_to_all x6, waiting for transfers between devices, to_all(): return lax.all_to_all(value, both, split_axis=0, concat_axis=0, tiled=True)  40.4 us
    ppermute x9, waiting for transfers between devices, joined(): lax.ppermute(send, axis, [(index, index ^ 1 << bit) for index in range(si...  32.7 us
  transfers between devices with their start and end apart: 63, of which 30 were waited for; matrix products, arithmetic and copies ran while one was open for 7% of the time, Pallas kernels for 28%

profile of v5, /device:TPU:8, one launch (start us, length us, event | category | flops | bytes accessed | tf_op | source)
XLA Modules:
  0.0 936.6 jit_solution(9366811818338724321)
XLA Ops:
  24.1 20.3 %all_to_all.35 = f32[32,4,1024]{2,1,0:T(4,128)S(1)} all-to-all(f32[32,4,1024]{2,1,0:T(4,128)S(1)} %reshape.250), channel_id=1, replica_groups=mesh['frame'=8,'row'=4] {'frame','row'}, dimensions={0} | all-to-all | bytes 1048576 | tf_op jit(solution)/shard_map/all_to_all | solution.py:1100
  50.5 15.8 %all-to-all-done.1 = f32[32,4,1024]{2,1,0:T(4,128)S(1)} async-done(((f32[32,4,1024]{2,1,0:T(4,128)}), f32[32,4,1024]{2,1,0:T(4,128)S(1)}, u32[]{:S(2)}, u32[]{:S(2)}) %all-to-all-start.1) | async-done | bytes 524320 | tf_op jit(solution)/shard_map/all_to_all | solution.py:1100
  76.8 18.3 %all-to-all-done.2 = f32[32,16,192]{2,1,0:T(8,128)S(1)} async-done(((f32[32,16,192]{2,1,0:T(8,128)}), f32[32,16,192]{2,1,0:T(8,128)S(1)}, u32[]{:S(2)}, u32[]{:S(2)}) %all-to-all-start.2) | async-done | bytes 393248 | tf_op jit(solution)/shard_map/all_to_all | solution.py:1100
  96.5 9.0 project.2
  109.6 9.1 project.3
  119.9 9.6 %collective-permute-done.refs_1_ = bf16[3,512,256]{2,1,0:T(8,128)(2,1)S(1)} collective-permute-done((bf16[3,512,256]{2,1,0:T(8,128)(2,1)}, bf16[3,512,256]{2,1,0:T(8,128)(2,1)S(1)}, u32[]{:S(2)}, u32[]{:S(2)}) %collective-permute-start) | collective-permute-done | bytes 786464 | tf_op jit(solution)/shard_map/ppermute | solution.py:987
  139.0 22.1 %collective-permute-done.2.refs_3_ = bf16[3,512,256]{2,1,0:T(8,128)(2,1)} collective-permute-done((bf16[3,512,256]{2,1,0:T(8,128)(2,1)}, bf16[3,512,256]{2,1,0:T(8,128)(2,1)}, u32[]{:S(2)}, u32[]{:S(2)}) %collective-permute-start.2) | collective-permute-done | bytes 786464 | tf_op jit(solution)/shard_map/ppermute | solution.py:987
  161.1 32.2 %attend.2 = (bf16[512,256]{1,0:T(8,128)(2,1)}, bf16[512,256]{1,0:T(8,128)(2,1)}, bf16[512,256]{1,0:T(8,128)(2,1)}, bf16[512,256]{1,0:T(8,128)(2,1)}, f32[2048,256]{1,0:T(8,128)}, /*index=5*/f32[2048,256]{1,0:T(8,128)}) custom-call(bf16[3,512,256]{2,1,0:T(8,128)(2,1)} %get-tuple-element.107.refs_0_, bf16[3,512,256]{2,1,0:T(8,128)(2,1)} %copy-done.58, ...), custom_call_target="tpu_custom_call" | custom-call | flops 17179869184 | bytes 8388608 | tf_op jit(solution)/shard_map/attend/pallas_call | solution.py:302
  196.8 13.0 %collective-permute-done.8.refs_3_ = bf16[3,512,256]{2,1,0:T(8,128)(2,1)S(1)} collective-permute-done((bf16[3,512,256]{2,1,0:T(8,128)(2,1)}, bf16[3,512,256]{2,1,0:T(8,128)(2,1)S(1)}, u32[]{:S(2)}, u32[]{:S(2)}) %collective-permute-start.8) | collective-permute-done | bytes 786464 | tf_op jit(solution)/shard_map/ppermute | solution.py:987
  210.8 32.1 %attend.3 = (bf16[512,256]{1,0:T(8,128)(2,1)}, bf16[512,256]{1,0:T(8,128)(2,1)}, bf16[512,256]{1,0:T(8,128)(2,1)}, bf16[512,256]{1,0:T(8,128)(2,1)}, f32[2048,256]{1,0:T(8,128)}, /*index=5*/f32[2048,256]{1,0:T(8,128)}) custom-call(bf16[3,512,256]{2,1,0:T(8,128)(2,1)} %get-tuple-element.116.refs_0_, bf16[3,512,256]{2,1,0:T(8,128)(2,1)} %copy-done.55, ...), custom_call_target="tpu_custom_call" | custom-call | flops 17179869184 | bytes 8388608 | tf_op jit(solution)/shard_map/attend/pallas_call | solution.py:302
  246.4 18.0 %all-gather.3.cloned.1.call-done.wo_ref.wu_ref.wd_ref = bf16[32,288,1024]{2,1,0:T(8,128)(2,1)} async-done(((bf16[1,288,1024]{2,1,0:T(8,128)(2,1)}), bf16[32,288,1024]{2,1,0:T(8,128)(2,1)}) %all-gather.3.cloned.1.call-update) | async-done | bytes 18874384 | tf_op jit(solution)/shard_map/all_gather | solution.py:1067
  264.4 33.5 %middle.2 = (bf16[512,256]{1,0:T(8,128)(2,1)}, bf16[512,256]{1,0:T(8,128)(2,1)}, bf16[512,256]{1,0:T(8,128)(2,1)}, bf16[512,256]{1,0:T(8,128)(2,1)}, bf16[1,512,...) custom-call(s32[1]{0:T(128)} %bitcast.me_ref, ...), custom_call_target="tpu_custom_call" | custom-call | flops 19327352832 | bytes 41943040 | tf_op jit(solution)/shard_map/middle/pallas_call | solution.py:508
  298.8 33.1 %middle.3 = (bf16[512,256]{1,0:T(8,128)(2,1)}, bf16[512,256]{1,0:T(8,128)(2,1)}, bf16[512,256]{1,0:T(8,128)(2,1)}, bf16[512,256]{1,0:T(8,128)(2,1)}, bf16[1,512,...) custom-call(s32[1]{0:T(128)} %bitcast.me_ref, ...), custom_call_target="tpu_custom_call" | custom-call | flops 19327352832 | bytes 41943040 | tf_op jit(solution)/shard_map/middle/pallas_call | solution.py:508
  331.9 9.1 early_send_0.1
  341.0 11.4 %early_send_1.1 = bf16[4,4,160,1024]{3,2,1,0:T(8,128)(2,1)} custom-call(s32[4]{0:T(128)} %pad_add_fusion.number_ref, bf16[512,4096]{1,0:T(8,128)(2,1)} %get-tuple-element.132.refs_0_.refs_4_, bf16[512,4096]{1,0:T(8,128)(2,1)} %get-tuple-element.133.refs_1_.refs_5_, bf16[512,1024]{1,0:T(8,128)(2,1)} %get-tuple-element.134.refs_2_.refs_6_, ...), custom_call_target="tpu_custom_call" | custom-call | flops 5368709120 | bytes 20971520 | tf_op jit(solution)/shard_map/early_send_1/pallas_call | solution.py:728
  356.4 11.0 %collective-permute-done.12.refs_12_ = bf16[4,4,128,1024]{3,2,1,0:T(8,128)(2,1)} collective-permute-done((bf16[4,4,128,1024]{3,2,1,0:T(8,128)(2,1)}, bf16[4,4,128,1024]{3,2,1,0:T(8,128)(2,1)}, u32[]{:S(2)}, u32[]{:S(2)}) %collective-permute-start.12) | collective-permute-done | bytes 4194336 | tf_op jit(solution)/shard_map/ppermute | solution.py:88
  368.7 22.9 %early_keep.1 = (f32[2,4,288,1024]{3,2,1,0:T(8,128)}, bf16[2,4,288,1024]{3,2,1,0:T(8,128)(2,1)}) custom-call(s32[4]{0:T(128)} %pad_add_fusion.number_ref, bf16[512,4096]{1,0:T(8,128)(2,1)} %get-tuple-element.127.refs_0_, bf16[512,4096]{1,0:T(8,128)(2,1)} %get-tuple-element.128.refs_1_, bf16[512,1024]{1,0:T(8,128)(2,1)} %get-tuple-element.129.refs_2_, ...), custom_call_target="tpu_custom_call" | custom-call | flops 9663676416 | bytes 41943040 | tf_op jit(solution)/shard_map/early_keep/pallas_call | solution.py:757
  395.2 51.8 %attend_back.3 = (bf16[3,512,256]{2,1,0:T(8,128)(2,1)}, bf16[3,512,256]{2,1,0:T(8,128)(2,1)}, bf16[3,512,256]{2,1,0:T(8,128)(2,1)}, bf16[3,512,256]{2,1,0:T(8,128)(2,1)}) custom-call(bf16[3,512,256]{2,1,0:T(8,128)(2,1)} %get-tuple-element.107.refs_0_, bf16[3,512,256]{2,1,0:T(8,128)(2,1)} %copy-done.58, bf16[3,512,256]{2,1,0:T(8,128)(2,1)} %copy-done.59, ...), custom_call_target="tpu_custom_call" | custom-call | flops 42949672960 | bytes 12582912 | tf_op jit(solution)/shard_map/attend_back/pallas_call | solution.py:392
  451.3 27.5 %attend_back.4 = (bf16[3,512,128]{2,1,0:T(8,128)(2,1)}, bf16[3,512,128]{2,1,0:T(8,128)(2,1)}, bf16[3,512,128]{2,1,0:T(8,128)(2,1)}, bf16[3,512,128]{2,1,0:T(8,128)(2,1)}) custom-call(bf16[3,512,256]{2,1,0:T(8,128)(2,1)} %get-tuple-element.116.refs_0_, bf16[3,512,256]{2,1,0:T(8,128)(2,1)} %copy-done.55, bf16[3,512,256]{2,1,0:T(8,128)(2,1)} %copy-done.56, ...), custom_call_target="tpu_custom_call" | custom-call | flops 21474836480 | bytes 12582912 | tf_op jit(solution)/shard_map/attend_back/pallas_call | solution.py:392
  484.5 28.4 %attend_back.5 = (bf16[3,512,128]{2,1,0:T(8,128)(2,1)}, bf16[3,512,128]{2,1,0:T(8,128)(2,1)}, bf16[3,512,128]{2,1,0:T(8,128)(2,1)}, bf16[3,512,128]{2,1,0:T(8,128)(2,1)}) custom-call(bf16[3,512,256]{2,1,0:T(8,128)(2,1)} %get-tuple-element.116.refs_0_, bf16[3,512,256]{2,1,0:T(8,128)(2,1)} %copy-done.55, bf16[3,512,256]{2,1,0:T(8,128)(2,1)} %copy-done.56, ...), custom_call_target="tpu_custom_call" | custom-call | flops 21474836480 | bytes 12582912 | tf_op jit(solution)/shard_map/attend_back/pallas_call | solution.py:392
  535.0 9.8 %last.2 = (bf16[512,3072]{1,0:T(8,128)(2,1)}, f32[1,512,1024]{2,1,0:T(8,128)}, f32[2,2,4,1024]{3,2,1,0:T(4,128)}) custom-call(s32[1]{0:T(128)} %bitcast.me_ref, bf16[2,512,1024]{2,1,0:T(8,128)(2,1)} %bitcast.151, f32[4,4,6144]{2,1,0:T(4,128)} %reshape_reshape.4.mod_ref, f32[1024,128]{1,0:T(8,128)} %copy.139.cos_ref, ...), custom_call_target="tpu_custom_call" | custom-call | flops 3221225472 | bytes 20971520 | tf_op jit(solution)/shard_map/last/pallas_call | solution.py:589
  546.8 8.7 collective-permute-done.25
  588.7 10.0 %last.3 = (bf16[512,3072]{1,0:T(8,128)(2,1)}, f32[1,512,1024]{2,1,0:T(8,128)}, f32[2,2,4,1024]{3,2,1,0:T(4,128)}) custom-call(s32[1]{0:T(128)} %bitcast.me_ref, bf16[2,512,1024]{2,1,0:T(8,128)(2,1)} %bitcast.152, f32[4,4,6144]{2,1,0:T(4,128)} %reshape_reshape.4.mod_ref, f32[1024,128]{1,0:T(8,128)} %copy.139.cos_ref, ...), custom_call_target="tpu_custom_call" | custom-call | flops 3221225472 | bytes 20971520 | tf_op jit(solution)/shard_map/last/pallas_call | solution.py:589
  614.5 8.7 late_keep.1
  678.4 9.5 %collective-permute-done.35 = bf16[2,2,96,512]{3,2,1,0:T(8,128)(2,1)S(1)} collective-permute-done((bf16[2,2,96,512]{3,2,1,0:T(8,128)(2,1)}, bf16[2,2,96,512]{3,2,1,0:T(8,128)(2,1)S(1)}, u32[]{:S(2)}, u32[]{:S(2)}) %collective-permute-start.35) | collective-permute-done | bytes 393248 | tf_op jit(solution)/shard_map/ppermute | solution.py:68
  702.1 9.5 %collective-permute-done.37 = bf16[96,1024]{1,0:T(8,128)(2,1)S(1)} collective-permute-done((bf16[96,1024]{1,0:T(8,128)(2,1)S(1)}, bf16[96,1024]{1,0:T(8,128)(2,1)S(1)}, u32[]{:S(2)}, u32[]{:S(2)}) %collective-permute-start.37) | collective-permute-done | bytes 196640 | tf_op jit(solution)/shard_map/ppermute | solution.py:145
  711.6 9.2 collective-permute-done.38
  756.1 14.0 %collective-permute-done.46 = bf16[128,1024]{1,0:T(8,128)(2,1)S(1)} collective-permute-done((bf16[128,1024]{1,0:T(8,128)(2,1)S(1)}, bf16[128,1024]{1,0:T(8,128)(2,1)S(1)}, u32[]{:S(2)}, u32[]{:S(2)}) %collective-permute-start.46) | collective-permute-done | bytes 262176 | tf_op jit(solution)/shard_map/ppermute | solution.py:996
  778.9 12.5 %collective-permute-done.48 = bf16[256,1024]{1,0:T(8,128)(2,1)S(1)} collective-permute-done((bf16[256,1024]{1,0:T(8,128)(2,1)S(1)}, bf16[256,1024]{1,0:T(8,128)(2,1)S(1)}, u32[]{:S(2)}, u32[]{:S(2)}) %collective-permute-start.48) | collective-permute-done | bytes 524320 | tf_op jit(solution)/shard_map/ppermute | solution.py:1021
  795.7 20.0 %collective-permute-done.49 = bf16[512,1024]{1,0:T(8,128)(2,1)S(1)} collective-permute-done((bf16[512,1024]{1,0:T(8,128)(2,1)S(1)}, bf16[512,1024]{1,0:T(8,128)(2,1)S(1)}, u32[]{:S(2)}, u32[]{:S(2)}) %collective-permute-start.49) | collective-permute-done | bytes 1048608 | tf_op jit(solution)/shard_map/ppermute | solution.py:1021
  826.9 70.1 %newton.1 = bf16[512,1024]{1,0:T(8,128)(2,1)} custom-call(bf16[1024,1024]{1,0:T(8,128)(2,1)} %pad_maximum_fusion.2.refs_0_, bf16[1024,1024]{1,0:T(8,128)(2,1)} %constant_dynamic-update-slice_fusion.refs_1_, bf16[1024,1024]{1,0:T(8,128)(2,1)} %collective-permute-done.50.refs_2_, bf16[1024,1024]{1,0:T(8,128)(2,1)} %collective-permute-done.51.refs_3_), custom_call_target="tpu_custom_call" | custom-call | flops 60000002048 | bytes 20000000 | tf_op jit(solution)/shard_map/newton/pallas_call | solution.py:940
  912.3 12.5 %collective-permute-done.54 = bf16[128,1024]{1,0:T(8,128)(2,1)S(1)} collective-permute-done((bf16[128,1024]{1,0:T(8,128)(2,1)S(1)}, bf16[128,1024]{1,0:T(8,128)(2,1)S(1)}, u32[]{:S(2)}, u32[]{:S(2)}) %collective-permute-start.54) | collective-permute-done | bytes 262176 | tf_op jit(solution)/shard_map/ppermute | solution.py:996
  (409 shorter events, 290.6 us)
Async XLA Ops:
  7.2 89.3 %all-gather.5.cloned.1.call-start = ((), (), s32[]{:S(2)}) async-start(), calls=%async_computation.8 | async-start | bytes 6488064 | tf_op jit(solution)/shard_map/all_gather | solution.py:1065
  9.0 255.4 %all-gather.3.cloned.1.call-start = ((), (), s32[]{:S(2)}) async-start(), calls=%async_computation.7 | async-start | bytes 19464192 | tf_op jit(solution)/shard_map/all_gather | solution.py:1067
  105.5 33.5 %collective-permute-start.1 = (bf16[3,512,256]{2,1,0:T(8,128)(2,1)}, bf16[3,512,256]{2,1,0:T(8,128)(2,1)S(1)}, u32[]{:S(2)}, u32[]{:S(2)}) collective-permute-start(bf16[3,512,256]{2,1,0:T(8,128)(2,1)} %get-tuple-element.109), channel_id=1, source_target_pairs={{0,2},{1,3},{2,0},{3,1},{4,6},{5,7},{6,4},{7,5},{8,10},{9,11},{10,... | collective-permute-start | bytes 2359304 | tf_op jit(solution)/shard_map/ppermute | solution.py:987
  106.8 54.3 %collective-permute-start.2 = (bf16[3,512,256]{2,1,0:T(8,128)(2,1)}, bf16[3,512,256]{2,1,0:T(8,128)(2,1)}, u32[]{:S(2)}, u32[]{:S(2)}) collective-permute-start(bf16[3,512,256]{2,1,0:T(8,128)(2,1)} %get-tuple-element.110), channel_id=1, source_target_pairs={{0,3},{1,2},{2,1},{3,0},{4,7},{5,6},{6,5},{7,4},{8,11},{9,10},{10,... | collective-permute-start | bytes 2359304 | tf_op jit(solution)/shard_map/ppermute | solution.py:987
  118.7 75.8 %collective-permute-start.6 = (bf16[3,512,256]{2,1,0:T(8,128)(2,1)}, bf16[3,512,256]{2,1,0:T(8,128)(2,1)S(1)}, u32[]{:S(2)}, u32[]{:S(2)}) collective-permute-start(bf16[3,512,256]{2,1,0:T(8,128)(2,1)} %get-tuple-element.117), channel_id=1, source_target_pairs={{0,1},{1,0},{2,3},{3,2},{4,5},{5,4},{6,7},{7,6},{8,9},{9,8},{10,11... | collective-permute-start | bytes 2359304 | tf_op jit(solution)/shard_map/ppermute | solution.py:987
  118.7 78.1 %collective-permute-start.7 = (bf16[3,512,256]{2,1,0:T(8,128)(2,1)}, bf16[3,512,256]{2,1,0:T(8,128)(2,1)S(1)}, u32[]{:S(2)}, u32[]{:S(2)}) collective-permute-start(bf16[3,512,256]{2,1,0:T(8,128)(2,1)} %get-tuple-element.118), channel_id=1, source_target_pairs={{0,2},{1,3},{2,0},{3,1},{4,6},{5,7},{6,4},{7,5},{8,10},{9,11},{10,... | collective-permute-start | bytes 2359304 | tf_op jit(solution)/shard_map/ppermute | solution.py:987
  129.5 80.3 %collective-permute-start.8 = (bf16[3,512,256]{2,1,0:T(8,128)(2,1)}, bf16[3,512,256]{2,1,0:T(8,128)(2,1)S(1)}, u32[]{:S(2)}, u32[]{:S(2)}) collective-permute-start(bf16[3,512,256]{2,1,0:T(8,128)(2,1)} %get-tuple-element.119), channel_id=1, source_target_pairs={{0,3},{1,2},{2,1},{3,0},{4,7},{5,6},{6,5},{7,4},{8,11},{9,10},{10,... | collective-permute-start | bytes 2359304 | tf_op jit(solution)/shard_map/ppermute | solution.py:987
  193.3 51.8 %collective-permute-start.3 = (bf16[512,256]{1,0:T(8,128)(2,1)}, bf16[512,256]{1,0:T(8,128)(2,1)S(1)}, u32[]{:S(2)}, u32[]{:S(2)}) collective-permute-start(bf16[512,256]{1,0:T(8,128)(2,1)} %get-tuple-element.112), channel_id=1, source_target_pairs={{0,1},{1,0},{2,3},{3,2},{4,5},{5,4},{6,7},{7,6},{8,9},{9,8},{10,11... | collective-permute-start | bytes 786440 | tf_op jit(solution)/shard_map/ppermute | solution.py:987
  194.0 52.4 %collective-permute-start.4 = (bf16[512,256]{1,0:T(8,128)(2,1)}, bf16[512,256]{1,0:T(8,128)(2,1)S(1)}, u32[]{:S(2)}, u32[]{:S(2)}) collective-permute-start(bf16[512,256]{1,0:T(8,128)(2,1)} %get-tuple-element.113), channel_id=1, source_target_pairs={{0,2},{1,3},{2,0},{3,1},{4,6},{5,7},{6,4},{7,5},{8,10},{9,11},{10,... | collective-permute-start | bytes 786440 | tf_op jit(solution)/shard_map/ppermute | solution.py:987
  194.5 51.9 %collective-permute-start.5 = (bf16[512,256]{1,0:T(8,128)(2,1)}, bf16[512,256]{1,0:T(8,128)(2,1)S(1)}, u32[]{:S(2)}, u32[]{:S(2)}) collective-permute-start(bf16[512,256]{1,0:T(8,128)(2,1)} %get-tuple-element.114), channel_id=1, source_target_pairs={{0,3},{1,2},{2,1},{3,0},{4,7},{5,6},{6,5},{7,4},{8,11},{9,10},{10,... | collective-permute-start | bytes 786440 | tf_op jit(solution)/shard_map/ppermute | solution.py:987
  242.9 55.0 %collective-permute-start.10 = (bf16[512,256]{1,0:T(8,128)(2,1)}, bf16[512,256]{1,0:T(8,128)(2,1)S(1)}, u32[]{:S(2)}, u32[]{:S(2)}) collective-permute-start(bf16[512,256]{1,0:T(8,128)(2,1)} %get-tuple-element.122), channel_id=1, source_target_pairs={{0,2},{1,3},{2,0},{3,1},{4,6},{5,7},{6,4},{7,5},{8,10},{9,11},{10,... | collective-permute-start | bytes 786440 | tf_op jit(solution)/shard_map/ppermute | solution.py:987
  243.8 54.1 %collective-permute-start.11 = (bf16[512,256]{1,0:T(8,128)(2,1)}, bf16[512,256]{1,0:T(8,128)(2,1)S(1)}, u32[]{:S(2)}, u32[]{:S(2)}) collective-permute-start(bf16[512,256]{1,0:T(8,128)(2,1)} %get-tuple-element.123), channel_id=1, source_target_pairs={{0,3},{1,2},{2,1},{3,0},{4,7},{5,6},{6,5},{7,4},{8,11},{9,10},{10,... | collective-permute-start | bytes 786440 | tf_op jit(solution)/shard_map/ppermute | solution.py:987
  245.0 52.9 %collective-permute-start.9 = (bf16[512,256]{1,0:T(8,128)(2,1)}, bf16[512,256]{1,0:T(8,128)(2,1)S(1)}, u32[]{:S(2)}, u32[]{:S(2)}) collective-permute-start(bf16[512,256]{1,0:T(8,128)(2,1)} %get-tuple-element.121), channel_id=1, source_target_pairs={{0,1},{1,0},{2,3},{3,2},{4,5},{5,4},{6,7},{7,6},{8,9},{9,8},{10,11... | collective-permute-start | bytes 786440 | tf_op jit(solution)/shard_map/ppermute | solution.py:987
  352.9 38.7 %collective-permute-start.14 = (bf16[512,256]{1,0:T(8,128)(2,1)S(1)}, bf16[512,256]{1,0:T(8,128)(2,1)S(1)}, u32[]{:S(2)}, u32[]{:S(2)}) collective-permute-start(bf16[512,256]{1,0:T(8,128)(2,1)S(1)} %copy-done.70), channel_id=1, source_target_pairs={{0,1},{1,0},{2,3},{3,2},{4,5},{5,4},{6,7},{7,6},{8,9},{9,8},{10,11... | collective-permute-start | bytes 786440 | tf_op jit(solution)/shard_map/ppermute | solution.py:987
  353.5 40.5 %collective-permute-start.15 = (bf16[512,256]{1,0:T(8,128)(2,1)S(1)}, bf16[512,256]{1,0:T(8,128)(2,1)S(1)}, u32[]{:S(2)}, u32[]{:S(2)}) collective-permute-start(bf16[512,256]{1,0:T(8,128)(2,1)S(1)} %copy-done.68), channel_id=1, source_target_pairs={{0,2},{1,3},{2,0},{3,1},{4,6},{5,7},{6,4},{7,5},{8,10},{9,11},{10,... | collective-permute-start | bytes 786440 | tf_op jit(solution)/shard_map/ppermute | solution.py:987
  354.1 40.4 %collective-permute-start.16 = (bf16[512,256]{1,0:T(8,128)(2,1)S(1)}, bf16[512,256]{1,0:T(8,128)(2,1)S(1)}, u32[]{:S(2)}, u32[]{:S(2)}) collective-permute-start(bf16[512,256]{1,0:T(8,128)(2,1)S(1)} %copy-done.65), channel_id=1, source_target_pairs={{0,3},{1,2},{2,1},{3,0},{4,7},{5,6},{6,5},{7,4},{8,11},{9,10},{10,... | collective-permute-start | bytes 786440 | tf_op jit(solution)/shard_map/ppermute | solution.py:987
  367.4 81.7 %collective-permute-start.17 = (bf16[512,256]{1,0:T(8,128)(2,1)S(1)}, bf16[512,256]{1,0:T(8,128)(2,1)S(1)}, u32[]{:S(2)}, u32[]{:S(2)}) collective-permute-start(bf16[512,256]{1,0:T(8,128)(2,1)S(1)} %copy-done.66), channel_id=1, source_target_pairs={{0,1},{1,0},{2,3},{3,2},{4,5},{5,4},{6,7},{7,6},{8,9},{9,8},{10,11... | collective-permute-start | bytes 786440 | tf_op jit(solution)/shard_map/ppermute | solution.py:987
  368.0 81.9 %collective-permute-start.18 = (bf16[512,256]{1,0:T(8,128)(2,1)S(1)}, bf16[512,256]{1,0:T(8,128)(2,1)S(1)}, u32[]{:S(2)}, u32[]{:S(2)}) collective-permute-start(bf16[512,256]{1,0:T(8,128)(2,1)S(1)} %copy-done.64), channel_id=1, source_target_pairs={{0,2},{1,3},{2,0},{3,1},{4,6},{5,7},{6,4},{7,5},{8,10},{9,11},{10,... | collective-permute-start | bytes 786440 | tf_op jit(solution)/shard_map/ppermute | solution.py:987
  391.6 59.0 %collective-permute-start.19 = (bf16[512,256]{1,0:T(8,128)(2,1)S(1)}, bf16[512,256]{1,0:T(8,128)(2,1)S(1)}, u32[]{:S(2)}, u32[]{:S(2)}) collective-permute-start(bf16[512,256]{1,0:T(8,128)(2,1)S(1)} %copy-done.63), channel_id=1, source_target_pairs={{0,3},{1,2},{2,1},{3,0},{4,7},{5,6},{6,5},{7,4},{8,11},{9,10},{10,... | collective-permute-start | bytes 786440 | tf_op jit(solution)/shard_map/ppermute | solution.py:987
  394.0 119.0 %collective-permute-start.23 = (bf16[2,4,288,1024]{3,2,1,0:T(8,128)(2,1)}, bf16[2,4,288,1024]{3,2,1,0:T(8,128)(2,1)}, u32[]{:S(2)}, u32[]{:S(2)}) collective-permute-start(bf16[2,4,288,1024]{3,2,1,0:T(8,128)(2,1)} %get-tuple-element.141), channel_id=1, source_target_pairs={{0,8},{4,12},{8,0},{12,4},{16,24},{20,28},{24,16},{28,20},{1,9},{5... | collective-permute-start | bytes 14155784 | tf_op jit(solution)/shard_map/ppermute | solution.py:68
  447.0 31.8 %collective-permute-start.20 = (bf16[3,512,256]{2,1,0:T(8,128)(2,1)}, bf16[3,512,256]{2,1,0:T(8,128)(2,1)S(1)}, u32[]{:S(2)}, u32[]{:S(2)}) collective-permute-start(bf16[3,512,256]{2,1,0:T(8,128)(2,1)} %get-tuple-element.158), channel_id=1, source_target_pairs={{0,1},{1,0},{2,3},{3,2},{4,5},{5,4},{6,7},{7,6},{8,9},{9,8},{10,11... | collective-permute-start | bytes 2359304 | tf_op jit(solution)/shard_map/ppermute | solution.py:987
  449.1 35.4 %collective-permute-start.21 = (bf16[3,512,256]{2,1,0:T(8,128)(2,1)}, bf16[3,512,256]{2,1,0:T(8,128)(2,1)S(1)}, u32[]{:S(2)}, u32[]{:S(2)}) collective-permute-start(bf16[3,512,256]{2,1,0:T(8,128)(2,1)} %get-tuple-element.159), channel_id=1, source_target_pairs={{0,2},{1,3},{2,0},{3,1},{4,6},{5,7},{6,4},{7,5},{8,10},{9,11},{10,... | collective-permute-start | bytes 2359304 | tf_op jit(solution)/shard_map/ppermute | solution.py:987
  449.9 34.5 %collective-permute-start.22 = (bf16[3,512,256]{2,1,0:T(8,128)(2,1)}, bf16[3,512,256]{2,1,0:T(8,128)(2,1)S(1)}, u32[]{:S(2)}, u32[]{:S(2)}) collective-permute-start(bf16[3,512,256]{2,1,0:T(8,128)(2,1)} %get-tuple-element.160), channel_id=1, source_target_pairs={{0,3},{1,2},{2,1},{3,0},{4,7},{5,6},{6,5},{7,4},{8,11},{9,10},{10,... | collective-permute-start | bytes 2359304 | tf_op jit(solution)/shard_map/ppermute | solution.py:987
  526.3 29.2 %collective-permute-start.25 = (bf16[2,2,288,512]{3,2,0,1:T(8,128)(2,1)}, bf16[2,2,288,512]{3,2,0,1:T(8,128)(2,1)}, u32[]{:S(2)}, u32[]{:S(2)}) collective-permute-start(bf16[2,2,288,512]{3,2,0,1:T(8,128)(2,1)} %fusion.1), channel_id=1, source_target_pairs={{0,2},{1,3},{2,0},{3,1},{4,6},{5,7},{6,4},{7,5},{8,10},{9,11},{10,... | collective-permute-start | bytes 3538952 | tf_op jit(solution)/shard_map/ppermute | solution.py:68
  528.9 38.6 %collective-permute-start.24 = (bf16[2,2,288,512]{3,2,0,1:T(8,128)(2,1)S(1)}, bf16[2,2,288,512]{3,2,0,1:T(8,128)(2,1)}, u32[]{:S(2)}, u32[]{:S(2)}) collective-permute-start(bf16[2,2,288,512]{3,2,0,1:T(8,128)(2,1)S(1)} %fusion), channel_id=1, source_target_pairs={{0,1},{1,0},{2,3},{3,2},{4,5},{5,4},{6,7},{7,6},{8,9},{9,8},{10,11... | collective-permute-start | bytes 3538952 | tf_op jit(solution)/shard_map/ppermute | solution.py:68
  529.6 36.7 %collective-permute-start.26 = (bf16[3,512,128]{2,1,0:T(8,128)(2,1)}, bf16[3,512,128]{2,1,0:T(8,128)(2,1)S(1)}, u32[]{:S(2)}, u32[]{:S(2)}) collective-permute-start(bf16[3,512,128]{2,1,0:T(8,128)(2,1)} %get-tuple-element.171), channel_id=1, source_target_pairs={{0,1},{1,0},{2,3},{3,2},{4,5},{5,4},{6,7},{7,6},{8,9},{9,8},{10,11... | collective-permute-start | bytes 1179656 | tf_op jit(solution)/shard_map/ppermute | solution.py:987
  531.0 40.0 %collective-permute-start.27 = (bf16[3,512,128]{2,1,0:T(8,128)(2,1)}, bf16[3,512,128]{2,1,0:T(8,128)(2,1)}, u32[]{:S(2)}, u32[]{:S(2)}) collective-permute-start(bf16[3,512,128]{2,1,0:T(8,128)(2,1)} %get-tuple-element.172), channel_id=1, source_target_pairs={{0,2},{1,3},{2,0},{3,1},{4,6},{5,7},{6,4},{7,5},{8,10},{9,11},{10,... | collective-permute-start | bytes 1179656 | tf_op jit(solution)/shard_map/ppermute | solution.py:987
  532.2 43.4 %collective-permute-start.28 = (bf16[3,512,128]{2,1,0:T(8,128)(2,1)}, bf16[3,512,128]{2,1,0:T(8,128)(2,1)}, u32[]{:S(2)}, u32[]{:S(2)}) collective-permute-start(bf16[3,512,128]{2,1,0:T(8,128)(2,1)} %get-tuple-element.173), channel_id=1, source_target_pairs={{0,3},{1,2},{2,1},{3,0},{4,7},{5,6},{6,5},{7,4},{8,11},{9,10},{10,... | collective-permute-start | bytes 1179656 | tf_op jit(solution)/shard_map/ppermute | solution.py:987
  555.5 27.8 %collective-permute-start.29 = (bf16[3,512,128]{2,1,0:T(8,128)(2,1)S(1)}, bf16[3,512,128]{2,1,0:T(8,128)(2,1)}, u32[]{:S(2)}, u32[]{:S(2)}) collective-permute-start(bf16[3,512,128]{2,1,0:T(8,128)(2,1)S(1)} %copy-done.62), channel_id=1, source_target_pairs={{0,1},{1,0},{2,3},{3,2},{4,5},{5,4},{6,7},{7,6},{8,9},{9,8},{10,11... | collective-permute-start | bytes 1179656 | tf_op jit(solution)/shard_map/ppermute | solution.py:987
  630.2 32.4 %all-to-all-start.3 = ((f32[32,16,192]{2,1,0:T(8,128)}), f32[32,16,192]{2,1,0:T(8,128)}, u32[]{:S(2)}, u32[]{:S(2)}) async-start(f32[32,16,192]{2,1,0:T(8,128)} %bitcast.145), calls=%async_computation.3 | async-start | bytes 1048576 | tf_op jit(solution)/shard_map/all_to_all | solution.py:1100
  639.1 34.6 %collective-permute-start.42 = (bf16[288,1024]{1,0:T(8,128)(2,1)}, bf16[288,1024]{1,0:T(8,128)(2,1)}, u32[]{:S(2)}, u32[]{:S(2)}) collective-permute-start(bf16[288,1024]{1,0:T(8,128)(2,1)} %fusion.10), channel_id=1, source_target_pairs={{0,16},{4,20},{8,24},{12,28},{16,0},{20,4},{24,8},{28,12},{1,17},{... | collective-permute-start | bytes 1769480 | tf_op jit(solution)/shard_map/ppermute | solution.py:145
  691.4 38.6 %all-to-all-start.5 = ((f32[32,4,1024]{2,1,0:T(4,128)}), f32[32,4,1024]{2,1,0:T(4,128)}, u32[]{:S(2)}, u32[]{:S(2)}) async-start(f32[32,4,1024]{2,1,0:T(4,128)} %broadcast_in_dim.17), calls=%async_computation.5 | async-start | bytes 1048576 | tf_op jit(solution)/shard_map/all_to_all | solution.py:1100
  (114 other events, 1478.4 us)
Sparse Core Ops, SparseCore 0:
  11.5 81.7 all-gather.4
  96.2 168.1 all-gather.2

commit v6 on v5

--- a/solution.py
+++ b/solution.py
@@ -75,7 +75,7 @@
     return lax.optimization_barrier((value, *others))[0]
 
 
-def scatter_steps(groups, name, by_frame, ready):
+def scatter_steps(groups, name, by_frame, ready, keep_ready=()):
     frame_bits = lax.axis_size("frame").bit_length() - 1
     row_bits = lax.axis_size("row").bit_length() - 1
     row, frame = lax.axis_index("row"), lax.axis_index("frame")
@@ -87,6 +87,7 @@
         send = send_sums(numbers, group, f"{name}_send_{at}")
         came.append(lax.ppermute(send, "frame", [(index, index ^ 1) for index in range(size)]))
         numbers = held(numbers, send)
+    numbers = held(numbers, *keep_ready)
     keep, send = keep_sums(numbers, groups, came, name + "_keep", by_frame)
     hold = yield send
     names = [("frame", bit) for bit in reversed(range(1, frame_bits))]
@@ -1181,7 +1182,7 @@
             parts += swap(slots)
             ready = [slots[0], *before[1:]]
         d_pieces.append(parts)
-    state = early.send([slots[0]])
+    state = []
     lasts = []
     for clip in clips:
         lasts.append(
@@ -1195,14 +1196,21 @@
     input_grad = jnp.concatenate([item[1] for item in lasts], axis=0).reshape(shape_five)
     one_sums = [item[2] for item in lasts]
     d_modulation = frame_sums(one_sums, two_sums)
-    late = scatter_steps([[([item[0] for item in lasts], hidden_one)]], "late", False, [d_modulation])
+    state = early.send([lasts[-1][2]])
+    late = scatter_steps(
+        [[([item[0] for item in lasts], hidden_one)]],
+        "late",
+        False,
+        [d_modulation],
+        state if isinstance(state, list) else (),
+    )
     late_state = next(late)
-    early_sum = finished(early, early.send(late_state))
-    state = late_state
-    g_qkv = finished(late, state)
+    late_row = late.send([])
+    early_sum = finished(early, early.send(late_row))
+    state = late.send([])
 
     mod_parts = to_all(jnp.moveaxis(d_modulation.reshape(frame_total, device_total, ada_width), 1, 0))
-    mod_parts = held(mod_parts, *late_state)
+    mod_parts = held(mod_parts, *late_row)
     mod_mine = (
         jnp.sum(mod_parts.reshape(frame_devices, row_devices, frame_total, ada_width), axis=1)
         .reshape(frames_all, ada_width)
@@ -1211,7 +1219,9 @@
     g_ada = jnp.einsum("fd,fe->de", cond_all, mod_mine, preferred_element_type=full_type)
     g_bias = jnp.sum(mod_mine.astype(full_type), axis=0)
     d_cond_parts = jnp.einsum("fe,de->fd", mod_mine, ada_low, preferred_element_type=full_type)
-    d_cond = jnp.sum(to_all(d_cond_parts.reshape(device_total, frames_each, model_width)), axis=0)
+    d_cond = to_all(d_cond_parts.reshape(device_total, frames_each, model_width))
+    d_cond = jnp.sum(held(d_cond, *state) if isinstance(state, list) else d_cond, axis=0)
+    g_qkv = finished(late, state)
     d_embedded_mine = jax.vjp(jax.nn.silu, embedded_mine)[1](d_cond)[0]
     d_embedded = from_all(d_embedded_mine).reshape(frames_all, model_width)
     g_table = jnp.dot(level_hot.astype(full_type).T, d_embedded, precision=highest)

time: 941 us -> 930 us (0.988)
  waiting for transfers between devices: 286 us -> 275 us
    ppermute x27, waiting for transfers between devices: 83.5 us -> 54.8 us  [swap(): lax.ppermute(slots[slot], 'row', [(index, index ^ slot) for index in rang...]
    all_to_all x6, waiting for transfers between devices: 40.4 us -> 52.1 us  [to_all(): return lax.all_to_all(value, both, split_axis=0, concat_axis=0, tiled=True)]
  transfers between devices with their start and end apart: 63 -> 63, of which waited for: 30 -> 25; matrix products, arithmetic and copies ran while one was open for 7% -> 7% of each run, Pallas kernels for 28% -> 28%
where the time goes in v6:
time: 930 us; the launch traced here: 926 us
  Pallas kernels  408 us (44%)
  waiting for transfers between devices  275 us (30%)
  starting transfers between devices  92.7 us (10%)
  other arithmetic  48.5 us (5%)
  local copies, waits for them, and re-layouts  45.4 us (5%)
  blocking collectives  28.8 us (3%)
  between operations  23.5 us (3%)
    pallas_call x3, Pallas kernels, attend_back(): pl.pallas_call(functools.partial(attend_back_kernel, slots, 512), grid=(c...  107 us
    pallas_call x1, Pallas kernels, newton(): pl.pallas_call(functools.partial(newton_kernel, rows, unroll, pieces), ou...  70.1 us
    pallas_call x2, Pallas kernels, middle(): pl.pallas_call(functools.partial(middle_kernel, slots), grid=(steps,), in...  66.6 us
    pallas_call x2, Pallas kernels, attend(): pl.pallas_call(functools.partial(attend_kernel, slots, 256), grid=(group...  64.3 us
    ppermute x27, waiting for transfers between devices, swap(): lax.ppermute(slots[slot], 'row', [(index, index ^ slot) for index in rang...  54.8 us
    all_to_all x6, waiting for transfers between devices, to_all(): return lax.all_to_all(value, both, split_axis=0, concat_axis=0, tiled=True)  52.1 us
    ppermute x6, waiting for transfers between devices, frame_swap(): out.append(lax.ppermute(slots[slot], 'frame', pairs))  41.8 us
    ppermute x9, waiting for transfers between devices, joined(): lax.ppermute(send, axis, [(index, index ^ 1 << bit) for index in range(si...  40 us
  transfers between devices with their start and end apart: 63, of which 25 were waited for; matrix products, arithmetic and copies ran while one was open for 7% of the time, Pallas kernels for 28%

profile of v6, /device:TPU:8, one launch (start us, length us, event | category | flops | bytes accessed | tf_op | source)
XLA Modules:
  0.0 925.7 jit_solution(6628580860613639392)
XLA Ops:
  14.1 8.4 all-reduce.2
  24.1 20.3 %all_to_all.35 = f32[32,4,1024]{2,1,0:T(4,128)S(1)} all-to-all(f32[32,4,1024]{2,1,0:T(4,128)S(1)} %reshape.250), channel_id=1, replica_groups=mesh['frame'=8,'row'=4] {'frame','row'}, dimensions={0} | all-to-all | bytes 1048576 | tf_op jit(solution)/shard_map/all_to_all | solution.py:1101
  50.5 17.7 %all-to-all-done.1 = f32[32,4,1024]{2,1,0:T(4,128)S(1)} async-done(((f32[32,4,1024]{2,1,0:T(4,128)}), f32[32,4,1024]{2,1,0:T(4,128)S(1)}, u32[]{:S(2)}, u32[]{:S(2)}) %all-to-all-start.1) | async-done | bytes 524320 | tf_op jit(solution)/shard_map/all_to_all | solution.py:1101
  79.3 16.3 %all-to-all-done.2 = f32[32,16,192]{2,1,0:T(8,128)S(1)} async-done(((f32[32,16,192]{2,1,0:T(8,128)}), f32[32,16,192]{2,1,0:T(8,128)S(1)}, u32[]{:S(2)}, u32[]{:S(2)}) %all-to-all-start.2) | async-done | bytes 393248 | tf_op jit(solution)/shard_map/all_to_all | solution.py:1101
  96.9 9.0 project.2
  110.1 9.1 project.3
  130.5 31.1 %collective-permute-done.2.refs_3_ = bf16[3,512,256]{2,1,0:T(8,128)(2,1)} collective-permute-done((bf16[3,512,256]{2,1,0:T(8,128)(2,1)}, bf16[3,512,256]{2,1,0:T(8,128)(2,1)}, u32[]{:S(2)}, u32[]{:S(2)}) %collective-permute-start.2) | collective-permute-done | bytes 786464 | tf_op jit(solution)/shard_map/ppermute | solution.py:988
  161.6 32.1 %attend.2 = (bf16[512,256]{1,0:T(8,128)(2,1)}, bf16[512,256]{1,0:T(8,128)(2,1)}, bf16[512,256]{1,0:T(8,128)(2,1)}, bf16[512,256]{1,0:T(8,128)(2,1)}, f32[2048,256]{1,0:T(8,128)}, /*index=5*/f32[2048,256]{1,0:T(8,128)}) custom-call(bf16[3,512,256]{2,1,0:T(8,128)(2,1)} %get-tuple-element.108.refs_0_, bf16[3,512,256]{2,1,0:T(8,128)(2,1)} %copy-done.60, ...), custom_call_target="tpu_custom_call" | custom-call | flops 17179869184 | bytes 8388608 | tf_op jit(solution)/shard_map/attend/pallas_call | solution.py:303
  197.3 13.1 %collective-permute-done.8.refs_3_ = bf16[3,512,256]{2,1,0:T(8,128)(2,1)S(1)} collective-permute-done((bf16[3,512,256]{2,1,0:T(8,128)(2,1)}, bf16[3,512,256]{2,1,0:T(8,128)(2,1)S(1)}, u32[]{:S(2)}, u32[]{:S(2)}) %collective-permute-start.8) | collective-permute-done | bytes 786464 | tf_op jit(solution)/shard_map/ppermute | solution.py:988
  211.3 32.1 %attend.3 = (bf16[512,256]{1,0:T(8,128)(2,1)}, bf16[512,256]{1,0:T(8,128)(2,1)}, bf16[512,256]{1,0:T(8,128)(2,1)}, bf16[512,256]{1,0:T(8,128)(2,1)}, f32[2048,256]{1,0:T(8,128)}, /*index=5*/f32[2048,256]{1,0:T(8,128)}) custom-call(bf16[3,512,256]{2,1,0:T(8,128)(2,1)} %get-tuple-element.117.refs_0_, bf16[3,512,256]{2,1,0:T(8,128)(2,1)} %copy-done.57, ...), custom_call_target="tpu_custom_call" | custom-call | flops 17179869184 | bytes 8388608 | tf_op jit(solution)/shard_map/attend/pallas_call | solution.py:303
  247.0 16.8 %all-gather.3.cloned.1.call-done.wo_ref.wu_ref.wd_ref = bf16[32,288,1024]{2,1,0:T(8,128)(2,1)} async-done(((bf16[1,288,1024]{2,1,0:T(8,128)(2,1)}), bf16[32,288,1024]{2,1,0:T(8,128)(2,1)}) %all-gather.3.cloned.1.call-update) | async-done | bytes 18874384 | tf_op jit(solution)/shard_map/all_gather | solution.py:1068
  263.8 33.5 %middle.2 = (bf16[512,256]{1,0:T(8,128)(2,1)}, bf16[512,256]{1,0:T(8,128)(2,1)}, bf16[512,256]{1,0:T(8,128)(2,1)}, bf16[512,256]{1,0:T(8,128)(2,1)}, bf16[1,512,...) custom-call(s32[1]{0:T(128)} %bitcast.me_ref, ...), custom_call_target="tpu_custom_call" | custom-call | flops 19327352832 | bytes 41943040 | tf_op jit(solution)/shard_map/middle/pallas_call | solution.py:509
  298.2 33.1 %middle.3 = (bf16[512,256]{1,0:T(8,128)(2,1)}, bf16[512,256]{1,0:T(8,128)(2,1)}, bf16[512,256]{1,0:T(8,128)(2,1)}, bf16[512,256]{1,0:T(8,128)(2,1)}, bf16[1,512,...) custom-call(s32[1]{0:T(128)} %bitcast.me_ref, ...), custom_call_target="tpu_custom_call" | custom-call | flops 19327352832 | bytes 41943040 | tf_op jit(solution)/shard_map/middle/pallas_call | solution.py:509
  331.3 9.1 early_send_0.1
  340.4 11.4 %early_send_1.1 = bf16[4,4,160,1024]{3,2,1,0:T(8,128)(2,1)} custom-call(s32[4]{0:T(128)} %pad_add_fusion.number_ref, bf16[512,4096]{1,0:T(8,128)(2,1)} %get-tuple-element.133.refs_0_.refs_4_, bf16[512,4096]{1,0:T(8,128)(2,1)} %get-tuple-element.134.refs_1_.refs_5_, bf16[512,1024]{1,0:T(8,128)(2,1)} %get-tuple-element.135.refs_2_.refs_6_, ...), custom_call_target="tpu_custom_call" | custom-call | flops 5368709120 | bytes 20971520 | tf_op jit(solution)/shard_map/early_send_1/pallas_call | solution.py:729
  355.8 11.0 %collective-permute-done.12.refs_12_ = bf16[4,4,128,1024]{3,2,1,0:T(8,128)(2,1)} collective-permute-done((bf16[4,4,128,1024]{3,2,1,0:T(8,128)(2,1)}, bf16[4,4,128,1024]{3,2,1,0:T(8,128)(2,1)}, u32[]{:S(2)}, u32[]{:S(2)}) %collective-permute-start.12) | collective-permute-done | bytes 4194336 | tf_op jit(solution)/shard_map/ppermute | solution.py:88
  368.1 22.9 %early_keep.1 = (f32[2,4,288,1024]{3,2,1,0:T(8,128)}, bf16[2,4,288,1024]{3,2,1,0:T(8,128)(2,1)}) custom-call(s32[4]{0:T(128)} %pad_add_fusion.number_ref, bf16[512,4096]{1,0:T(8,128)(2,1)} %get-tuple-element.128.refs_0_, bf16[512,4096]{1,0:T(8,128)(2,1)} %get-tuple-element.129.refs_1_, bf16[512,1024]{1,0:T(8,128)(2,1)} %get-tuple-element.130.refs_2_, ...), custom_call_target="tpu_custom_call" | custom-call | flops 9663676416 | bytes 41943040 | tf_op jit(solution)/shard_map/early_keep/pallas_call | solution.py:758
  395.7 51.8 %attend_back.3 = (bf16[3,512,256]{2,1,0:T(8,128)(2,1)}, bf16[3,512,256]{2,1,0:T(8,128)(2,1)}, bf16[3,512,256]{2,1,0:T(8,128)(2,1)}, bf16[3,512,256]{2,1,0:T(8,128)(2,1)}) custom-call(bf16[3,512,256]{2,1,0:T(8,128)(2,1)} %get-tuple-element.108.refs_0_, bf16[3,512,256]{2,1,0:T(8,128)(2,1)} %copy-done.60, bf16[3,512,256]{2,1,0:T(8,128)(2,1)} %copy-done.61, ...), custom_call_target="tpu_custom_call" | custom-call | flops 42949672960 | bytes 12582912 | tf_op jit(solution)/shard_map/attend_back/pallas_call | solution.py:393
  451.8 27.5 %attend_back.4 = (bf16[3,512,128]{2,1,0:T(8,128)(2,1)}, bf16[3,512,128]{2,1,0:T(8,128)(2,1)}, bf16[3,512,128]{2,1,0:T(8,128)(2,1)}, bf16[3,512,128]{2,1,0:T(8,128)(2,1)}) custom-call(bf16[3,512,256]{2,1,0:T(8,128)(2,1)} %get-tuple-element.117.refs_0_, bf16[3,512,256]{2,1,0:T(8,128)(2,1)} %copy-done.57, bf16[3,512,256]{2,1,0:T(8,128)(2,1)} %copy-done.58, ...), custom_call_target="tpu_custom_call" | custom-call | flops 21474836480 | bytes 12582912 | tf_op jit(solution)/shard_map/attend_back/pallas_call | solution.py:393
  485.4 28.1 %attend_back.5 = (bf16[3,512,128]{2,1,0:T(8,128)(2,1)}, bf16[3,512,128]{2,1,0:T(8,128)(2,1)}, bf16[3,512,128]{2,1,0:T(8,128)(2,1)}, bf16[3,512,128]{2,1,0:T(8,128)(2,1)}) custom-call(bf16[3,512,256]{2,1,0:T(8,128)(2,1)} %get-tuple-element.117.refs_0_, bf16[3,512,256]{2,1,0:T(8,128)(2,1)} %copy-done.57, bf16[3,512,256]{2,1,0:T(8,128)(2,1)} %copy-done.58, ...), custom_call_target="tpu_custom_call" | custom-call | flops 21474836480 | bytes 12582912 | tf_op jit(solution)/shard_map/attend_back/pallas_call | solution.py:393
  514.3 9.9 %last.2 = (bf16[512,3072]{1,0:T(8,128)(2,1)}, f32[1,512,1024]{2,1,0:T(8,128)}, f32[2,2,4,1024]{3,2,1,0:T(4,128)}) custom-call(s32[1]{0:T(128)} %bitcast.me_ref, bf16[2,512,1024]{2,1,0:T(8,128)(2,1)} %bitcast.151, f32[4,4,6144]{2,1,0:T(4,128)} %reshape_reshape.4.mod_ref, f32[1024,128]{1,0:T(8,128)} %copy.139.cos_ref, ...), custom_call_target="tpu_custom_call" | custom-call | flops 3221225472 | bytes 20971520 | tf_op jit(solution)/shard_map/last/pallas_call | solution.py:590
  540.9 9.9 %last.3 = (bf16[512,3072]{1,0:T(8,128)(2,1)}, f32[1,512,1024]{2,1,0:T(8,128)}, f32[2,2,4,1024]{3,2,1,0:T(4,128)}) custom-call(s32[1]{0:T(128)} %bitcast.me_ref, bf16[2,512,1024]{2,1,0:T(8,128)(2,1)} %bitcast.152, f32[4,4,6144]{2,1,0:T(4,128)} %reshape_reshape.4.mod_ref, f32[1024,128]{1,0:T(8,128)} %copy.139.cos_ref, ...), custom_call_target="tpu_custom_call" | custom-call | flops 3221225472 | bytes 20971520 | tf_op jit(solution)/shard_map/last/pallas_call | solution.py:590
  567.2 22.2 %collective-permute-done.31 = bf16[2,2,288,512]{3,2,0,1:T(8,128)(2,1)} collective-permute-done((bf16[2,2,288,512]{3,2,0,1:T(8,128)(2,1)S(1)}, bf16[2,2,288,512]{3,2,0,1:T(8,128)(2,1)}, u32[]{:S(2)}, u32[]{:S(2)}) %collective-permute-start.31) | collective-permute-done | bytes 1179680 | tf_op jit(solution)/shard_map/ppermute | solution.py:68
  595.9 8.9 late_keep.1
  619.9 12.0 %collective-permute-done.33 = bf16[2,2,2,96,512]{4,3,1,0,2:T(8,128)(2,1)} collective-permute-done((bf16[2,2,2,96,512]{4,3,1,0,2:T(8,128)(2,1)}, bf16[2,2,2,96,512]{4,3,1,0,2:T(8,128)(2,1)}, u32[]{:S(2)}, u32[]{:S(2)}) %collective-permute-start.33) | collective-permute-done | bytes 786464 | tf_op jit(solution)/shard_map/ppermute | solution.py:68
  662.9 12.6 %all-to-all-done.4 = f32[32,4,1024]{2,1,0:T(4,128)} async-done(((f32[32,4,1024]{2,1,0:T(4,128)}), f32[32,4,1024]{2,1,0:T(4,128)}, u32[]{:S(2)}, u32[]{:S(2)}) %all-to-all-start.4) | async-done | bytes 524320 | tf_op jit(solution)/shard_map/all_to_all | solution.py:1101
  698.0 10.4 %collective-permute-done.38 = bf16[96,1024]{1,0:T(8,128)(2,1)S(1)} collective-permute-done((bf16[96,1024]{1,0:T(8,128)(2,1)}, bf16[96,1024]{1,0:T(8,128)(2,1)S(1)}, u32[]{:S(2)}, u32[]{:S(2)}) %collective-permute-start.38) | collective-permute-done | bytes 196640 | tf_op jit(solution)/shard_map/ppermute | solution.py:146
  743.7 14.0 %collective-permute-done.46 = bf16[128,1024]{1,0:T(8,128)(2,1)S(1)} collective-permute-done((bf16[128,1024]{1,0:T(8,128)(2,1)S(1)}, bf16[128,1024]{1,0:T(8,128)(2,1)S(1)}, u32[]{:S(2)}, u32[]{:S(2)}) %collective-permute-start.46) | collective-permute-done | bytes 262176 | tf_op jit(solution)/shard_map/ppermute | solution.py:997
  766.5 12.5 %collective-permute-done.48 = bf16[256,1024]{1,0:T(8,128)(2,1)S(1)} collective-permute-done((bf16[256,1024]{1,0:T(8,128)(2,1)S(1)}, bf16[256,1024]{1,0:T(8,128)(2,1)S(1)}, u32[]{:S(2)}, u32[]{:S(2)}) %collective-permute-start.48) | collective-permute-done | bytes 524320 | tf_op jit(solution)/shard_map/ppermute | solution.py:1022
  783.3 20.1 %collective-permute-done.49 = bf16[512,1024]{1,0:T(8,128)(2,1)S(1)} collective-permute-done((bf16[512,1024]{1,0:T(8,128)(2,1)S(1)}, bf16[512,1024]{1,0:T(8,128)(2,1)S(1)}, u32[]{:S(2)}, u32[]{:S(2)}) %collective-permute-start.49) | collective-permute-done | bytes 1048608 | tf_op jit(solution)/shard_map/ppermute | solution.py:1022
  814.3 70.1 %newton.1 = bf16[512,1024]{1,0:T(8,128)(2,1)} custom-call(bf16[1024,1024]{1,0:T(8,128)(2,1)} %copy-done.18, bf16[1024,1024]{1,0:T(8,128)(2,1)} %constant_dynamic-update-slice_fusion.refs_1_, bf16[1024,1024]{1,0:T(8,128)(2,1)} %collective-permute-done.50.refs_2_, bf16[1024,1024]{1,0:T(8,128)(2,1)} %collective-permute-done.51.refs_3_), custom_call_target="tpu_custom_call" | custom-call | flops 60000002048 | bytes 20000000 | tf_op jit(solution)/shard_map/newton/pallas_call | solution.py:941
  899.7 12.6 %collective-permute-done.54 = bf16[128,1024]{1,0:T(8,128)(2,1)S(1)} collective-permute-done((bf16[128,1024]{1,0:T(8,128)(2,1)S(1)}, bf16[128,1024]{1,0:T(8,128)(2,1)S(1)}, u32[]{:S(2)}, u32[]{:S(2)}) %collective-permute-start.54) | collective-permute-done | bytes 262176 | tf_op jit(solution)/shard_map/ppermute | solution.py:997
  (407 shorter events, 252.7 us)
Async XLA Ops:
  7.2 89.7 %all-gather.5.cloned.1.call-start = ((), (), s32[]{:S(2)}) async-start(), calls=%async_computation.8 | async-start | bytes 6488064 | tf_op jit(solution)/shard_map/all_gather | solution.py:1066
  9.0 254.8 %all-gather.3.cloned.1.call-start = ((), (), s32[]{:S(2)}) async-start(), calls=%async_computation.7 | async-start | bytes 19464192 | tf_op jit(solution)/shard_map/all_gather | solution.py:1068
  107.7 53.9 %collective-permute-start.2 = (bf16[3,512,256]{2,1,0:T(8,128)(2,1)}, bf16[3,512,256]{2,1,0:T(8,128)(2,1)}, u32[]{:S(2)}, u32[]{:S(2)}) collective-permute-start(bf16[3,512,256]{2,1,0:T(8,128)(2,1)} %get-tuple-element.111), channel_id=1, source_target_pairs={{0,3},{1,2},{2,1},{3,0},{4,7},{5,6},{6,5},{7,4},{8,11},{9,10},{10,... | collective-permute-start | bytes 2359304 | tf_op jit(solution)/shard_map/ppermute | solution.py:988
  119.2 75.3 %collective-permute-start.6 = (bf16[3,512,256]{2,1,0:T(8,128)(2,1)}, bf16[3,512,256]{2,1,0:T(8,128)(2,1)S(1)}, u32[]{:S(2)}, u32[]{:S(2)}) collective-permute-start(bf16[3,512,256]{2,1,0:T(8,128)(2,1)} %get-tuple-element.118), channel_id=1, source_target_pairs={{0,1},{1,0},{2,3},{3,2},{4,5},{5,4},{6,7},{7,6},{8,9},{9,8},{10,11... | collective-permute-start | bytes 2359304 | tf_op jit(solution)/shard_map/ppermute | solution.py:988
  119.5 77.8 %collective-permute-start.7 = (bf16[3,512,256]{2,1,0:T(8,128)(2,1)}, bf16[3,512,256]{2,1,0:T(8,128)(2,1)S(1)}, u32[]{:S(2)}, u32[]{:S(2)}) collective-permute-start(bf16[3,512,256]{2,1,0:T(8,128)(2,1)} %get-tuple-element.119), channel_id=1, source_target_pairs={{0,2},{1,3},{2,0},{3,1},{4,6},{5,7},{6,4},{7,5},{8,10},{9,11},{10,... | collective-permute-start | bytes 2359304 | tf_op jit(solution)/shard_map/ppermute | solution.py:988
  128.8 81.6 %collective-permute-start.8 = (bf16[3,512,256]{2,1,0:T(8,128)(2,1)}, bf16[3,512,256]{2,1,0:T(8,128)(2,1)S(1)}, u32[]{:S(2)}, u32[]{:S(2)}) collective-permute-start(bf16[3,512,256]{2,1,0:T(8,128)(2,1)} %get-tuple-element.120), channel_id=1, source_target_pairs={{0,3},{1,2},{2,1},{3,0},{4,7},{5,6},{6,5},{7,4},{8,11},{9,10},{10,... | collective-permute-start | bytes 2359304 | tf_op jit(solution)/shard_map/ppermute | solution.py:988
  193.8 51.6 %collective-permute-start.3 = (bf16[512,256]{1,0:T(8,128)(2,1)}, bf16[512,256]{1,0:T(8,128)(2,1)S(1)}, u32[]{:S(2)}, u32[]{:S(2)}) collective-permute-start(bf16[512,256]{1,0:T(8,128)(2,1)} %get-tuple-element.113), channel_id=1, source_target_pairs={{0,1},{1,0},{2,3},{3,2},{4,5},{5,4},{6,7},{7,6},{8,9},{9,8},{10,11... | collective-permute-start | bytes 786440 | tf_op jit(solution)/shard_map/ppermute | solution.py:988
  194.2 52.8 %collective-permute-start.4 = (bf16[512,256]{1,0:T(8,128)(2,1)}, bf16[512,256]{1,0:T(8,128)(2,1)S(1)}, u32[]{:S(2)}, u32[]{:S(2)}) collective-permute-start(bf16[512,256]{1,0:T(8,128)(2,1)} %get-tuple-element.114), channel_id=1, source_target_pairs={{0,2},{1,3},{2,0},{3,1},{4,6},{5,7},{6,4},{7,5},{8,10},{9,11},{10,... | collective-permute-start | bytes 786440 | tf_op jit(solution)/shard_map/ppermute | solution.py:988
  194.5 52.5 %collective-permute-start.5 = (bf16[512,256]{1,0:T(8,128)(2,1)}, bf16[512,256]{1,0:T(8,128)(2,1)S(1)}, u32[]{:S(2)}, u32[]{:S(2)}) collective-permute-start(bf16[512,256]{1,0:T(8,128)(2,1)} %get-tuple-element.115), channel_id=1, source_target_pairs={{0,3},{1,2},{2,1},{3,0},{4,7},{5,6},{6,5},{7,4},{8,11},{9,10},{10,... | collective-permute-start | bytes 786440 | tf_op jit(solution)/shard_map/ppermute | solution.py:988
  243.4 53.9 %collective-permute-start.10 = (bf16[512,256]{1,0:T(8,128)(2,1)}, bf16[512,256]{1,0:T(8,128)(2,1)S(1)}, u32[]{:S(2)}, u32[]{:S(2)}) collective-permute-start(bf16[512,256]{1,0:T(8,128)(2,1)} %get-tuple-element.123), channel_id=1, source_target_pairs={{0,2},{1,3},{2,0},{3,1},{4,6},{5,7},{6,4},{7,5},{8,10},{9,11},{10,... | collective-permute-start | bytes 786440 | tf_op jit(solution)/shard_map/ppermute | solution.py:988
  243.5 53.8 %collective-permute-start.11 = (bf16[512,256]{1,0:T(8,128)(2,1)}, bf16[512,256]{1,0:T(8,128)(2,1)S(1)}, u32[]{:S(2)}, u32[]{:S(2)}) collective-permute-start(bf16[512,256]{1,0:T(8,128)(2,1)} %get-tuple-element.124), channel_id=1, source_target_pairs={{0,3},{1,2},{2,1},{3,0},{4,7},{5,6},{6,5},{7,4},{8,11},{9,10},{10,... | collective-permute-start | bytes 786440 | tf_op jit(solution)/shard_map/ppermute | solution.py:988
  245.3 52.0 %collective-permute-start.9 = (bf16[512,256]{1,0:T(8,128)(2,1)}, bf16[512,256]{1,0:T(8,128)(2,1)S(1)}, u32[]{:S(2)}, u32[]{:S(2)}) collective-permute-start(bf16[512,256]{1,0:T(8,128)(2,1)} %get-tuple-element.122), channel_id=1, source_target_pairs={{0,1},{1,0},{2,3},{3,2},{4,5},{5,4},{6,7},{7,6},{8,9},{9,8},{10,11... | collective-permute-start | bytes 786440 | tf_op jit(solution)/shard_map/ppermute | solution.py:988
  352.3 38.7 %collective-permute-start.14 = (bf16[512,256]{1,0:T(8,128)(2,1)S(1)}, bf16[512,256]{1,0:T(8,128)(2,1)S(1)}, u32[]{:S(2)}, u32[]{:S(2)}) collective-permute-start(bf16[512,256]{1,0:T(8,128)(2,1)S(1)} %copy-done.69), channel_id=1, source_target_pairs={{0,1},{1,0},{2,3},{3,2},{4,5},{5,4},{6,7},{7,6},{8,9},{9,8},{10,11... | collective-permute-start | bytes 786440 | tf_op jit(solution)/shard_map/ppermute | solution.py:988
  352.9 40.5 %collective-permute-start.15 = (bf16[512,256]{1,0:T(8,128)(2,1)S(1)}, bf16[512,256]{1,0:T(8,128)(2,1)S(1)}, u32[]{:S(2)}, u32[]{:S(2)}) collective-permute-start(bf16[512,256]{1,0:T(8,128)(2,1)S(1)} %copy-done.67), channel_id=1, source_target_pairs={{0,2},{1,3},{2,0},{3,1},{4,6},{5,7},{6,4},{7,5},{8,10},{9,11},{10,... | collective-permute-start | bytes 786440 | tf_op jit(solution)/shard_map/ppermute | solution.py:988
  353.5 41.5 %collective-permute-start.16 = (bf16[512,256]{1,0:T(8,128)(2,1)S(1)}, bf16[512,256]{1,0:T(8,128)(2,1)S(1)}, u32[]{:S(2)}, u32[]{:S(2)}) collective-permute-start(bf16[512,256]{1,0:T(8,128)(2,1)S(1)} %copy-done.64), channel_id=1, source_target_pairs={{0,3},{1,2},{2,1},{3,0},{4,7},{5,6},{6,5},{7,4},{8,11},{9,10},{10,... | collective-permute-start | bytes 786440 | tf_op jit(solution)/shard_map/ppermute | solution.py:988
  366.8 81.2 %collective-permute-start.20 = (bf16[512,256]{1,0:T(8,128)(2,1)S(1)}, bf16[512,256]{1,0:T(8,128)(2,1)S(1)}, u32[]{:S(2)}, u32[]{:S(2)}) collective-permute-start(bf16[512,256]{1,0:T(8,128)(2,1)S(1)} %copy-done.66), channel_id=1, source_target_pairs={{0,1},{1,0},{2,3},{3,2},{4,5},{5,4},{6,7},{7,6},{8,9},{9,8},{10,11... | collective-permute-start | bytes 786440 | tf_op jit(solution)/shard_map/ppermute | solution.py:988
  367.4 81.7 %collective-permute-start.21 = (bf16[512,256]{1,0:T(8,128)(2,1)S(1)}, bf16[512,256]{1,0:T(8,128)(2,1)S(1)}, u32[]{:S(2)}, u32[]{:S(2)}) collective-permute-start(bf16[512,256]{1,0:T(8,128)(2,1)S(1)} %copy-done.63), channel_id=1, source_target_pairs={{0,2},{1,3},{2,0},{3,1},{4,6},{5,7},{6,4},{7,5},{8,10},{9,11},{10,... | collective-permute-start | bytes 786440 | tf_op jit(solution)/shard_map/ppermute | solution.py:988
  391.0 60.1 %collective-permute-start.22 = (bf16[512,256]{1,0:T(8,128)(2,1)S(1)}, bf16[512,256]{1,0:T(8,128)(2,1)S(1)}, u32[]{:S(2)}, u32[]{:S(2)}) collective-permute-start(bf16[512,256]{1,0:T(8,128)(2,1)S(1)} %copy-done.62), channel_id=1, source_target_pairs={{0,3},{1,2},{2,1},{3,0},{4,7},{5,6},{6,5},{7,4},{8,11},{9,10},{10,... | collective-permute-start | bytes 786440 | tf_op jit(solution)/shard_map/ppermute | solution.py:988
  393.4 130.8 %collective-permute-start.23 = (bf16[2,4,288,1024]{3,2,1,0:T(8,128)(2,1)}, bf16[2,4,288,1024]{3,2,1,0:T(8,128)(2,1)}, u32[]{:S(2)}, u32[]{:S(2)}) collective-permute-start(bf16[2,4,288,1024]{3,2,1,0:T(8,128)(2,1)} %get-tuple-element.142), channel_id=1, source_target_pairs={{0,8},{4,12},{8,0},{12,4},{16,24},{20,28},{24,16},{28,20},{1,9},{5... | collective-permute-start | bytes 14155784 | tf_op jit(solution)/shard_map/ppermute | solution.py:68
  447.5 32.2 %collective-permute-start.17 = (bf16[3,512,256]{2,1,0:T(8,128)(2,1)}, bf16[3,512,256]{2,1,0:T(8,128)(2,1)S(1)}, u32[]{:S(2)}, u32[]{:S(2)}) collective-permute-start(bf16[3,512,256]{2,1,0:T(8,128)(2,1)} %get-tuple-element.150), channel_id=1, source_target_pairs={{0,1},{1,0},{2,3},{3,2},{4,5},{5,4},{6,7},{7,6},{8,9},{9,8},{10,11... | collective-permute-start | bytes 2359304 | tf_op jit(solution)/shard_map/ppermute | solution.py:988
  448.0 32.7 %collective-permute-start.18 = (bf16[3,512,256]{2,1,0:T(8,128)(2,1)}, bf16[3,512,256]{2,1,0:T(8,128)(2,1)S(1)}, u32[]{:S(2)}, u32[]{:S(2)}) collective-permute-start(bf16[3,512,256]{2,1,0:T(8,128)(2,1)} %get-tuple-element.151), channel_id=1, source_target_pairs={{0,2},{1,3},{2,0},{3,1},{4,6},{5,7},{6,4},{7,5},{8,10},{9,11},{10,... | collective-permute-start | bytes 2359304 | tf_op jit(solution)/shard_map/ppermute | solution.py:988
  449.1 36.3 %collective-permute-start.19 = (bf16[3,512,256]{2,1,0:T(8,128)(2,1)}, bf16[3,512,256]{2,1,0:T(8,128)(2,1)S(1)}, u32[]{:S(2)}, u32[]{:S(2)}) collective-permute-start(bf16[3,512,256]{2,1,0:T(8,128)(2,1)} %get-tuple-element.152), channel_id=1, source_target_pairs={{0,3},{1,2},{2,1},{3,0},{4,7},{5,6},{6,5},{7,4},{8,11},{9,10},{10,... | collective-permute-start | bytes 2359304 | tf_op jit(solution)/shard_map/ppermute | solution.py:988
  479.3 52.6 %collective-permute-start.24 = (bf16[3,512,128]{2,1,0:T(8,128)(2,1)}, bf16[3,512,128]{2,1,0:T(8,128)(2,1)S(1)}, u32[]{:S(2)}, u32[]{:S(2)}) collective-permute-start(bf16[3,512,128]{2,1,0:T(8,128)(2,1)} %get-tuple-element.167), channel_id=1, source_target_pairs={{0,1},{1,0},{2,3},{3,2},{4,5},{5,4},{6,7},{7,6},{8,9},{9,8},{10,11... | collective-permute-start | bytes 1179656 | tf_op jit(solution)/shard_map/ppermute | solution.py:988
  479.7 57.4 %collective-permute-start.25 = (bf16[3,512,128]{2,1,0:T(8,128)(2,1)}, bf16[3,512,128]{2,1,0:T(8,128)(2,1)}, u32[]{:S(2)}, u32[]{:S(2)}) collective-permute-start(bf16[3,512,128]{2,1,0:T(8,128)(2,1)} %get-tuple-element.168), channel_id=1, source_target_pairs={{0,2},{1,3},{2,0},{3,1},{4,6},{5,7},{6,4},{7,5},{8,10},{9,11},{10,... | collective-permute-start | bytes 1179656 | tf_op jit(solution)/shard_map/ppermute | solution.py:988
  480.8 57.9 %collective-permute-start.26 = (bf16[3,512,128]{2,1,0:T(8,128)(2,1)}, bf16[3,512,128]{2,1,0:T(8,128)(2,1)}, u32[]{:S(2)}, u32[]{:S(2)}) collective-permute-start(bf16[3,512,128]{2,1,0:T(8,128)(2,1)} %get-tuple-element.169), channel_id=1, source_target_pairs={{0,3},{1,2},{2,1},{3,0},{4,7},{5,6},{6,5},{7,4},{8,11},{9,10},{10,... | collective-permute-start | bytes 1179656 | tf_op jit(solution)/shard_map/ppermute | solution.py:988
  560.8 35.2 %collective-permute-start.32 = (bf16[4,4,96,1024]{3,2,1,0:T(8,128)(2,1)}, bf16[4,4,96,1024]{3,2,1,0:T(8,128)(2,1)}, u32[]{:S(2)}, u32[]{:S(2)}) collective-permute-start(bf16[4,4,96,1024]{3,2,1,0:T(8,128)(2,1)} %late_send_0.1), channel_id=1, source_target_pairs={{0,4},{4,0},{8,12},{12,8},{16,20},{20,16},{24,28},{28,24},{1,5},{5... | collective-permute-start | bytes 9437192 | tf_op jit(solution)/shard_map/ppermute | solution.py:88
  562.0 30.0 %collective-permute-start.30 = (bf16[2,2,288,512]{3,2,0,1:T(8,128)(2,1)S(1)}, bf16[2,2,288,512]{3,2,0,1:T(8,128)(2,1)}, u32[]{:S(2)}, u32[]{:S(2)}) collective-permute-start(bf16[2,2,288,512]{3,2,0,1:T(8,128)(2,1)S(1)} %fusion), channel_id=1, source_target_pairs={{0,1},{1,0},{2,3},{3,2},{4,5},{5,4},{6,7},{7,6},{8,9},{9,8},{10,11... | collective-permute-start | bytes 3538952 | tf_op jit(solution)/shard_map/ppermute | solution.py:68
  616.7 30.4 %collective-permute-start.41 = (bf16[2,288,512]{2,1,0:T(8,128)(2,1)}, bf16[2,288,512]{2,1,0:T(8,128)(2,1)}, u32[]{:S(2)}, u32[]{:S(2)}) collective-permute-start(bf16[2,288,512]{2,1,0:T(8,128)(2,1)} %fusion.9), channel_id=1, source_target_pairs={{0,1},{1,0},{2,3},{3,2},{4,5},{5,4},{6,7},{7,6},{8,9},{9,8},{10,11... | collective-permute-start | bytes 1769480 | tf_op jit(solution)/shard_map/ppermute | solution.py:68
  618.2 30.1 %collective-permute-start.40 = (bf16[2,288,512]{2,1,0:T(8,128)(2,1)}, bf16[2,288,512]{2,1,0:T(8,128)(2,1)}, u32[]{:S(2)}, u32[]{:S(2)}) collective-permute-start(bf16[2,288,512]{2,1,0:T(8,128)(2,1)} %fusion.8), channel_id=1, source_target_pairs={{0,2},{1,3},{2,0},{3,1},{4,6},{5,7},{6,4},{7,5},{8,10},{9,11},{10,... | collective-permute-start | bytes 1769480 | tf_op jit(solution)/shard_map/ppermute | solution.py:68
  642.2 33.3 %all-to-all-start.4 = ((f32[32,4,1024]{2,1,0:T(4,128)}), f32[32,4,1024]{2,1,0:T(4,128)}, u32[]{:S(2)}, u32[]{:S(2)}) async-start(f32[32,4,1024]{2,1,0:T(4,128)} %copy.152), calls=%async_computation.4 | async-start | bytes 1048576 | tf_op jit(solution)/shard_map/all_to_all | solution.py:1101
  649.7 39.2 %collective-permute-start.42 = (bf16[288,1024]{1,0:T(8,128)(2,1)S(1)}, bf16[288,1024]{1,0:T(8,128)(2,1)}, u32[]{:S(2)}, u32[]{:S(2)}) collective-permute-start(bf16[288,1024]{1,0:T(8,128)(2,1)S(1)} %fusion.10), channel_id=1, source_target_pairs={{0,16},{4,20},{8,24},{12,28},{16,0},{20,4},{24,8},{28,12},{1,17},{... | collective-permute-start | bytes 1769480 | tf_op jit(solution)/shard_map/ppermute | solution.py:146
  677.6 41.7 %all-to-all-start.5 = ((f32[32,4,1024]{2,1,0:T(4,128)}), f32[32,4,1024]{2,1,0:T(4,128)}, u32[]{:S(2)}, u32[]{:S(2)}) async-start(f32[32,4,1024]{2,1,0:T(4,128)} %broadcast_in_dim.17), calls=%async_computation.5 | async-start | bytes 1048576 | tf_op jit(solution)/shard_map/all_to_all | solution.py:1101
  (113 other events, 1521.6 us)
Sparse Core Ops, SparseCore 0:
  11.5 79.6 all-gather.4
  94.0 169.7 all-gather.2

commit v7 on v6

--- a/solution.py
+++ b/solution.py
@@ -1196,21 +1196,21 @@
     input_grad = jnp.concatenate([item[1] for item in lasts], axis=0).reshape(shape_five)
     one_sums = [item[2] for item in lasts]
     d_modulation = frame_sums(one_sums, two_sums)
-    state = early.send([lasts[-1][2]])
+    ada_width = ada_master.shape[1]
+    mod_parts = to_all(jnp.moveaxis(d_modulation.reshape(frame_total, device_total, ada_width), 1, 0))
     late = scatter_steps(
         [[([item[0] for item in lasts], hidden_one)]],
         "late",
         False,
         [d_modulation],
-        state if isinstance(state, list) else (),
+        [mod_parts],
     )
     late_state = next(late)
     late_row = late.send([])
     early_sum = finished(early, early.send(late_row))
     state = late.send([])
 
-    mod_parts = to_all(jnp.moveaxis(d_modulation.reshape(frame_total, device_total, ada_width), 1, 0))
-    mod_parts = held(mod_parts, *late_row)
+    mod_parts = held(mod_parts, *late_state)
     mod_mine = (
         jnp.sum(mod_parts.reshape(frame_devices, row_devices, frame_total, ada_width), axis=1)
         .reshape(frames_all, ada_width)

time: 930 us -> 936 us (level)
  waiting for transfers between devices: 275 us -> 290 us
    unnamed x174 -> x176, local copies, waits for them, and re-layouts: 18.8 us -> 14.8 us
  transfers between devices with their start and end apart: 63 -> 63, of which waited for: 25 -> 26; matrix products, arithmetic and copies ran while one was open for 7% -> 7% of each run, Pallas kernels for 28% -> 27%
where the time goes in v7:
time: 936 us; the launch traced here: 932 us
  Pallas kernels  408 us (44%)
  waiting for transfers between devices  290 us (31%)
  starting transfers between devices  88 us (9%)
  local copies, waits for them, and re-layouts  45.1 us (5%)
  other arithmetic  43.4 us (5%)
  blocking collectives  28.8 us (3%)
  between operations  23.4 us (2%)
    pallas_call x3, Pallas kernels, attend_back(): pl.pallas_call(functools.partial(attend_back_kernel, slots, 512), grid=(c...  107 us
    pallas_call x1, Pallas kernels, newton(): pl.pallas_call(functools.partial(newton_kernel, rows, unroll, pieces), ou...  70.1 us
    pallas_call x2, Pallas kernels, middle(): pl.pallas_call(functools.partial(middle_kernel, slots), grid=(steps,), in...  66.6 us
    pallas_call x2, Pallas kernels, attend(): pl.pallas_call(functools.partial(attend_kernel, slots, 256), grid=(group...  64.3 us
    all_to_all x6, waiting for transfers between devices, to_all(): return lax.all_to_all(value, both, split_axis=0, concat_axis=0, tiled=True)  61.3 us
    ppermute x27, waiting for transfers between devices, swap(): lax.ppermute(slots[slot], 'row', [(index, index ^ slot) for index in rang...  54.1 us
    ppermute x6, waiting for transfers between devices, frame_swap(): out.append(lax.ppermute(slots[slot], 'frame', pairs))  41.8 us
    ppermute x9, waiting for transfers between devices, joined(): lax.ppermute(send, axis, [(index, index ^ 1 << bit) for index in range(si...  39.3 us
  transfers between devices with their start and end apart: 63, of which 26 were waited for; matrix products, arithmetic and copies ran while one was open for 7% of the time, Pallas kernels for 27%

profile of v7, /device:TPU:8, one launch (start us, length us, event | category | flops | bytes accessed | tf_op | source)
XLA Modules:
  0.0 931.9 jit_solution(10925233060108213365)
XLA Ops:
  14.1 8.4 all-reduce.2
  24.1 20.3 %all_to_all.35 = f32[32,4,1024]{2,1,0:T(4,128)S(1)} all-to-all(f32[32,4,1024]{2,1,0:T(4,128)S(1)} %reshape.250), channel_id=1, replica_groups=mesh['frame'=8,'row'=4] {'frame','row'}, dimensions={0} | all-to-all | bytes 1048576 | tf_op jit(solution)/shard_map/all_to_all | solution.py:1101
  50.5 17.7 %all-to-all-done.1 = f32[32,4,1024]{2,1,0:T(4,128)S(1)} async-done(((f32[32,4,1024]{2,1,0:T(4,128)}), f32[32,4,1024]{2,1,0:T(4,128)S(1)}, u32[]{:S(2)}, u32[]{:S(2)}) %all-to-all-start.1) | async-done | bytes 524320 | tf_op jit(solution)/shard_map/all_to_all | solution.py:1101
  79.2 16.3 %all-to-all-done.2 = f32[32,16,192]{2,1,0:T(8,128)S(1)} async-done(((f32[32,16,192]{2,1,0:T(8,128)}), f32[32,16,192]{2,1,0:T(8,128)S(1)}, u32[]{:S(2)}, u32[]{:S(2)}) %all-to-all-start.2) | async-done | bytes 393248 | tf_op jit(solution)/shard_map/all_to_all | solution.py:1101
  96.9 9.1 project.2
  110.1 9.1 project.3
  130.5 31.2 %collective-permute-done.2.refs_3_ = bf16[3,512,256]{2,1,0:T(8,128)(2,1)} collective-permute-done((bf16[3,512,256]{2,1,0:T(8,128)(2,1)}, bf16[3,512,256]{2,1,0:T(8,128)(2,1)}, u32[]{:S(2)}, u32[]{:S(2)}) %collective-permute-start.2) | collective-permute-done | bytes 786464 | tf_op jit(solution)/shard_map/ppermute | solution.py:988
  161.7 32.2 %attend.2 = (bf16[512,256]{1,0:T(8,128)(2,1)}, bf16[512,256]{1,0:T(8,128)(2,1)}, bf16[512,256]{1,0:T(8,128)(2,1)}, bf16[512,256]{1,0:T(8,128)(2,1)}, f32[2048,256]{1,0:T(8,128)}, /*index=5*/f32[2048,256]{1,0:T(8,128)}) custom-call(bf16[3,512,256]{2,1,0:T(8,128)(2,1)} %get-tuple-element.106.refs_0_, bf16[3,512,256]{2,1,0:T(8,128)(2,1)} %copy-done.60, ...), custom_call_target="tpu_custom_call" | custom-call | flops 17179869184 | bytes 8388608 | tf_op jit(solution)/shard_map/attend/pallas_call | solution.py:303
  197.4 13.1 %collective-permute-done.8.refs_3_ = bf16[3,512,256]{2,1,0:T(8,128)(2,1)S(1)} collective-permute-done((bf16[3,512,256]{2,1,0:T(8,128)(2,1)}, bf16[3,512,256]{2,1,0:T(8,128)(2,1)S(1)}, u32[]{:S(2)}, u32[]{:S(2)}) %collective-permute-start.8) | collective-permute-done | bytes 786464 | tf_op jit(solution)/shard_map/ppermute | solution.py:988
  211.4 32.1 %attend.3 = (bf16[512,256]{1,0:T(8,128)(2,1)}, bf16[512,256]{1,0:T(8,128)(2,1)}, bf16[512,256]{1,0:T(8,128)(2,1)}, bf16[512,256]{1,0:T(8,128)(2,1)}, f32[2048,256]{1,0:T(8,128)}, /*index=5*/f32[2048,256]{1,0:T(8,128)}) custom-call(bf16[3,512,256]{2,1,0:T(8,128)(2,1)} %get-tuple-element.115.refs_0_, bf16[3,512,256]{2,1,0:T(8,128)(2,1)} %copy-done.57, ...), custom_call_target="tpu_custom_call" | custom-call | flops 17179869184 | bytes 8388608 | tf_op jit(solution)/shard_map/attend/pallas_call | solution.py:303
  247.0 16.8 %all-gather.3.cloned.1.call-done.wo_ref.wu_ref.wd_ref = bf16[32,288,1024]{2,1,0:T(8,128)(2,1)} async-done(((bf16[1,288,1024]{2,1,0:T(8,128)(2,1)}), bf16[32,288,1024]{2,1,0:T(8,128)(2,1)}) %all-gather.3.cloned.1.call-update) | async-done | bytes 18874384 | tf_op jit(solution)/shard_map/all_gather | solution.py:1068
  263.8 33.5 %middle.2 = (bf16[512,256]{1,0:T(8,128)(2,1)}, bf16[512,256]{1,0:T(8,128)(2,1)}, bf16[512,256]{1,0:T(8,128)(2,1)}, bf16[512,256]{1,0:T(8,128)(2,1)}, bf16[1,512,...) custom-call(s32[1]{0:T(128)} %bitcast.me_ref, ...), custom_call_target="tpu_custom_call" | custom-call | flops 19327352832 | bytes 41943040 | tf_op jit(solution)/shard_map/middle/pallas_call | solution.py:509
  298.2 33.1 %middle.3 = (bf16[512,256]{1,0:T(8,128)(2,1)}, bf16[512,256]{1,0:T(8,128)(2,1)}, bf16[512,256]{1,0:T(8,128)(2,1)}, bf16[512,256]{1,0:T(8,128)(2,1)}, bf16[1,512,...) custom-call(s32[1]{0:T(128)} %bitcast.me_ref, ...), custom_call_target="tpu_custom_call" | custom-call | flops 19327352832 | bytes 41943040 | tf_op jit(solution)/shard_map/middle/pallas_call | solution.py:509
  331.3 9.1 early_send_0.1
  340.4 11.4 %early_send_1.1 = bf16[4,4,160,1024]{3,2,1,0:T(8,128)(2,1)} custom-call(s32[4]{0:T(128)} %pad_add_fusion.number_ref, bf16[512,4096]{1,0:T(8,128)(2,1)} %get-tuple-element.131.refs_0_.refs_4_, bf16[512,4096]{1,0:T(8,128)(2,1)} %get-tuple-element.132.refs_1_.refs_5_, bf16[512,1024]{1,0:T(8,128)(2,1)} %get-tuple-element.133.refs_2_.refs_6_, ...), custom_call_target="tpu_custom_call" | custom-call | flops 5368709120 | bytes 20971520 | tf_op jit(solution)/shard_map/early_send_1/pallas_call | solution.py:729
  355.8 11.0 %collective-permute-done.12.refs_12_ = bf16[4,4,128,1024]{3,2,1,0:T(8,128)(2,1)} collective-permute-done((bf16[4,4,128,1024]{3,2,1,0:T(8,128)(2,1)}, bf16[4,4,128,1024]{3,2,1,0:T(8,128)(2,1)}, u32[]{:S(2)}, u32[]{:S(2)}) %collective-permute-start.12) | collective-permute-done | bytes 4194336 | tf_op jit(solution)/shard_map/ppermute | solution.py:88
  368.1 22.9 %early_keep.1 = (f32[2,4,288,1024]{3,2,1,0:T(8,128)}, bf16[2,4,288,1024]{3,2,1,0:T(8,128)(2,1)}) custom-call(s32[4]{0:T(128)} %pad_add_fusion.number_ref, bf16[512,4096]{1,0:T(8,128)(2,1)} %get-tuple-element.126.refs_0_, bf16[512,4096]{1,0:T(8,128)(2,1)} %get-tuple-element.127.refs_1_, bf16[512,1024]{1,0:T(8,128)(2,1)} %get-tuple-element.128.refs_2_, ...), custom_call_target="tpu_custom_call" | custom-call | flops 9663676416 | bytes 41943040 | tf_op jit(solution)/shard_map/early_keep/pallas_call | solution.py:758
  395.8 51.8 %attend_back.3 = (bf16[3,512,256]{2,1,0:T(8,128)(2,1)}, bf16[3,512,256]{2,1,0:T(8,128)(2,1)}, bf16[3,512,256]{2,1,0:T(8,128)(2,1)}, bf16[3,512,256]{2,1,0:T(8,128)(2,1)}) custom-call(bf16[3,512,256]{2,1,0:T(8,128)(2,1)} %get-tuple-element.106.refs_0_, bf16[3,512,256]{2,1,0:T(8,128)(2,1)} %copy-done.60, bf16[3,512,256]{2,1,0:T(8,128)(2,1)} %copy-done.61, ...), custom_call_target="tpu_custom_call" | custom-call | flops 42949672960 | bytes 12582912 | tf_op jit(solution)/shard_map/attend_back/pallas_call | solution.py:393
  451.9 27.5 %attend_back.4 = (bf16[3,512,128]{2,1,0:T(8,128)(2,1)}, bf16[3,512,128]{2,1,0:T(8,128)(2,1)}, bf16[3,512,128]{2,1,0:T(8,128)(2,1)}, bf16[3,512,128]{2,1,0:T(8,128)(2,1)}) custom-call(bf16[3,512,256]{2,1,0:T(8,128)(2,1)} %get-tuple-element.115.refs_0_, bf16[3,512,256]{2,1,0:T(8,128)(2,1)} %copy-done.57, bf16[3,512,256]{2,1,0:T(8,128)(2,1)} %copy-done.58, ...), custom_call_target="tpu_custom_call" | custom-call | flops 21474836480 | bytes 12582912 | tf_op jit(solution)/shard_map/attend_back/pallas_call | solution.py:393
  485.5 28.1 %attend_back.5 = (bf16[3,512,128]{2,1,0:T(8,128)(2,1)}, bf16[3,512,128]{2,1,0:T(8,128)(2,1)}, bf16[3,512,128]{2,1,0:T(8,128)(2,1)}, bf16[3,512,128]{2,1,0:T(8,128)(2,1)}) custom-call(bf16[3,512,256]{2,1,0:T(8,128)(2,1)} %get-tuple-element.115.refs_0_, bf16[3,512,256]{2,1,0:T(8,128)(2,1)} %copy-done.57, bf16[3,512,256]{2,1,0:T(8,128)(2,1)} %copy-done.58, ...), custom_call_target="tpu_custom_call" | custom-call | flops 21474836480 | bytes 12582912 | tf_op jit(solution)/shard_map/attend_back/pallas_call | solution.py:393
  514.3 9.9 %last.2 = (bf16[512,3072]{1,0:T(8,128)(2,1)}, f32[1,512,1024]{2,1,0:T(8,128)}, f32[2,2,4,1024]{3,2,1,0:T(4,128)}) custom-call(s32[1]{0:T(128)} %bitcast.me_ref, bf16[2,512,1024]{2,1,0:T(8,128)(2,1)} %bitcast.151, f32[4,4,6144]{2,1,0:T(4,128)} %reshape_reshape.4.mod_ref, f32[1024,128]{1,0:T(8,128)} %copy.139.cos_ref, ...), custom_call_target="tpu_custom_call" | custom-call | flops 3221225472 | bytes 20971520 | tf_op jit(solution)/shard_map/last/pallas_call | solution.py:590
  541.0 9.9 %last.3 = (bf16[512,3072]{1,0:T(8,128)(2,1)}, f32[1,512,1024]{2,1,0:T(8,128)}, f32[2,2,4,1024]{3,2,1,0:T(4,128)}) custom-call(s32[1]{0:T(128)} %bitcast.me_ref, bf16[2,512,1024]{2,1,0:T(8,128)(2,1)} %bitcast.152, f32[4,4,6144]{2,1,0:T(4,128)} %reshape_reshape.4.mod_ref, f32[1024,128]{1,0:T(8,128)} %copy.139.cos_ref, ...), custom_call_target="tpu_custom_call" | custom-call | flops 3221225472 | bytes 20971520 | tf_op jit(solution)/shard_map/last/pallas_call | solution.py:590
  568.1 15.3 %all-to-all-done.3 = f32[32,16,192]{2,1,0:T(8,128)S(1)} async-done(((f32[32,16,192]{2,1,0:T(8,128)}), f32[32,16,192]{2,1,0:T(8,128)S(1)}, u32[]{:S(2)}, u32[]{:S(2)}) %all-to-all-start.3) | async-done | bytes 393248 | tf_op jit(solution)/shard_map/all_to_all | solution.py:1101
  583.4 8.7 late_keep.1
  602.5 11.5 %collective-permute-done.31 = bf16[2,2,2,96,512]{4,3,1,0,2:T(8,128)(2,1)S(1)} collective-permute-done((bf16[2,2,2,96,512]{4,3,1,0,2:T(8,128)(2,1)S(1)}, bf16[2,2,2,96,512]{4,3,1,0,2:T(8,128)(2,1)S(1)}, u32[]{:S(2)}, u32[]{:S(2)}) %collective-permute-start.31) | collective-permute-done | bytes 786464 | tf_op jit(solution)/shard_map/ppermute | solution.py:68
  615.1 25.4 %collective-permute-done.32 = bf16[2,2,2,96,512]{4,3,2,1,0:T(8,128)(2,1)S(1)} collective-permute-done((bf16[2,2,2,96,512]{4,3,2,1,0:T(8,128)(2,1)S(1)}, bf16[2,2,2,96,512]{4,3,2,1,0:T(8,128)(2,1)S(1)}, u32[]{:S(2)}, u32[]{:S(2)}) %collective-permute-start.32) | collective-permute-done | bytes 786464 | tf_op jit(solution)/shard_map/ppermute | solution.py:68
  680.7 19.0 %collective-permute-done.36 = bf16[96,1024]{1,0:T(8,128)(2,1)} collective-permute-done((bf16[96,1024]{1,0:T(8,128)(2,1)}, bf16[96,1024]{1,0:T(8,128)(2,1)}, u32[]{:S(2)}, u32[]{:S(2)}) %collective-permute-start.36) | collective-permute-done | bytes 196640 | tf_op jit(solution)/shard_map/ppermute | solution.py:146
  749.9 14.0 %collective-permute-done.46 = bf16[128,1024]{1,0:T(8,128)(2,1)S(1)} collective-permute-done((bf16[128,1024]{1,0:T(8,128)(2,1)S(1)}, bf16[128,1024]{1,0:T(8,128)(2,1)S(1)}, u32[]{:S(2)}, u32[]{:S(2)}) %collective-permute-start.46) | collective-permute-done | bytes 262176 | tf_op jit(solution)/shard_map/ppermute | solution.py:997
  772.7 12.5 %collective-permute-done.48 = bf16[256,1024]{1,0:T(8,128)(2,1)S(1)} collective-permute-done((bf16[256,1024]{1,0:T(8,128)(2,1)S(1)}, bf16[256,1024]{1,0:T(8,128)(2,1)S(1)}, u32[]{:S(2)}, u32[]{:S(2)}) %collective-permute-start.48) | collective-permute-done | bytes 524320 | tf_op jit(solution)/shard_map/ppermute | solution.py:1022
  789.5 20.1 %collective-permute-done.49 = bf16[512,1024]{1,0:T(8,128)(2,1)S(1)} collective-permute-done((bf16[512,1024]{1,0:T(8,128)(2,1)S(1)}, bf16[512,1024]{1,0:T(8,128)(2,1)S(1)}, u32[]{:S(2)}, u32[]{:S(2)}) %collective-permute-start.49) | collective-permute-done | bytes 1048608 | tf_op jit(solution)/shard_map/ppermute | solution.py:1022
  820.5 70.1 %newton.1 = bf16[512,1024]{1,0:T(8,128)(2,1)} custom-call(bf16[1024,1024]{1,0:T(8,128)(2,1)} %copy-done.16, bf16[1024,1024]{1,0:T(8,128)(2,1)} %constant_dynamic-update-slice_fusion.refs_1_, bf16[1024,1024]{1,0:T(8,128)(2,1)} %collective-permute-done.50.refs_2_, bf16[1024,1024]{1,0:T(8,128)(2,1)} %collective-permute-done.51.refs_3_), custom_call_target="tpu_custom_call" | custom-call | flops 60000002048 | bytes 20000000 | tf_op jit(solution)/shard_map/newton/pallas_call | solution.py:941
  905.9 12.6 %collective-permute-done.54 = bf16[128,1024]{1,0:T(8,128)(2,1)S(1)} collective-permute-done((bf16[128,1024]{1,0:T(8,128)(2,1)S(1)}, bf16[128,1024]{1,0:T(8,128)(2,1)S(1)}, u32[]{:S(2)}, u32[]{:S(2)}) %collective-permute-start.54) | collective-permute-done | bytes 262176 | tf_op jit(solution)/shard_map/ppermute | solution.py:997
  (407 shorter events, 245.0 us)
Async XLA Ops:
  7.2 89.7 %all-gather.5.cloned.1.call-start = ((), (), s32[]{:S(2)}) async-start(), calls=%async_computation.8 | async-start | bytes 6488064 | tf_op jit(solution)/shard_map/all_gather | solution.py:1066
  9.0 254.8 %all-gather.3.cloned.1.call-start = ((), (), s32[]{:S(2)}) async-start(), calls=%async_computation.7 | async-start | bytes 19464192 | tf_op jit(solution)/shard_map/all_gather | solution.py:1068
  107.7 53.9 %collective-permute-start.2 = (bf16[3,512,256]{2,1,0:T(8,128)(2,1)}, bf16[3,512,256]{2,1,0:T(8,128)(2,1)}, u32[]{:S(2)}, u32[]{:S(2)}) collective-permute-start(bf16[3,512,256]{2,1,0:T(8,128)(2,1)} %get-tuple-element.109), channel_id=1, source_target_pairs={{0,3},{1,2},{2,1},{3,0},{4,7},{5,6},{6,5},{7,4},{8,11},{9,10},{10,... | collective-permute-start | bytes 2359304 | tf_op jit(solution)/shard_map/ppermute | solution.py:988
  119.2 75.3 %collective-permute-start.6 = (bf16[3,512,256]{2,1,0:T(8,128)(2,1)}, bf16[3,512,256]{2,1,0:T(8,128)(2,1)S(1)}, u32[]{:S(2)}, u32[]{:S(2)}) collective-permute-start(bf16[3,512,256]{2,1,0:T(8,128)(2,1)} %get-tuple-element.116), channel_id=1, source_target_pairs={{0,1},{1,0},{2,3},{3,2},{4,5},{5,4},{6,7},{7,6},{8,9},{9,8},{10,11... | collective-permute-start | bytes 2359304 | tf_op jit(solution)/shard_map/ppermute | solution.py:988
  119.5 77.9 %collective-permute-start.7 = (bf16[3,512,256]{2,1,0:T(8,128)(2,1)}, bf16[3,512,256]{2,1,0:T(8,128)(2,1)S(1)}, u32[]{:S(2)}, u32[]{:S(2)}) collective-permute-start(bf16[3,512,256]{2,1,0:T(8,128)(2,1)} %get-tuple-element.117), channel_id=1, source_target_pairs={{0,2},{1,3},{2,0},{3,1},{4,6},{5,7},{6,4},{7,5},{8,10},{9,11},{10,... | collective-permute-start | bytes 2359304 | tf_op jit(solution)/shard_map/ppermute | solution.py:988
  128.8 81.6 %collective-permute-start.8 = (bf16[3,512,256]{2,1,0:T(8,128)(2,1)}, bf16[3,512,256]{2,1,0:T(8,128)(2,1)S(1)}, u32[]{:S(2)}, u32[]{:S(2)}) collective-permute-start(bf16[3,512,256]{2,1,0:T(8,128)(2,1)} %get-tuple-element.118), channel_id=1, source_target_pairs={{0,3},{1,2},{2,1},{3,0},{4,7},{5,6},{6,5},{7,4},{8,11},{9,10},{10,... | collective-permute-start | bytes 2359304 | tf_op jit(solution)/shard_map/ppermute | solution.py:988
  193.8 51.5 %collective-permute-start.3 = (bf16[512,256]{1,0:T(8,128)(2,1)}, bf16[512,256]{1,0:T(8,128)(2,1)S(1)}, u32[]{:S(2)}, u32[]{:S(2)}) collective-permute-start(bf16[512,256]{1,0:T(8,128)(2,1)} %get-tuple-element.111), channel_id=1, source_target_pairs={{0,1},{1,0},{2,3},{3,2},{4,5},{5,4},{6,7},{7,6},{8,9},{9,8},{10,11... | collective-permute-start | bytes 786440 | tf_op jit(solution)/shard_map/ppermute | solution.py:988
  194.2 52.8 %collective-permute-start.4 = (bf16[512,256]{1,0:T(8,128)(2,1)}, bf16[512,256]{1,0:T(8,128)(2,1)S(1)}, u32[]{:S(2)}, u32[]{:S(2)}) collective-permute-start(bf16[512,256]{1,0:T(8,128)(2,1)} %get-tuple-element.112), channel_id=1, source_target_pairs={{0,2},{1,3},{2,0},{3,1},{4,6},{5,7},{6,4},{7,5},{8,10},{9,11},{10,... | collective-permute-start | bytes 786440 | tf_op jit(solution)/shard_map/ppermute | solution.py:988
  194.5 52.5 %collective-permute-start.5 = (bf16[512,256]{1,0:T(8,128)(2,1)}, bf16[512,256]{1,0:T(8,128)(2,1)S(1)}, u32[]{:S(2)}, u32[]{:S(2)}) collective-permute-start(bf16[512,256]{1,0:T(8,128)(2,1)} %get-tuple-element.113), channel_id=1, source_target_pairs={{0,3},{1,2},{2,1},{3,0},{4,7},{5,6},{6,5},{7,4},{8,11},{9,10},{10,... | collective-permute-start | bytes 786440 | tf_op jit(solution)/shard_map/ppermute | solution.py:988
  243.5 53.8 %collective-permute-start.10 = (bf16[512,256]{1,0:T(8,128)(2,1)}, bf16[512,256]{1,0:T(8,128)(2,1)S(1)}, u32[]{:S(2)}, u32[]{:S(2)}) collective-permute-start(bf16[512,256]{1,0:T(8,128)(2,1)} %get-tuple-element.121), channel_id=1, source_target_pairs={{0,2},{1,3},{2,0},{3,1},{4,6},{5,7},{6,4},{7,5},{8,10},{9,11},{10,... | collective-permute-start | bytes 786440 | tf_op jit(solution)/shard_map/ppermute | solution.py:988
  243.5 53.8 %collective-permute-start.11 = (bf16[512,256]{1,0:T(8,128)(2,1)}, bf16[512,256]{1,0:T(8,128)(2,1)S(1)}, u32[]{:S(2)}, u32[]{:S(2)}) collective-permute-start(bf16[512,256]{1,0:T(8,128)(2,1)} %get-tuple-element.122), channel_id=1, source_target_pairs={{0,3},{1,2},{2,1},{3,0},{4,7},{5,6},{6,5},{7,4},{8,11},{9,10},{10,... | collective-permute-start | bytes 786440 | tf_op jit(solution)/shard_map/ppermute | solution.py:988
  245.3 52.0 %collective-permute-start.9 = (bf16[512,256]{1,0:T(8,128)(2,1)}, bf16[512,256]{1,0:T(8,128)(2,1)S(1)}, u32[]{:S(2)}, u32[]{:S(2)}) collective-permute-start(bf16[512,256]{1,0:T(8,128)(2,1)} %get-tuple-element.120), channel_id=1, source_target_pairs={{0,1},{1,0},{2,3},{3,2},{4,5},{5,4},{6,7},{7,6},{8,9},{9,8},{10,11... | collective-permute-start | bytes 786440 | tf_op jit(solution)/shard_map/ppermute | solution.py:988
  352.3 38.7 %collective-permute-start.14 = (bf16[512,256]{1,0:T(8,128)(2,1)S(1)}, bf16[512,256]{1,0:T(8,128)(2,1)S(1)}, u32[]{:S(2)}, u32[]{:S(2)}) collective-permute-start(bf16[512,256]{1,0:T(8,128)(2,1)S(1)} %copy-done.70), channel_id=1, source_target_pairs={{0,1},{1,0},{2,3},{3,2},{4,5},{5,4},{6,7},{7,6},{8,9},{9,8},{10,11... | collective-permute-start | bytes 786440 | tf_op jit(solution)/shard_map/ppermute | solution.py:988
  352.9 40.5 %collective-permute-start.15 = (bf16[512,256]{1,0:T(8,128)(2,1)S(1)}, bf16[512,256]{1,0:T(8,128)(2,1)S(1)}, u32[]{:S(2)}, u32[]{:S(2)}) collective-permute-start(bf16[512,256]{1,0:T(8,128)(2,1)S(1)} %copy-done.68), channel_id=1, source_target_pairs={{0,2},{1,3},{2,0},{3,1},{4,6},{5,7},{6,4},{7,5},{8,10},{9,11},{10,... | collective-permute-start | bytes 786440 | tf_op jit(solution)/shard_map/ppermute | solution.py:988
  353.5 41.6 %collective-permute-start.16 = (bf16[512,256]{1,0:T(8,128)(2,1)S(1)}, bf16[512,256]{1,0:T(8,128)(2,1)S(1)}, u32[]{:S(2)}, u32[]{:S(2)}) collective-permute-start(bf16[512,256]{1,0:T(8,128)(2,1)S(1)} %copy-done.65), channel_id=1, source_target_pairs={{0,3},{1,2},{2,1},{3,0},{4,7},{5,6},{6,5},{7,4},{8,11},{9,10},{10,... | collective-permute-start | bytes 786440 | tf_op jit(solution)/shard_map/ppermute | solution.py:988
  366.8 81.2 %collective-permute-start.20 = (bf16[512,256]{1,0:T(8,128)(2,1)S(1)}, bf16[512,256]{1,0:T(8,128)(2,1)S(1)}, u32[]{:S(2)}, u32[]{:S(2)}) collective-permute-start(bf16[512,256]{1,0:T(8,128)(2,1)S(1)} %copy-done.67), channel_id=1, source_target_pairs={{0,1},{1,0},{2,3},{3,2},{4,5},{5,4},{6,7},{7,6},{8,9},{9,8},{10,11... | collective-permute-start | bytes 786440 | tf_op jit(solution)/shard_map/ppermute | solution.py:988
  367.4 81.7 %collective-permute-start.21 = (bf16[512,256]{1,0:T(8,128)(2,1)S(1)}, bf16[512,256]{1,0:T(8,128)(2,1)S(1)}, u32[]{:S(2)}, u32[]{:S(2)}) collective-permute-start(bf16[512,256]{1,0:T(8,128)(2,1)S(1)} %copy-done.64), channel_id=1, source_target_pairs={{0,2},{1,3},{2,0},{3,1},{4,6},{5,7},{6,4},{7,5},{8,10},{9,11},{10,... | collective-permute-start | bytes 786440 | tf_op jit(solution)/shard_map/ppermute | solution.py:988
  391.0 60.2 %collective-permute-start.22 = (bf16[512,256]{1,0:T(8,128)(2,1)S(1)}, bf16[512,256]{1,0:T(8,128)(2,1)S(1)}, u32[]{:S(2)}, u32[]{:S(2)}) collective-permute-start(bf16[512,256]{1,0:T(8,128)(2,1)S(1)} %copy-done.63), channel_id=1, source_target_pairs={{0,3},{1,2},{2,1},{3,0},{4,7},{5,6},{6,5},{7,4},{8,11},{9,10},{10,... | collective-permute-start | bytes 786440 | tf_op jit(solution)/shard_map/ppermute | solution.py:988
  393.4 130.8 %collective-permute-start.23 = (bf16[2,4,288,1024]{3,2,1,0:T(8,128)(2,1)}, bf16[2,4,288,1024]{3,2,1,0:T(8,128)(2,1)}, u32[]{:S(2)}, u32[]{:S(2)}) collective-permute-start(bf16[2,4,288,1024]{3,2,1,0:T(8,128)(2,1)} %get-tuple-element.140), channel_id=1, source_target_pairs={{0,8},{4,12},{8,0},{12,4},{16,24},{20,28},{24,16},{28,20},{1,9},{5... | collective-permute-start | bytes 14155784 | tf_op jit(solution)/shard_map/ppermute | solution.py:68
  448.1 32.7 %collective-permute-start.18 = (bf16[3,512,256]{2,1,0:T(8,128)(2,1)}, bf16[3,512,256]{2,1,0:T(8,128)(2,1)S(1)}, u32[]{:S(2)}, u32[]{:S(2)}) collective-permute-start(bf16[3,512,256]{2,1,0:T(8,128)(2,1)} %get-tuple-element.149), channel_id=1, source_target_pairs={{0,2},{1,3},{2,0},{3,1},{4,6},{5,7},{6,4},{7,5},{8,10},{9,11},{10,... | collective-permute-start | bytes 2359304 | tf_op jit(solution)/shard_map/ppermute | solution.py:988
  449.1 36.4 %collective-permute-start.19 = (bf16[3,512,256]{2,1,0:T(8,128)(2,1)}, bf16[3,512,256]{2,1,0:T(8,128)(2,1)S(1)}, u32[]{:S(2)}, u32[]{:S(2)}) collective-permute-start(bf16[3,512,256]{2,1,0:T(8,128)(2,1)} %get-tuple-element.150), channel_id=1, source_target_pairs={{0,3},{1,2},{2,1},{3,0},{4,7},{5,6},{6,5},{7,4},{8,11},{9,10},{10,... | collective-permute-start | bytes 2359304 | tf_op jit(solution)/shard_map/ppermute | solution.py:988
  479.4 52.6 %collective-permute-start.24 = (bf16[3,512,128]{2,1,0:T(8,128)(2,1)}, bf16[3,512,128]{2,1,0:T(8,128)(2,1)S(1)}, u32[]{:S(2)}, u32[]{:S(2)}) collective-permute-start(bf16[3,512,128]{2,1,0:T(8,128)(2,1)} %get-tuple-element.165), channel_id=1, source_target_pairs={{0,1},{1,0},{2,3},{3,2},{4,5},{5,4},{6,7},{7,6},{8,9},{9,8},{10,11... | collective-permute-start | bytes 1179656 | tf_op jit(solution)/shard_map/ppermute | solution.py:988
  479.7 58.3 %collective-permute-start.25 = (bf16[3,512,128]{2,1,0:T(8,128)(2,1)}, bf16[3,512,128]{2,1,0:T(8,128)(2,1)}, u32[]{:S(2)}, u32[]{:S(2)}) collective-permute-start(bf16[3,512,128]{2,1,0:T(8,128)(2,1)} %get-tuple-element.166), channel_id=1, source_target_pairs={{0,2},{1,3},{2,0},{3,1},{4,6},{5,7},{6,4},{7,5},{8,10},{9,11},{10,... | collective-permute-start | bytes 1179656 | tf_op jit(solution)/shard_map/ppermute | solution.py:988
  480.8 58.5 %collective-permute-start.26 = (bf16[3,512,128]{2,1,0:T(8,128)(2,1)}, bf16[3,512,128]{2,1,0:T(8,128)(2,1)}, u32[]{:S(2)}, u32[]{:S(2)}) collective-permute-start(bf16[3,512,128]{2,1,0:T(8,128)(2,1)} %get-tuple-element.167), channel_id=1, source_target_pairs={{0,3},{1,2},{2,1},{3,0},{4,7},{5,6},{6,5},{7,4},{8,11},{9,10},{10,... | collective-permute-start | bytes 1179656 | tf_op jit(solution)/shard_map/ppermute | solution.py:988
  594.6 49.0 %collective-permute-start.40 = (bf16[2,2,288,512]{3,2,0,1:T(8,128)(2,1)}, bf16[2,2,288,512]{3,2,0,1:T(8,128)(2,1)S(1)}, u32[]{:S(2)}, u32[]{:S(2)}) collective-permute-start(bf16[2,2,288,512]{3,2,0,1:T(8,128)(2,1)} %fusion.1), channel_id=1, source_target_pairs={{0,2},{1,3},{2,0},{3,1},{4,6},{5,7},{6,4},{7,5},{8,10},{9,11},{10,... | collective-permute-start | bytes 3538952 | tf_op jit(solution)/shard_map/ppermute | solution.py:68
  595.5 49.6 %collective-permute-start.38 = (bf16[2,2,288,512]{3,2,0,1:T(8,128)(2,1)}, bf16[2,2,288,512]{3,2,0,1:T(8,128)(2,1)S(1)}, u32[]{:S(2)}, u32[]{:S(2)}) collective-permute-start(bf16[2,2,288,512]{3,2,0,1:T(8,128)(2,1)} %fusion), channel_id=1, source_target_pairs={{0,1},{1,0},{2,3},{3,2},{4,5},{5,4},{6,7},{7,6},{8,9},{9,8},{10,11... | collective-permute-start | bytes 3538952 | tf_op jit(solution)/shard_map/ppermute | solution.py:68
  596.6 43.9 %collective-permute-start.32 = (bf16[2,2,2,96,512]{4,3,2,1,0:T(8,128)(2,1)S(1)}, bf16[2,2,2,96,512]{4,3,2,1,0:T(8,128)(2,1)S(1)}, u32[]{:S(2)}, u32[]{:S(2)}) collective-permute-start(bf16[2,2,2,96,512]{4,3,2,1,0:T(8,128)(2,1)S(1)} %bitcast.170), channel_id=1, source_target_pairs={{0,2},{1,3},{2,0},{3,1},{4,6},{5,7},{6,4},{7,5},{8,10},{9,11},{10,... | collective-permute-start | bytes 2359304 | tf_op jit(solution)/shard_map/ppermute | solution.py:68
  615.1 42.7 %collective-permute-start.33 = (bf16[2,2,96,512]{3,2,1,0:T(8,128)(2,1)}, bf16[2,2,96,512]{3,2,1,0:T(8,128)(2,1)}, u32[]{:S(2)}, u32[]{:S(2)}) collective-permute-start(bf16[2,2,96,512]{3,2,1,0:T(8,128)(2,1)} %fusion.12), channel_id=1, source_target_pairs={{0,2},{1,3},{2,0},{3,1},{4,6},{5,7},{6,4},{7,5},{8,10},{9,11},{10,... | collective-permute-start | bytes 1179656 | tf_op jit(solution)/shard_map/ppermute | solution.py:68
  661.5 38.2 %collective-permute-start.36 = (bf16[96,1024]{1,0:T(8,128)(2,1)}, bf16[96,1024]{1,0:T(8,128)(2,1)}, u32[]{:S(2)}, u32[]{:S(2)}) collective-permute-start(bf16[96,1024]{1,0:T(8,128)(2,1)} %get-tuple-element.336), channel_id=1, source_target_pairs={{0,16},{4,20},{8,24},{12,28},{16,0},{20,4},{24,8},{28,12},{1,17},{... | collective-permute-start | bytes 589832 | tf_op jit(solution)/shard_map/ppermute | solution.py:146
  664.1 42.6 %collective-permute-start.37 = (bf16[96,1024]{1,0:T(8,128)(2,1)}, bf16[96,1024]{1,0:T(8,128)(2,1)}, u32[]{:S(2)}, u32[]{:S(2)}) collective-permute-start(bf16[96,1024]{1,0:T(8,128)(2,1)} %get-tuple-element.335), channel_id=1, source_target_pairs={{0,24},{4,28},{8,16},{12,20},{16,8},{20,12},{24,0},{28,4},{1,25},{... | collective-permute-start | bytes 589832 | tf_op jit(solution)/shard_map/ppermute | solution.py:146
  669.6 47.3 %collective-permute-start.42 = (bf16[288,1024]{1,0:T(8,128)(2,1)S(1)}, bf16[288,1024]{1,0:T(8,128)(2,1)}, u32[]{:S(2)}, u32[]{:S(2)}) collective-permute-start(bf16[288,1024]{1,0:T(8,128)(2,1)S(1)} %fusion.10), channel_id=1, source_target_pairs={{0,16},{4,20},{8,24},{12,28},{16,0},{20,4},{24,8},{28,12},{1,17},{... | collective-permute-start | bytes 1769480 | tf_op jit(solution)/shard_map/ppermute | solution.py:146
  675.2 51.0 %all-to-all-start.5 = ((f32[32,4,1024]{2,1,0:T(4,128)}), f32[32,4,1024]{2,1,0:T(4,128)}, u32[]{:S(2)}, u32[]{:S(2)}) async-start(f32[32,4,1024]{2,1,0:T(4,128)} %broadcast_in_dim.17), calls=%async_computation.5 | async-start | bytes 1048576 | tf_op jit(solution)/shard_map/all_to_all | solution.py:1101
  (114 other events, 1471.2 us)
Sparse Core Ops, SparseCore 0:
  11.5 79.5 all-gather.4
  94.0 169.7 all-gather.2
